TPU v7x, 32 devices: a whole 2x2x4 slice. The times are simulated.
32 devices in a mesh: img: 4 (over y, x), row: 4 (over z), col: 2 (over core).
Axes of the slice: x: 2, y: 2, z: 4, core: 2. Of those that a mesh axis runs over, the one named last changes fastest.
Arguments:
- tokens: bfloat16 [4, 128, 32, 1152], P('img', 'row', 'col'), may hold values from -30 to 30
- qkv_weight: bfloat16 [1152, 1728], replicated, may hold values from -1 to 1
- out_weight: bfloat16 [1152, 576], replicated, may hold values from -0.25 to 0.25
- upstream: bfloat16 [4, 128, 32, 1152], P('img', 'row', 'col'), may hold values from -6 to 6
Outputs:
- sublayer_out: bfloat16 [4, 128, 32, 1152], P('img', 'row', 'col')
- tokens_grad: bfloat16 [4, 128, 32, 1152], P('img', 'row', 'col')
- qkv_grad: float32 [1152, 1728], P(('row', 'col'))
- out_grad: float32 [1152, 576], P(('row', 'col'))
All inputs are finite; a program needn't handle non-finite values.
Results may differ from a plain program's by a relative error of at most 0.015.
Values may be sent and summed in bfloat16 or wider, within the bound.
No kernel may reach another device: no remote copies, remote signals or barrier semaphores. Data moves between devices by JAX's collectives and lax.ppermute only.
A program may use at most 128 MiB of HBM per device.

v0:
```python
import jax
import jax.numpy as jnp
from jax import lax
from jax.sharding import PartitionSpec as P

H = 8
DH = 72
REACH = 8
WINDOW = 17


masked_score = -1e30
query_side = 8


def with_halo(block, sides, width):
    for axis, dim in sides:
        count = lax.axis_size(axis)
        forward = [(i, i + 1) for i in range(count - 1)]
        backward = [(target, source) for source, target in forward]
        low = lax.ppermute(
            lax.slice_in_dim(block, block.shape[dim] - width, None, axis=dim), axis, forward
        )
        high = lax.ppermute(lax.slice_in_dim(block, 0, width, axis=dim), axis, backward)
        block = jnp.concatenate([low, block, high], axis=dim)
    return block


def passed_along(shard, axis, by):
    devices = lax.axis_size(axis)
    pairs = [(i, i + by) for i in range(devices) if 0 <= i + by < devices]
    return lax.ppermute(shard, axis, pairs)


def window_starts(first_row, count, extent):
    places = first_row + jnp.arange(count, dtype=jnp.int32)
    return jnp.clip(places - REACH, 0, extent - WINDOW)


def strip_setup(strip_id, tile_rows, tile_cols):
    band_side = query_side + 2 * REACH
    ext_cols = tile_cols + 2 * REACH
    row_first = lax.axis_index("row") * tile_rows
    col_first = lax.axis_index("col") * tile_cols
    frame_rows = tile_rows * lax.axis_size("row")
    frame_cols = tile_cols * lax.axis_size("col")
    glob_row = row_first + strip_id * query_side
    band_row = jnp.clip(glob_row - REACH, 0, frame_rows - WINDOW)
    row_starts = window_starts(glob_row, query_side, frame_rows)
    col_starts = window_starts(col_first, tile_cols, frame_cols)
    key_rows = band_row + jnp.arange(band_side, dtype=jnp.int32)
    key_cols = col_first - REACH + jnp.arange(ext_cols, dtype=jnp.int32)
    row_ok = (key_rows[None, :] >= row_starts[:, None]) & (
        key_rows[None, :] <= row_starts[:, None] + 2 * REACH
    )
    col_ok = (key_cols[None, :] >= col_starts[:, None]) & (
        key_cols[None, :] <= col_starts[:, None] + 2 * REACH
    )
    joined = row_ok[:, None, :, None] & col_ok[None, :, None, :]
    in_window = joined.reshape(query_side * tile_cols, band_side * ext_cols)
    return (band_row - row_first + REACH, in_window)


def cut_band(extended, band_top):
    band_side = query_side + 2 * REACH
    band = lax.dynamic_slice_in_dim(extended, band_top, band_side, 0)
    band = band.reshape(band_side * extended.shape[1], 2, H, DH)
    return (band[:, 0], band[:, 1])


def strip_probs(query_blk, key_band, in_window):
    scores = jnp.einsum(
        "qhd,khd->hqk", query_blk, key_band, preferred_element_type=jnp.float32
    ) * DH ** (-0.5)
    scores = jnp.where(in_window[None], scores, masked_score)
    row_max = jnp.max(scores, axis=2, keepdims=True)
    shifted = jnp.exp(scores - row_max)
    return shifted / jnp.sum(shifted, axis=2, keepdims=True)


def local(tokens, qkv_weight, out_weight, upstream):
    tile_rows = tokens.shape[1]
    tile_cols = tokens.shape[2]
    width = tokens.shape[3]
    token_count = tile_rows * tile_cols
    inner = H * DH
    ext_rows = tile_rows + 2 * REACH
    ext_cols = tile_cols + 2 * REACH
    band_side = query_side + 2 * REACH
    strips = tile_rows // query_side
    strip_tokens = query_side * tile_cols
    strip_ids = jnp.arange(strips, dtype=jnp.int32)
    token_rows = tokens.reshape(token_count, width)
    grad_rows = upstream.reshape(token_count, width)
    projected = jnp.dot(token_rows, qkv_weight, preferred_element_type=jnp.float32).astype(
        jnp.bfloat16
    )
    query_strips = projected[:, :inner].reshape(strips, strip_tokens, H, DH)
    keyvals = projected[:, inner:].reshape(1, tile_rows, tile_cols, 2 * inner)
    extended = with_halo(keyvals, (("row", 1), ("col", 2)), REACH)
    extended = extended.reshape(ext_rows, ext_cols, 2 * inner)

    def forward_strip(operands):
        strip_id, query_blk = operands
        band_top, in_window = strip_setup(strip_id, tile_rows, tile_cols)
        key_band, value_band = cut_band(extended, band_top)
        attn_prob = strip_probs(query_blk, key_band, in_window)
        attended_blk = jnp.einsum(
            "hqk,khd->qhd",
            attn_prob.astype(jnp.bfloat16),
            value_band,
            preferred_element_type=jnp.float32,
        )
        return (attended_blk.astype(jnp.bfloat16), attn_prob)

    attended_strips, kept_probs = lax.map(forward_strip, (strip_ids, query_strips))
    attended = attended_strips.reshape(token_count, inner)
    sublayer_out = lax.dot_general(
        attended, out_weight, (((1,), (1,)), ((), ())), preferred_element_type=jnp.float32
    ).astype(jnp.bfloat16)
    grad_att = jnp.dot(grad_rows, out_weight, preferred_element_type=jnp.float32).astype(
        jnp.bfloat16
    )
    grad_strips = grad_att.reshape(strips, strip_tokens, H, DH)

    def backward_strip(accum, strip_id, query_blk, grad_blk, attn_prob):
        band_top, in_window = strip_setup(strip_id, tile_rows, tile_cols)
        key_band, value_band = cut_band(extended, band_top)
        prob_low = attn_prob.astype(jnp.bfloat16)
        dprob = jnp.einsum("qhd,khd->hqk", grad_blk, value_band, preferred_element_type=jnp.float32)
        row_dot = jnp.sum(attn_prob * dprob, axis=2, keepdims=True)
        dscore = (attn_prob * (dprob - row_dot) * DH ** (-0.5)).astype(jnp.bfloat16)
        dquery = jnp.einsum("hqk,khd->qhd", dscore, key_band, preferred_element_type=jnp.float32)
        dkey = jnp.einsum("hqk,qhd->khd", dscore, query_blk, preferred_element_type=jnp.float32)
        dvalue = jnp.einsum("hqk,qhd->khd", prob_low, grad_blk, preferred_element_type=jnp.float32)
        band_grad = jnp.concatenate(
            [dkey.reshape(band_side, ext_cols, inner), dvalue.reshape(band_side, ext_cols, inner)],
            axis=2,
        )
        current = lax.dynamic_slice_in_dim(accum, band_top, band_side, 0)
        accum = lax.dynamic_update_slice_in_dim(accum, current + band_grad, band_top, 0)
        return (accum, dquery)

    empty_grads = jnp.zeros((ext_rows, ext_cols, 2 * inner), jnp.float32)

    def backward_kept(accum, operands):
        strip_id, query_blk, grad_blk, attn_prob = operands
        return backward_strip(accum, strip_id, query_blk, grad_blk, attn_prob)

    returned, dquery_strips = lax.scan(
        backward_kept, empty_grads, (strip_ids, query_strips, grad_strips, kept_probs)
    )
    dquery_rows = dquery_strips.reshape(token_count, inner)
    top_band = returned[:REACH]
    bottom_band = returned[ext_rows - REACH :]
    from_below = passed_along(top_band.astype(jnp.bfloat16), "row", -1).astype(top_band.dtype)
    from_above = passed_along(bottom_band.astype(jnp.bfloat16), "row", 1).astype(bottom_band.dtype)
    inner_rows = returned[REACH : ext_rows - REACH]
    inner_rows = inner_rows.at[:REACH].add(from_above).at[tile_rows - REACH :].add(from_below)
    left_band = inner_rows[:, :REACH]
    right_band = inner_rows[:, ext_cols - REACH :]
    from_right = passed_along(left_band.astype(jnp.bfloat16), "col", -1).astype(left_band.dtype)
    from_left = passed_along(right_band.astype(jnp.bfloat16), "col", 1).astype(right_band.dtype)
    middle = inner_rows[:, REACH : ext_cols - REACH]
    middle = middle.at[:, :REACH].add(from_left).at[:, tile_cols - REACH :].add(from_right)
    dqkv = jnp.concatenate([dquery_rows, middle.reshape(token_count, 2 * inner)], axis=1).astype(
        jnp.bfloat16
    )
    tokens_grad = lax.dot_general(
        dqkv, qkv_weight, (((1,), (1,)), ((), ())), preferred_element_type=jnp.float32
    ).astype(jnp.bfloat16)
    first_term = lax.dot_general(
        token_rows, dqkv, (((0,), (0,)), ((), ())), preferred_element_type=jnp.float32
    )
    second_term = lax.dot_general(
        grad_rows, attended, (((0,), (0,)), ((), ())), preferred_element_type=jnp.float32
    )
    shares = lax.psum_scatter(
        jnp.concatenate([first_term, second_term], axis=1),
        ("row", "col"),
        scatter_dimension=0,
        tiled=True,
    )
    shares = lax.psum(shares.astype(jnp.bfloat16), "img").astype(jnp.float32)
    return (
        sublayer_out.reshape(tokens.shape),
        tokens_grad.reshape(tokens.shape),
        shares[:, : 3 * inner],
        shares[:, 3 * inner :],
    )


def solution(mesh):
    return jax.shard_map(
        local,
        mesh=mesh,
        in_specs=(P("img", "row", "col", None), P(), P(), P("img", "row", "col", None)),
        out_specs=(
            P("img", "row", "col", None),
            P("img", "row", "col", None),
            P(("row", "col"), None),
            P(("row", "col"), None),
        ),
        check_vma=False,
    )
```

profile of v0, /device:TPU:0, one launch (start us, length us, event | category | flops | bytes accessed | tf_op | source)
XLA Modules:
  0.0 659.5 jit_solution(17657073562442343007)
XLA Ops:
  7.2 5.1 convolution_convert_fusion
  16.3 4.9 collective-permute-start
  22.6 4.9 collective-permute-done
  27.5 4.1 collective-permute-done.1
  46.2 4.0 maximum_bitcast_fusion
  50.2 127.8 %while.33 = (s32[]{:T(128)}, bf16[4,128,8,72]{1,3,2,0:T(8,128)(2,1)}, f32[4,8,128,768]{3,2,1,0:T(8,128)}, s32[4]{0:T(128)S(1)}, bf16[48,32,1152]{2,1,0:T(8,128)(...) while((s32[]{:T(128)}, ...), condition=%wide.region_3.4_spmd, body=%wide.region_0.3_spmd.sunk | while | flops 233745376 | bytes 48087144 | solution.py:116
  53.1 6.4 reshape.375
  70.0 4.3 fusion.107
  78.6 3.6 fusion.108
  85.1 6.4 reshape.375
  101.9 4.3 fusion.107
  110.6 3.6 fusion.108
  117.1 6.4 reshape.375
  129.4 3.5 fusion.106
  133.9 4.3 fusion.107
  142.6 3.6 fusion.108
  149.0 6.4 reshape.375
  161.4 3.5 fusion.106
  165.9 4.3 fusion.107
  174.5 3.6 fusion.108
  178.6 3.7 broadcast_in_dim.71
  182.3 227.2 %while.34 = (s32[]{:T(128)}, f32[48,32,1152]{2,1,0:T(8,128)}, bf16[4,128,8,72]{1,3,2,0:T(8,128)(2,1)}, s32[4]{0:T(128)}, bf16[4,128,8,72]{1,3,2,0:T(8,128)(2,1)}...) while((s32[]{:T(128)}, f32[48,32,1152]{2,1,0:T(8,128)}, ...), condition=%wide.region_6.7_spmd, body=%wide.region_4.6_spmd.sunk | while | flops 571934464 | bytes 75894736 | solution.py:150
  185.8 6.4 reshape.377
  192.2 3.8 fusion.117
  198.9 4.3 fusion.118
  203.2 3.8 fusion.119
  212.9 4.1 reshape.378
  216.9 3.6 fusion.116
  223.9 4.1 reshape.376
  227.9 5.7 fusion.120
  242.6 6.4 reshape.377
  249.0 3.8 fusion.117
  255.7 4.3 fusion.118
  260.0 3.8 fusion.119
  269.6 4.1 reshape.378
  273.7 3.6 fusion.116
  280.7 4.1 reshape.376
  284.7 5.7 fusion.120
  299.3 6.4 reshape.377
  305.7 3.8 fusion.117
  312.5 4.3 fusion.118
  316.8 3.8 fusion.119
  326.4 4.1 reshape.378
  330.5 3.6 fusion.116
  337.4 4.1 reshape.376
  341.5 5.7 fusion.120
  356.2 6.4 reshape.377
  362.5 3.8 fusion.117
  369.3 4.3 fusion.118
  373.6 3.8 fusion.119
  383.2 4.1 reshape.378
  387.3 3.6 fusion.116
  394.2 4.1 reshape.376
  398.3 5.7 fusion.120
  409.4 3.6 convert.17
  413.1 3.7 collective-permute-start.4
  418.5 11.2 %collective-permute-done.4 = bf16[8,32,1152]{2,1,0:T(8,128)(2,1)S(1)} collective-permute-done((bf16[8,32,1152]{2,1,0:T(8,128)(2,1)S(1)}, bf16[8,32,1152]{2,1,0:T(8,128)(2,1)S(1)}, u32[]{:S(2)}, u32[]{:S(2)}) %collective-permute-start.4) | collective-permute-done | bytes 589856 | tf_op jit(solution)/shard_map/ppermute | solution.py:32
  429.8 4.6 collective-permute-done.5
  452.6 6.0 convolution_bitcast_fusion.2
  458.6 8.8 %pad_maximum_fusion = f32[1152,2304]{0,1:T(8,128)} fusion(f32[1152,576]{0,1:T(8,128)} %convolution_bitcast_fusion.3, f32[1152,1728]{0,1:T(8,128)} %convolution_bitcast_fusion.2), kind=kLoop, calls=%fused_computation.62 | loop fusion | flops 2654208 | bytes 21233664 | tf_op jit(solution)/shard_map/concatenate | solution.py:179
  467.4 12.7 %copy.44 = f32[1152,2304]{1,0:T(8,128)} copy(f32[1152,2304]{0,1:T(8,128)} %pad_maximum_fusion) | data formatting | bytes 21233664
  480.1 111.5 %reduce-scatter.4.cloned.1.call-done = f32[144,2304]{1,0:T(8,128)} async-done(((f32[1152,2304]{1,0:T(8,128)}), f32[144,2304]{1,0:T(8,128)}) %reduce-scatter.4.cloned.1.call-update) | async-done | bytes 1327120
  596.8 3.6 convolution_convert_fusion.1
  600.4 47.5 %all-reduce.2.cloned.1.call-done = bf16[144,2304]{0,1:T(8,128)(2,1)} async-done(((bf16[144,2304]{0,1:T(8,128)(2,1)}), bf16[144,2304]{0,1:T(8,128)(2,1)}) %all-reduce.2.cloned.1.call-update) | async-done | bytes 663568 | tf_op jit(solution)/shard_map/psum | solution.py:184
  (208 shorter events, 192.9 us)
Async XLA Ops:
  7.2 33.5 %copy-start = (bf16[1152,576]{0,1:T(8,128)(2,1)S(1)}, bf16[1152,576]{0,1:T(8,128)(2,1)}, u32[]{:S(2)}) copy-start(bf16[1152,576]{0,1:T(8,128)(2,1)} %param.18) | copy-start | bytes 3981316
  7.2 584.5 %reduce-scatter.4.cloned.1.call-start = ((), (), s32[]{:S(2)}) async-start(), calls=%async_computation.2 | async-start | bytes 11943936
  12.3 1.2 copy-start.5
  16.3 11.2 %collective-permute-start = (bf16[1,8,16,1152]{3,2,1,0:T(8,128)(2,1)S(1)}, bf16[1,8,16,1152]{3,2,1,0:T(8,128)(2,1)S(1)}, u32[]{:S(2)}, u32[]{:S(2)}) collective-permute-start(bf16[1,8,16,1152]{3,2,1,0:T(8,128)(2,1)S(1)} %get-tuple-element.358), channel_id=1, source_target_pairs={{0,2},{2,4},{4,6},{1,3},{3,5},{5,7},{8,10},{10,12},{12,14},{9,11},... | collective-permute-start | bytes 884744 | tf_op jit(solution)/shard_map/ppermute | solution.py:21
  21.3 10.4 %collective-permute-start.1 = (bf16[1,8,16,1152]{3,2,1,0:T(8,128)(2,1)S(1)}, bf16[1,8,16,1152]{3,2,1,0:T(8,128)(2,1)S(1)}, u32[]{:S(2)}, u32[]{:S(2)}) collective-permute-start(bf16[1,8,16,1152]{3,2,1,0:T(8,128)(2,1)S(1)} %get-tuple-element.359), channel_id=1, source_target_pairs={{2,0},{4,2},{6,4},{3,1},{5,3},{7,5},{10,8},{12,10},{14,12},{11,9},... | collective-permute-start | bytes 884744 | tf_op jit(solution)/shard_map/ppermute | solution.py:24
  31.7 0.7 copy-start.6
  32.6 5.1 slice-start.2
  34.0 12.2 %collective-permute-start.2 = (bf16[1,48,8,1152]{3,2,1,0:T(8,128)(2,1)}, bf16[1,48,8,1152]{3,2,1,0:T(8,128)(2,1)}, u32[]{:S(2)}, u32[]{:S(2)}) collective-permute-start(bf16[1,48,8,1152]{3,2,1,0:T(8,128)(2,1)} %get-tuple-element.356), channel_id=1, source_target_pairs={{0,1},{2,3},{4,5},{6,7},{8,9},{10,11},{12,13},{14,15},{16,17},{18,... | collective-permute-start | bytes 2654216 | tf_op jit(solution)/shard_map/ppermute | solution.py:21
  36.2 10.0 %collective-permute-start.3 = (bf16[1,48,8,1152]{3,2,1,0:T(8,128)(2,1)}, bf16[1,48,8,1152]{3,2,1,0:T(8,128)(2,1)}, u32[]{:S(2)}, u32[]{:S(2)}) collective-permute-start(bf16[1,48,8,1152]{3,2,1,0:T(8,128)(2,1)} %get-tuple-element.357), channel_id=1, source_target_pairs={{1,0},{3,2},{5,4},{7,6},{9,8},{11,10},{13,12},{15,14},{17,16},{19,... | collective-permute-start | bytes 2654216 | tf_op jit(solution)/shard_map/ppermute | solution.py:24
  74.2 2.7 copy-start.2
  106.2 2.7 copy-start.2
  138.2 2.6 copy-start.2
  170.2 2.6 copy-start.2
  192.2 6.7 %copy-start.4 = (bf16[4,128,8,72]{1,3,2,0:T(8,128)(2,1)S(1)}, bf16[4,128,8,72]{1,3,2,0:T(8,128)(2,1)}, u32[]{:S(2)}) copy-start(bf16[4,128,8,72]{1,3,2,0:T(8,128)(2,1)} %get-tuple-element.559) | copy-start | bytes 1769476 | tf_op jit(solution)/shard_map/while
  198.0 0.9 copy-start.1
  227.9 8.4 %copy-start.10 = (bf16[4,128,8,72]{1,3,2,0:T(8,128)(2,1)S(1)}, bf16[4,128,8,72]{1,3,2,0:T(8,128)(2,1)}, u32[]{:S(2)}) copy-start(bf16[4,128,8,72]{1,3,2,0:T(8,128)(2,1)} %get-tuple-element.537) | copy-start | bytes 1769476 | tf_op jit(solution)/shard_map/while
  238.2 0.8 copy-start.11
  249.0 6.7 %copy-start.4 = (bf16[4,128,8,72]{1,3,2,0:T(8,128)(2,1)S(1)}, bf16[4,128,8,72]{1,3,2,0:T(8,128)(2,1)}, u32[]{:S(2)}) copy-start(bf16[4,128,8,72]{1,3,2,0:T(8,128)(2,1)} %get-tuple-element.559) | copy-start | bytes 1769476 | tf_op jit(solution)/shard_map/while
  254.8 0.9 copy-start.1
  284.7 8.4 %copy-start.10 = (bf16[4,128,8,72]{1,3,2,0:T(8,128)(2,1)S(1)}, bf16[4,128,8,72]{1,3,2,0:T(8,128)(2,1)}, u32[]{:S(2)}) copy-start(bf16[4,128,8,72]{1,3,2,0:T(8,128)(2,1)} %get-tuple-element.537) | copy-start | bytes 1769476 | tf_op jit(solution)/shard_map/while
  295.0 0.8 copy-start.11
  305.7 6.7 %copy-start.4 = (bf16[4,128,8,72]{1,3,2,0:T(8,128)(2,1)S(1)}, bf16[4,128,8,72]{1,3,2,0:T(8,128)(2,1)}, u32[]{:S(2)}) copy-start(bf16[4,128,8,72]{1,3,2,0:T(8,128)(2,1)} %get-tuple-element.559) | copy-start | bytes 1769476 | tf_op jit(solution)/shard_map/while
  311.5 0.9 copy-start.1
  341.5 8.5 %copy-start.10 = (bf16[4,128,8,72]{1,3,2,0:T(8,128)(2,1)S(1)}, bf16[4,128,8,72]{1,3,2,0:T(8,128)(2,1)}, u32[]{:S(2)}) copy-start(bf16[4,128,8,72]{1,3,2,0:T(8,128)(2,1)} %get-tuple-element.537) | copy-start | bytes 1769476 | tf_op jit(solution)/shard_map/while
  351.8 0.8 copy-start.11
  362.5 6.7 %copy-start.4 = (bf16[4,128,8,72]{1,3,2,0:T(8,128)(2,1)S(1)}, bf16[4,128,8,72]{1,3,2,0:T(8,128)(2,1)}, u32[]{:S(2)}) copy-start(bf16[4,128,8,72]{1,3,2,0:T(8,128)(2,1)} %get-tuple-element.559) | copy-start | bytes 1769476 | tf_op jit(solution)/shard_map/while
  368.4 0.9 copy-start.1
  398.3 8.4 %copy-start.10 = (bf16[4,128,8,72]{1,3,2,0:T(8,128)(2,1)S(1)}, bf16[4,128,8,72]{1,3,2,0:T(8,128)(2,1)}, u32[]{:S(2)}) copy-start(bf16[4,128,8,72]{1,3,2,0:T(8,128)(2,1)} %get-tuple-element.537) | copy-start | bytes 1769476 | tf_op jit(solution)/shard_map/while
  408.6 0.8 copy-start.11
  409.4 8.7 %slice-start = ((s8[7077888]{0:T(1024)(128)(4,1)}), s8[4194304]{0:T(1024)(128)(4,1)S(1)}, s32[]{:S(2)}) async-start(s8[7077888]{0:T(1024)(128)(4,1)} %bitcast.152), calls=%async_computation.3 | async-start | bytes 8388608
  409.4 8.7 %slice-start.1 = ((s8[7077888]{0:T(1024)(128)(4,1)}), s8[2883584]{0:T(1024)(128)(4,1)S(1)}, s32[]{:S(2)}) async-start(s8[7077888]{0:T(1024)(128)(4,1)} %bitcast.152), calls=%async_computation.4 | async-start | bytes 5767168
  413.1 16.5 %collective-permute-start.4 = (bf16[8,32,1152]{2,1,0:T(8,128)(2,1)S(1)}, bf16[8,32,1152]{2,1,0:T(8,128)(2,1)S(1)}, u32[]{:S(2)}, u32[]{:S(2)}) collective-permute-start(bf16[8,32,1152]{2,1,0:T(8,128)(2,1)S(1)} %get-tuple-element.353), channel_id=1, source_target_pairs={{0,2},{2,4},{4,6},{1,3},{3,5},{5,7},{8,10},{10,12},{12,14},{9,11},... | collective-permute-start | bytes 1769480 | tf_op jit(solution)/shard_map/ppermute | solution.py:32
  416.8 17.6 %collective-permute-start.5 = (bf16[8,32,1152]{2,1,0:T(8,128)(2,1)S(1)}, bf16[8,32,1152]{2,1,0:T(8,128)(2,1)S(1)}, u32[]{:S(2)}, u32[]{:S(2)}) collective-permute-start(bf16[8,32,1152]{2,1,0:T(8,128)(2,1)S(1)} %get-tuple-element.352), channel_id=1, source_target_pairs={{2,0},{4,2},{6,4},{3,1},{5,3},{7,5},{10,8},{12,10},{14,12},{11,9},... | collective-permute-start | bytes 1769480 | tf_op jit(solution)/shard_map/ppermute | solution.py:32
  434.7 2.2 copy-start.3
  434.7 6.3 copy-start.13
  436.8 6.0 copy-start.7
  437.9 11.5 %collective-permute-start.6 = (bf16[32,8,1152]{2,1,0:T(8,128)(2,1)}, bf16[32,8,1152]{2,1,0:T(8,128)(2,1)}, u32[]{:S(2)}, u32[]{:S(2)}) collective-permute-start(bf16[32,8,1152]{2,1,0:T(8,128)(2,1)} %get-tuple-element.355), channel_id=1, source_target_pairs={{0,1},{2,3},{4,5},{6,7},{8,9},{10,11},{12,13},{14,15},{16,17},{18,... | collective-permute-start | bytes 1769480 | tf_op jit(solution)/shard_map/ppermute | solution.py:32
  441.5 9.5 %collective-permute-start.7 = (bf16[32,8,1152]{2,1,0:T(8,128)(2,1)}, bf16[32,8,1152]{2,1,0:T(8,128)(2,1)}, u32[]{:S(2)}, u32[]{:S(2)}) collective-permute-start(bf16[32,8,1152]{2,1,0:T(8,128)(2,1)} %get-tuple-element.354), channel_id=1, source_target_pairs={{1,0},{3,2},{5,4},{7,6},{9,8},{11,10},{13,12},{15,14},{17,16},{19,... | collective-permute-start | bytes 1769480 | tf_op jit(solution)/shard_map/ppermute | solution.py:32
  442.8 2.4 copy-start.12
  450.9 1.6 copy-start.8
  450.9 1.6 copy-start.15
  480.1 167.9 %all-reduce.2.cloned.1.call-start = ((), (), s32[]{:S(2)}) async-start(), calls=%async_computation.1 | async-start | bytes 2359296 | tf_op jit(solution)/shard_map/psum | solution.py:184
  594.1 2.2 copy-start.9
  594.1 2.7 copy-start.14
Sparse Core Ops, SparseCore 0:
  480.2 111.3 reduce-scatter.3
  595.1 52.8 all-reduce.1
where the time goes:
time: 663 us; the launch traced here: 660 us
  local copies, waits for them, and re-layouts  251 us (38%)
  waiting for transfers between devices  184 us (28%)
  matrix products  115 us (17%)
  other arithmetic  70.7 us (11%)
  starting transfers between devices  19.3 us (3%)
  between operations  14.4 us (2%)
    unnamed x3, waiting for transfers between devices  112 us
    reshape x8, local copies, waits for them, and re-layouts, cut_band(): band = band.reshape(band_side * extended.shape[1], 2, H, DH)  51.1 us
    psum x1, waiting for transfers between devices, local(): shares = lax.psum(shares.astype(jnp.bfloat16), 'img').astype(jnp.float32)  47.5 us
    while x56, local copies, waits for them, and re-layouts  45.7 us
    slice x8, local copies, waits for them, and re-layouts, cut_band(): return (band[:, 0], band[:, 1])  28 us
    dynamic_update_slice x4, other arithmetic, backward_strip(): lax.dynamic_update_slice_in_dim(accum, current + band_grad, band_top, 0)  22.8 us
    unnamed x30, local copies, waits for them, and re-layouts  21.8 us
    sub x4, matrix products, backward_strip(): dscore = (attn_prob * (dprob - row_dot) * DH ** (-0.5)).astype(jnp.bfloat16)  17.2 us
  transfers between devices with their start and end apart: 10, of which 6 were waited for; matrix products, arithmetic and copies ran while one was open for 4% of the time, Pallas kernels for 0%

commit v1 on v0

v1 whole, which is shorter than its diff:
```python
import jax
import jax.numpy as jnp
from jax import lax
from jax.experimental import pallas as pl
from jax.experimental.pallas import tpu as pltpu
from jax.sharding import PartitionSpec as P

H = 8
DH = 72
INNER = H * DH
REACH = 8
WINDOW = 17
SIDE = 8
PAIRS = H // 2
SLAB = 256
V_SHIFT = 64
MASKED = -1e30
SCALE = DH ** (-0.5)


def shifted_pairs(count, by):
    return [(i, i + by) for i in range(count) if 0 <= i + by < count]


def nt_dot(a, b):
    return lax.dot_general(a, b, (((1,), (1,)), ((), ())), preferred_element_type=jnp.float32)


def attention_kernel(
    start_ref,
    q_ref,
    g_ref,
    own_ref,
    rows_ref,
    cols_ref,
    corner_ref,
    bias_ref,
    o_ref,
    dq_ref,
    tile_grad_ref,
    side_grad_ref,
    kv,
    kvt,
    acc,
    ot,
    dqt,
):
    strips = own_ref.shape[0]
    chunk_own = own_ref.shape[1]
    chunk_side = cols_ref.shape[1]
    chunk = chunk_own + chunk_side
    band = 3 * chunk
    last = strips + 1

    def place(slot, own, side):
        kv[slot, :chunk_own] = own
        kv[slot, chunk_own:] = side
        kvt[slot, :, :chunk_own] = own.T
        padded = jnp.concatenate([side, jnp.zeros((128 - chunk_side, 2 * INNER), side.dtype)], axis=0) if chunk_side < 128 else side
        kvt[slot, :, chunk_own:] = padded.T[:, :chunk_side]

    for s in range(strips):
        place(s + 1, own_ref[s], cols_ref[s])
    place(0, rows_ref[0], corner_ref[0])
    place(last, rows_ref[1], corner_ref[1])
    acc[...] = jnp.zeros_like(acc)

    lane = lax.broadcasted_iota(jnp.int32, (1, SLAB), 1)

    def lanes_of(first):
        inside = (lane >= first) & (lane < first + DH)
        return jnp.where(inside, 1.0, 0.0).astype(jnp.bfloat16)

    def strip(s, carry):
        top = start_ref[s]
        rows = pl.ds(pl.multiple_of(s * chunk_own, chunk_own), chunk_own)
        bias = bias_ref[s]
        bias = jnp.concatenate([bias, bias], axis=1)
        for i in range(PAIRS):
            q = q_ref[rows, 128 * i : 128 * i + SLAB]
            g = g_ref[rows, 128 * i : 128 * i + SLAB]
            q2 = jnp.concatenate([q * lanes_of(16 * i), q * lanes_of(16 * i + DH)], axis=0)
            g2 = jnp.concatenate(
                [g * lanes_of(V_SHIFT + 16 * i), g * lanes_of(V_SHIFT + 16 * i + DH)], axis=0
            )
            k_lanes = slice(128 * i, 128 * i + SLAB)
            v_lanes = slice(512 + 128 * i, 512 + 128 * i + SLAB)
            keys = kv[pl.ds(top, 3), :, k_lanes].reshape(band, SLAB)
            values = kv[pl.ds(top, 3), :, v_lanes].reshape(band, SLAB)
            scores = nt_dot(keys, q2) * SCALE + bias
            shifted = jnp.exp(scores - jnp.max(scores, axis=0, keepdims=True))
            prob = shifted * (1.0 / jnp.sum(shifted, axis=0, keepdims=True))
            prob_low = prob.astype(jnp.bfloat16)
            dprob = nt_dot(values, g2)
            row_dot = jnp.sum(prob * dprob, axis=0, keepdims=True)
            dscore = (prob * (dprob - row_dot) * SCALE).astype(jnp.bfloat16)
            dk = jnp.dot(dscore, q2, preferred_element_type=jnp.float32)
            dv = jnp.dot(prob_low, g2, preferred_element_type=jnp.float32)
            acc[pl.ds(top, 3), :, k_lanes] += dk.reshape(3, chunk, SLAB)
            acc[pl.ds(top, 3), :, v_lanes] += dv.reshape(3, chunk, SLAB)
            k_rows = slice(2 * DH * i, 2 * DH * (i + 1))
            v_rows = slice(INNER + 2 * DH * i, INNER + 2 * DH * (i + 1))
            att = jnp.zeros((2 * DH, SLAB), jnp.float32)
            dqv = jnp.zeros((2 * DH, SLAB), jnp.float32)
            for j in range(3):
                part = slice(chunk * j, chunk * (j + 1))
                att += jnp.dot(kvt[top + j, v_rows, :], prob_low[part], preferred_element_type=jnp.float32)
                dqv += jnp.dot(kvt[top + j, k_rows, :], dscore[part], preferred_element_type=jnp.float32)
            first = 2 * DH * i
            ot[first : first + DH, :] = att[:DH, :chunk_own]
            ot[first + DH : first + 2 * DH, :] = att[DH:, chunk_own:]
            dqt[first : first + DH, :] = dqv[:DH, :chunk_own]
            dqt[first + DH : first + 2 * DH, :] = dqv[DH:, chunk_own:]
        o_ref[rows, :] = ot[...].T[:, :INNER].astype(jnp.bfloat16)
        dq_ref[rows, :] = dqt[...].T[:, :INNER].astype(jnp.bfloat16)
        return carry

    lax.fori_loop(0, strips, strip, 0)
    tile_grad_ref[...] = acc[:, :chunk_own, :]
    side_grad_ref[...] = acc[:, chunk_own:, :].astype(jnp.bfloat16)


def attention(start, projected, grads, own, rows, cols, corner, bias):
    strips, chunk_own, width = own.shape
    chunk_side = cols.shape[1]
    chunk = chunk_own + chunk_side
    token_count = strips * chunk_own
    whole = lambda a: pl.BlockSpec(a.shape, lambda _: (0,) * a.ndim)
    outs = (
        jax.ShapeDtypeStruct((token_count, INNER), jnp.bfloat16),
        jax.ShapeDtypeStruct((token_count, INNER), jnp.bfloat16),
        jax.ShapeDtypeStruct((strips + 2, chunk_own, width), jnp.float32),
        jax.ShapeDtypeStruct((strips + 2, chunk_side, width), jnp.bfloat16),
    )
    return pl.pallas_call(
        attention_kernel,
        grid=(1,),
        out_shape=outs,
        in_specs=[
            pl.BlockSpec(memory_space=pltpu.SMEM),
            pl.BlockSpec((token_count, 640), lambda _: (0, 0)),
            whole(grads),
            whole(own),
            whole(rows),
            whole(cols),
            whole(corner),
            whole(bias),
        ],
        out_specs=tuple(whole(o) for o in outs),
        scratch_shapes=[
            pltpu.VMEM((strips + 2, chunk, width), jnp.bfloat16),
            pltpu.VMEM((strips + 2, width, chunk), jnp.bfloat16),
            pltpu.VMEM((strips + 2, chunk, width), jnp.float32),
            pltpu.VMEM((640, chunk_own), jnp.float32),
            pltpu.VMEM((640, chunk_own), jnp.float32),
        ],
        compiler_params=pltpu.CompilerParams(vmem_limit_bytes=48 * 1024 * 1024),
        cost_estimate=pl.CostEstimate(
            flops=12 * token_count * 3 * chunk * 2 * INNER,
            bytes_accessed=16 * 1024 * 1024,
            transcendentals=token_count * 3 * chunk * H,
        ),
        name="window_attention",
    )(start, projected, grads, own, rows, cols, corner, bias)


def window_starts(places, extent):
    return jnp.clip(places - REACH, 0, extent - WINDOW)


def window_bias(tile_rows, tile_cols, two_columns):
    row_id = lax.axis_index("row")
    col_id = lax.axis_index("col")
    frame_rows = tile_rows * lax.axis_size("row")
    frame_cols = tile_cols * lax.axis_size("col")
    strips = tile_rows // SIDE
    col_first = col_id * tile_cols
    strip_id = jnp.arange(strips, dtype=jnp.int32)
    first_chunk = row_id * strips - 1
    band_chunk = jnp.clip(row_id * strips + strip_id - 1, 0, frame_rows // SIDE - 3)
    side = jnp.arange(SIDE, dtype=jnp.int32)
    own_cols = col_first + jnp.arange(tile_cols, dtype=jnp.int32)
    low, high = col_first - REACH + side, col_first + tile_cols + side
    spans = [own_cols, jnp.where(col_id == 0, high, low)] if two_columns else [own_cols, low, high]
    chunk_rows = jnp.concatenate([jnp.repeat(side, span.shape[0]) for span in spans])
    chunk_cols = jnp.concatenate([jnp.tile(span, SIDE) for span in spans])
    in_band = jnp.concatenate([SIDE * j + chunk_rows for j in range(3)])
    key_col = jnp.tile(chunk_cols, 3)
    key_row = SIDE * band_chunk[:, None] + in_band[None, :]
    query_row = row_id * tile_rows + SIDE * strip_id[:, None] + jnp.repeat(side, tile_cols)[None, :]
    row_start = window_starts(query_row, frame_rows)
    col_start = window_starts(jnp.tile(own_cols, SIDE), frame_cols)
    row_off = key_row[:, :, None] - row_start[:, None, :]
    col_off = key_col[:, None] - col_start[None, :]
    row_ok = (row_off >= 0) & (row_off < WINDOW)
    col_ok = (col_off >= 0) & (col_off < WINDOW)
    bias = jnp.where(row_ok & col_ok[None], 0.0, MASKED).astype(jnp.float32)
    return (band_chunk - first_chunk).astype(jnp.int32), bias


def swap_halves(block, axis_dim):
    own = lax.axis_index("col")
    kept = lax.dynamic_index_in_dim(block, own, axis_dim, keepdims=False)
    sent = lax.dynamic_index_in_dim(block, 1 - own, axis_dim, keepdims=False)
    return kept, lax.ppermute(sent, "col", [(0, 1), (1, 0)])


def exchange_sum(block, axis):
    got = lax.all_to_all(block, axis, split_axis=0, concat_axis=0, tiled=True)
    return jnp.sum(got.astype(jnp.float32), axis=0).astype(jnp.bfloat16)


def summed_shares(part):
    rows, cols, images = (lax.axis_size(a) for a in ("row", "col", "img"))
    width = part.shape[1]
    share = part.shape[0] // (rows * cols)
    if cols != 2 or share % images:
        held = lax.psum_scatter(part, ("row", "col"), scatter_dimension=0, tiled=True)
        return lax.psum(held, "img").astype(jnp.float32)
    kept, got = swap_halves(part.reshape(rows, 2, share, width), 1)
    held = (kept.astype(jnp.float32) + got.astype(jnp.float32)).astype(jnp.bfloat16)
    small = share // images
    held = held.reshape(rows, images, small, width).transpose(1, 0, 2, 3)
    held = exchange_sum(held, "img")
    held = exchange_sum(held, "row")
    return lax.all_gather(held, "img", axis=0, tiled=True).astype(jnp.float32)


def local(tokens, qkv_weight, out_weight, upstream):
    _, tile_rows, tile_cols, width = tokens.shape
    token_count = tile_rows * tile_cols
    strips = tile_rows // SIDE
    chunk_own = SIDE * tile_cols
    row_count, col_count = lax.axis_size("row"), lax.axis_size("col")
    two_columns = col_count == 2
    col_id = lax.axis_index("col")
    token_rows = tokens.reshape(token_count, width)
    grad_rows = upstream.reshape(token_count, width)
    down, up = shifted_pairs(row_count, 1), shifted_pairs(row_count, -1)
    swap = [(0, 1), (1, 0)]

    projected = jnp.dot(token_rows, qkv_weight, preferred_element_type=jnp.float32).astype(
        jnp.bfloat16
    )
    keyvals = projected[:, INNER:]
    above = lax.ppermute(keyvals[token_count - chunk_own :], "row", down)
    below = lax.ppermute(keyvals[:chunk_own], "row", up)

    def side_columns(block, rows):
        block = block.reshape(rows, tile_cols, 2 * INNER)
        if two_columns:
            near = lax.dynamic_slice_in_dim(block, (1 - col_id) * (tile_cols - REACH), REACH, 1)
            got = [lax.ppermute(near, "col", swap)]
        else:
            got = [
                lax.ppermute(block[:, tile_cols - REACH :], "col", shifted_pairs(col_count, 1)),
                lax.ppermute(block[:, :REACH], "col", shifted_pairs(col_count, -1)),
            ]
        got = [g.reshape(rows // SIDE, SIDE * REACH, 2 * INNER) for g in got]
        return got[0] if two_columns else jnp.concatenate(got, axis=1)

    cols = side_columns(keyvals, tile_rows)
    rows = jnp.stack([above, below])
    corner = side_columns(rows, 2 * SIDE)
    start, bias = window_bias(tile_rows, tile_cols, two_columns)
    grad_att = jnp.dot(grad_rows, out_weight, preferred_element_type=jnp.float32).astype(
        jnp.bfloat16
    )
    grads = jnp.pad(grad_att, ((0, 0), (V_SHIFT, 0)))
    own = keyvals.reshape(strips, chunk_own, 2 * INNER)
    attended, dquery, tile_grad, side_grad = attention(
        start, projected, grads, own, rows, cols, corner, bias
    )

    def outer(a, b):
        return lax.dot_general(
            a, b, (((0,), (0,)), ((), ())), preferred_element_type=jnp.float32
        ).astype(jnp.bfloat16)

    early = jnp.concatenate([outer(token_rows, dquery), outer(grad_rows, attended)], axis=1)
    early = summed_shares(early)
    sublayer_out = lax.dot_general(
        attended, out_weight, (((1,), (1,)), ((), ())), preferred_element_type=jnp.float32
    ).astype(jnp.bfloat16)

    def spread(side, first):
        side = side.reshape(strips + 2, SIDE, REACH, 2 * INNER).astype(jnp.float32)
        zeros = jnp.zeros((strips + 2, SIDE, tile_cols - REACH, 2 * INNER), jnp.float32)
        order = [side, zeros] if first else [zeros, side]
        return jnp.concatenate(order, axis=2).reshape(strips + 2, chunk_own, 2 * INNER)

    if two_columns:
        got = lax.ppermute(side_grad, "col", swap)
        tile_grad += jnp.where(col_id == 0, spread(got, False), spread(got, True))
    else:
        half = SIDE * REACH
        to_left = lax.ppermute(side_grad[:, :half], "col", shifted_pairs(col_count, -1))
        to_right = lax.ppermute(side_grad[:, half:], "col", shifted_pairs(col_count, 1))
        tile_grad += spread(to_left, False) + spread(to_right, True)
    from_below = lax.ppermute(tile_grad[0].astype(jnp.bfloat16), "row", up)
    from_above = lax.ppermute(tile_grad[strips + 1].astype(jnp.bfloat16), "row", down)
    dkv = tile_grad[1 : strips + 1]
    dkv = dkv.at[0].add(from_above.astype(jnp.float32))
    dkv = dkv.at[strips - 1].add(from_below.astype(jnp.float32))
    dkv = dkv.reshape(token_count, 2 * INNER).astype(jnp.bfloat16)
    late = summed_shares(outer(token_rows, dkv))
    dqkv = jnp.concatenate([dquery, dkv], axis=1)
    tokens_grad = lax.dot_general(
        dqkv, qkv_weight, (((1,), (1,)), ((), ())), preferred_element_type=jnp.float32
    ).astype(jnp.bfloat16)
    return (
        sublayer_out.reshape(tokens.shape),
        tokens_grad.reshape(tokens.shape),
        jnp.concatenate([early[:, :INNER], late], axis=1),
        early[:, INNER:],
    )


def solution(mesh):
    return jax.shard_map(
        local,
        mesh=mesh,
        in_specs=(P("img", "row", "col", None), P(), P(), P("img", "row", "col", None)),
        out_specs=(
            P("img", "row", "col", None),
            P("img", "row", "col", None),
            P(("row", "col"), None),
            P(("row", "col"), None),
        ),
        check_vma=False,
    )
```

time: 663 us -> 179 us (0.27)
  local copies, waits for them, and re-layouts: 251 us -> 28.8 us
  waiting for transfers between devices: 184 us -> 43.8 us
  matrix products: 115 us -> 21.7 us
  other arithmetic: 70.7 us -> 17.5 us
  Pallas kernels: 0 us -> 19.9 us
  blocking collectives: 0 us -> 17.9 us
  between operations: 14.4 us -> 1 us
  starting transfers between devices: 19.3 us -> 26.7 us
    unnamed x3 -> x0, waiting for transfers between devices: 112 us -> none
    reshape x20 -> x2, local copies, waits for them, and re-layouts: 88.4 us -> 0.16 us  [window_bias(): jnp.repeat(side, span.shape[0])]
    dot_general x26 -> x3, matrix products: 83.7 us -> 5.27 us  [outer(): lax.dot_general(a, b, (((0,), (0,)), ((), ())), preferred_element_type=jn...]
    while x59 -> x0, local copies, waits for them, and re-layouts: 49.1 us -> none
    psum x1 -> x0, waiting for transfers between devices: 47.5 us -> none  [local(): shares = lax.psum(shares.astype(jnp.bfloat16), 'img').astype(jnp.float32)]
    slice x20 -> x4, local copies, waits for them, and re-layouts: 37.8 us -> 3.69 us  [the longest x1 1.82 us: local(): dkv = tile_grad[1:strips + 1]]
    all_to_all x0 -> x4, waiting for transfers between devices: none -> 31.5 us  [exchange_sum(): got = lax.all_to_all(block, axis, split_axis=0, concat_axis=0, tiled=True)]
    dynamic_update_slice x8 -> x0, other arithmetic: 31.4 us -> none  [the longest x4 22.8 us: backward_strip(): lax.dynamic_update_slice_in_dim(accum, current + band_grad, band_top, 0)]
  transfers between devices with their start and end apart: 10 -> 13, of which waited for: 6 -> 5; matrix products, arithmetic and copies ran while one was open for 4% -> 30% of each run, Pallas kernels for 0% -> 0%
where the time goes in v1:
time: 179 us; the launch traced here: 177 us
  waiting for transfers between devices  43.8 us (24%)
  local copies, waits for them, and re-layouts  28.8 us (16%)
  starting transfers between devices  26.7 us (15%)
  matrix products  21.7 us (12%)
  Pallas kernels  19.9 us (11%)
  blocking collectives  17.9 us (10%)
  other arithmetic  17.5 us (10%)
    all_to_all x4, waiting for transfers between devices, exchange_sum(): got = lax.all_to_all(block, axis, split_axis=0, concat_axis=0, tiled=True)  31.5 us
    pallas_call x1, Pallas kernels, attention(): pl.pallas_call(attention_kernel, grid=(1,), out_shape=outs, in_specs=[pl....  19.9 us
    all_gather x2, blocking collectives, summed_shares(): return lax.all_gather(held, 'img', axis=0, tiled=True).astype(jnp.float32)  17.9 us
    all_to_all x4, starting transfers between devices, exchange_sum(): got = lax.all_to_all(block, axis, split_axis=0, concat_axis=0, tiled=True)  14.9 us
    ppermute x1, waiting for transfers between devices, local(): from_below = lax.ppermute(tile_grad[0].astype(jnp.bfloat16), 'row', up)  8.69 us
    dot_general x1, matrix products, local(): lax.dot_general(dqkv, qkv_weight, (((1,), (1,)), ((), ())), preferred_ele...  6.08 us
    unnamed x23, local copies, waits for them, and re-layouts  5.61 us
    dot_general x3, matrix products, outer(): lax.dot_general(a, b, (((0,), (0,)), ((), ())), preferred_element_type=jn...  5.27 us
  transfers between devices with their start and end apart: 13, of which 5 were waited for; matrix products, arithmetic and copies ran while one was open for 30% of the time, Pallas kernels for 0%

profile of v1, /device:TPU:0, one launch (start us, length us, event | category | flops | bytes accessed | tf_op | source)
XLA Modules:
  0.0 177.4 jit_solution(309044046133308381)
XLA Ops:
  0.6 5.2 %convolution_convert_fusion.3.q_ref = bf16[512,1728]{1,0:T(8,128)(2,1)S(1)} fusion(bf16[512,1152]{1,0:T(8,128)(2,1)} %bitcast.86, bf16[1152,1728]{0,1:T(8,128)(2,1)} %param.9), kind=kOutput, calls=%fused_computation.5 | convolution fusion | flops 2039316480 | bytes 6930432 | tf_op jit(solution)/shard_map/dot_general | solution.py:242
  5.8 0.2 fusion.15
  6.1 4.9 %collective-permute-start = (bf16[128,1152]{1,0:T(8,128)(2,1)S(1)}, bf16[128,1152]{1,0:T(8,128)(2,1)S(1)}, u32[]{:S(2)}, u32[]{:S(2)}) collective-permute-start(bf16[128,1152]{1,0:T(8,128)(2,1)S(1)} %get-tuple-element.40), channel_id=1, source_target_pairs={{0,2},{2,4},{4,6},{1,3},{3,5},{5,7},{8,10},{10,12},{12,14},{9,11},... | collective-permute-start | bytes 884744 | tf_op jit(solution)/shard_map/ppermute | solution.py:246
  11.0 1.3 collective-permute-start.1
  12.3 0.7 slice.83
  13.1 0.9 constant_dynamic-slice_fusion.3
  14.0 0.1 tile.13
  14.0 0.1 tile.11
  14.2 0.1 sub.71
  14.2 0.1 reshape.266
  14.3 0.1 reshape.267
  14.6 0.1 fusion.12
  14.9 3.0 %convolution_convert_fusion.6 = bf16[512,576]{0,1:T(8,128)(2,1)} fusion(bf16[512,1152]{1,0:T(8,128)(2,1)} %bitcast.84, bf16[1152,576]{0,1:T(8,128)(2,1)S(1)} %copy-done), kind=kOutput, calls=%fused_computation.23 | convolution fusion | flops 679772160 | bytes 3096576 | tf_op jit(solution)/shard_map/dot_general | solution.py:266
  17.9 3.6 %collective-permute-done.1 = bf16[128,1152]{1,0:T(8,128)(2,1)} collective-permute-done((bf16[128,1152]{1,0:T(8,128)(2,1)S(1)}, bf16[128,1152]{1,0:T(8,128)(2,1)}, u32[]{:S(2)}, u32[]{:S(2)}) %collective-permute-start.1) | collective-permute-done | bytes 294944 | tf_op jit(solution)/shard_map/ppermute | solution.py:247
  21.5 1.0 pad_maximum_fusion.2.rows_ref
  22.5 0.7 constant_dynamic-slice_fusion.2
  23.3 2.1 %copy.31 = bf16[512,576]{1,0:T(8,128)(2,1)} copy(bf16[512,576]{0,1:T(8,128)(2,1)} %convolution_convert_fusion.6) | data formatting | bytes 1179648 | tf_op jit(solution)/shard_map/convert_element_type | solution.py:266
  25.4 1.5 pad.10.g_ref
  26.9 1.3 fusion.9.bias_ref
  28.2 19.9 %window_attention.1 = (bf16[512,576]{1,0:T(8,128)(2,1)S(1)}, bf16[512,576]{1,0:T(8,128)(2,1)S(1)}, f32[6,128,1152]{2,1,0:T(8,128)}, bf16[6,64,1152]{2,1,0:T(8,128)(2,1)}) custom-call(s32[4]{0:T(128)S(1)} %broadcast_subtract_fusion.start_ref, bf16[512,1728]{1,0:T(8,128)(2,1)} %copy-done.7, bf16[512,640]{1,0:T(8,128)(2,1)S(1)} %pad.10.g_ref, ...), custom_call_target="tpu_custom_call" | custom-call | flops 4076863488 | bytes 16777216 | tf_op jit(solution)/shard_map/window_attention/pallas_call | solution.py:135
  48.2 0.9 copy-done.1
  49.0 0.8 copy-done.3
  49.8 0.5 collective-permute-start.4
  50.4 2.6 %fusion = bf16[1152,576]{0,1:T(8,128)(2,1)S(1)} fusion(bf16[512,576]{1,0:T(8,128)(2,1)} %copy-done.1, bf16[512,1152]{1,0:T(8,128)(2,1)} %bitcast.87), kind=kOutput, calls=%fused_computation.8 | convolution fusion | flops 680140800 | bytes 3096576 | tf_op jit(solution)/shard_map/dot_general | solution.py:276
  52.9 1.0 fusion.1
  53.9 0.1 bitcast_convert_fusion
  54.1 0.3 pad_select_fusion
  54.4 1.7 copy-done.6
  56.1 2.4 %fusion.14 = (bf16[6,128,1152]{2,1,0:T(8,128)(2,1)S(1)}, f32[6,128,1152]{2,1,0:T(8,128)}) fusion(f32[6,128,1152]{2,1,0:T(8,128)S(1)} %copy-done.6, f32[6,8,16,1152]{3,2,1,0:T(8,128)S(1)} %pad_select_fusion), kind=kLoop, calls=%fused_computation.59 | loop fusion | flops 1769472 | bytes 12386304 | tf_op jit(solution)/shard_map/convert.10
  58.5 3.5 %collective-permute-start.5 = (bf16[128,1152]{1,0:T(8,128)(2,1)S(1)}, bf16[128,1152]{1,0:T(8,128)(2,1)S(1)}, u32[]{:S(2)}, u32[]{:S(2)}) collective-permute-start(bf16[128,1152]{1,0:T(8,128)(2,1)S(1)} %get-tuple-element.43), channel_id=1, source_target_pairs={{0,2},{2,4},{4,6},{1,3},{3,5},{5,7},{8,10},{10,12},{12,14},{9,11},... | collective-permute-start | bytes 884744 | tf_op jit(solution)/shard_map/ppermute | solution.py:301
  62.0 1.8 pad_maximum_fusion
  63.7 5.2 %copy.32 = bf16[1152,1152]{1,0:T(8,128)(2,1)} copy(bf16[1152,1152]{0,1:T(8,128)(2,1)} %pad_maximum_fusion) | data formatting | bytes 5308416 | tf_op jit(solution)/shard_map/concatenate | solution.py:280
  69.0 1.4 dynamic-slice_bitcast_fusion
  70.5 1.8 %slice.86 = f32[4,128,1152]{2,1,0:T(8,128)S(1)} slice(f32[6,128,1152]{2,1,0:T(8,128)} %get-tuple-element.37), slice={[1:5], [0:128], [0:1152]} | slice | bytes 4718592 | tf_op jit(solution)/shard_map/slice | solution.py:302
  72.3 1.5 collective-permute-start.6
  73.8 1.1 fusion.11
  74.9 8.7 %collective-permute-done.6 = bf16[128,1152]{1,0:T(8,128)(2,1)S(1)} collective-permute-done((bf16[128,1152]{1,0:T(8,128)(2,1)S(1)}, bf16[128,1152]{1,0:T(8,128)(2,1)S(1)}, u32[]{:S(2)}, u32[]{:S(2)}) %collective-permute-start.6) | collective-permute-done | bytes 294944 | tf_op jit(solution)/shard_map/ppermute | solution.py:300
  83.6 0.1 fusion.10
  83.7 0.1 convert_element_type.101
  83.9 1.5 copy-done.10
  85.4 1.8 convolution_convert_fusion
  87.2 1.3 constant_dynamic-slice_fusion.1
  88.4 1.6 copy.44
  90.0 0.6 copy-done.5
  90.7 0.3 fusion.3
  91.0 1.6 copy.33
  92.6 3.7 %all-to-all-start = ((bf16[4,4,36,1152]{3,1,2,0:T(4,128)(2,1)}), bf16[4,4,36,1152]{3,1,2,0:T(4,128)(2,1)S(1)}, u32[]{:S(2)}, u32[]{:S(2)}) async-start(bf16[4,4,36,1152]{3,1,2,0:T(4,128)(2,1)} %bitcast.76), calls=%async_computation | async-start | bytes 2654208 | tf_op jit(solution)/shard_map/all_to_all | solution.py:209
  96.3 3.5 %fusion.2 = bf16[4,144,1152]{2,0,1:T(4,128)(2,1)} fusion(bf16[4,144,1152]{2,0,1:T(4,128)(2,1)} %collective-permute-done.8, bf16[4,1,144,1152]{3,2,1,0:T(8,128)(2,1)} %get-tuple-element.38), kind=kLoop, calls=%fused_computation.12 | loop fusion | flops 2654208 | bytes 3981312 | tf_op jit(solution)/shard_map/convert_element_type | solution.py:221
  99.8 13.3 %all-to-all-done = bf16[4,4,36,1152]{3,1,2,0:T(4,128)(2,1)S(1)} async-done(((bf16[4,4,36,1152]{3,1,2,0:T(4,128)(2,1)}), bf16[4,4,36,1152]{3,1,2,0:T(4,128)(2,1)S(1)}, u32[]{:S(2)}, u32[]{:S(2)}) %all-to-all-start) | async-done | bytes 1327136 | tf_op jit(solution)/shard_map/all_to_all | solution.py:209
  113.1 4.3 %all-to-all-start.2 = ((bf16[4,4,36,1152]{3,1,2,0:T(4,128)(2,1)}), bf16[4,4,36,1152]{3,1,2,0:T(4,128)(2,1)}, u32[]{:S(2)}, u32[]{:S(2)}) async-start(bf16[4,4,36,1152]{3,1,2,0:T(4,128)(2,1)} %bitcast.77), calls=%async_computation.2 | async-start | bytes 2654208 | tf_op jit(solution)/shard_map/all_to_all | solution.py:209
  117.3 1.6 reduce_sum.48
  118.9 1.8 copy.34
  120.7 12.8 %all-to-all-done.2 = bf16[4,4,36,1152]{3,1,2,0:T(4,128)(2,1)} async-done(((bf16[4,4,36,1152]{3,1,2,0:T(4,128)(2,1)}), bf16[4,4,36,1152]{3,1,2,0:T(4,128)(2,1)}, u32[]{:S(2)}, u32[]{:S(2)}) %all-to-all-start.2) | async-done | bytes 1327136 | tf_op jit(solution)/shard_map/all_to_all | solution.py:209
  133.5 3.5 %all-to-all-start.1 = ((bf16[4,36,1152]{2,1,0:T(8,128)(2,1)}), bf16[4,36,1152]{2,1,0:T(8,128)(2,1)S(1)}, u32[]{:S(2)}, u32[]{:S(2)}) async-start(bf16[4,36,1152]{2,1,0:T(8,128)(2,1)} %copy.34), calls=%async_computation.1 | async-start | bytes 737280 | tf_op jit(solution)/shard_map/all_to_all | solution.py:209
  137.0 2.2 %convolution_convert_fusion.5 = bf16[512,1152]{1,0:T(8,128)(2,1)} fusion(bf16[512,576]{1,0:T(8,128)(2,1)S(1)} %copy-done.4, bf16[1152,576]{0,1:T(8,128)(2,1)S(1)} %copy-done), kind=kOutput, calls=%fused_computation.7 | convolution fusion | flops 680067072 | bytes 3096576 | tf_op jit(solution)/shard_map/dot_general | solution.py:282
  139.1 2.2 %reduce_sum.50 = bf16[4,36,1152]{2,0,1:T(4,128)(2,1)S(1)} reduce(bf16[4,4,36,1152]{3,1,2,0:T(4,128)(2,1)} %all-to-all-done.2, bf16[]{:T(256)} %constant.108.clone.1), dimensions={0}, to_apply=%region_2.3 | reduce | flops 497664 | bytes 1658882 | tf_op jit(solution)/shard_map/reduce_sum | solution.py:210
  141.3 0.8 copy.37
  142.1 5.4 %all-to-all-done.1 = bf16[4,36,1152]{2,1,0:T(8,128)(2,1)S(1)} async-done(((bf16[4,36,1152]{2,1,0:T(8,128)(2,1)}), bf16[4,36,1152]{2,1,0:T(8,128)(2,1)S(1)}, u32[]{:S(2)}, u32[]{:S(2)}) %all-to-all-start.1) | async-done | bytes 331808 | tf_op jit(solution)/shard_map/all_to_all | solution.py:209
  147.5 3.5 %all-to-all-start.3 = ((bf16[4,36,1152]{2,1,0:T(8,128)(2,1)}), bf16[4,36,1152]{2,1,0:T(8,128)(2,1)S(1)}, u32[]{:S(2)}, u32[]{:S(2)}) async-start(bf16[4,36,1152]{2,1,0:T(8,128)(2,1)} %copy.37), calls=%async_computation.3 | async-start | bytes 737280 | tf_op jit(solution)/shard_map/all_to_all | solution.py:209
  151.0 6.1 %convolution_convert_fusion.4 = bf16[512,1152]{1,0:T(8,128)(2,1)} fusion(bf16[1152,1728]{0,1:T(8,128)(2,1)} %param.9, bf16[512,1152]{1,0:T(8,128)(2,1)} %bitcast.80, bf16[512,576]{1,0:T(8,128)(2,1)S(1)} %copy-done.2), kind=kOutput, calls=%fused_computation.6 | convolution fusion | flops 2042560512 | bytes 6930432 | tf_op jit(solution)/shard_map/dot_general | solution.py:308
  157.2 9.1 %all-gather = bf16[4,36,1152]{2,1,0:T(8,128)(2,1)S(1)} all-gather(bf16[1,36,1152]{2,1,0:T(8,128)(2,1)S(1)} %bitcast.82), channel_id=1, replica_groups=mesh['img'=4,'row'=4,'col'=2] {'img'}, dimensions={0}, use_global_device_ids=true | all-gather | bytes 414720 | tf_op jit(solution)/shard_map/all_gather | solution.py:226
  166.3 0.9 fusion.16
  167.3 8.8 %all-gather.1 = bf16[4,36,1152]{2,1,0:T(8,128)(2,1)S(1)} all-gather(bf16[1,36,1152]{2,1,0:T(8,128)(2,1)S(1)} %bitcast.81), channel_id=1, replica_groups=mesh['img'=4,'row'=4,'col'=2] {'img'}, dimensions={0}, use_global_device_ids=true | all-gather | bytes 414720 | tf_op jit(solution)/shard_map/all_gather | solution.py:226
  176.2 1.2 pad_maximum_fusion.1
  (53 shorter events, 0.8 us)
Async XLA Ops:
  0.6 14.2 %copy-start = (bf16[1152,576]{0,1:T(8,128)(2,1)S(1)}, bf16[1152,576]{0,1:T(8,128)(2,1)}, u32[]{:S(2)}) copy-start(bf16[1152,576]{0,1:T(8,128)(2,1)} %param.10) | copy-start | bytes 3981316
  5.8 6.5 %copy-start.7 = (bf16[512,1728]{1,0:T(8,128)(2,1)}, bf16[512,1728]{1,0:T(8,128)(2,1)S(1)}, u32[]{:S(2)}) copy-start(bf16[512,1728]{1,0:T(8,128)(2,1)S(1)} %convolution_convert_fusion.3.q_ref) | copy-start | bytes 5308420
  6.1 11.8 %collective-permute-start = (bf16[128,1152]{1,0:T(8,128)(2,1)S(1)}, bf16[128,1152]{1,0:T(8,128)(2,1)S(1)}, u32[]{:S(2)}, u32[]{:S(2)}) collective-permute-start(bf16[128,1152]{1,0:T(8,128)(2,1)S(1)} %get-tuple-element.40), channel_id=1, source_target_pairs={{0,2},{2,4},{4,6},{1,3},{3,5},{5,7},{8,10},{10,12},{12,14},{9,11},... | collective-permute-start | bytes 884744 | tf_op jit(solution)/shard_map/ppermute | solution.py:246
  11.0 10.5 %collective-permute-start.1 = (bf16[128,1152]{1,0:T(8,128)(2,1)S(1)}, bf16[128,1152]{1,0:T(8,128)(2,1)}, u32[]{:S(2)}, u32[]{:S(2)}) collective-permute-start(bf16[128,1152]{1,0:T(8,128)(2,1)S(1)} %get-tuple-element.41), channel_id=1, source_target_pairs={{2,0},{4,2},{6,4},{3,1},{5,3},{7,5},{10,8},{12,10},{14,12},{11,9},... | collective-permute-start | bytes 884744 | tf_op jit(solution)/shard_map/ppermute | solution.py:247
  13.9 14.3 %collective-permute-start.2 = (bf16[32,8,1152]{2,1,0:T(8,128)(2,1)}, bf16[32,8,1152]{2,1,0:T(8,128)(2,1)}, u32[]{:S(2)}, u32[]{:S(2)}) collective-permute-start(bf16[32,8,1152]{2,1,0:T(8,128)(2,1)} %constant_dynamic-slice_fusion.3), channel_id=1, source_target_pairs={{0,1},{1,0},{2,3},{3,2},{4,5},{5,4},{6,7},{7,6},{8,9},{9,8},{10,11... | collective-permute-start | bytes 1769480 | tf_op jit(solution)/shard_map/ppermute | solution.py:253
  23.3 5.0 %collective-permute-start.3 = (bf16[16,8,1152]{2,1,0:T(8,128)(2,1)}, bf16[16,8,1152]{2,1,0:T(8,128)(2,1)S(1)}, u32[]{:S(2)}, u32[]{:S(2)}) collective-permute-start(bf16[16,8,1152]{2,1,0:T(8,128)(2,1)} %constant_dynamic-slice_fusion.2), channel_id=1, source_target_pairs={{0,1},{1,0},{2,3},{3,2},{4,5},{5,4},{6,7},{7,6},{8,9},{9,8},{10,11... | collective-permute-start | bytes 884744 | tf_op jit(solution)/shard_map/ppermute | solution.py:253
  48.2 0.9 copy-start.1
  49.0 0.8 copy-start.3
  49.8 4.1 %collective-permute-start.4 = (bf16[6,64,1152]{2,1,0:T(8,128)(2,1)}, bf16[6,64,1152]{2,1,0:T(8,128)(2,1)S(1)}, u32[]{:S(2)}, u32[]{:S(2)}) collective-permute-start(bf16[6,64,1152]{2,1,0:T(8,128)(2,1)} %get-tuple-element.35), channel_id=1, source_target_pairs={{0,1},{1,0},{2,3},{3,2},{4,5},{5,4},{6,7},{7,6},{8,9},{9,8},{10,11... | collective-permute-start | bytes 2654216 | tf_op jit(solution)/shard_map/ppermute | solution.py:293
  50.4 2.6 %copy-start.4 = (bf16[512,576]{1,0:T(8,128)(2,1)S(1)}, bf16[512,576]{1,0:T(8,128)(2,1)}, u32[]{:S(2)}) copy-start(bf16[512,576]{1,0:T(8,128)(2,1)} %copy-done.3) | copy-start | bytes 1769476
  50.4 2.6 %copy-start.9 = (bf16[1,32,16,1152]{3,2,1,0:T(8,128)(2,1)S(1)}, bf16[1,32,16,1152]{3,2,1,0:T(8,128)(2,1)}, u32[]{:S(2)}) copy-start(bf16[1,32,16,1152]{3,2,1,0:T(8,128)(2,1)} %param.11) | copy-start | bytes 3538948
  54.1 2.0 %copy-start.6 = (f32[6,128,1152]{2,1,0:T(8,128)S(1)}, f32[6,128,1152]{2,1,0:T(8,128)}, u32[]{:S(2)}) copy-start(f32[6,128,1152]{2,1,0:T(8,128)} %get-tuple-element.34) | copy-start | bytes 10616836
  58.5 15.3 %collective-permute-start.5 = (bf16[128,1152]{1,0:T(8,128)(2,1)S(1)}, bf16[128,1152]{1,0:T(8,128)(2,1)S(1)}, u32[]{:S(2)}, u32[]{:S(2)}) collective-permute-start(bf16[128,1152]{1,0:T(8,128)(2,1)S(1)} %get-tuple-element.43), channel_id=1, source_target_pairs={{0,2},{2,4},{4,6},{1,3},{3,5},{5,7},{8,10},{10,12},{12,14},{9,11},... | collective-permute-start | bytes 884744 | tf_op jit(solution)/shard_map/ppermute | solution.py:301
  70.4 19.6 %collective-permute-start.7 = (bf16[4,144,1152]{2,1,0:T(8,128)(2,1)S(1)}, bf16[4,144,1152]{2,1,0:T(8,128)(2,1)S(1)}, u32[]{:S(2)}, u32[]{:S(2)}) collective-permute-start(bf16[4,144,1152]{2,1,0:T(8,128)(2,1)S(1)} %dynamic-slice_bitcast_fusion), channel_id=1, source_target_pairs={{0,1},{1,0},{2,3},{3,2},{4,5},{5,4},{6,7},{7,6},{8,9},{9,8},{10,11... | collective-permute-start | bytes 3981320 | tf_op jit(solution)/shard_map/ppermute | solution.py:205
  72.3 11.3 %collective-permute-start.6 = (bf16[128,1152]{1,0:T(8,128)(2,1)S(1)}, bf16[128,1152]{1,0:T(8,128)(2,1)S(1)}, u32[]{:S(2)}, u32[]{:S(2)}) collective-permute-start(bf16[128,1152]{1,0:T(8,128)(2,1)S(1)} %get-tuple-element.42), channel_id=1, source_target_pairs={{2,0},{4,2},{6,4},{3,1},{5,3},{7,5},{10,8},{12,10},{14,12},{11,9},... | collective-permute-start | bytes 884744 | tf_op jit(solution)/shard_map/ppermute | solution.py:300
  83.7 1.7 copy-start.10
  83.8 3.3 %copy-start.8 = (bf16[4,128,1152]{2,1,0:T(8,128)(2,1)}, bf16[4,128,1152]{2,1,0:T(8,128)(2,1)S(1)}, u32[]{:S(2)}) copy-start(bf16[4,128,1152]{2,1,0:T(8,128)(2,1)S(1)} %convert_element_type.101) | copy-start | bytes 3538948
  88.4 2.2 %copy-start.5 = (bf16[1152,1152]{1,0:T(8,128)(2,1)S(1)}, bf16[1152,1152]{1,0:T(8,128)(2,1)}, u32[]{:S(2)}) copy-start(bf16[1152,1152]{1,0:T(8,128)(2,1)} %copy.32) | copy-start | bytes 7962628
  90.0 6.3 %collective-permute-start.8 = (bf16[4,144,1152]{2,0,1:T(4,128)(2,1)}, bf16[4,144,1152]{2,0,1:T(4,128)(2,1)}, u32[]{:S(2)}, u32[]{:S(2)}) collective-permute-start(bf16[4,144,1152]{2,0,1:T(4,128)(2,1)} %bitcast.69), channel_id=1, source_target_pairs={{0,1},{1,0},{2,3},{3,2},{4,5},{5,4},{6,7},{7,6},{8,9},{9,8},{10,11... | collective-permute-start | bytes 3981320 | tf_op jit(solution)/shard_map/ppermute | solution.py:205
  92.6 20.5 %all-to-all-start = ((bf16[4,4,36,1152]{3,1,2,0:T(4,128)(2,1)}), bf16[4,4,36,1152]{3,1,2,0:T(4,128)(2,1)S(1)}, u32[]{:S(2)}, u32[]{:S(2)}) async-start(bf16[4,4,36,1152]{3,1,2,0:T(4,128)(2,1)} %bitcast.76), calls=%async_computation | async-start | bytes 2654208 | tf_op jit(solution)/shard_map/all_to_all | solution.py:209
  113.1 20.4 %all-to-all-start.2 = ((bf16[4,4,36,1152]{3,1,2,0:T(4,128)(2,1)}), bf16[4,4,36,1152]{3,1,2,0:T(4,128)(2,1)}, u32[]{:S(2)}, u32[]{:S(2)}) async-start(bf16[4,4,36,1152]{3,1,2,0:T(4,128)(2,1)} %bitcast.77), calls=%async_computation.2 | async-start | bytes 2654208 | tf_op jit(solution)/shard_map/all_to_all | solution.py:209
  133.5 14.0 %all-to-all-start.1 = ((bf16[4,36,1152]{2,1,0:T(8,128)(2,1)}), bf16[4,36,1152]{2,1,0:T(8,128)(2,1)S(1)}, u32[]{:S(2)}, u32[]{:S(2)}) async-start(bf16[4,36,1152]{2,1,0:T(8,128)(2,1)} %copy.34), calls=%async_computation.1 | async-start | bytes 737280 | tf_op jit(solution)/shard_map/all_to_all | solution.py:209
  139.1 11.9 %copy-start.2 = (bf16[512,576]{1,0:T(8,128)(2,1)S(1)}, bf16[512,576]{1,0:T(8,128)(2,1)}, u32[]{:S(2)}) copy-start(bf16[512,576]{1,0:T(8,128)(2,1)} %copy-done.1) | copy-start | bytes 1769476
  147.5 19.6 %all-to-all-start.3 = ((bf16[4,36,1152]{2,1,0:T(8,128)(2,1)}), bf16[4,36,1152]{2,1,0:T(8,128)(2,1)S(1)}, u32[]{:S(2)}, u32[]{:S(2)}) async-start(bf16[4,36,1152]{2,1,0:T(8,128)(2,1)} %copy.37), calls=%async_computation.3 | async-start | bytes 737280 | tf_op jit(solution)/shard_map/all_to_all | solution.py:209

commit v2 on v1

v2 whole, which is shorter than its diff:
```python
import jax
import jax.numpy as jnp
from jax import lax
from jax.experimental import pallas as pl
from jax.experimental.pallas import tpu as pltpu
from jax.sharding import PartitionSpec as P

H = 8
DH = 72
INNER = H * DH
REACH = 8
WINDOW = 17
SIDE = 8
PAIRS = H // 2
SLAB = 256
V_SHIFT = 64
MASKED = -1e30
SCALE = DH ** (-0.5)


def shifted_pairs(count, by):
    return [(i, i + by) for i in range(count) if 0 <= i + by < count]


def dot(a, b):
    return jnp.dot(a, b, preferred_element_type=jnp.float32)


def nt_dot(a, b):
    return lax.dot_general(a, b, (((1,), (1,)), ((), ())), preferred_element_type=jnp.float32)


def attention_kernel(
    start_ref,
    q_ref,
    own_ref,
    g_ref,
    halo_ref,
    weight_ref,
    bias_ref,
    o_ref,
    dq_ref,
    grad_ref,
    kv,
    kvt,
    acc,
    qt,
    gt,
    ot,
    dqt,
):
    strips = bias_ref.shape[0]
    chunk = kv.shape[1]
    chunk_own = own_ref.shape[0] // strips
    chunk_side = chunk - chunk_own
    band = 3 * chunk
    token_count = own_ref.shape[0]
    side_first = token_count + 2 * chunk_own
    last = strips + 1
    own_at = [token_count] + [chunk_own * s for s in range(strips)] + [token_count + chunk_own]
    side_order = [strips] + list(range(strips)) + [strips + 1]
    side_at = [side_first + chunk_side * s for s in side_order]

    def place(slot, first, part):
        count = part.shape[0]
        kv[slot, first : first + count] = part
        if count < 128:
            filler = jnp.zeros((128 - count, 2 * INNER), part.dtype)
            part = jnp.concatenate([part, filler], axis=0)
        kvt[slot, :, first : first + count] = part.T[:, :count]

    qt[...] = q_ref[...].T
    gt[...] = g_ref[...].T
    for s in range(strips):
        place(s + 1, 0, own_ref[chunk_own * s : chunk_own * (s + 1)])
    halo_kv = dot(halo_ref[...], weight_ref[:, INNER - 64 :]).astype(jnp.bfloat16)[:, 64:]
    for slot in range(strips + 2):
        at = side_at[slot] - token_count
        place(slot, chunk_own, halo_kv[at : at + chunk_side])
    place(0, 0, halo_kv[:chunk_own])
    place(last, 0, halo_kv[chunk_own : 2 * chunk_own])
    acc[...] = jnp.zeros_like(acc)

    row = lax.broadcasted_iota(jnp.int32, (2 * DH, chunk_own), 0)
    first_head = row < DH
    mask_a = jnp.where(first_head, 1.0, 0.0).astype(jnp.bfloat16)
    mask_b = jnp.where(first_head, 0.0, 1.0).astype(jnp.bfloat16)
    ones = jnp.ones((16, chunk), jnp.bfloat16)

    def pair_block(part, above):
        block = jnp.concatenate([part * mask_a, part * mask_b], axis=1)
        parts = [block]
        if above:
            parts = [jnp.zeros((above, block.shape[1]), block.dtype)] + parts
        below = SLAB - 2 * DH - above
        if below:
            parts = parts + [jnp.zeros((below, block.shape[1]), block.dtype)]
        return jnp.concatenate(parts, axis=0)

    def pick(both):
        return jnp.where(first_head, both[:, :chunk_own], both[:, chunk_own:])

    def strip(s, carry):
        top = start_ref[s]
        rows = pl.ds(pl.multiple_of(s * chunk_own, chunk_own), chunk_own)
        bias = bias_ref[s]
        bias = jnp.concatenate([bias, bias], axis=1)
        for i in range(PAIRS):
            heads = slice(2 * DH * i, 2 * DH * (i + 1))
            k_lanes = slice(128 * i, 128 * i + SLAB)
            v_lanes = slice(512 + 128 * i, 512 + 128 * i + SLAB)
            grads = gt[heads, rows]
            q2 = pair_block(qt[heads, rows], 16 * i)
            g2 = pair_block(grads, V_SHIFT + 16 * i)
            keys = kv[pl.ds(top, 3), :, k_lanes].reshape(band, SLAB)
            values = kv[pl.ds(top, 3), :, v_lanes].reshape(band, SLAB)
            scores = dot(keys, q2) * SCALE + bias
            prob = jnp.exp(scores - jnp.max(scores, axis=0, keepdims=True)).astype(jnp.bfloat16)
            total = jnp.zeros((16, SLAB), jnp.float32)
            att = jnp.zeros((2 * DH, SLAB), jnp.float32)
            for j in range(3):
                part = prob[chunk * j : chunk * (j + 1)]
                v_rows = slice(INNER + 2 * DH * i, INNER + 2 * DH * (i + 1))
                att += dot(kvt[top + j, v_rows, :], part)
                total += dot(ones, part)
            inv = 1.0 / total[:1]
            att = pick(att * inv)
            ot[heads, :] = att
            dots = att * grads.astype(jnp.float32)
            row_dot = jnp.concatenate(
                [
                    jnp.sum(dots[:DH], axis=0, keepdims=True),
                    jnp.sum(dots[DH:], axis=0, keepdims=True),
                ],
                axis=1,
            )
            inv_scale = inv * SCALE
            dprob = dot(values, g2)
            dscore = prob.astype(jnp.float32) * (dprob * inv_scale - row_dot * inv_scale)
            dscore = dscore.astype(jnp.bfloat16)
            dqv = jnp.zeros((2 * DH, SLAB), jnp.float32)
            for j in range(3):
                dqv += dot(kvt[top + j, heads, :], dscore[chunk * j : chunk * (j + 1)])
            dqt[heads, :] = pick(dqv)
            dk = nt_dot(dscore, q2)
            dv = nt_dot(prob, (g2.astype(jnp.float32) * inv).astype(jnp.bfloat16))
            acc[pl.ds(top, 3), :, k_lanes] += dk.reshape(3, chunk, SLAB)
            acc[pl.ds(top, 3), :, v_lanes] += dv.reshape(3, chunk, SLAB)
        o_ref[rows, :] = ot[...].T[:, :INNER].astype(jnp.bfloat16)
        dq_ref[rows, :] = dqt[...].T[:, :INNER].astype(jnp.bfloat16)
        return carry

    lax.fori_loop(0, strips, strip, 0)
    for slot in range(strips + 2):
        grad_ref[own_at[slot] : own_at[slot] + chunk_own, :] = acc[slot, :chunk_own].astype(
            jnp.bfloat16
        )
        grad_ref[side_at[slot] : side_at[slot] + chunk_side, :] = acc[slot, chunk_own:].astype(
            jnp.bfloat16
        )


def attention(start, projected, own, grads, halo, weight, bias):
    strips, band, chunk_own = bias.shape
    chunk = band // 3
    token_count, width = own.shape
    key_count = token_count + halo.shape[0]
    whole = lambda a: pl.BlockSpec(a.shape, lambda _: (0,) * a.ndim)
    outs = (
        jax.ShapeDtypeStruct((token_count, INNER), jnp.bfloat16),
        jax.ShapeDtypeStruct((token_count, INNER), jnp.bfloat16),
        jax.ShapeDtypeStruct((key_count, width), jnp.bfloat16),
    )
    return pl.pallas_call(
        attention_kernel,
        grid=(1,),
        out_shape=outs,
        in_specs=[
            pl.BlockSpec(memory_space=pltpu.SMEM),
            pl.BlockSpec((token_count, 640), lambda _: (0, 0)),
            whole(own),
            whole(grads),
            whole(halo),
            whole(weight),
            whole(bias),
        ],
        out_specs=tuple(whole(o) for o in outs),
        scratch_shapes=[
            pltpu.VMEM((strips + 2, chunk, width), jnp.bfloat16),
            pltpu.VMEM((strips + 2, width, chunk), jnp.bfloat16),
            pltpu.VMEM((strips + 2, chunk, width), jnp.float32),
            pltpu.VMEM((640, token_count), jnp.bfloat16),
            pltpu.VMEM((INNER, token_count), jnp.bfloat16),
            pltpu.VMEM((640, chunk_own), jnp.float32),
            pltpu.VMEM((640, chunk_own), jnp.float32),
        ],
        compiler_params=pltpu.CompilerParams(vmem_limit_bytes=52 * 1024 * 1024),
        cost_estimate=pl.CostEstimate(
            flops=12 * token_count * band * 2 * INNER,
            bytes_accessed=16 * 1024 * 1024,
            transcendentals=token_count * band * H,
        ),
        name="window_attention",
    )(start, projected, own, grads, halo, weight, bias)


def window_starts(places, extent):
    return jnp.clip(places - REACH, 0, extent - WINDOW)


def window_bias(tile_rows, tile_cols, two_columns):
    row_id = lax.axis_index("row")
    col_id = lax.axis_index("col")
    frame_rows = tile_rows * lax.axis_size("row")
    frame_cols = tile_cols * lax.axis_size("col")
    strips = tile_rows // SIDE
    col_first = col_id * tile_cols
    strip_id = jnp.arange(strips, dtype=jnp.int32)
    first_chunk = row_id * strips - 1
    band_chunk = jnp.clip(row_id * strips + strip_id - 1, 0, frame_rows // SIDE - 3)
    side = jnp.arange(SIDE, dtype=jnp.int32)
    own_cols = col_first + jnp.arange(tile_cols, dtype=jnp.int32)
    low, high = col_first - REACH + side, col_first + tile_cols + side
    spans = [own_cols, jnp.where(col_id == 0, high, low)] if two_columns else [own_cols, low, high]
    chunk_rows = jnp.concatenate([jnp.repeat(side, span.shape[0]) for span in spans])
    chunk_cols = jnp.concatenate([jnp.tile(span, SIDE) for span in spans])
    in_band = jnp.concatenate([SIDE * j + chunk_rows for j in range(3)])
    key_col = jnp.tile(chunk_cols, 3)
    key_row = SIDE * band_chunk[:, None] + in_band[None, :]
    query_row = row_id * tile_rows + SIDE * strip_id[:, None] + jnp.repeat(side, tile_cols)[None, :]
    row_start = window_starts(query_row, frame_rows)
    col_start = window_starts(jnp.tile(own_cols, SIDE), frame_cols)
    row_off = key_row[:, :, None] - row_start[:, None, :]
    col_off = key_col[:, None] - col_start[None, :]
    row_ok = (row_off >= 0) & (row_off < WINDOW)
    col_ok = (col_off >= 0) & (col_off < WINDOW)
    bias = jnp.where(row_ok & col_ok[None], 0.0, MASKED).astype(jnp.float32)
    return (band_chunk - first_chunk).astype(jnp.int32), bias


def swap_halves(block, axis_dim):
    own = lax.axis_index("col")
    kept = lax.dynamic_index_in_dim(block, own, axis_dim, keepdims=False)
    sent = lax.dynamic_index_in_dim(block, 1 - own, axis_dim, keepdims=False)
    return kept, lax.ppermute(sent, "col", [(0, 1), (1, 0)])


def exchange_sum(block, axis):
    got = lax.all_to_all(block, axis, split_axis=0, concat_axis=0, tiled=True)
    return jnp.sum(got.astype(jnp.float32), axis=0).astype(jnp.bfloat16)


def summed_shares(part):
    rows, cols, images = (lax.axis_size(a) for a in ("row", "col", "img"))
    width = part.shape[1]
    share = part.shape[0] // (rows * cols)
    if cols != 2:
        held = lax.psum_scatter(part, ("row", "col"), scatter_dimension=0, tiled=True)
        return lax.psum(held, "img").astype(jnp.float32)
    kept, got = swap_halves(part.reshape(rows, 2, share, width), 1)
    held = (kept.astype(jnp.float32) + got.astype(jnp.float32)).astype(jnp.bfloat16)
    small = -(-share // (8 * images)) * 8
    held = jnp.pad(held, ((0, 0), (0, images * small - share), (0, 0)))
    held = held.reshape(rows, images, small, width).transpose(1, 0, 2, 3)
    held = exchange_sum(held, "img")
    held = exchange_sum(held, "row")
    held = jnp.broadcast_to(held[None], (images, small, width))
    held = lax.all_to_all(held, "img", split_axis=0, concat_axis=0, tiled=True)
    return held.reshape(images * small, width)[:share].astype(jnp.float32)


def local(tokens, qkv_weight, out_weight, upstream):
    _, tile_rows, tile_cols, width = tokens.shape
    token_count = tile_rows * tile_cols
    strips = tile_rows // SIDE
    chunk_own = SIDE * tile_cols
    row_count, col_count = lax.axis_size("row"), lax.axis_size("col")
    two_columns = col_count == 2
    col_id = lax.axis_index("col")
    token_rows = tokens.reshape(token_count, width)
    grad_rows = upstream.reshape(token_count, width)
    grid = tokens.reshape(tile_rows, tile_cols, width)
    turns = (0,) if two_columns else (-1, 1)

    def moved(block, down, turn=None):
        pairs = []
        for r in range(row_count):
            for c in range(col_count):
                to_c = c if turn is None else (1 - c if turn == 0 else c + turn)
                if 0 <= r + down < row_count and 0 <= to_c < col_count:
                    pairs.append((r * col_count + c, (r + down) * col_count + to_c))
        return lax.ppermute(block, ("row", "col"), pairs)

    def edge(block, turn):
        if turn == 0:
            return lax.dynamic_slice_in_dim(block, (1 - col_id) * (tile_cols - REACH), REACH, 1)
        return block[:, tile_cols - REACH :] if turn == 1 else block[:, :REACH]

    def side_of(rows, down):
        got = [moved(edge(rows, t), down, t) for t in sorted(turns, reverse=True)]
        got = [g.reshape(-1, SIDE * REACH, width) for g in got]
        got = got[0] if two_columns else jnp.concatenate(got, axis=1)
        return got.reshape(-1, width)

    bottom, top = grid[tile_rows - SIDE :], grid[:SIDE]
    above = moved(bottom, 1).reshape(chunk_own, width)
    below = moved(top, -1).reshape(chunk_own, width)
    halo = jnp.concatenate(
        [above, below, side_of(grid, 0), side_of(bottom, 1), side_of(top, -1)], axis=0
    )

    projected = dot(token_rows, qkv_weight).astype(jnp.bfloat16)
    grad_att = dot(grad_rows, out_weight).astype(jnp.bfloat16)
    start, bias = window_bias(tile_rows, tile_cols, two_columns)
    attended, dquery, ext_grad = attention(
        start, projected, projected[:, INNER:], grad_att, halo, qkv_weight, bias
    )

    def outer(a, b):
        return lax.dot_general(
            a, b, (((0,), (0,)), ((), ())), preferred_element_type=jnp.float32
        ).astype(jnp.bfloat16)

    early = jnp.concatenate([outer(token_rows, dquery), outer(grad_rows, attended)], axis=1)
    late = outer(jnp.concatenate([token_rows, halo], axis=0), ext_grad)
    early = summed_shares(early)
    late = summed_shares(late)
    sublayer_out = nt_dot(attended, out_weight).astype(jnp.bfloat16)

    def spread(side, first):
        side = side.reshape(-1, SIDE, REACH, 2 * INNER).astype(jnp.float32)
        zeros = jnp.zeros((side.shape[0], SIDE, tile_cols - REACH, 2 * INNER), jnp.float32)
        order = [side, zeros] if first else [zeros, side]
        return jnp.concatenate(order, axis=2).reshape(-1, 2 * INNER)

    side_first = token_count + 2 * chunk_own
    inner_grad, side_grad = ext_grad[:side_first].astype(jnp.float32), ext_grad[side_first:]
    if two_columns:
        got = moved(side_grad, 0, 0)
        returned = jnp.where(col_id == 0, spread(got, False), spread(got, True))
    else:
        halves = side_grad.reshape(strips + 2, 2, SIDE * REACH, 2 * INNER)
        returned = spread(moved(halves[:, 0], 0, -1), False) + spread(moved(halves[:, 1], 0, 1), True)
    inner_grad = inner_grad + returned
    dkv = inner_grad[:token_count]
    to_above = inner_grad[token_count : token_count + chunk_own].astype(jnp.bfloat16)
    to_below = inner_grad[token_count + chunk_own :].astype(jnp.bfloat16)
    from_below = moved(to_above, -1).astype(jnp.float32)
    from_above = moved(to_below, 1).astype(jnp.float32)
    rest = jnp.zeros((token_count - chunk_own, 2 * INNER), jnp.float32)
    dkv = dkv + jnp.concatenate([from_above, rest], axis=0)
    dkv = dkv + jnp.concatenate([rest, from_below], axis=0)
    dqkv = jnp.concatenate([dquery, dkv.astype(jnp.bfloat16)], axis=1)
    tokens_grad = nt_dot(dqkv, qkv_weight).astype(jnp.bfloat16)
    return (
        sublayer_out.reshape(tokens.shape),
        tokens_grad.reshape(tokens.shape),
        jnp.concatenate([early[:, :INNER], late], axis=1),
        early[:, INNER:],
    )


def solution(mesh):
    return jax.shard_map(
        local,
        mesh=mesh,
        in_specs=(P("img", "row", "col", None), P(), P(), P("img", "row", "col", None)),
        out_specs=(
            P("img", "row", "col", None),
            P("img", "row", "col", None),
            P(("row", "col"), None),
            P(("row", "col"), None),
        ),
        check_vma=False,
    )
```

time: 179 us -> 201 us (1.12)
  starting transfers between devices: 26.7 us -> 47.4 us
  blocking collectives: 17.9 us -> 0 us
  local copies, waits for them, and re-layouts: 28.8 us -> 45.3 us
  waiting for transfers between devices: 43.8 us -> 34.4 us
  other arithmetic: 17.5 us -> 24.3 us
  Pallas kernels: 19.9 us -> 24.4 us
    all_gather x2 -> x0, blocking collectives: 17.9 us -> none  [summed_shares(): return lax.all_gather(held, 'img', axis=0, tiled=True).astype(jnp.float32)]
    unnamed x23 -> x27, local copies, waits for them, and re-layouts: 5.61 us -> 18 us
    ppermute x7 -> x8, waiting for transfers between devices: 12.3 us -> 0.02 us  [moved(): return lax.ppermute(block, ('row', 'col'), pairs)]
    all_to_all x0 -> x2, starting transfers between devices: none -> 7.61 us  [summed_shares(): held = lax.all_to_all(held, 'img', split_axis=0, concat_axis=0, tiled=True)]
    ppermute x7 -> x8, starting transfers between devices: 11.7 us -> 18.7 us  [moved(): return lax.ppermute(block, ('row', 'col'), pairs)]
    all_to_all x4, starting transfers between devices: 14.9 us -> 20.6 us  [exchange_sum(): got = lax.all_to_all(block, axis, split_axis=0, concat_axis=0, tiled=True)]
    convert_element_type x2 -> x4, other arithmetic: 0.25 us -> 5.71 us  [the longest x1 2.86 us: local(): dqkv = jnp.concatenate([dquery, dkv.astype(jnp.bfloat16)], axis=1)]
    slice x3 -> x4, local copies, waits for them, and re-layouts: 2.79 us -> 8.14 us  [the longest x1 3.06 us: local(): projected[:, INNER:]]
  transfers between devices with their start and end apart: 13 -> 16, of which waited for: 5 -> 4; matrix products, arithmetic and copies ran while one was open for 30% -> 36% of each run, Pallas kernels for 0% -> 0%
where the time goes in v2:
time: 201 us; the launch traced here: 200 us
  starting transfers between devices  47.4 us (24%)
  local copies, waits for them, and re-layouts  45.3 us (23%)
  waiting for transfers between devices  34.4 us (17%)
  Pallas kernels  24.4 us (12%)
  other arithmetic  24.3 us (12%)
  matrix products  23 us (11%)
    all_to_all x4, waiting for transfers between devices, exchange_sum(): got = lax.all_to_all(block, axis, split_axis=0, concat_axis=0, tiled=True)  29.6 us
    pallas_call x1, Pallas kernels, attention(): pl.pallas_call(attention_kernel, grid=(1,), out_shape=outs, in_specs=[pl....  24.4 us
    all_to_all x4, starting transfers between devices, exchange_sum(): got = lax.all_to_all(block, axis, split_axis=0, concat_axis=0, tiled=True)  20.6 us
    ppermute x8, starting transfers between devices, moved(): return lax.ppermute(block, ('row', 'col'), pairs)  18.7 us
    unnamed x27, local copies, waits for them, and re-layouts  18 us
    dot_general x2, matrix products, nt_dot(): lax.dot_general(a, b, (((1,), (1,)), ((), ())), preferred_element_type=jn...  8.25 us
    dot_general x3, matrix products, outer(): lax.dot_general(a, b, (((0,), (0,)), ((), ())), preferred_element_type=jn...  7.65 us
    all_to_all x2, starting transfers between devices, summed_shares(): held = lax.all_to_all(held, 'img', split_axis=0, concat_axis=0, tiled=True)  7.61 us
  transfers between devices with their start and end apart: 16, of which 4 were waited for; matrix products, arithmetic and copies ran while one was open for 36% of the time, Pallas kernels for 0%

profile of v2, /device:TPU:0, one launch (start us, length us, event | category | flops | bytes accessed | tf_op | source)
XLA Modules:
  0.0 199.8 jit_solution(13505851605496165569)
XLA Ops:
  0.7 2.1 %dynamic-slice_bitcast_fusion.2 = bf16[32,8,1152]{2,1,0:T(8,128)(2,1)} fusion(bf16[1,32,16,1152]{3,2,1,0:T(8,128)(2,1)} %param.4, s32[]{:T(128)S(6)} %select_n.41), kind=kLoop, calls=%fused_computation.32 | loop fusion | bytes 1179652 | tf_op jit(solution)/shard_map/dynamic_slice | solution.py:296
  2.7 0.5 collective-permute-start.2
  3.2 1.9 fusion.16
  5.1 0.7 dynamic-slice_bitcast_fusion.4
  5.8 5.3 %collective-permute-start.3 = (bf16[8,8,1152]{2,1,0:T(8,128)(2,1)}, bf16[8,8,1152]{2,1,0:T(8,128)(2,1)}, u32[]{:S(2)}, u32[]{:S(2)}) collective-permute-start(bf16[8,8,1152]{2,1,0:T(8,128)(2,1)} %dynamic-slice_bitcast_fusion.4), channel_id=1, source_target_pairs={{0,3},{1,2},{2,5},{3,4},{4,7},{5,6},{8,11},{9,10},{10,13},{11,12},... | collective-permute-start | bytes 442376 | tf_op jit(solution)/shard_map/ppermute | solution.py:292
  11.1 0.7 dynamic-slice_bitcast_fusion.3
  11.8 1.3 collective-permute-start.4
  13.1 4.9 %collective-permute-start = (bf16[8,16,1152]{2,1,0:T(8,128)(2,1)}, bf16[8,16,1152]{2,1,0:T(8,128)(2,1)}, u32[]{:S(2)}, u32[]{:S(2)}) collective-permute-start(bf16[8,16,1152]{2,1,0:T(8,128)(2,1)} %get-tuple-element.15), channel_id=1, source_target_pairs={{0,2},{1,3},{2,4},{3,5},{4,6},{5,7},{8,10},{9,11},{10,12},{11,13},... | collective-permute-start | bytes 884744 | tf_op jit(solution)/shard_map/ppermute | solution.py:292
  17.9 1.3 collective-permute-start.1
  19.9 1.1 constant_dynamic-update-slice_fusion.5
  21.0 6.1 %convolution_convert_fusion.3.q_ref = bf16[512,1728]{1,0:T(8,128)(2,1)} fusion(bf16[512,1152]{1,0:T(8,128)(2,1)S(1)} %bitcast.74, bf16[1152,1728]{0,1:T(8,128)(2,1)} %param.5), kind=kOutput, calls=%fused_computation.5 | convolution fusion | flops 2039316480 | bytes 6930432 | tf_op jit(solution)/shard_map/dot_general | solution.py:26
  27.5 1.0 convolution_convert_fusion.6
  28.4 1.5 fusion.11.bias_ref
  29.9 6.5 %copy.36.weight_ref = bf16[1152,1728]{1,0:T(8,128)(2,1)} copy(bf16[1152,1728]{0,1:T(8,128)(2,1)} %param.5) | data formatting | bytes 7962624 | tf_op args[1]
  36.4 0.3 copy.35.g_ref
  36.7 3.1 %slice.58.own_ref = bf16[512,1152]{1,0:T(8,128)(2,1)} slice(bf16[512,1728]{1,0:T(8,128)(2,1)} %convolution_convert_fusion.3.q_ref), slice={[0:512], [576:1728]} | slice | bytes 2359296 | tf_op jit(solution)/shard_map/slice | solution.py:316
  39.7 1.7 constant_dynamic-update-slice_fusion.4
  41.5 1.7 constant_dynamic-update-slice_fusion.3
  43.2 2.0 bitcast_dynamic-update-slice_fusion
  45.2 1.6 bitcast_dynamic-update-slice_fusion.4
  46.7 0.7 bitcast_dynamic-update-slice_fusion.2
  47.4 1.2 copy-done.7
  48.6 24.4 %window_attention.1 = (bf16[512,576]{1,0:T(8,128)(2,1)S(1)}, bf16[512,576]{1,0:T(8,128)(2,1)S(1)}, bf16[1152,1152]{1,0:T(8,128)(2,1)}) custom-call(s32[4]{0:T(128)S(1)} %broadcast_subtract_fusion.start_ref, bf16[512,1728]{1,0:T(8,128)(2,1)} %convolution_convert_fusion.3.q_ref, bf16[512,1152]{1,0:T(8,128)(2,1)} %slice.58.own_ref, ...), custom_call_target="tpu_custom_call" | custom-call | flops 4076863488 | bytes 16777216 | tf_op jit(solution)/shard_map/window_attention/pallas_call | solution.py:174
  73.0 1.0 fusion.1
  74.0 0.3 copy-done.2
  74.3 1.0 fusion
  75.2 1.7 pad_maximum_fusion
  76.9 5.2 %copy.37 = bf16[1152,1152]{1,0:T(8,128)(2,1)} copy(bf16[1152,1152]{0,1:T(8,128)(2,1)} %pad_maximum_fusion) | data formatting | bytes 5308416 | tf_op jit(solution)/shard_map/concatenate | solution.py:324
  82.2 2.6 %dynamic-slice_bitcast_fusion.1 = bf16[4,144,1152]{2,1,0:T(8,128)(2,1)} fusion(bf16[4,2,144,1152]{3,2,1,0:T(8,128)(2,1)} %bitcast.69, s32[]{:T(128)S(6)} %select_n.49), kind=kLoop, calls=%fused_computation.24 | loop fusion | bytes 2654212 | tf_op jit(solution)/shard_map/jit(dynamic_index_in_dim)/squeeze | solution.py:244
  85.1 5.7 %convolution_convert_fusion = bf16[1152,1152]{1,0:T(8,128)(2,1)S(1)} fusion(bf16[1152,1152]{1,0:T(8,128)(2,1)} %get-tuple-element.26, bf16[1152,1152]{1,0:T(8,128)(2,1)S(1)} %copy-done.5), kind=kOutput, calls=%fused_computation | convolution fusion | flops 3058974720 | bytes 7962624 | tf_op jit(solution)/shard_map/dot_general | solution.py:320
  90.8 1.5 copy-done.3
  92.3 1.2 dynamic-slice_bitcast_fusion
  93.5 0.3 collective-permute-start.9
  93.8 1.2 slice.50
  95.3 2.0 %fusion.3 = bf16[4,144,1152]{2,1,0:T(8,128)(2,1)S(1)} fusion(bf16[4,144,1152]{2,1,0:T(8,128)(2,1)} %collective-permute-done.8, bf16[4,2,144,1152]{3,2,1,0:T(8,128)(2,1)} %bitcast.70, s32[]{:T(128)S(6)} %select_n.48), kind=kLoop, calls=%fused_computation.14 | loop fusion | flops 2654208 | bytes 3981316 | tf_op jit(solution)/shard_map/convert_element_type | solution.py:261
  97.5 1.2 copy.38
  98.7 4.4 %all-to-all-start = ((bf16[4,4,40,1152]{3,2,1,0:T(8,128)(2,1)}), bf16[4,4,40,1152]{3,2,1,0:T(8,128)(2,1)}, u32[]{:S(2)}, u32[]{:S(2)}) async-start(bf16[4,4,40,1152]{3,2,1,0:T(8,128)(2,1)} %copy.38), calls=%async_computation | async-start | bytes 2949120 | tf_op jit(solution)/shard_map/all_to_all | solution.py:249
  103.1 2.8 %convert.16 = f32[6,8,8,1152]{3,2,1,0:T(8,128)} convert(bf16[6,8,8,1152]{3,2,1,0:T(8,128)(2,1)} %bitcast.14) | non-fusion elementwise | flops 442368 | bytes 2654208 | tf_op jit(solution)/shard_map/convert_element_type | solution.py:331
  105.9 1.6 fusion.2
  107.6 1.3 copy.40
  109.0 13.1 %all-to-all-done = bf16[4,4,40,1152]{3,2,1,0:T(8,128)(2,1)} async-done(((bf16[4,4,40,1152]{3,2,1,0:T(8,128)(2,1)}), bf16[4,4,40,1152]{3,2,1,0:T(8,128)(2,1)}, u32[]{:S(2)}, u32[]{:S(2)}) %all-to-all-start) | async-done | bytes 1474592 | tf_op jit(solution)/shard_map/all_to_all | solution.py:249
  122.1 4.3 %all-to-all-start.3 = ((bf16[4,4,40,1152]{3,2,1,0:T(8,128)(2,1)}), bf16[4,4,40,1152]{3,2,1,0:T(8,128)(2,1)}, u32[]{:S(2)}, u32[]{:S(2)}) async-start(bf16[4,4,40,1152]{3,2,1,0:T(8,128)(2,1)} %copy.40), calls=%async_computation.3 | async-start | bytes 2949120 | tf_op jit(solution)/shard_map/all_to_all | solution.py:249
  126.4 2.4 %pad_select_fusion = f32[6,8,16,1152]{3,2,1,0:T(8,128)S(1)} fusion(f32[6,8,8,1152]{3,2,1,0:T(8,128)} %convert.16, pred[]{:T(512)S(6)} %eq.4), kind=kLoop, calls=%fused_computation.2 | loop fusion | flops 884736 | bytes 5308417 | tf_op jit(solution)/shard_map/jit(_where)/select_n | solution.py:340
  128.9 0.4 copy-done.6
  129.2 2.8 %fusion.14 = (bf16[768,1152]{1,0:T(8,128)(2,1)}, f32[768,1152]{1,0:T(8,128)}) fusion(f32[6,8,16,1152]{3,2,1,0:T(8,128)S(1)} %pad_select_fusion, bf16[1152,1152]{1,0:T(8,128)(2,1)S(1)} %copy-done.6), kind=kLoop, calls=%fused_computation.67 | loop fusion | flops 2654208 | bytes 10616832 | tf_op jit(solution)/shard_map/convert.12
  132.0 2.4 %reduce_sum.48 = bf16[4,40,1152]{2,1,0:T(8,128)(2,1)} reduce(bf16[4,4,40,1152]{3,2,1,0:T(8,128)(2,1)} %all-to-all-done, bf16[]{:T(256)} %constant.70.clone.1), dimensions={0}, to_apply=%region_0.1 | reduce | flops 552960 | bytes 1843202 | tf_op jit(solution)/shard_map/reduce_sum | solution.py:250
  134.4 10.2 %all-to-all-done.3 = bf16[4,4,40,1152]{3,2,1,0:T(8,128)(2,1)} async-done(((bf16[4,4,40,1152]{3,2,1,0:T(8,128)(2,1)}), bf16[4,4,40,1152]{3,2,1,0:T(8,128)(2,1)}, u32[]{:S(2)}, u32[]{:S(2)}) %all-to-all-start.3) | async-done | bytes 1474592 | tf_op jit(solution)/shard_map/all_to_all | solution.py:249
  144.6 5.5 %all-to-all-start.1 = ((bf16[4,40,1152]{2,1,0:T(8,128)(2,1)}), bf16[4,40,1152]{2,1,0:T(8,128)(2,1)S(1)}, u32[]{:S(2)}, u32[]{:S(2)}) async-start(bf16[4,40,1152]{2,1,0:T(8,128)(2,1)} %reduce_sum.48), calls=%async_computation.1 | async-start | bytes 737280 | tf_op jit(solution)/shard_map/all_to_all | solution.py:249
  150.1 1.9 fusion.15
  152.0 3.9 %collective-permute-start.6 = (bf16[128,1152]{1,0:T(8,128)(2,1)}, bf16[128,1152]{1,0:T(8,128)(2,1)S(1)}, u32[]{:S(2)}, u32[]{:S(2)}) collective-permute-start(bf16[128,1152]{1,0:T(8,128)(2,1)} %get-tuple-element.12), channel_id=1, source_target_pairs={{0,2},{1,3},{2,4},{3,5},{4,6},{5,7},{8,10},{9,11},{10,12},{11,13},... | collective-permute-start | bytes 884744 | tf_op jit(solution)/shard_map/ppermute | solution.py:292
  155.9 1.3 collective-permute-start.7
  157.2 2.2 %convolution_convert_fusion.5 = bf16[512,1152]{1,0:T(8,128)(2,1)} fusion(bf16[512,576]{1,0:T(8,128)(2,1)S(1)} %get-tuple-element.7, bf16[1152,576]{0,1:T(8,128)(2,1)S(1)} %copy-done), kind=kOutput, calls=%fused_computation.7 | convolution fusion | flops 680067072 | bytes 3096576 | tf_op jit(solution)/shard_map/dot_general | solution.py:30
  159.4 2.4 %reduce_sum.50 = bf16[4,40,1152]{2,1,0:T(8,128)(2,1)} reduce(bf16[4,4,40,1152]{3,2,1,0:T(8,128)(2,1)} %all-to-all-done.3, bf16[]{:T(256)} %constant.70.clone.1), dimensions={0}, to_apply=%region_2.3 | reduce | flops 552960 | bytes 1843202 | tf_op jit(solution)/shard_map/reduce_sum | solution.py:250
  161.8 6.4 %all-to-all-start.4 = ((bf16[4,40,1152]{2,1,0:T(8,128)(2,1)}), bf16[4,40,1152]{2,1,0:T(8,128)(2,1)S(1)}, u32[]{:S(2)}, u32[]{:S(2)}) async-start(bf16[4,40,1152]{2,1,0:T(8,128)(2,1)} %reduce_sum.50), calls=%async_computation.4 | async-start | bytes 737280 | tf_op jit(solution)/shard_map/all_to_all | solution.py:249
  168.3 2.9 %fusion.5 = bf16[512,1152]{1,0:T(8,128)(2,1)} fusion(f32[768,1152]{1,0:T(8,128)} %get-tuple-element.11, bf16[128,1152]{1,0:T(8,128)(2,1)} %collective-permute-done.7, bf16[128,1152]{1,0:T(8,128)(2,1)S(1)} %collective-permute-done.6), kind=kLoop, calls=%fused_computation.17 | loop fusion | flops 2949120 | bytes 4128768 | tf_op jit(solution)/shard_map/convert_element_type | solution.py:353
  171.2 6.3 %all-to-all-done.4 = bf16[4,40,1152]{2,1,0:T(8,128)(2,1)S(1)} async-done(((bf16[4,40,1152]{2,1,0:T(8,128)(2,1)}), bf16[4,40,1152]{2,1,0:T(8,128)(2,1)S(1)}, u32[]{:S(2)}, u32[]{:S(2)}) %all-to-all-start.4) | async-done | bytes 368672 | tf_op jit(solution)/shard_map/all_to_all | solution.py:249
  177.5 0.8 broadcast_in_dim.45
  178.2 3.5 %all-to-all-start.2 = ((bf16[4,40,1152]{2,1,0:T(8,128)(2,1)}), bf16[4,40,1152]{2,1,0:T(8,128)(2,1)S(1)}, u32[]{:S(2)}, u32[]{:S(2)}) async-start(bf16[4,40,1152]{2,1,0:T(8,128)(2,1)} %broadcast_in_dim.45), calls=%async_computation.2 | async-start | bytes 737280 | tf_op jit(solution)/shard_map/all_to_all | solution.py:268
  181.7 6.1 %convolution_convert_fusion.4 = bf16[512,1152]{1,0:T(8,128)(2,1)} fusion(bf16[1152,1728]{0,1:T(8,128)(2,1)} %param.5, bf16[512,1152]{1,0:T(8,128)(2,1)} %fusion.5, bf16[512,576]{1,0:T(8,128)(2,1)S(1)} %get-tuple-element.8), kind=kOutput, calls=%fused_computation.6 | convolution fusion | flops 2042560512 | bytes 6930432 | tf_op jit(solution)/shard_map/dot_general | solution.py:30
  187.9 0.8 broadcast_in_dim.46
  188.6 4.2 %all-to-all-start.5 = ((bf16[4,40,1152]{2,1,0:T(8,128)(2,1)}), bf16[4,40,1152]{2,1,0:T(8,128)(2,1)S(1)}, u32[]{:S(2)}, u32[]{:S(2)}) async-start(bf16[4,40,1152]{2,1,0:T(8,128)(2,1)} %broadcast_in_dim.46), calls=%async_computation.5 | async-start | bytes 737280 | tf_op jit(solution)/shard_map/all_to_all | solution.py:268
  192.8 0.9 fusion.17
  193.7 4.8 %all-to-all-done.5 = bf16[4,40,1152]{2,1,0:T(8,128)(2,1)S(1)} async-done(((bf16[4,40,1152]{2,1,0:T(8,128)(2,1)}), bf16[4,40,1152]{2,1,0:T(8,128)(2,1)S(1)}, u32[]{:S(2)}, u32[]{:S(2)}) %all-to-all-start.5) | async-done | bytes 368672 | tf_op jit(solution)/shard_map/all_to_all | solution.py:268
  198.6 1.2 pad_maximum_fusion.1
  (61 shorter events, 1.9 us)
Async XLA Ops:
  0.6 26.8 %copy-start = (bf16[1152,576]{0,1:T(8,128)(2,1)S(1)}, bf16[1152,576]{0,1:T(8,128)(2,1)}, u32[]{:S(2)}) copy-start(bf16[1152,576]{0,1:T(8,128)(2,1)} %param.6) | copy-start | bytes 3981316
  0.7 19.2 %copy-start.1 = (bf16[1,32,16,1152]{3,2,1,0:T(8,128)(2,1)S(1)}, bf16[1,32,16,1152]{3,2,1,0:T(8,128)(2,1)}, u32[]{:S(2)}) copy-start(bf16[1,32,16,1152]{3,2,1,0:T(8,128)(2,1)} %param.4) | copy-start | bytes 3538948
  2.7 40.4 %collective-permute-start.2 = (bf16[32,8,1152]{2,1,0:T(8,128)(2,1)}, bf16[32,8,1152]{2,1,0:T(8,128)(2,1)}, u32[]{:S(2)}, u32[]{:S(2)}) collective-permute-start(bf16[32,8,1152]{2,1,0:T(8,128)(2,1)} %dynamic-slice_bitcast_fusion.2), channel_id=1, source_target_pairs={{0,1},{1,0},{2,3},{3,2},{4,5},{5,4},{6,7},{7,6},{8,9},{9,8},{10,11... | collective-permute-start | bytes 1769480 | tf_op jit(solution)/shard_map/ppermute | solution.py:292
  5.8 39.3 %collective-permute-start.3 = (bf16[8,8,1152]{2,1,0:T(8,128)(2,1)}, bf16[8,8,1152]{2,1,0:T(8,128)(2,1)}, u32[]{:S(2)}, u32[]{:S(2)}) collective-permute-start(bf16[8,8,1152]{2,1,0:T(8,128)(2,1)} %dynamic-slice_bitcast_fusion.4), channel_id=1, source_target_pairs={{0,3},{1,2},{2,5},{3,4},{4,7},{5,6},{8,11},{9,10},{10,13},{11,12},... | collective-permute-start | bytes 442376 | tf_op jit(solution)/shard_map/ppermute | solution.py:292
  11.8 35.0 %collective-permute-start.4 = (bf16[8,8,1152]{2,1,0:T(8,128)(2,1)}, bf16[8,8,1152]{2,1,0:T(8,128)(2,1)S(1)}, u32[]{:S(2)}, u32[]{:S(2)}) collective-permute-start(bf16[8,8,1152]{2,1,0:T(8,128)(2,1)} %dynamic-slice_bitcast_fusion.3), channel_id=1, source_target_pairs={{2,1},{3,0},{4,3},{5,2},{6,5},{7,4},{10,9},{11,8},{12,11},{13,10},... | collective-permute-start | bytes 442376 | tf_op jit(solution)/shard_map/ppermute | solution.py:292
  13.1 26.7 %collective-permute-start = (bf16[8,16,1152]{2,1,0:T(8,128)(2,1)}, bf16[8,16,1152]{2,1,0:T(8,128)(2,1)}, u32[]{:S(2)}, u32[]{:S(2)}) collective-permute-start(bf16[8,16,1152]{2,1,0:T(8,128)(2,1)} %get-tuple-element.15), channel_id=1, source_target_pairs={{0,2},{1,3},{2,4},{3,5},{4,6},{5,7},{8,10},{9,11},{10,12},{11,13},... | collective-permute-start | bytes 884744 | tf_op jit(solution)/shard_map/ppermute | solution.py:292
  17.9 23.5 %collective-permute-start.1 = (bf16[8,16,1152]{2,1,0:T(8,128)(2,1)}, bf16[8,16,1152]{2,1,0:T(8,128)(2,1)}, u32[]{:S(2)}, u32[]{:S(2)}) collective-permute-start(bf16[8,16,1152]{2,1,0:T(8,128)(2,1)} %get-tuple-element.16), channel_id=1, source_target_pairs={{2,0},{3,1},{4,2},{5,3},{6,4},{7,5},{10,8},{11,9},{12,10},{13,11},... | collective-permute-start | bytes 884744 | tf_op jit(solution)/shard_map/ppermute | solution.py:292
  21.0 6.4 %copy-start.8 = (bf16[1,32,16,1152]{3,2,1,0:T(8,128)(2,1)S(1)}, bf16[1,32,16,1152]{3,2,1,0:T(8,128)(2,1)}, u32[]{:S(2)}) copy-start(bf16[1,32,16,1152]{3,2,1,0:T(8,128)(2,1)} %param.7) | copy-start | bytes 3538948
  47.4 1.2 copy-start.7
  48.6 24.4 %copy-start.9 = (bf16[1,32,16,1152]{3,2,1,0:T(8,128)(2,1)S(1)}, bf16[1,32,16,1152]{3,2,1,0:T(8,128)(2,1)}, u32[]{:S(2)}) copy-start(bf16[1,32,16,1152]{3,2,1,0:T(8,128)(2,1)} %param.7) | copy-start | bytes 3538948
  73.0 1.3 copy-start.2
  82.2 2.9 %copy-start.5 = (bf16[1152,1152]{1,0:T(8,128)(2,1)S(1)}, bf16[1152,1152]{1,0:T(8,128)(2,1)}, u32[]{:S(2)}) copy-start(bf16[1152,1152]{1,0:T(8,128)(2,1)} %get-tuple-element.9) | copy-start | bytes 7962628
  84.8 10.5 %collective-permute-start.8 = (bf16[4,144,1152]{2,1,0:T(8,128)(2,1)}, bf16[4,144,1152]{2,1,0:T(8,128)(2,1)}, u32[]{:S(2)}, u32[]{:S(2)}) collective-permute-start(bf16[4,144,1152]{2,1,0:T(8,128)(2,1)} %dynamic-slice_bitcast_fusion.1), channel_id=1, source_target_pairs={{0,1},{1,0},{2,3},{3,2},{4,5},{5,4},{6,7},{7,6},{8,9},{9,8},{10,11... | collective-permute-start | bytes 3981320 | tf_op jit(solution)/shard_map/ppermute | solution.py:245
  90.8 1.5 copy-start.3
  93.5 12.3 %collective-permute-start.9 = (bf16[4,144,1152]{2,1,0:T(8,128)(2,1)}, bf16[4,144,1152]{2,1,0:T(8,128)(2,1)}, u32[]{:S(2)}, u32[]{:S(2)}) collective-permute-start(bf16[4,144,1152]{2,1,0:T(8,128)(2,1)} %dynamic-slice_bitcast_fusion), channel_id=1, source_target_pairs={{0,1},{1,0},{2,3},{3,2},{4,5},{5,4},{6,7},{7,6},{8,9},{9,8},{10,11... | collective-permute-start | bytes 3981320 | tf_op jit(solution)/shard_map/ppermute | solution.py:245
  95.1 8.1 %collective-permute-start.5 = (bf16[384,1152]{1,0:T(8,128)(2,1)S(1)}, bf16[384,1152]{1,0:T(8,128)(2,1)}, u32[]{:S(2)}, u32[]{:S(2)}) collective-permute-start(bf16[384,1152]{1,0:T(8,128)(2,1)S(1)} %slice.50), channel_id=1, source_target_pairs={{0,1},{1,0},{2,3},{3,2},{4,5},{5,4},{6,7},{7,6},{8,9},{9,8},{10,11... | collective-permute-start | bytes 2654216 | tf_op jit(solution)/shard_map/ppermute | solution.py:292
  98.7 23.4 %all-to-all-start = ((bf16[4,4,40,1152]{3,2,1,0:T(8,128)(2,1)}), bf16[4,4,40,1152]{3,2,1,0:T(8,128)(2,1)}, u32[]{:S(2)}, u32[]{:S(2)}) async-start(bf16[4,4,40,1152]{3,2,1,0:T(8,128)(2,1)} %copy.38), calls=%async_computation | async-start | bytes 2949120 | tf_op jit(solution)/shard_map/all_to_all | solution.py:249
  103.1 2.8 %copy-start.4 = (bf16[1152,1152]{1,0:T(8,128)(2,1)S(1)}, bf16[1152,1152]{1,0:T(8,128)(2,1)}, u32[]{:S(2)}) copy-start(bf16[1152,1152]{1,0:T(8,128)(2,1)} %copy-done.3) | copy-start | bytes 7962628
  122.1 22.5 %all-to-all-start.3 = ((bf16[4,4,40,1152]{3,2,1,0:T(8,128)(2,1)}), bf16[4,4,40,1152]{3,2,1,0:T(8,128)(2,1)}, u32[]{:S(2)}, u32[]{:S(2)}) async-start(bf16[4,4,40,1152]{3,2,1,0:T(8,128)(2,1)} %copy.40), calls=%async_computation.3 | async-start | bytes 2949120 | tf_op jit(solution)/shard_map/all_to_all | solution.py:249
  126.4 2.8 %copy-start.6 = (bf16[1152,1152]{1,0:T(8,128)(2,1)S(1)}, bf16[1152,1152]{1,0:T(8,128)(2,1)}, u32[]{:S(2)}) copy-start(bf16[1152,1152]{1,0:T(8,128)(2,1)} %get-tuple-element.9) | copy-start | bytes 7962628
  144.6 17.2 %all-to-all-start.1 = ((bf16[4,40,1152]{2,1,0:T(8,128)(2,1)}), bf16[4,40,1152]{2,1,0:T(8,128)(2,1)S(1)}, u32[]{:S(2)}, u32[]{:S(2)}) async-start(bf16[4,40,1152]{2,1,0:T(8,128)(2,1)} %reduce_sum.48), calls=%async_computation.1 | async-start | bytes 737280 | tf_op jit(solution)/shard_map/all_to_all | solution.py:249
  152.0 16.3 %collective-permute-start.6 = (bf16[128,1152]{1,0:T(8,128)(2,1)}, bf16[128,1152]{1,0:T(8,128)(2,1)S(1)}, u32[]{:S(2)}, u32[]{:S(2)}) collective-permute-start(bf16[128,1152]{1,0:T(8,128)(2,1)} %get-tuple-element.12), channel_id=1, source_target_pairs={{0,2},{1,3},{2,4},{3,5},{4,6},{5,7},{8,10},{9,11},{10,12},{11,13},... | collective-permute-start | bytes 884744 | tf_op jit(solution)/shard_map/ppermute | solution.py:292
  155.9 12.3 %collective-permute-start.7 = (bf16[128,1152]{1,0:T(8,128)(2,1)}, bf16[128,1152]{1,0:T(8,128)(2,1)}, u32[]{:S(2)}, u32[]{:S(2)}) collective-permute-start(bf16[128,1152]{1,0:T(8,128)(2,1)} %get-tuple-element.13), channel_id=1, source_target_pairs={{2,0},{3,1},{4,2},{5,3},{6,4},{7,5},{10,8},{11,9},{12,10},{13,11},... | collective-permute-start | bytes 884744 | tf_op jit(solution)/shard_map/ppermute | solution.py:292
  161.8 15.6 %all-to-all-start.4 = ((bf16[4,40,1152]{2,1,0:T(8,128)(2,1)}), bf16[4,40,1152]{2,1,0:T(8,128)(2,1)S(1)}, u32[]{:S(2)}, u32[]{:S(2)}) async-start(bf16[4,40,1152]{2,1,0:T(8,128)(2,1)} %reduce_sum.50), calls=%async_computation.4 | async-start | bytes 737280 | tf_op jit(solution)/shard_map/all_to_all | solution.py:249
  178.2 9.6 %all-to-all-start.2 = ((bf16[4,40,1152]{2,1,0:T(8,128)(2,1)}), bf16[4,40,1152]{2,1,0:T(8,128)(2,1)S(1)}, u32[]{:S(2)}, u32[]{:S(2)}) async-start(bf16[4,40,1152]{2,1,0:T(8,128)(2,1)} %broadcast_in_dim.45), calls=%async_computation.2 | async-start | bytes 737280 | tf_op jit(solution)/shard_map/all_to_all | solution.py:268
  188.6 9.9 %all-to-all-start.5 = ((bf16[4,40,1152]{2,1,0:T(8,128)(2,1)}), bf16[4,40,1152]{2,1,0:T(8,128)(2,1)S(1)}, u32[]{:S(2)}, u32[]{:S(2)}) async-start(bf16[4,40,1152]{2,1,0:T(8,128)(2,1)} %broadcast_in_dim.46), calls=%async_computation.5 | async-start | bytes 737280 | tf_op jit(solution)/shard_map/all_to_all | solution.py:268

commit v3 on v2

--- a/solution.py
+++ b/solution.py
@@ -35,8 +35,9 @@
     q_ref,
     own_ref,
     g_ref,
-    halo_ref,
-    weight_ref,
+    rows_ref,
+    cols_ref,
+    corner_ref,
     bias_ref,
     o_ref,
     dq_ref,
@@ -45,7 +46,6 @@
     kvt,
     acc,
     qt,
-    gt,
     ot,
     dqt,
 ):
@@ -70,15 +70,15 @@
         kvt[slot, :, first : first + count] = part.T[:, :count]
 
     qt[...] = q_ref[...].T
-    gt[...] = g_ref[...].T
+    dqt[INNER:, :] = jnp.zeros((64, chunk_own), jnp.float32)
+    ot[:64, :] = jnp.zeros((64, chunk_own), jnp.float32)
     for s in range(strips):
         place(s + 1, 0, own_ref[chunk_own * s : chunk_own * (s + 1)])
-    halo_kv = dot(halo_ref[...], weight_ref[:, INNER - 64 :]).astype(jnp.bfloat16)[:, 64:]
-    for slot in range(strips + 2):
-        at = side_at[slot] - token_count
-        place(slot, chunk_own, halo_kv[at : at + chunk_side])
-    place(0, 0, halo_kv[:chunk_own])
-    place(last, 0, halo_kv[chunk_own : 2 * chunk_own])
+    for s in range(strips):
+        place(s + 1, chunk_own, cols_ref[chunk_side * s : chunk_side * (s + 1)])
+    for slot, at in ((0, 0), (last, 1)):
+        place(slot, 0, rows_ref[chunk_own * at : chunk_own * (at + 1)])
+        place(slot, chunk_own, corner_ref[chunk_side * at : chunk_side * (at + 1)])
     acc[...] = jnp.zeros_like(acc)
 
     row = lax.broadcasted_iota(jnp.int32, (2 * DH, chunk_own), 0)
@@ -105,49 +105,58 @@
         rows = pl.ds(pl.multiple_of(s * chunk_own, chunk_own), chunk_own)
         bias = bias_ref[s]
         bias = jnp.concatenate([bias, bias], axis=1)
+        heads = [slice(2 * DH * i, 2 * DH * (i + 1)) for i in range(PAIRS)]
+        k_lanes = [slice(128 * i, 128 * i + SLAB) for i in range(PAIRS)]
+        v_lanes = [slice(512 + 128 * i, 512 + 128 * i + SLAB) for i in range(PAIRS)]
+
+        def band_of(lanes):
+            return kv[pl.ds(top, 3), :, lanes].reshape(band, SLAB)
+
+        def from_keys(lines, weights):
+            got = jnp.zeros((2 * DH, SLAB), jnp.float32)
+            for j in range(3):
+                got += dot(kvt[top + j, lines, :], weights[chunk * j : chunk * (j + 1)])
+            return got
+
+        q2 = [pair_block(qt[heads[i], rows], 16 * i) for i in range(PAIRS)]
+        g2 = [pair_block(g_ref[heads[i], rows], V_SHIFT + 16 * i) for i in range(PAIRS)]
+        prob, inv, row_dot, dscore = [], [], [], []
         for i in range(PAIRS):
-            heads = slice(2 * DH * i, 2 * DH * (i + 1))
-            k_lanes = slice(128 * i, 128 * i + SLAB)
-            v_lanes = slice(512 + 128 * i, 512 + 128 * i + SLAB)
-            grads = gt[heads, rows]
-            q2 = pair_block(qt[heads, rows], 16 * i)
-            g2 = pair_block(grads, V_SHIFT + 16 * i)
-            keys = kv[pl.ds(top, 3), :, k_lanes].reshape(band, SLAB)
-            values = kv[pl.ds(top, 3), :, v_lanes].reshape(band, SLAB)
-            scores = dot(keys, q2) * SCALE + bias
-            prob = jnp.exp(scores - jnp.max(scores, axis=0, keepdims=True)).astype(jnp.bfloat16)
+            scores = dot(band_of(k_lanes[i]), q2[i]) * SCALE + bias
+            top_score = jnp.max(scores, axis=0, keepdims=True)
+            prob.append(jnp.exp(scores - top_score).astype(jnp.bfloat16))
+        for i in range(PAIRS):
             total = jnp.zeros((16, SLAB), jnp.float32)
-            att = jnp.zeros((2 * DH, SLAB), jnp.float32)
             for j in range(3):
-                part = prob[chunk * j : chunk * (j + 1)]
-                v_rows = slice(INNER + 2 * DH * i, INNER + 2 * DH * (i + 1))
-                att += dot(kvt[top + j, v_rows, :], part)
-                total += dot(ones, part)
-            inv = 1.0 / total[:1]
-            att = pick(att * inv)
-            ot[heads, :] = att
-            dots = att * grads.astype(jnp.float32)
-            row_dot = jnp.concatenate(
-                [
-                    jnp.sum(dots[:DH], axis=0, keepdims=True),
-                    jnp.sum(dots[DH:], axis=0, keepdims=True),
-                ],
-                axis=1,
+                total += dot(ones, prob[i][chunk * j : chunk * (j + 1)])
+            inv.append(1.0 / total[:1])
+            v_rows = slice(INNER + heads[i].start, INNER + heads[i].stop)
+            att = pick(from_keys(v_rows, prob[i]) * inv[i])
+            ot[64 + heads[i].start : 64 + heads[i].stop, :] = att
+            dots = att * g_ref[heads[i], rows].astype(jnp.float32)
+            row_dot.append(
+                jnp.concatenate(
+                    [
+                        jnp.sum(dots[:DH], axis=0, keepdims=True),
+                        jnp.sum(dots[DH:], axis=0, keepdims=True),
+                    ],
+                    axis=1,
+                )
             )
-            inv_scale = inv * SCALE
-            dprob = dot(values, g2)
-            dscore = prob.astype(jnp.float32) * (dprob * inv_scale - row_dot * inv_scale)
-            dscore = dscore.astype(jnp.bfloat16)
-            dqv = jnp.zeros((2 * DH, SLAB), jnp.float32)
-            for j in range(3):
-                dqv += dot(kvt[top + j, heads, :], dscore[chunk * j : chunk * (j + 1)])
-            dqt[heads, :] = pick(dqv)
-            dk = nt_dot(dscore, q2)
-            dv = nt_dot(prob, (g2.astype(jnp.float32) * inv).astype(jnp.bfloat16))
-            acc[pl.ds(top, 3), :, k_lanes] += dk.reshape(3, chunk, SLAB)
-            acc[pl.ds(top, 3), :, v_lanes] += dv.reshape(3, chunk, SLAB)
-        o_ref[rows, :] = ot[...].T[:, :INNER].astype(jnp.bfloat16)
-        dq_ref[rows, :] = dqt[...].T[:, :INNER].astype(jnp.bfloat16)
+        for i in range(PAIRS):
+            dprob = dot(band_of(v_lanes[i]), g2[i])
+            inv_scale = inv[i] * SCALE
+            change = dprob * inv_scale - row_dot[i] * inv_scale
+            dscore.append((prob[i].astype(jnp.float32) * change).astype(jnp.bfloat16))
+        for i in range(PAIRS):
+            dv = nt_dot(prob[i], (g2[i].astype(jnp.float32) * inv[i]).astype(jnp.bfloat16))
+            acc[pl.ds(top, 3), :, v_lanes[i]] += dv.reshape(3, chunk, SLAB)
+        for i in range(PAIRS):
+            dqt[heads[i], :] = pick(from_keys(heads[i], dscore[i]))
+            dk = nt_dot(dscore[i], q2[i])
+            acc[pl.ds(top, 3), :, k_lanes[i]] += dk.reshape(3, chunk, SLAB)
+        o_ref[rows, :] = ot[...].T.astype(jnp.bfloat16)
+        dq_ref[rows, :] = dqt[...].T.astype(jnp.bfloat16)
         return carry
 
     lax.fori_loop(0, strips, strip, 0)
@@ -160,15 +169,15 @@
         )
 
 
-def attention(start, projected, own, grads, halo, weight, bias):
+def attention(start, projected, own, grads, rows, cols, corner, bias):
     strips, band, chunk_own = bias.shape
     chunk = band // 3
     token_count, width = own.shape
-    key_count = token_count + halo.shape[0]
+    key_count = token_count + rows.shape[0] + cols.shape[0] + corner.shape[0]
     whole = lambda a: pl.BlockSpec(a.shape, lambda _: (0,) * a.ndim)
     outs = (
-        jax.ShapeDtypeStruct((token_count, INNER), jnp.bfloat16),
-        jax.ShapeDtypeStruct((token_count, INNER), jnp.bfloat16),
+        jax.ShapeDtypeStruct((token_count, INNER + 64), jnp.bfloat16),
+        jax.ShapeDtypeStruct((token_count, INNER + 64), jnp.bfloat16),
         jax.ShapeDtypeStruct((key_count, width), jnp.bfloat16),
     )
     return pl.pallas_call(
@@ -180,8 +189,9 @@
             pl.BlockSpec((token_count, 640), lambda _: (0, 0)),
             whole(own),
             whole(grads),
-            whole(halo),
-            whole(weight),
+            whole(rows),
+            whole(cols),
+            whole(corner),
             whole(bias),
         ],
         out_specs=tuple(whole(o) for o in outs),
@@ -190,7 +200,6 @@
             pltpu.VMEM((strips + 2, width, chunk), jnp.bfloat16),
             pltpu.VMEM((strips + 2, chunk, width), jnp.float32),
             pltpu.VMEM((640, token_count), jnp.bfloat16),
-            pltpu.VMEM((INNER, token_count), jnp.bfloat16),
             pltpu.VMEM((640, chunk_own), jnp.float32),
             pltpu.VMEM((640, chunk_own), jnp.float32),
         ],
@@ -201,7 +210,50 @@
             transcendentals=token_count * band * H,
         ),
         name="window_attention",
-    )(start, projected, own, grads, halo, weight, bias)
+    )(start, projected, own, grads, rows, cols, corner, bias)
+
+
+def outer_kernel(own_ref, *refs):
+    pairs = (len(refs) - 3) // 2
+    operands, (sent_ref, kept_ref, turned) = refs[: 2 * pairs], refs[2 * pairs :]
+    share = sent_ref.shape[0] // 4
+    for p in range(pairs):
+        turned[p] = operands[2 * p][...].T
+    for out_ref, half in ((sent_ref, 1 - own_ref[0]), (kept_ref, own_ref[0])):
+        products = []
+        for p in range(pairs):
+            picked = [
+                turned[p, pl.ds(pl.multiple_of((2 * r + half) * share, 16), share), :]
+                for r in range(4)
+            ]
+            products.append(dot(jnp.concatenate(picked, axis=0), operands[2 * p + 1][...]))
+        if pairs == 1:
+            out_ref[...] = products[0].astype(jnp.bfloat16)
+        else:
+            first, second = products
+            out_ref[:, :512] = first[:, :512].astype(jnp.bfloat16)
+            out_ref[:, 512:640] = (first[:, 512:] + second[:, :128]).astype(jnp.bfloat16)
+            out_ref[:, 640:] = second[:, 128:].astype(jnp.bfloat16)
+
+
+def outer_halves(*operands):
+    rows, width = operands[0].shape
+    whole = lambda a: pl.BlockSpec(a.shape, lambda _: (0,) * a.ndim)
+    out = jax.ShapeDtypeStruct((width // 2, 2 * INNER), jnp.bfloat16)
+    own = lax.axis_index("col").astype(jnp.int32).reshape(1)
+    return pl.pallas_call(
+        outer_kernel,
+        grid=(1,),
+        out_shape=(out, out),
+        in_specs=[pl.BlockSpec(memory_space=pltpu.SMEM)] + [whole(a) for a in operands],
+        out_specs=(whole(out), whole(out)),
+        scratch_shapes=[pltpu.VMEM((len(operands) // 2, width, rows), jnp.bfloat16)],
+        compiler_params=pltpu.CompilerParams(vmem_limit_bytes=40 * 1024 * 1024),
+        cost_estimate=pl.CostEstimate(
+            flops=2 * rows * width * 2 * INNER, bytes_accessed=5 * 1024 * 1024, transcendentals=0
+        ),
+        name="weight_grad_halves",
+    )(own, *operands)
 
 
 def window_starts(places, extent):
@@ -238,35 +290,39 @@
     return (band_chunk - first_chunk).astype(jnp.int32), bias
 
 
-def swap_halves(block, axis_dim):
-    own = lax.axis_index("col")
-    kept = lax.dynamic_index_in_dim(block, own, axis_dim, keepdims=False)
-    sent = lax.dynamic_index_in_dim(block, 1 - own, axis_dim, keepdims=False)
-    return kept, lax.ppermute(sent, "col", [(0, 1), (1, 0)])
-
-
 def exchange_sum(block, axis):
     got = lax.all_to_all(block, axis, split_axis=0, concat_axis=0, tiled=True)
     return jnp.sum(got.astype(jnp.float32), axis=0).astype(jnp.bfloat16)
 
 
-def summed_shares(part):
-    rows, cols, images = (lax.axis_size(a) for a in ("row", "col", "img"))
-    width = part.shape[1]
-    share = part.shape[0] // (rows * cols)
-    if cols != 2:
-        held = lax.psum_scatter(part, ("row", "col"), scatter_dimension=0, tiled=True)
-        return lax.psum(held, "img").astype(jnp.float32)
-    kept, got = swap_halves(part.reshape(rows, 2, share, width), 1)
+def image_shares(sent, kept):
+    rows, images = lax.axis_size("row"), lax.axis_size("img")
+    width = sent.shape[1]
+    share = sent.shape[0] // rows
+    kept = kept.reshape(rows, share, width)
+    got = lax.ppermute(sent, "col", [(0, 1), (1, 0)]).reshape(rows, share, width)
     held = (kept.astype(jnp.float32) + got.astype(jnp.float32)).astype(jnp.bfloat16)
     small = -(-share // (8 * images)) * 8
     held = jnp.pad(held, ((0, 0), (0, images * small - share), (0, 0)))
     held = held.reshape(rows, images, small, width).transpose(1, 0, 2, 3)
-    held = exchange_sum(held, "img")
-    held = exchange_sum(held, "row")
-    held = jnp.broadcast_to(held[None], (images, small, width))
+    return held
+
+
+def row_shares(early, late, share):
+    rows, images = lax.axis_size("row"), lax.axis_size("img")
+    _, small, width = early.shape
+    held = exchange_sum(jnp.concatenate([early, late], axis=1), "row")
+    held = jnp.broadcast_to(held[None], (images, 2 * small, width))
     held = lax.all_to_all(held, "img", split_axis=0, concat_axis=0, tiled=True)
-    return held.reshape(images * small, width)[:share].astype(jnp.float32)
+    held = held.reshape(images, 2, small, width).astype(jnp.float32)
+    early = held[:, 0].reshape(images * small, width)[:share]
+    late = held[:, 1].reshape(images * small, width)[:share]
+    return early, late
+
+
+def plain_shares(part):
+    held = lax.psum_scatter(part, ("row", "col"), scatter_dimension=0, tiled=True)
+    return lax.psum(held, "img").astype(jnp.float32)
 
 
 def local(tokens, qkv_weight, out_weight, upstream):
@@ -279,7 +335,6 @@
     col_id = lax.axis_index("col")
     token_rows = tokens.reshape(token_count, width)
     grad_rows = upstream.reshape(token_count, width)
-    grid = tokens.reshape(tile_rows, tile_cols, width)
     turns = (0,) if two_columns else (-1, 1)
 
     def moved(block, down, turn=None):
@@ -296,24 +351,26 @@
             return lax.dynamic_slice_in_dim(block, (1 - col_id) * (tile_cols - REACH), REACH, 1)
         return block[:, tile_cols - REACH :] if turn == 1 else block[:, :REACH]
 
-    def side_of(rows, down):
-        got = [moved(edge(rows, t), down, t) for t in sorted(turns, reverse=True)]
-        got = [g.reshape(-1, SIDE * REACH, width) for g in got]
+    def side_of(block):
+        block = block.reshape(-1, tile_cols, 2 * INNER)
+        got = [moved(edge(block, t), 0, t) for t in sorted(turns, reverse=True)]
+        got = [g.reshape(-1, SIDE * REACH, 2 * INNER) for g in got]
         got = got[0] if two_columns else jnp.concatenate(got, axis=1)
-        return got.reshape(-1, width)
-
-    bottom, top = grid[tile_rows - SIDE :], grid[:SIDE]
-    above = moved(bottom, 1).reshape(chunk_own, width)
-    below = moved(top, -1).reshape(chunk_own, width)
-    halo = jnp.concatenate(
-        [above, below, side_of(grid, 0), side_of(bottom, 1), side_of(top, -1)], axis=0
-    )
+        return got.reshape(-1, 2 * INNER)
 
     projected = dot(token_rows, qkv_weight).astype(jnp.bfloat16)
-    grad_att = dot(grad_rows, out_weight).astype(jnp.bfloat16)
+    keyvals = projected[:, INNER:]
+    above = moved(keyvals[token_count - chunk_own :], 1)
+    below = moved(keyvals[:chunk_own], -1)
+    cols = side_of(keyvals)
+    rows = jnp.concatenate([above, below], axis=0)
+    corner = side_of(rows)
+    grad_att = lax.dot_general(
+        out_weight, grad_rows, (((0,), (1,)), ((), ())), preferred_element_type=jnp.float32
+    ).astype(jnp.bfloat16)
     start, bias = window_bias(tile_rows, tile_cols, two_columns)
     attended, dquery, ext_grad = attention(
-        start, projected, projected[:, INNER:], grad_att, halo, qkv_weight, bias
+        start, projected, keyvals, grad_att, rows, cols, corner, bias
     )
 
     def outer(a, b):
@@ -321,10 +378,12 @@
             a, b, (((0,), (0,)), ((), ())), preferred_element_type=jnp.float32
         ).astype(jnp.bfloat16)
 
-    early = jnp.concatenate([outer(token_rows, dquery), outer(grad_rows, attended)], axis=1)
-    late = outer(jnp.concatenate([token_rows, halo], axis=0), ext_grad)
-    early = summed_shares(early)
-    late = summed_shares(late)
+    simple = two_columns and row_count == 4
+    if simple:
+        early = image_shares(*outer_halves(token_rows, dquery, grad_rows, attended))
+        early, ext_grad = lax.optimization_barrier((early, ext_grad))
+        early = exchange_sum(early, "img")
+    dquery, attended = dquery[:, :INNER], attended[:, 64:]
     sublayer_out = nt_dot(attended, out_weight).astype(jnp.bfloat16)
 
     def spread(side, first):
@@ -350,7 +409,14 @@
     rest = jnp.zeros((token_count - chunk_own, 2 * INNER), jnp.float32)
     dkv = dkv + jnp.concatenate([from_above, rest], axis=0)
     dkv = dkv + jnp.concatenate([rest, from_below], axis=0)
-    dqkv = jnp.concatenate([dquery, dkv.astype(jnp.bfloat16)], axis=1)
+    dkv = dkv.astype(jnp.bfloat16)
+    if simple:
+        late = exchange_sum(image_shares(*outer_halves(token_rows, dkv)), "img")
+        early, late = row_shares(early, late, width // (row_count * col_count))
+    else:
+        early = jnp.concatenate([outer(token_rows, dquery), outer(grad_rows, attended)], axis=1)
+        early, late = plain_shares(early), plain_shares(outer(token_rows, dkv))
+    dqkv = jnp.concatenate([dquery, dkv], axis=1)
     tokens_grad = nt_dot(dqkv, qkv_weight).astype(jnp.bfloat16)
     return (
         sublayer_out.reshape(tokens.shape),

time: 201 us -> 162 us (0.81)
  waiting for transfers between devices: 34.4 us -> 71.5 us
  local copies, waits for them, and re-layouts: 45.3 us -> 13.3 us
  starting transfers between devices: 47.4 us -> 30.3 us
  other arithmetic: 24.3 us -> 9.91 us
  matrix products: 23 us -> 14.1 us
  Pallas kernels: 24.4 us -> 20.8 us
    all_to_all x4 -> x3, waiting for transfers between devices: 29.6 us -> 49.4 us  [exchange_sum(): got = lax.all_to_all(block, axis, split_axis=0, concat_axis=0, tiled=True)]
    ppermute x8 -> x7, waiting for transfers between devices: 0.02 us -> 14.9 us  [moved(): return lax.ppermute(block, ('row', 'col'), pairs)]
    unnamed x27 -> x26, local copies, waits for them, and re-layouts: 18 us -> 4.85 us
    pallas_call x1, Pallas kernels: 24.4 us -> 15.2 us  [attention(): pl.pallas_call(attention_kernel, grid=(1,), out_shape=outs, in_specs=[pl....]
    all_to_all x4 -> x3, starting transfers between devices: 20.6 us -> 12.1 us  [exchange_sum(): got = lax.all_to_all(block, axis, split_axis=0, concat_axis=0, tiled=True)]
    dot_general x3 -> x1, matrix products: 7.65 us -> 0.96 us  [local(): lax.dot_general(out_weight, grad_rows, (((0,), (1,)), ((), ())), preferre...]
    concatenate x2 -> x1, local copies, waits for them, and re-layouts: 5.92 us -> 0.03 us  [local(): rows = jnp.concatenate([above, below], axis=0)]
    pallas_call x0 -> x2, Pallas kernels: none -> 5.59 us  [outer_halves(): pl.pallas_call(outer_kernel, grid=(1,), out_shape=(out, out), in_specs=[p...]
  transfers between devices with their start and end apart: 16 -> 13, of which waited for: 4 -> 10; matrix products, arithmetic and copies ran while one was open for 36% -> 12% of each run, Pallas kernels for 0% -> 0%
where the time goes in v3:
time: 162 us; the launch traced here: 161 us
  waiting for transfers between devices  71.5 us (44%)
  starting transfers between devices  30.3 us (19%)
  Pallas kernels  20.8 us (13%)
  matrix products  14.1 us (9%)
  local copies, waits for them, and re-layouts  13.3 us (8%)
  other arithmetic  9.91 us (6%)
    all_to_all x3, waiting for transfers between devices, exchange_sum(): got = lax.all_to_all(block, axis, split_axis=0, concat_axis=0, tiled=True)  49.4 us
    pallas_call x1, Pallas kernels, attention(): pl.pallas_call(attention_kernel, grid=(1,), out_shape=outs, in_specs=[pl....  15.2 us
    ppermute x7, waiting for transfers between devices, moved(): return lax.ppermute(block, ('row', 'col'), pairs)  14.9 us
    ppermute x7, starting transfers between devices, moved(): return lax.ppermute(block, ('row', 'col'), pairs)  13.8 us
    all_to_all x3, starting transfers between devices, exchange_sum(): got = lax.all_to_all(block, axis, split_axis=0, concat_axis=0, tiled=True)  12.1 us
    dot_general x2, matrix products, nt_dot(): lax.dot_general(a, b, (((1,), (1,)), ((), ())), preferred_element_type=jn...  7.95 us
    pallas_call x2, Pallas kernels, outer_halves(): pl.pallas_call(outer_kernel, grid=(1,), out_shape=(out, out), in_specs=[p...  5.59 us
    dot_general x1, matrix products, dot(): return jnp.dot(a, b, preferred_element_type=jnp.float32)  5.15 us
  transfers between devices with their start and end apart: 13, of which 10 were waited for; matrix products, arithmetic and copies ran while one was open for 12% of the time, Pallas kernels for 0%

profile of v3, /device:TPU:0, one launch (start us, length us, event | category | flops | bytes accessed | tf_op | source)
XLA Modules:
  0.0 160.8 jit_solution(1744254676174872464)
XLA Ops:
  0.6 5.2 %convolution_convert_fusion.q_ref = bf16[512,1728]{1,0:T(8,128)(2,1)S(1)} fusion(bf16[512,1152]{1,0:T(8,128)(2,1)} %bitcast.36, bf16[1152,1728]{0,1:T(8,128)(2,1)} %param.5), kind=kOutput, calls=%fused_computation.2 | convolution fusion | flops 2039316480 | bytes 6930432 | tf_op jit(solution)/shard_map/dot_general | solution.py:26
  5.8 1.3 fusion.12
  7.1 1.3 collective-permute-start.1
  8.4 6.3 %collective-permute-start = (bf16[128,1152]{1,0:T(8,128)(2,1)}, bf16[128,1152]{1,0:T(8,128)(2,1)}, u32[]{:S(2)}, u32[]{:S(2)}) collective-permute-start(bf16[128,1152]{1,0:T(8,128)(2,1)} %get-tuple-element.25), channel_id=1, source_target_pairs={{0,2},{1,3},{2,4},{3,5},{4,6},{5,7},{8,10},{9,11},{10,12},{11,13},... | collective-permute-start | bytes 884744 | tf_op jit(solution)/shard_map/ppermute | solution.py:347
  14.7 0.7 slice.67.own_ref
  15.5 0.1 collective-permute-start.2
  15.7 0.1 tile.11
  15.8 0.1 tile.13
  15.9 0.1 sub.69
  15.9 0.1 reshape.196
  16.0 0.1 reshape.195
  16.2 0.1 add_clamp_fusion
  16.2 0.1 pad_add_fusion
  16.3 0.1 broadcast_add_fusion
  16.4 0.1 fusion.9
  16.6 1.3 fusion.7.bias_ref
  17.9 2.7 %collective-permute-done = bf16[128,1152]{1,0:T(8,128)(2,1)} collective-permute-done((bf16[128,1152]{1,0:T(8,128)(2,1)}, bf16[128,1152]{1,0:T(8,128)(2,1)}, u32[]{:S(2)}, u32[]{:S(2)}) %collective-permute-start) | collective-permute-done | bytes 294944 | tf_op jit(solution)/shard_map/ppermute | solution.py:347
  20.5 1.0 constant_dynamic-update-slice_fusion.1
  21.6 0.1 collective-permute-start.3
  21.7 1.0 convolution_convert_fusion.3.g_ref
  22.7 0.6 collective-permute-done.3
  23.3 15.2 %window_attention.1 = (bf16[512,640]{1,0:T(8,128)(2,1)}, bf16[512,640]{1,0:T(8,128)(2,1)}, bf16[1152,1152]{1,0:T(8,128)(2,1)}) custom-call(s32[4]{0:T(128)S(1)} %broadcast_subtract_fusion.start_ref, bf16[512,1728]{1,0:T(8,128)(2,1)} %copy-done.11, bf16[512,1152]{1,0:T(8,128)(2,1)} %copy-done.9, bf16[576,512]{1,0:T(8,128)(2,1)S(1)} %convolution_convert_fusion.3.g_ref, ...), custom_call_target="tpu_custom_call" | custom-call | flops 4076863488 | bytes 16777216 | tf_op jit(solution)/shard_map/window_attention/pallas_call | solution.py:183
  38.5 1.1 copy-done.5
  39.5 1.1 copy-done.7
  40.6 2.6 %weight_grad_halves.2 = (bf16[576,1152]{1,0:T(8,128)(2,1)S(1)}, bf16[576,1152]{1,0:T(8,128)(2,1)S(1)}) custom-call(s32[1]{0:T(128)} %bitcast.7.own_ref, bf16[512,1152]{1,0:T(8,128)(2,1)S(1)} %bitcast.37, bf16[512,640]{1,0:T(8,128)(2,1)S(1)} %copy-done.5, bf16[512,1152]{1,0:T(8,128)(2,1)S(1)} %bitcast.35, bf16[512,640]{1,0:T(8,128)(2,1)S(1)} %copy-done.7), custom_call_target="tpu_custom_call" | custom-call | flops 1358954496 | bytes 5242880 | tf_op jit(solution)/shard_map/weight_grad_halves/pallas_call | solution.py:244
  43.3 0.2 collective-permute-start.4
  43.5 2.9 %collective-permute-done.4 = bf16[576,1152]{1,0:T(8,128)(2,1)S(1)} collective-permute-done((bf16[576,1152]{1,0:T(8,128)(2,1)S(1)}, bf16[576,1152]{1,0:T(8,128)(2,1)S(1)}, u32[]{:S(2)}, u32[]{:S(2)}) %collective-permute-start.4) | collective-permute-done | bytes 1327136 | tf_op jit(solution)/shard_map/ppermute | solution.py:303
  46.4 0.3 add_convert_fusion.1
  46.7 0.1 pad.13
  46.8 1.6 %copy-done.10 = bf16[1152,1152]{1,0:T(8,128)(2,1)S(1)} copy-done((bf16[1152,1152]{1,0:T(8,128)(2,1)S(1)}, bf16[1152,1152]{1,0:T(8,128)(2,1)}, u32[]{:S(2)}) %copy-start.10) | copy-done | bytes 2654232
  48.5 0.1 slice.58
  48.5 0.2 collective-permute-start.5
  48.7 2.3 %collective-permute-done.5 = bf16[384,1152]{1,0:T(8,128)(2,1)S(1)} collective-permute-done((bf16[384,1152]{1,0:T(8,128)(2,1)S(1)}, bf16[384,1152]{1,0:T(8,128)(2,1)S(1)}, u32[]{:S(2)}, u32[]{:S(2)}) %collective-permute-start.5) | collective-permute-done | bytes 884768 | tf_op jit(solution)/shard_map/ppermute | solution.py:347
  51.0 0.1 convert.14
  51.2 0.3 pad_select_fusion
  51.5 0.4 fusion.11
  51.9 4.4 %collective-permute-start.6 = (bf16[128,1152]{1,0:T(8,128)(2,1)S(1)}, bf16[128,1152]{1,0:T(8,128)(2,1)S(1)}, u32[]{:S(2)}, u32[]{:S(2)}) collective-permute-start(bf16[128,1152]{1,0:T(8,128)(2,1)S(1)} %get-tuple-element.26), channel_id=1, source_target_pairs={{0,2},{1,3},{2,4},{3,5},{4,6},{5,7},{8,10},{9,11},{10,12},{11,13},... | collective-permute-start | bytes 884744 | tf_op jit(solution)/shard_map/ppermute | solution.py:347
  56.4 1.5 collective-permute-start.7
  57.8 5.1 %collective-permute-done.6 = bf16[128,1152]{1,0:T(8,128)(2,1)S(1)} collective-permute-done((bf16[128,1152]{1,0:T(8,128)(2,1)S(1)}, bf16[128,1152]{1,0:T(8,128)(2,1)S(1)}, u32[]{:S(2)}, u32[]{:S(2)}) %collective-permute-start.6) | collective-permute-done | bytes 294944 | tf_op jit(solution)/shard_map/ppermute | solution.py:347
  62.9 4.3 %collective-permute-done.7 = bf16[128,1152]{1,0:T(8,128)(2,1)S(1)} collective-permute-done((bf16[128,1152]{1,0:T(8,128)(2,1)S(1)}, bf16[128,1152]{1,0:T(8,128)(2,1)S(1)}, u32[]{:S(2)}, u32[]{:S(2)}) %collective-permute-start.7) | collective-permute-done | bytes 294944 | tf_op jit(solution)/shard_map/ppermute | solution.py:347
  67.2 0.2 fusion.1.refs_1_
  67.4 3.0 %weight_grad_halves.3 = (bf16[576,1152]{1,0:T(8,128)(2,1)}, bf16[576,1152]{1,0:T(8,128)(2,1)S(1)}) custom-call(s32[1]{0:T(128)} %bitcast.7.own_ref, bf16[512,1152]{1,0:T(8,128)(2,1)S(1)} %bitcast.38, bf16[512,1152]{1,0:T(8,128)(2,1)S(1)} %fusion.1.refs_1_), custom_call_target="tpu_custom_call" | custom-call | flops 1358954496 | bytes 5242880 | tf_op jit(solution)/shard_map/weight_grad_halves/pallas_call | solution.py:244
  70.3 1.2 copy.15
  71.6 4.3 %all-to-all-start = ((bf16[4,4,40,1152]{3,2,1,0:T(8,128)(2,1)}), bf16[4,4,40,1152]{3,2,1,0:T(8,128)(2,1)}, u32[]{:S(2)}, u32[]{:S(2)}) async-start(bf16[4,4,40,1152]{3,2,1,0:T(8,128)(2,1)} %copy.15), calls=%async_computation | async-start | bytes 2949120 | tf_op jit(solution)/shard_map/all_to_all | solution.py:294
  75.9 1.6 %add_convert_fusion = bf16[576,1152]{1,0:T(8,128)(2,1)S(1)} fusion(bf16[576,1152]{1,0:T(8,128)(2,1)} %collective-permute-done.8, bf16[576,1152]{1,0:T(8,128)(2,1)S(1)} %get-tuple-element.20), kind=kLoop, calls=%fused_computation.5 | loop fusion | flops 2654208 | bytes 3981312 | tf_op jit(solution)/shard_map/convert_element_type | solution.py:304
  77.5 0.1 pad.14
  77.7 1.2 copy.16
  78.9 16.2 %all-to-all-done = bf16[4,4,40,1152]{3,2,1,0:T(8,128)(2,1)} async-done(((bf16[4,4,40,1152]{3,2,1,0:T(8,128)(2,1)}), bf16[4,4,40,1152]{3,2,1,0:T(8,128)(2,1)}, u32[]{:S(2)}, u32[]{:S(2)}) %all-to-all-start) | async-done | bytes 1474592 | tf_op jit(solution)/shard_map/all_to_all | solution.py:294
  95.1 3.6 %all-to-all-start.1 = ((bf16[4,4,40,1152]{3,2,1,0:T(8,128)(2,1)}), bf16[4,4,40,1152]{3,2,1,0:T(8,128)(2,1)S(1)}, u32[]{:S(2)}, u32[]{:S(2)}) async-start(bf16[4,4,40,1152]{3,2,1,0:T(8,128)(2,1)} %copy.16), calls=%async_computation.1 | async-start | bytes 2949120 | tf_op jit(solution)/shard_map/all_to_all | solution.py:294
  98.7 1.6 %reduce_sum.36 = bf16[4,40,1152]{2,1,0:T(8,128)(2,1)S(1)} reduce(bf16[4,4,40,1152]{3,2,1,0:T(8,128)(2,1)} %all-to-all-done, bf16[]{:T(256)} %constant.55.clone.1), dimensions={0}, to_apply=%region_0.1 | reduce | flops 552960 | bytes 1843202 | tf_op jit(solution)/shard_map/reduce_sum | solution.py:295
  100.3 16.7 %all-to-all-done.1 = bf16[4,4,40,1152]{3,2,1,0:T(8,128)(2,1)S(1)} async-done(((bf16[4,4,40,1152]{3,2,1,0:T(8,128)(2,1)}), bf16[4,4,40,1152]{3,2,1,0:T(8,128)(2,1)S(1)}, u32[]{:S(2)}, u32[]{:S(2)}) %all-to-all-start.1) | async-done | bytes 1474592 | tf_op jit(solution)/shard_map/all_to_all | solution.py:294
  117.0 0.2 reduce_sum.37
  117.2 0.9 pad_maximum_fusion.1
  118.2 4.2 %all-to-all-start.2 = ((bf16[4,80,1152]{2,1,0:T(8,128)(2,1)}), bf16[4,80,1152]{2,1,0:T(8,128)(2,1)}, u32[]{:S(2)}, u32[]{:S(2)}) async-start(bf16[4,80,1152]{2,1,0:T(8,128)(2,1)} %pad_maximum_fusion.1), calls=%async_computation.2 | async-start | bytes 1474560 | tf_op jit(solution)/shard_map/all_to_all | solution.py:294
  122.4 2.2 %convolution_convert_fusion.2 = bf16[512,1152]{1,0:T(8,128)(2,1)} fusion(bf16[1152,576]{0,1:T(8,128)(2,1)S(1)} %copy-done, bf16[512,640]{1,0:T(8,128)(2,1)S(1)} %copy-done.8), kind=kOutput, calls=%fused_computation.4 | convolution fusion | flops 680067072 | bytes 3162112 | tf_op jit(solution)/shard_map/dot_general | solution.py:30
  124.6 16.5 %all-to-all-done.2 = bf16[4,80,1152]{2,1,0:T(8,128)(2,1)} async-done(((bf16[4,80,1152]{2,1,0:T(8,128)(2,1)}), bf16[4,80,1152]{2,1,0:T(8,128)(2,1)}, u32[]{:S(2)}, u32[]{:S(2)}) %all-to-all-start.2) | async-done | bytes 737312 | tf_op jit(solution)/shard_map/all_to_all | solution.py:294
  141.1 1.2 reduce_sum.38
  142.3 0.9 broadcast_in_dim.39
  143.2 4.2 %all-to-all-start.3 = ((bf16[4,80,1152]{2,1,0:T(8,128)(2,1)}), bf16[4,80,1152]{2,1,0:T(8,128)(2,1)}, u32[]{:S(2)}, u32[]{:S(2)}) async-start(bf16[4,80,1152]{2,1,0:T(8,128)(2,1)} %broadcast_in_dim.39), calls=%async_computation.3 | async-start | bytes 1474560 | tf_op jit(solution)/shard_map/all_to_all | solution.py:316
  147.5 5.7 %convolution_convert_fusion.1 = bf16[512,1152]{1,0:T(8,128)(2,1)} fusion(bf16[1152,1728]{0,1:T(8,128)(2,1)} %param.5, bf16[512,1152]{1,0:T(8,128)(2,1)S(1)} %copy-done.2, bf16[512,576]{1,0:T(8,128)(2,1)S(1)} %bitcast.40), kind=kOutput, calls=%fused_computation.3 | convolution fusion | flops 2042560512 | bytes 6930432 | tf_op jit(solution)/shard_map/dot_general | solution.py:30
  153.2 4.2 %all-to-all-done.3 = bf16[4,80,1152]{2,1,0:T(8,128)(2,1)} async-done(((bf16[4,80,1152]{2,1,0:T(8,128)(2,1)}), bf16[4,80,1152]{2,1,0:T(8,128)(2,1)}, u32[]{:S(2)}, u32[]{:S(2)}) %all-to-all-start.3) | async-done | bytes 737312 | tf_op jit(solution)/shard_map/all_to_all | solution.py:316
  157.4 1.2 fusion.15
  158.7 0.9 fusion.14
  159.6 1.2 pad_maximum_fusion
  (46 shorter events, 0.4 us)
Async XLA Ops:
  0.6 21.1 %copy-start = (bf16[1152,576]{0,1:T(8,128)(2,1)S(1)}, bf16[1152,576]{0,1:T(8,128)(2,1)}, u32[]{:S(2)}) copy-start(bf16[1152,576]{0,1:T(8,128)(2,1)} %param.6) | copy-start | bytes 3981316
  5.8 8.9 %copy-start.11 = (bf16[512,1728]{1,0:T(8,128)(2,1)}, bf16[512,1728]{1,0:T(8,128)(2,1)S(1)}, u32[]{:S(2)}) copy-start(bf16[512,1728]{1,0:T(8,128)(2,1)S(1)} %convolution_convert_fusion.q_ref) | copy-start | bytes 5308420
  7.1 14.4 %collective-permute-start.1 = (bf16[128,1152]{1,0:T(8,128)(2,1)}, bf16[128,1152]{1,0:T(8,128)(2,1)S(1)}, u32[]{:S(2)}, u32[]{:S(2)}) collective-permute-start(bf16[128,1152]{1,0:T(8,128)(2,1)} %get-tuple-element.24), channel_id=1, source_target_pairs={{2,0},{3,1},{4,2},{5,3},{6,4},{7,5},{10,8},{11,9},{12,10},{13,11},... | collective-permute-start | bytes 884744 | tf_op jit(solution)/shard_map/ppermute | solution.py:347
  8.4 12.1 %collective-permute-start = (bf16[128,1152]{1,0:T(8,128)(2,1)}, bf16[128,1152]{1,0:T(8,128)(2,1)}, u32[]{:S(2)}, u32[]{:S(2)}) collective-permute-start(bf16[128,1152]{1,0:T(8,128)(2,1)} %get-tuple-element.25), channel_id=1, source_target_pairs={{0,2},{1,3},{2,4},{3,5},{4,6},{5,7},{8,10},{9,11},{10,12},{11,13},... | collective-permute-start | bytes 884744 | tf_op jit(solution)/shard_map/ppermute | solution.py:347
  15.4 6.1 %copy-start.9 = (bf16[512,1152]{1,0:T(8,128)(2,1)}, bf16[512,1152]{1,0:T(8,128)(2,1)S(1)}, u32[]{:S(2)}) copy-start(bf16[512,1152]{1,0:T(8,128)(2,1)S(1)} %slice.67.own_ref) | copy-start | bytes 3538948
  15.5 7.8 %collective-permute-start.2 = (bf16[32,8,1152]{2,1,0:T(8,128)(2,1)S(1)}, bf16[32,8,1152]{2,1,0:T(8,128)(2,1)}, u32[]{:S(2)}, u32[]{:S(2)}) collective-permute-start(bf16[32,8,1152]{2,1,0:T(8,128)(2,1)S(1)} %constant_dynamic-slice_fusion.1), channel_id=1, source_target_pairs={{0,1},{1,0},{2,3},{3,2},{4,5},{5,4},{6,7},{7,6},{8,9},{9,8},{10,11... | collective-permute-start | bytes 1769480 | tf_op jit(solution)/shard_map/ppermute | solution.py:347
  16.5 5.2 %copy-start.3 = (bf16[1,32,16,1152]{3,2,1,0:T(8,128)(2,1)S(1)}, bf16[1,32,16,1152]{3,2,1,0:T(8,128)(2,1)}, u32[]{:S(2)}) copy-start(bf16[1,32,16,1152]{3,2,1,0:T(8,128)(2,1)} %param.7) | copy-start | bytes 3538948
  21.6 1.6 %collective-permute-start.3 = (bf16[16,8,1152]{2,1,0:T(8,128)(2,1)S(1)}, bf16[16,8,1152]{2,1,0:T(8,128)(2,1)S(1)}, u32[]{:S(2)}, u32[]{:S(2)}) collective-permute-start(bf16[16,8,1152]{2,1,0:T(8,128)(2,1)S(1)} %constant_dynamic-slice_fusion), channel_id=1, source_target_pairs={{0,1},{1,0},{2,3},{3,2},{4,5},{5,4},{6,7},{7,6},{8,9},{9,8},{10,11... | collective-permute-start | bytes 884744 | tf_op jit(solution)/shard_map/ppermute | solution.py:347
  23.3 15.2 %copy-start.4 = (bf16[1,32,16,1152]{3,2,1,0:T(8,128)(2,1)S(1)}, bf16[1,32,16,1152]{3,2,1,0:T(8,128)(2,1)}, u32[]{:S(2)}) copy-start(bf16[1,32,16,1152]{3,2,1,0:T(8,128)(2,1)} %param.4) | copy-start | bytes 3538948
  38.5 1.1 copy-start.5
  39.5 1.1 copy-start.7
  43.3 3.1 %collective-permute-start.4 = (bf16[576,1152]{1,0:T(8,128)(2,1)S(1)}, bf16[576,1152]{1,0:T(8,128)(2,1)S(1)}, u32[]{:S(2)}, u32[]{:S(2)}) collective-permute-start(bf16[576,1152]{1,0:T(8,128)(2,1)S(1)} %get-tuple-element.16), channel_id=1, source_target_pairs={{0,1},{1,0},{2,3},{3,2},{4,5},{5,4},{6,7},{7,6},{8,9},{9,8},{10,11... | collective-permute-start | bytes 3981320 | tf_op jit(solution)/shard_map/ppermute | solution.py:303
  46.7 1.8 %copy-start.10 = (bf16[1152,1152]{1,0:T(8,128)(2,1)S(1)}, bf16[1152,1152]{1,0:T(8,128)(2,1)}, u32[]{:S(2)}) copy-start(bf16[1152,1152]{1,0:T(8,128)(2,1)} %get-tuple-element.18) | copy-start | bytes 7962628
  48.5 2.5 %collective-permute-start.5 = (bf16[384,1152]{1,0:T(8,128)(2,1)S(1)}, bf16[384,1152]{1,0:T(8,128)(2,1)S(1)}, u32[]{:S(2)}, u32[]{:S(2)}) collective-permute-start(bf16[384,1152]{1,0:T(8,128)(2,1)S(1)} %slice.58), channel_id=1, source_target_pairs={{0,1},{1,0},{2,3},{3,2},{4,5},{5,4},{6,7},{7,6},{8,9},{9,8},{10,11... | collective-permute-start | bytes 2654216 | tf_op jit(solution)/shard_map/ppermute | solution.py:347
  51.9 10.9 %collective-permute-start.6 = (bf16[128,1152]{1,0:T(8,128)(2,1)S(1)}, bf16[128,1152]{1,0:T(8,128)(2,1)S(1)}, u32[]{:S(2)}, u32[]{:S(2)}) collective-permute-start(bf16[128,1152]{1,0:T(8,128)(2,1)S(1)} %get-tuple-element.26), channel_id=1, source_target_pairs={{0,2},{1,3},{2,4},{3,5},{4,6},{5,7},{8,10},{9,11},{10,12},{11,13},... | collective-permute-start | bytes 884744 | tf_op jit(solution)/shard_map/ppermute | solution.py:347
  56.4 10.8 %collective-permute-start.7 = (bf16[128,1152]{1,0:T(8,128)(2,1)S(1)}, bf16[128,1152]{1,0:T(8,128)(2,1)S(1)}, u32[]{:S(2)}, u32[]{:S(2)}) collective-permute-start(bf16[128,1152]{1,0:T(8,128)(2,1)S(1)} %get-tuple-element.27), channel_id=1, source_target_pairs={{2,0},{3,1},{4,2},{5,3},{6,4},{7,5},{10,8},{11,9},{12,10},{13,11},... | collective-permute-start | bytes 884744 | tf_op jit(solution)/shard_map/ppermute | solution.py:347
  67.4 3.0 %copy-start.1 = (bf16[512,1152]{1,0:T(8,128)(2,1)}, bf16[512,1152]{1,0:T(8,128)(2,1)S(1)}, u32[]{:S(2)}) copy-start(bf16[512,1152]{1,0:T(8,128)(2,1)S(1)} %fusion.1.refs_1_) | copy-start | bytes 3538948
  70.3 5.6 %collective-permute-start.8 = (bf16[576,1152]{1,0:T(8,128)(2,1)}, bf16[576,1152]{1,0:T(8,128)(2,1)}, u32[]{:S(2)}, u32[]{:S(2)}) collective-permute-start(bf16[576,1152]{1,0:T(8,128)(2,1)} %get-tuple-element.21), channel_id=1, source_target_pairs={{0,1},{1,0},{2,3},{3,2},{4,5},{5,4},{6,7},{7,6},{8,9},{9,8},{10,11... | collective-permute-start | bytes 3981320 | tf_op jit(solution)/shard_map/ppermute | solution.py:303
  71.6 23.5 %all-to-all-start = ((bf16[4,4,40,1152]{3,2,1,0:T(8,128)(2,1)}), bf16[4,4,40,1152]{3,2,1,0:T(8,128)(2,1)}, u32[]{:S(2)}, u32[]{:S(2)}) async-start(bf16[4,4,40,1152]{3,2,1,0:T(8,128)(2,1)} %copy.15), calls=%async_computation | async-start | bytes 2949120 | tf_op jit(solution)/shard_map/all_to_all | solution.py:294
  95.1 21.9 %all-to-all-start.1 = ((bf16[4,4,40,1152]{3,2,1,0:T(8,128)(2,1)}), bf16[4,4,40,1152]{3,2,1,0:T(8,128)(2,1)S(1)}, u32[]{:S(2)}, u32[]{:S(2)}) async-start(bf16[4,4,40,1152]{3,2,1,0:T(8,128)(2,1)} %copy.16), calls=%async_computation.1 | async-start | bytes 2949120 | tf_op jit(solution)/shard_map/all_to_all | solution.py:294
  117.2 5.1 %copy-start.8 = (bf16[512,640]{1,0:T(8,128)(2,1)S(1)}, bf16[512,640]{1,0:T(8,128)(2,1)}, u32[]{:S(2)}) copy-start(bf16[512,640]{1,0:T(8,128)(2,1)} %get-tuple-element.13.refs_3_) | copy-start | bytes 1966084
  118.2 22.9 %all-to-all-start.2 = ((bf16[4,80,1152]{2,1,0:T(8,128)(2,1)}), bf16[4,80,1152]{2,1,0:T(8,128)(2,1)}, u32[]{:S(2)}, u32[]{:S(2)}) async-start(bf16[4,80,1152]{2,1,0:T(8,128)(2,1)} %pad_maximum_fusion.1), calls=%async_computation.2 | async-start | bytes 1474560 | tf_op jit(solution)/shard_map/all_to_all | solution.py:294
  124.6 22.8 %copy-start.2 = (bf16[512,1152]{1,0:T(8,128)(2,1)S(1)}, bf16[512,1152]{1,0:T(8,128)(2,1)}, u32[]{:S(2)}) copy-start(bf16[512,1152]{1,0:T(8,128)(2,1)} %copy-done.1) | copy-start | bytes 3538948
  124.6 22.8 %copy-start.6 = (bf16[512,640]{1,0:T(8,128)(2,1)S(1)}, bf16[512,640]{1,0:T(8,128)(2,1)}, u32[]{:S(2)}) copy-start(bf16[512,640]{1,0:T(8,128)(2,1)} %get-tuple-element.14.refs_1_) | copy-start | bytes 1966084
  143.2 14.2 %all-to-all-start.3 = ((bf16[4,80,1152]{2,1,0:T(8,128)(2,1)}), bf16[4,80,1152]{2,1,0:T(8,128)(2,1)}, u32[]{:S(2)}, u32[]{:S(2)}) async-start(bf16[4,80,1152]{2,1,0:T(8,128)(2,1)} %broadcast_in_dim.39), calls=%async_computation.3 | async-start | bytes 1474560 | tf_op jit(solution)/shard_map/all_to_all | solution.py:316

commit v4 on v3

--- a/solution.py
+++ b/solution.py
@@ -256,6 +256,56 @@
     )(own, *operands)
 
 
+def late_kernel(
+    own_ref, first, second, third, tokens_ref, inner_ref, side_ref, above_ref, below_ref,
+    sent_ref, kept_ref, grad_ref, turned,
+):
+    own = own_ref[0]
+    count = inner_ref.shape[0]
+    share = sent_ref.shape[0] // 4
+    edge = above_ref.shape[0]
+    width = inner_ref.shape[1]
+    side = side_ref[: count // 2].astype(jnp.float32).reshape(-1, REACH, width)
+    is_left = (own == 0).astype(jnp.float32)
+    side = jnp.concatenate([side * (1.0 - is_left), side * is_left], axis=1)
+    total = inner_ref[...].astype(jnp.float32) + side.reshape(count, width)
+    grad_ref[:edge] = (total[:edge] + above_ref[...].astype(jnp.float32)).astype(jnp.bfloat16)
+    grad_ref[edge : count - edge] = total[edge : count - edge].astype(jnp.bfloat16)
+    grad_ref[count - edge :] = (
+        total[count - edge :] + below_ref[...].astype(jnp.float32)
+    ).astype(jnp.bfloat16)
+    turned[...] = tokens_ref[...].T
+    for out_ref, half in ((sent_ref, 1 - own), (kept_ref, own)):
+        picked = [
+            turned[pl.ds(pl.multiple_of((2 * r + half) * share, 16), share), :] for r in range(4)
+        ]
+        product = dot(jnp.concatenate(picked, axis=0), grad_ref[...])
+        out_ref[...] = product.astype(jnp.bfloat16)
+
+
+def late_halves(earlier, token_rows, ext_grad, side, above, below):
+    rows, width = token_rows.shape
+    whole = lambda a: pl.BlockSpec(a.shape, lambda _: (0,) * a.ndim)
+    out = jax.ShapeDtypeStruct((width // 2, 2 * INNER), jnp.bfloat16)
+    grad = jax.ShapeDtypeStruct((rows, 2 * INNER), jnp.bfloat16)
+    own = lax.axis_index("col").astype(jnp.int32).reshape(1)
+    return pl.pallas_call(
+        late_kernel,
+        grid=(1,),
+        out_shape=(out, out, grad),
+        in_specs=[pl.BlockSpec(memory_space=pltpu.SMEM)]
+        + [pl.BlockSpec(memory_space=pl.ANY)] * 3
+        + [whole(token_rows), whole(grad), whole(side), whole(above), whole(below)],
+        out_specs=(whole(out), whole(out), whole(grad)),
+        scratch_shapes=[pltpu.VMEM((width, rows), jnp.bfloat16)],
+        compiler_params=pltpu.CompilerParams(vmem_limit_bytes=40 * 1024 * 1024),
+        cost_estimate=pl.CostEstimate(
+            flops=2 * rows * width * 2 * INNER, bytes_accessed=7 * 1024 * 1024, transcendentals=0
+        ),
+        name="late_weight_grad_halves",
+    )(own, *earlier, token_rows, ext_grad, side, above, below)
+
+
 def window_starts(places, extent):
     return jnp.clip(places - REACH, 0, extent - WINDOW)
 
@@ -290,12 +340,40 @@
     return (band_chunk - first_chunk).astype(jnp.int32), bias
 
 
-def exchange_sum(block, axis):
-    got = lax.all_to_all(block, axis, split_axis=0, concat_axis=0, tiled=True)
-    return jnp.sum(got.astype(jnp.float32), axis=0).astype(jnp.bfloat16)
-
-
-def image_shares(sent, kept):
+def after(value, *earlier):
+    return lax.optimization_barrier((value,) + earlier)[0]
+
+
+def cut(block, axis, take):
+    own = lax.axis_index(axis)
+    return [take(block, own ^ step) for step in range(lax.axis_size(axis))]
+
+
+def exchange_sum(parts, axis, *earlier):
+    kept, got = parts[0], []
+    for step, part in enumerate(parts[1:], 1):
+        pairs = [(i, i ^ step) for i in range(lax.axis_size(axis))]
+        got.append(lax.ppermute(part, axis, pairs))
+    if earlier:
+        kept = after(kept, *earlier)
+    total = kept.astype(jnp.float32)
+    for g in got:
+        total += g.astype(jnp.float32)
+    return total.astype(jnp.bfloat16)
+
+
+def gathered(block, axis):
+    own = lax.axis_index(axis)
+    count = lax.axis_size(axis)
+    whole = jnp.zeros((count,) + block.shape, block.dtype)
+    whole = lax.dynamic_update_index_in_dim(whole, block, own, 0)
+    for step in range(1, count):
+        got = lax.ppermute(block, axis, [(i, i ^ step) for i in range(count)])
+        whole = lax.dynamic_update_index_in_dim(whole, got, own ^ step, 0)
+    return whole
+
+
+def core_sum(sent, kept):
     rows, images = lax.axis_size("row"), lax.axis_size("img")
     width = sent.shape[1]
     share = sent.shape[0] // rows
@@ -303,21 +381,21 @@
     got = lax.ppermute(sent, "col", [(0, 1), (1, 0)]).reshape(rows, share, width)
     held = (kept.astype(jnp.float32) + got.astype(jnp.float32)).astype(jnp.bfloat16)
     small = -(-share // (8 * images)) * 8
-    held = jnp.pad(held, ((0, 0), (0, images * small - share), (0, 0)))
-    held = held.reshape(rows, images, small, width).transpose(1, 0, 2, 3)
-    return held
-
-
-def row_shares(early, late, share):
-    rows, images = lax.axis_size("row"), lax.axis_size("img")
-    _, small, width = early.shape
-    held = exchange_sum(jnp.concatenate([early, late], axis=1), "row")
-    held = jnp.broadcast_to(held[None], (images, 2 * small, width))
-    held = lax.all_to_all(held, "img", split_axis=0, concat_axis=0, tiled=True)
-    held = held.reshape(images, 2, small, width).astype(jnp.float32)
-    early = held[:, 0].reshape(images * small, width)[:share]
-    late = held[:, 1].reshape(images * small, width)[:share]
-    return early, late
+    return jnp.pad(held, ((0, 0), (0, images * small - share), (0, 0)))
+
+
+def image_parts(held):
+    small = held.shape[1] // lax.axis_size("img")
+    return cut(held, "img", lambda h, j: lax.dynamic_slice_in_dim(h, small * j, small, 1))
+
+
+def row_parts(held):
+    return cut(held, "row", lambda h, r: lax.dynamic_index_in_dim(h, r, 0, keepdims=False))
+
+
+def whole_share(held, share):
+    whole = gathered(held, "img")
+    return whole.reshape(-1, held.shape[1])[:share].astype(jnp.float32)
 
 
 def plain_shares(part):
@@ -378,11 +456,9 @@
             a, b, (((0,), (0,)), ((), ())), preferred_element_type=jnp.float32
         ).astype(jnp.bfloat16)
 
-    simple = two_columns and row_count == 4
+    simple = two_columns and row_count == 4 and lax.axis_size("img") == 4
     if simple:
-        early = image_shares(*outer_halves(token_rows, dquery, grad_rows, attended))
-        early, ext_grad = lax.optimization_barrier((early, ext_grad))
-        early = exchange_sum(early, "img")
+        early = image_parts(core_sum(*outer_halves(token_rows, dquery, grad_rows, attended)))
     dquery, attended = dquery[:, :INNER], attended[:, 64:]
     sublayer_out = nt_dot(attended, out_weight).astype(jnp.bfloat16)
 
@@ -393,26 +469,36 @@
         return jnp.concatenate(order, axis=2).reshape(-1, 2 * INNER)
 
     side_first = token_count + 2 * chunk_own
-    inner_grad, side_grad = ext_grad[:side_first].astype(jnp.float32), ext_grad[side_first:]
+    side_grad = ext_grad[side_first:]
     if two_columns:
         got = moved(side_grad, 0, 0)
-        returned = jnp.where(col_id == 0, spread(got, False), spread(got, True))
+        returned = lambda part: jnp.where(col_id == 0, spread(part, False), spread(part, True))
     else:
         halves = side_grad.reshape(strips + 2, 2, SIDE * REACH, 2 * INNER)
-        returned = spread(moved(halves[:, 0], 0, -1), False) + spread(moved(halves[:, 1], 0, 1), True)
-    inner_grad = inner_grad + returned
-    dkv = inner_grad[:token_count]
-    to_above = inner_grad[token_count : token_count + chunk_own].astype(jnp.bfloat16)
-    to_below = inner_grad[token_count + chunk_own :].astype(jnp.bfloat16)
-    from_below = moved(to_above, -1).astype(jnp.float32)
-    from_above = moved(to_below, 1).astype(jnp.float32)
-    rest = jnp.zeros((token_count - chunk_own, 2 * INNER), jnp.float32)
-    dkv = dkv + jnp.concatenate([from_above, rest], axis=0)
-    dkv = dkv + jnp.concatenate([rest, from_below], axis=0)
-    dkv = dkv.astype(jnp.bfloat16)
+        got = jnp.stack([moved(halves[:, 0], 0, -1), moved(halves[:, 1], 0, 1)], axis=1)
+        returned = lambda part: spread(part[:, 0], False) + spread(part[:, 1], True)
+    got = got.reshape(strips + 2, -1, SIDE * REACH, 2 * INNER)
+    outer_grad = ext_grad[token_count:side_first].astype(jnp.float32) + returned(got[strips:])
+    outer_grad = outer_grad.astype(jnp.bfloat16)
+    from_below = moved(outer_grad[:chunk_own], -1)
+    from_above = moved(outer_grad[chunk_own:], 1)
     if simple:
-        late = exchange_sum(image_shares(*outer_halves(token_rows, dkv)), "img")
-        early, late = row_shares(early, late, width // (row_count * col_count))
+        side = got.reshape(-1, 2 * INNER)
+        sent, kept, dkv = late_halves(early[1:], token_rows, ext_grad, side, from_above, from_below)
+    else:
+        dkv = ext_grad[:token_count].astype(jnp.float32) + returned(got[:strips])
+        rest = jnp.zeros((token_count - chunk_own, 2 * INNER), jnp.float32)
+        dkv = dkv + jnp.concatenate([from_above.astype(jnp.float32), rest], axis=0)
+        dkv = dkv + jnp.concatenate([rest, from_below.astype(jnp.float32)], axis=0)
+        dkv = dkv.astype(jnp.bfloat16)
+    if simple:
+        late = image_parts(core_sum(sent, kept))
+        early = exchange_sum(early, "img")
+        late = exchange_sum(late, "img", early)
+        early = exchange_sum(row_parts(early), "row")
+        late = exchange_sum(row_parts(late), "row", early)
+        share = width // (row_count * col_count)
+        early, late = whole_share(early, share), whole_share(late, share)
     else:
         early = jnp.concatenate([outer(token_rows, dquery), outer(grad_rows, attended)], axis=1)
         early, late = plain_shares(early), plain_shares(outer(token_rows, dkv))

time: 162 us -> 125 us (0.77)
  waiting for transfers between devices: 71.5 us -> 36.4 us
  starting transfers between devices: 30.3 us -> 38 us
  other arithmetic: 9.91 us -> 4.47 us
  matrix products: 14.1 us -> 12 us
    all_to_all x4 -> x0, waiting for transfers between devices: 53.6 us -> none  [the longest x3 49.4 us: exchange_sum(): got = lax.all_to_all(block, axis, split_axis=0, concat_axis=0, tiled=True)]
    ppermute x2 -> x20, starting transfers between devices: 0.21 us -> 26.6 us  [the longest x12 16.5 us: exchange_sum(): got.append(lax.ppermute(part, axis, pairs))]
    ppermute x2 -> x20, waiting for transfers between devices: 2.92 us -> 25.6 us  [the longest x12 21.7 us: exchange_sum(): got.append(lax.ppermute(part, axis, pairs))]
    all_to_all x4 -> x0, starting transfers between devices: 16.3 us -> none  [the longest x3 12.1 us: exchange_sum(): got = lax.all_to_all(block, axis, split_axis=0, concat_axis=0, tiled=True)]
    ppermute x7, waiting for transfers between devices: 14.9 us -> 10.9 us  [moved(): return lax.ppermute(block, ('row', 'col'), pairs)]
    reduce_sum x3 -> x0, other arithmetic: 3.07 us -> none  [exchange_sum(): return jnp.sum(got.astype(jnp.float32), axis=0).astype(jnp.bfloat16)]
    pallas_call x2 -> x1, Pallas kernels: 5.59 us -> 2.64 us  [outer_halves(): pl.pallas_call(outer_kernel, grid=(1,), out_shape=(out, out), in_specs=[p...]
    ppermute x7, starting transfers between devices: 13.8 us -> 11.5 us  [moved(): return lax.ppermute(block, ('row', 'col'), pairs)]
  transfers between devices with their start and end apart: 13 -> 27, of which waited for: 10 -> 15; matrix products, arithmetic and copies ran while one was open for 12% -> 10% of each run, Pallas kernels for 0% -> 4%
where the time goes in v4:
time: 125 us; the launch traced here: 124 us
  starting transfers between devices  38 us (30%)
  waiting for transfers between devices  36.4 us (29%)
  Pallas kernels  19.8 us (16%)
  local copies, waits for them, and re-layouts  12.4 us (10%)
  matrix products  12 us (10%)
  other arithmetic  4.47 us (4%)
    ppermute x12, waiting for transfers between devices, exchange_sum(): got.append(lax.ppermute(part, axis, pairs))  21.7 us
    ppermute x12, starting transfers between devices, exchange_sum(): got.append(lax.ppermute(part, axis, pairs))  16.5 us
    pallas_call x1, Pallas kernels, attention(): pl.pallas_call(attention_kernel, grid=(1,), out_shape=outs, in_specs=[pl....  15.1 us
    ppermute x7, starting transfers between devices, moved(): return lax.ppermute(block, ('row', 'col'), pairs)  11.5 us
    ppermute x7, waiting for transfers between devices, moved(): return lax.ppermute(block, ('row', 'col'), pairs)  10.9 us
    ppermute x6, starting transfers between devices, gathered(): got = lax.ppermute(block, axis, [(i, i ^ step) for i in range(count)])  9.6 us
    unnamed x22, local copies, waits for them, and re-layouts  6.08 us
    dot_general x2, matrix products, nt_dot(): lax.dot_general(a, b, (((1,), (1,)), ((), ())), preferred_element_type=jn...  5.85 us
  transfers between devices with their start and end apart: 27, of which 15 were waited for; matrix products, arithmetic and copies ran while one was open for 10% of the time, Pallas kernels for 4%

profile of v4, /device:TPU:0, one launch (start us, length us, event | category | flops | bytes accessed | tf_op | source)
XLA Modules:
  0.0 124.2 jit_solution(9614055102349841804)
XLA Ops:
  0.6 5.2 %convolution_convert_fusion.q_ref = bf16[512,1728]{1,0:T(8,128)(2,1)S(1)} fusion(bf16[512,1152]{1,0:T(8,128)(2,1)} %bitcast.60, bf16[1152,1728]{0,1:T(8,128)(2,1)} %param.5), kind=kOutput, calls=%fused_computation | convolution fusion | flops 2039316480 | bytes 6930432 | tf_op jit(solution)/shard_map/dot_general | solution.py:26
  5.8 1.3 %fusion.14 = (bf16[128,1152]{1,0:T(8,128)(2,1)}, bf16[128,1152]{1,0:T(8,128)(2,1)}) fusion(bf16[512,1728]{1,0:T(8,128)(2,1)S(1)} %convolution_convert_fusion.q_ref), kind=kLoop, calls=%fused_computation.74 | loop fusion | bytes 1179648 | tf_op jit(solution)/shard_map/slice | solution.py:442
  7.1 5.6 %collective-permute-start = (bf16[128,1152]{1,0:T(8,128)(2,1)}, bf16[128,1152]{1,0:T(8,128)(2,1)}, u32[]{:S(2)}, u32[]{:S(2)}) collective-permute-start(bf16[128,1152]{1,0:T(8,128)(2,1)} %get-tuple-element.29), channel_id=1, source_target_pairs={{0,2},{1,3},{2,4},{3,5},{4,6},{5,7},{8,10},{9,11},{10,12},{11,13},... | collective-permute-start | bytes 884744 | tf_op jit(solution)/shard_map/ppermute | solution.py:425
  12.8 1.3 %collective-permute-start.1 = (bf16[128,1152]{1,0:T(8,128)(2,1)}, bf16[128,1152]{1,0:T(8,128)(2,1)S(1)}, u32[]{:S(2)}, u32[]{:S(2)}) collective-permute-start(bf16[128,1152]{1,0:T(8,128)(2,1)} %get-tuple-element.28), channel_id=1, source_target_pairs={{2,0},{3,1},{4,2},{5,3},{6,4},{7,5},{10,8},{11,9},{12,10},{13,11},... | collective-permute-start | bytes 884744 | tf_op jit(solution)/shard_map/ppermute | solution.py:425
  14.1 0.7 slice.59.own_ref
  15.6 0.1 fusion.8
  15.9 1.3 %fusion.6.bias_ref = f32[4,576,128]{2,1,0:T(8,128)} fusion(s32[4,128]{1,0:T(4,128)S(1)} %add_clamp_fusion, s32[4,576]{1,0:T(4,128)S(1)} %broadcast_add_fusion, pred[576,128]{1,0:T(8,128)(4,1)S(1)} %fusion.8), kind=kLoop, calls=%fused_computation.16 | loop fusion | flops 1769472 | bytes 1264640 | tf_op jit(solution)/shard_map/jit(_where)/select_n | solution.py:339
  17.2 1.4 %collective-permute-done = bf16[128,1152]{1,0:T(8,128)(2,1)} collective-permute-done((bf16[128,1152]{1,0:T(8,128)(2,1)}, bf16[128,1152]{1,0:T(8,128)(2,1)}, u32[]{:S(2)}, u32[]{:S(2)}) %collective-permute-start) | collective-permute-done | bytes 294944 | tf_op jit(solution)/shard_map/ppermute | solution.py:425
  18.6 1.0 constant_dynamic-update-slice_fusion.1
  19.6 3.7 %collective-permute-done.1 = bf16[128,1152]{1,0:T(8,128)(2,1)S(1)} collective-permute-done((bf16[128,1152]{1,0:T(8,128)(2,1)}, bf16[128,1152]{1,0:T(8,128)(2,1)S(1)}, u32[]{:S(2)}, u32[]{:S(2)}) %collective-permute-start.1) | collective-permute-done | bytes 294944 | tf_op jit(solution)/shard_map/ppermute | solution.py:425
  23.5 1.0 convolution_convert_fusion.3.g_ref
  24.5 0.6 collective-permute-done.3
  25.0 15.1 %window_attention.1 = (bf16[512,640]{1,0:T(8,128)(2,1)}, bf16[512,640]{1,0:T(8,128)(2,1)}, bf16[1152,1152]{1,0:T(8,128)(2,1)}) custom-call(s32[4]{0:T(128)S(1)} %broadcast_subtract_fusion.start_ref, bf16[512,1728]{1,0:T(8,128)(2,1)} %copy-done.8, bf16[512,1152]{1,0:T(8,128)(2,1)} %copy-done.7, bf16[576,512]{1,0:T(8,128)(2,1)S(1)} %convolution_convert_fusion.3.g_ref, ...), custom_call_target="tpu_custom_call" | custom-call | flops 4076863488 | bytes 16777216 | tf_op jit(solution)/shard_map/window_attention/pallas_call | solution.py:183
  40.1 2.2 %slice.50 = bf16[384,1152]{1,0:T(8,128)(2,1)} slice(bf16[1152,1152]{1,0:T(8,128)(2,1)} %get-tuple-element.18.inner_ref), slice={[768:1152], [0:1152]} | slice | bytes 1769472 | tf_op jit(solution)/shard_map/slice | solution.py:472
  42.5 1.3 %copy-done.4 = bf16[1,32,16,1152]{3,2,1,0:T(8,128)(2,1)S(1)} copy-done((bf16[1,32,16,1152]{3,2,1,0:T(8,128)(2,1)S(1)}, bf16[1,32,16,1152]{3,2,1,0:T(8,128)(2,1)}, u32[]{:S(2)}) %copy-start.4) | copy-done | bytes 1179672
  43.8 1.1 copy-done.5
  44.9 1.1 copy-done.6
  45.9 2.6 %weight_grad_halves.1 = (bf16[576,1152]{1,0:T(8,128)(2,1)S(1)}, bf16[576,1152]{1,0:T(8,128)(2,1)S(1)}) custom-call(s32[1]{0:T(128)} %bitcast.7.own_ref, bf16[512,1152]{1,0:T(8,128)(2,1)S(1)} %bitcast.61, bf16[512,640]{1,0:T(8,128)(2,1)S(1)} %copy-done.5, bf16[512,1152]{1,0:T(8,128)(2,1)S(1)} %bitcast.65, bf16[512,640]{1,0:T(8,128)(2,1)S(1)} %copy-done.6), custom_call_target="tpu_custom_call" | custom-call | flops 1358954496 | bytes 5242880 | tf_op jit(solution)/shard_map/weight_grad_halves/pallas_call | solution.py:244
  48.6 0.4 collective-permute-start.4
  49.0 2.2 %convolution_convert_fusion.2 = bf16[512,1152]{1,0:T(8,128)(2,1)} fusion(bf16[1152,576]{0,1:T(8,128)(2,1)S(1)} %copy-done, bf16[512,640]{1,0:T(8,128)(2,1)S(1)} %copy-done.6), kind=kOutput, calls=%fused_computation.2 | convolution fusion | flops 680067072 | bytes 3162112 | tf_op jit(solution)/shard_map/dot_general | solution.py:30
  51.4 1.6 %copy-done.1 = bf16[1152,1152]{1,0:T(8,128)(2,1)S(1)} copy-done((bf16[1152,1152]{1,0:T(8,128)(2,1)S(1)}, bf16[1152,1152]{1,0:T(8,128)(2,1)}, u32[]{:S(2)}) %copy-start.1) | copy-done | bytes 2654232
  53.0 0.1 fusion.3
  53.2 2.8 %collective-permute-start.6 = (bf16[128,1152]{1,0:T(8,128)(2,1)S(1)}, bf16[128,1152]{1,0:T(8,128)(2,1)S(1)}, u32[]{:S(2)}, u32[]{:S(2)}) collective-permute-start(bf16[128,1152]{1,0:T(8,128)(2,1)S(1)} %get-tuple-element.40), channel_id=1, source_target_pairs={{0,2},{1,3},{2,4},{3,5},{4,6},{5,7},{8,10},{9,11},{10,12},{11,13},... | collective-permute-start | bytes 884744 | tf_op jit(solution)/shard_map/ppermute | solution.py:425
  56.0 1.5 %collective-permute-start.7 = (bf16[128,1152]{1,0:T(8,128)(2,1)S(1)}, bf16[128,1152]{1,0:T(8,128)(2,1)S(1)}, u32[]{:S(2)}, u32[]{:S(2)}) collective-permute-start(bf16[128,1152]{1,0:T(8,128)(2,1)S(1)} %get-tuple-element.39), channel_id=1, source_target_pairs={{2,0},{3,1},{4,2},{5,3},{6,4},{7,5},{10,8},{11,9},{12,10},{13,11},... | collective-permute-start | bytes 884744 | tf_op jit(solution)/shard_map/ppermute | solution.py:425
  57.5 0.3 add_convert_fusion.1
  57.8 0.2 pad_dynamic-slice_fusion.5
  58.0 2.5 %collective-permute-start.10 = (bf16[4,40,1152]{2,1,0:T(8,128)(2,1)S(1)}, bf16[4,40,1152]{2,1,0:T(8,128)(2,1)S(1)}, u32[]{:S(2)}, u32[]{:S(2)}) collective-permute-start(bf16[4,40,1152]{2,1,0:T(8,128)(2,1)S(1)} %get-tuple-element.34.third), channel_id=1, source_target_pairs={{0,24},{8,16},{16,8},{24,0},{1,25},{9,17},{17,9},{25,1},{2,26},{10... | collective-permute-start | bytes 1105928 | tf_op jit(solution)/shard_map/ppermute | solution.py:356
  60.5 0.5 collective-permute-start.8
  61.1 0.5 collective-permute-start.9
  61.6 1.0 collective-permute-done.6.above_ref
  62.6 4.1 %collective-permute-done.7.below_ref = bf16[128,1152]{1,0:T(8,128)(2,1)S(1)} collective-permute-done((bf16[128,1152]{1,0:T(8,128)(2,1)S(1)}, bf16[128,1152]{1,0:T(8,128)(2,1)S(1)}, u32[]{:S(2)}, u32[]{:S(2)}) %collective-permute-start.7) | collective-permute-done | bytes 294944 | tf_op jit(solution)/shard_map/ppermute | solution.py:425
  66.7 2.1 %late_weight_grad_halves.1 = (bf16[576,1152]{1,0:T(8,128)(2,1)S(1)}, bf16[576,1152]{1,0:T(8,128)(2,1)S(1)}, bf16[512,1152]{1,0:T(8,128)(2,1)S(1)}) custom-call(s32[1]{0:T(128)} %bitcast.7.own_ref, bf16[4,40,1152]{2,1,0:T(8,128)(2,1)S(1)} %get-tuple-element.36.first, bf16[4,40,1152]{2,1,0:T(8,128)(2,1)S(1)} %get-tuple-element.35.second, ...), custom_call_target="tpu_custom_call" | custom-call | flops 1358954496 | bytes 7340032 | tf_op jit(solution)/shard_map/late_weight_grad_halves/pallas_call | solution.py:292
  68.9 3.6 %convolution_convert_fusion.1 = bf16[512,1152]{1,0:T(8,128)(2,1)} fusion(bf16[1152,1728]{0,1:T(8,128)(2,1)S(1)} %copy-done.9, bf16[512,1152]{1,0:T(8,128)(2,1)S(1)} %get-tuple-element.19, bf16[512,576]{1,0:T(8,128)(2,1)S(1)} %bitcast.67), kind=kOutput, calls=%fused_computation.1 | convolution fusion | flops 2042560512 | bytes 6930432 | tf_op jit(solution)/shard_map/dot_general | solution.py:30
  72.5 4.8 %collective-permute-done.8 = bf16[4,40,1152]{2,1,0:T(8,128)(2,1)S(1)} collective-permute-done((bf16[4,40,1152]{2,1,0:T(8,128)(2,1)S(1)}, bf16[4,40,1152]{2,1,0:T(8,128)(2,1)S(1)}, u32[]{:S(2)}, u32[]{:S(2)}) %collective-permute-start.8) | collective-permute-done | bytes 368672 | tf_op jit(solution)/shard_map/ppermute | solution.py:356
  77.3 0.2 add_convert_fusion.3
  77.6 2.4 %collective-permute-start.11 = (bf16[40,1152]{1,0:T(8,128)(2,1)S(1)}, bf16[40,1152]{1,0:T(8,128)(2,1)S(1)}, u32[]{:S(2)}, u32[]{:S(2)}) collective-permute-start(bf16[40,1152]{1,0:T(8,128)(2,1)S(1)} %get-tuple-element.41), channel_id=1, source_target_pairs={{0,2},{2,0},{4,6},{6,4},{1,3},{3,1},{5,7},{7,5},{8,10},{10,8},{12,... | collective-permute-start | bytes 276488 | tf_op jit(solution)/shard_map/ppermute | solution.py:356
  80.0 1.3 %collective-permute-start.12 = (bf16[40,1152]{1,0:T(8,128)(2,1)S(1)}, bf16[40,1152]{1,0:T(8,128)(2,1)S(1)}, u32[]{:S(2)}, u32[]{:S(2)}) collective-permute-start(bf16[40,1152]{1,0:T(8,128)(2,1)S(1)} %get-tuple-element.43), channel_id=1, source_target_pairs={{0,4},{2,6},{4,0},{6,2},{1,5},{3,7},{5,1},{7,3},{8,12},{10,14},{12... | collective-permute-start | bytes 276488 | tf_op jit(solution)/shard_map/ppermute | solution.py:356
  81.3 1.2 collective-permute-start.13
  82.5 0.3 add_convert_fusion
  82.8 0.2 pad_dynamic-slice_fusion.3
  83.0 1.6 %collective-permute-start.18 = (bf16[4,40,1152]{2,1,0:T(8,128)(2,1)S(1)}, bf16[4,40,1152]{2,1,0:T(8,128)(2,1)S(1)}, u32[]{:S(2)}, u32[]{:S(2)}) collective-permute-start(bf16[4,40,1152]{2,1,0:T(8,128)(2,1)S(1)} %get-tuple-element.31), channel_id=1, source_target_pairs={{0,8},{8,0},{16,24},{24,16},{1,9},{9,1},{17,25},{25,17},{2,10},{10... | collective-permute-start | bytes 1105928 | tf_op jit(solution)/shard_map/ppermute | solution.py:356
  84.6 1.4 %collective-permute-start.19 = (bf16[4,40,1152]{2,1,0:T(8,128)(2,1)S(1)}, bf16[4,40,1152]{2,1,0:T(8,128)(2,1)S(1)}, u32[]{:S(2)}, u32[]{:S(2)}) collective-permute-start(bf16[4,40,1152]{2,1,0:T(8,128)(2,1)S(1)} %get-tuple-element.32), channel_id=1, source_target_pairs={{0,16},{8,24},{16,0},{24,8},{1,17},{9,25},{17,1},{25,9},{2,18},{10... | collective-permute-start | bytes 1105928 | tf_op jit(solution)/shard_map/ppermute | solution.py:356
  86.0 0.6 collective-permute-start.20
  86.6 3.5 %collective-permute-done.12 = bf16[40,1152]{1,0:T(8,128)(2,1)S(1)} collective-permute-done((bf16[40,1152]{1,0:T(8,128)(2,1)S(1)}, bf16[40,1152]{1,0:T(8,128)(2,1)S(1)}, u32[]{:S(2)}, u32[]{:S(2)}) %collective-permute-start.12) | collective-permute-done | bytes 92192 | tf_op jit(solution)/shard_map/ppermute | solution.py:356
  90.2 1.5 %collective-permute-start.14 = (bf16[40,1152]{1,0:T(8,128)(2,1)S(1)}, bf16[40,1152]{1,0:T(8,128)(2,1)S(1)}, u32[]{:S(2)}, u32[]{:S(2)}) collective-permute-start(bf16[40,1152]{1,0:T(8,128)(2,1)S(1)} %get-tuple-element.25), channel_id=1, source_target_pairs={{0,8},{8,0},{16,24},{24,16},{1,9},{9,1},{17,25},{25,17},{2,10},{10... | collective-permute-start | bytes 276488 | tf_op jit(solution)/shard_map/ppermute | solution.py:371
  91.7 1.5 %collective-permute-start.15 = (bf16[40,1152]{1,0:T(8,128)(2,1)S(1)}, bf16[40,1152]{1,0:T(8,128)(2,1)S(1)}, u32[]{:S(2)}, u32[]{:S(2)}) collective-permute-start(bf16[40,1152]{1,0:T(8,128)(2,1)S(1)} %get-tuple-element.25), channel_id=1, source_target_pairs={{0,16},{8,24},{16,0},{24,8},{1,17},{9,25},{17,1},{25,9},{2,18},{10... | collective-permute-start | bytes 276488 | tf_op jit(solution)/shard_map/ppermute | solution.py:371
  93.3 1.4 %collective-permute-done.18 = bf16[4,40,1152]{2,1,0:T(8,128)(2,1)S(1)} collective-permute-done((bf16[4,40,1152]{2,1,0:T(8,128)(2,1)S(1)}, bf16[4,40,1152]{2,1,0:T(8,128)(2,1)S(1)}, u32[]{:S(2)}, u32[]{:S(2)}) %collective-permute-start.18) | collective-permute-done | bytes 368672 | tf_op jit(solution)/shard_map/ppermute | solution.py:356
  94.6 2.3 %collective-permute-start.16 = (bf16[40,1152]{1,0:T(8,128)(2,1)S(1)}, bf16[40,1152]{1,0:T(8,128)(2,1)S(1)}, u32[]{:S(2)}, u32[]{:S(2)}) collective-permute-start(bf16[40,1152]{1,0:T(8,128)(2,1)S(1)} %get-tuple-element.25), channel_id=1, source_target_pairs={{0,24},{8,16},{16,8},{24,0},{1,25},{9,17},{17,9},{25,1},{2,26},{10... | collective-permute-start | bytes 276488 | tf_op jit(solution)/shard_map/ppermute | solution.py:371
  97.0 6.9 %collective-permute-done.19 = bf16[4,40,1152]{2,1,0:T(8,128)(2,1)S(1)} collective-permute-done((bf16[4,40,1152]{2,1,0:T(8,128)(2,1)S(1)}, bf16[4,40,1152]{2,1,0:T(8,128)(2,1)S(1)}, u32[]{:S(2)}, u32[]{:S(2)}) %collective-permute-start.19) | collective-permute-done | bytes 368672 | tf_op jit(solution)/shard_map/ppermute | solution.py:356
  103.9 0.2 add_convert_fusion.2
  104.1 1.0 collective-permute-start.21
  105.1 2.3 %collective-permute-start.22 = (bf16[40,1152]{1,0:T(8,128)(2,1)S(1)}, bf16[40,1152]{1,0:T(8,128)(2,1)S(1)}, u32[]{:S(2)}, u32[]{:S(2)}) collective-permute-start(bf16[40,1152]{1,0:T(8,128)(2,1)S(1)} %get-tuple-element.46), channel_id=1, source_target_pairs={{0,4},{2,6},{4,0},{6,2},{1,5},{3,7},{5,1},{7,3},{8,12},{10,14},{12... | collective-permute-start | bytes 276488 | tf_op jit(solution)/shard_map/ppermute | solution.py:356
  107.4 1.2 collective-permute-start.23
  108.6 0.7 collective-permute-done.21
  109.3 2.2 %collective-permute-done.22 = bf16[40,1152]{1,0:T(8,128)(2,1)S(1)} collective-permute-done((bf16[40,1152]{1,0:T(8,128)(2,1)S(1)}, bf16[40,1152]{1,0:T(8,128)(2,1)S(1)}, u32[]{:S(2)}, u32[]{:S(2)}) %collective-permute-start.22) | collective-permute-done | bytes 92192 | tf_op jit(solution)/shard_map/ppermute | solution.py:356
  111.5 2.2 %collective-permute-done.23 = bf16[40,1152]{1,0:T(8,128)(2,1)S(1)} collective-permute-done((bf16[40,1152]{1,0:T(8,128)(2,1)S(1)}, bf16[40,1152]{1,0:T(8,128)(2,1)S(1)}, u32[]{:S(2)}, u32[]{:S(2)}) %collective-permute-start.23) | collective-permute-done | bytes 92192 | tf_op jit(solution)/shard_map/ppermute | solution.py:356
  113.8 1.2 collective-permute-start.24
  115.1 1.4 %collective-permute-start.25 = (bf16[40,1152]{1,0:T(8,128)(2,1)S(1)}, bf16[40,1152]{1,0:T(8,128)(2,1)S(1)}, u32[]{:S(2)}, u32[]{:S(2)}) collective-permute-start(bf16[40,1152]{1,0:T(8,128)(2,1)S(1)} %get-tuple-element.27), channel_id=1, source_target_pairs={{0,16},{8,24},{16,0},{24,8},{1,17},{9,25},{17,1},{25,9},{2,18},{10... | collective-permute-start | bytes 276488 | tf_op jit(solution)/shard_map/ppermute | solution.py:371
  116.5 1.5 %collective-permute-start.26 = (bf16[40,1152]{1,0:T(8,128)(2,1)S(1)}, bf16[40,1152]{1,0:T(8,128)(2,1)S(1)}, u32[]{:S(2)}, u32[]{:S(2)}) collective-permute-start(bf16[40,1152]{1,0:T(8,128)(2,1)S(1)} %get-tuple-element.27), channel_id=1, source_target_pairs={{0,24},{8,16},{16,8},{24,0},{1,25},{9,17},{17,9},{25,1},{2,26},{10... | collective-permute-start | bytes 276488 | tf_op jit(solution)/shard_map/ppermute | solution.py:371
  118.0 0.4 collective-permute-done.24
  118.4 1.2 collective-permute-done.25
  119.7 2.3 %collective-permute-done.26 = bf16[40,1152]{1,0:T(8,128)(2,1)S(1)} collective-permute-done((bf16[40,1152]{1,0:T(8,128)(2,1)S(1)}, bf16[40,1152]{1,0:T(8,128)(2,1)S(1)}, u32[]{:S(2)}, u32[]{:S(2)}) %collective-permute-start.26) | collective-permute-done | bytes 92192 | tf_op jit(solution)/shard_map/ppermute | solution.py:371
  122.0 0.9 fusion.15
  123.0 1.2 pad_maximum_fusion
  (76 shorter events, 1.9 us)
Async XLA Ops:
  0.6 22.8 %copy-start = (bf16[1152,576]{0,1:T(8,128)(2,1)S(1)}, bf16[1152,576]{0,1:T(8,128)(2,1)}, u32[]{:S(2)}) copy-start(bf16[1152,576]{0,1:T(8,128)(2,1)} %param.6) | copy-start | bytes 3981316
  5.8 8.2 %copy-start.8 = (bf16[512,1728]{1,0:T(8,128)(2,1)}, bf16[512,1728]{1,0:T(8,128)(2,1)S(1)}, u32[]{:S(2)}) copy-start(bf16[512,1728]{1,0:T(8,128)(2,1)S(1)} %convolution_convert_fusion.q_ref) | copy-start | bytes 5308420
  7.1 11.5 %collective-permute-start = (bf16[128,1152]{1,0:T(8,128)(2,1)}, bf16[128,1152]{1,0:T(8,128)(2,1)}, u32[]{:S(2)}, u32[]{:S(2)}) collective-permute-start(bf16[128,1152]{1,0:T(8,128)(2,1)} %get-tuple-element.29), channel_id=1, source_target_pairs={{0,2},{1,3},{2,4},{3,5},{4,6},{5,7},{8,10},{9,11},{10,12},{11,13},... | collective-permute-start | bytes 884744 | tf_op jit(solution)/shard_map/ppermute | solution.py:425
  12.8 10.6 %collective-permute-start.1 = (bf16[128,1152]{1,0:T(8,128)(2,1)}, bf16[128,1152]{1,0:T(8,128)(2,1)S(1)}, u32[]{:S(2)}, u32[]{:S(2)}) collective-permute-start(bf16[128,1152]{1,0:T(8,128)(2,1)} %get-tuple-element.28), channel_id=1, source_target_pairs={{2,0},{3,1},{4,2},{5,3},{6,4},{7,5},{10,8},{11,9},{12,10},{13,11},... | collective-permute-start | bytes 884744 | tf_op jit(solution)/shard_map/ppermute | solution.py:425
  14.8 2.4 %copy-start.7 = (bf16[512,1152]{1,0:T(8,128)(2,1)}, bf16[512,1152]{1,0:T(8,128)(2,1)S(1)}, u32[]{:S(2)}) copy-start(bf16[512,1152]{1,0:T(8,128)(2,1)S(1)} %slice.59.own_ref) | copy-start | bytes 3538948
  14.9 10.2 %collective-permute-start.2 = (bf16[32,8,1152]{2,1,0:T(8,128)(2,1)S(1)}, bf16[32,8,1152]{2,1,0:T(8,128)(2,1)}, u32[]{:S(2)}, u32[]{:S(2)}) collective-permute-start(bf16[32,8,1152]{2,1,0:T(8,128)(2,1)S(1)} %constant_dynamic-slice_fusion.1), channel_id=1, source_target_pairs={{0,1},{1,0},{2,3},{3,2},{4,5},{5,4},{6,7},{7,6},{8,9},{9,8},{10,11... | collective-permute-start | bytes 1769480 | tf_op jit(solution)/shard_map/ppermute | solution.py:425
  15.9 7.6 %copy-start.3 = (bf16[1,32,16,1152]{3,2,1,0:T(8,128)(2,1)S(1)}, bf16[1,32,16,1152]{3,2,1,0:T(8,128)(2,1)}, u32[]{:S(2)}) copy-start(bf16[1,32,16,1152]{3,2,1,0:T(8,128)(2,1)} %param.7) | copy-start | bytes 3538948
  23.4 1.6 %collective-permute-start.3 = (bf16[16,8,1152]{2,1,0:T(8,128)(2,1)S(1)}, bf16[16,8,1152]{2,1,0:T(8,128)(2,1)S(1)}, u32[]{:S(2)}, u32[]{:S(2)}) collective-permute-start(bf16[16,8,1152]{2,1,0:T(8,128)(2,1)S(1)} %constant_dynamic-slice_fusion), channel_id=1, source_target_pairs={{0,1},{1,0},{2,3},{3,2},{4,5},{5,4},{6,7},{7,6},{8,9},{9,8},{10,11... | collective-permute-start | bytes 884744 | tf_op jit(solution)/shard_map/ppermute | solution.py:425
  40.1 2.4 %copy-start.2 = (bf16[1,32,16,1152]{3,2,1,0:T(8,128)(2,1)S(1)}, bf16[1,32,16,1152]{3,2,1,0:T(8,128)(2,1)}, u32[]{:S(2)}) copy-start(bf16[1,32,16,1152]{3,2,1,0:T(8,128)(2,1)} %param.4) | copy-start | bytes 3538948
  42.4 8.9 %collective-permute-start.5 = (bf16[384,1152]{1,0:T(8,128)(2,1)}, bf16[384,1152]{1,0:T(8,128)(2,1)S(1)}, u32[]{:S(2)}, u32[]{:S(2)}) collective-permute-start(bf16[384,1152]{1,0:T(8,128)(2,1)} %slice.50), channel_id=1, source_target_pairs={{0,1},{1,0},{2,3},{3,2},{4,5},{5,4},{6,7},{7,6},{8,9},{9,8},{10,11... | collective-permute-start | bytes 2654216 | tf_op jit(solution)/shard_map/ppermute | solution.py:425
  42.5 1.3 %copy-start.4 = (bf16[1,32,16,1152]{3,2,1,0:T(8,128)(2,1)S(1)}, bf16[1,32,16,1152]{3,2,1,0:T(8,128)(2,1)}, u32[]{:S(2)}) copy-start(bf16[1,32,16,1152]{3,2,1,0:T(8,128)(2,1)} %param.7) | copy-start | bytes 3538948
  43.8 1.1 copy-start.5
  44.8 1.1 copy-start.6
  48.6 8.9 %collective-permute-start.4 = (bf16[576,1152]{1,0:T(8,128)(2,1)S(1)}, bf16[576,1152]{1,0:T(8,128)(2,1)S(1)}, u32[]{:S(2)}, u32[]{:S(2)}) collective-permute-start(bf16[576,1152]{1,0:T(8,128)(2,1)S(1)} %get-tuple-element.17), channel_id=1, source_target_pairs={{0,1},{1,0},{2,3},{3,2},{4,5},{5,4},{6,7},{7,6},{8,9},{9,8},{10,11... | collective-permute-start | bytes 3981320 | tf_op jit(solution)/shard_map/ppermute | solution.py:381
  51.3 1.8 %copy-start.1 = (bf16[1152,1152]{1,0:T(8,128)(2,1)S(1)}, bf16[1152,1152]{1,0:T(8,128)(2,1)}, u32[]{:S(2)}) copy-start(bf16[1152,1152]{1,0:T(8,128)(2,1)} %get-tuple-element.18.inner_ref) | copy-start | bytes 7962628
  53.2 9.3 %collective-permute-start.6 = (bf16[128,1152]{1,0:T(8,128)(2,1)S(1)}, bf16[128,1152]{1,0:T(8,128)(2,1)S(1)}, u32[]{:S(2)}, u32[]{:S(2)}) collective-permute-start(bf16[128,1152]{1,0:T(8,128)(2,1)S(1)} %get-tuple-element.40), channel_id=1, source_target_pairs={{0,2},{1,3},{2,4},{3,5},{4,6},{5,7},{8,10},{9,11},{10,12},{11,13},... | collective-permute-start | bytes 884744 | tf_op jit(solution)/shard_map/ppermute | solution.py:425
  56.0 10.7 %collective-permute-start.7 = (bf16[128,1152]{1,0:T(8,128)(2,1)S(1)}, bf16[128,1152]{1,0:T(8,128)(2,1)S(1)}, u32[]{:S(2)}, u32[]{:S(2)}) collective-permute-start(bf16[128,1152]{1,0:T(8,128)(2,1)S(1)} %get-tuple-element.39), channel_id=1, source_target_pairs={{2,0},{3,1},{4,2},{5,3},{6,4},{7,5},{10,8},{11,9},{12,10},{13,11},... | collective-permute-start | bytes 884744 | tf_op jit(solution)/shard_map/ppermute | solution.py:425
  58.0 14.5 %collective-permute-start.10 = (bf16[4,40,1152]{2,1,0:T(8,128)(2,1)S(1)}, bf16[4,40,1152]{2,1,0:T(8,128)(2,1)S(1)}, u32[]{:S(2)}, u32[]{:S(2)}) collective-permute-start(bf16[4,40,1152]{2,1,0:T(8,128)(2,1)S(1)} %get-tuple-element.34.third), channel_id=1, source_target_pairs={{0,24},{8,16},{16,8},{24,0},{1,25},{9,17},{17,9},{25,1},{2,26},{10... | collective-permute-start | bytes 1105928 | tf_op jit(solution)/shard_map/ppermute | solution.py:356
  60.5 16.8 %collective-permute-start.8 = (bf16[4,40,1152]{2,1,0:T(8,128)(2,1)S(1)}, bf16[4,40,1152]{2,1,0:T(8,128)(2,1)S(1)}, u32[]{:S(2)}, u32[]{:S(2)}) collective-permute-start(bf16[4,40,1152]{2,1,0:T(8,128)(2,1)S(1)} %get-tuple-element.36.first), channel_id=1, source_target_pairs={{0,8},{8,0},{16,24},{24,16},{1,9},{9,1},{17,25},{25,17},{2,10},{10... | collective-permute-start | bytes 1105928 | tf_op jit(solution)/shard_map/ppermute | solution.py:356
  61.1 7.8 %copy-start.9 = (bf16[1152,1728]{0,1:T(8,128)(2,1)S(1)}, bf16[1152,1728]{0,1:T(8,128)(2,1)}, u32[]{:S(2)}) copy-start(bf16[1152,1728]{0,1:T(8,128)(2,1)} %param.5) | copy-start | bytes 11943940
  61.1 16.3 %collective-permute-start.9 = (bf16[4,40,1152]{2,1,0:T(8,128)(2,1)S(1)}, bf16[4,40,1152]{2,1,0:T(8,128)(2,1)S(1)}, u32[]{:S(2)}, u32[]{:S(2)}) collective-permute-start(bf16[4,40,1152]{2,1,0:T(8,128)(2,1)S(1)} %get-tuple-element.35.second), channel_id=1, source_target_pairs={{0,16},{8,24},{16,0},{24,8},{1,17},{9,25},{17,1},{25,9},{2,18},{10... | collective-permute-start | bytes 1105928 | tf_op jit(solution)/shard_map/ppermute | solution.py:356
  68.8 13.7 %collective-permute-start.17 = (bf16[576,1152]{1,0:T(8,128)(2,1)S(1)}, bf16[576,1152]{1,0:T(8,128)(2,1)S(1)}, u32[]{:S(2)}, u32[]{:S(2)}) collective-permute-start(bf16[576,1152]{1,0:T(8,128)(2,1)S(1)} %get-tuple-element.21), channel_id=1, source_target_pairs={{0,1},{1,0},{2,3},{3,2},{4,5},{5,4},{6,7},{7,6},{8,9},{9,8},{10,11... | collective-permute-start | bytes 3981320 | tf_op jit(solution)/shard_map/ppermute | solution.py:381
  77.6 8.4 %collective-permute-start.11 = (bf16[40,1152]{1,0:T(8,128)(2,1)S(1)}, bf16[40,1152]{1,0:T(8,128)(2,1)S(1)}, u32[]{:S(2)}, u32[]{:S(2)}) collective-permute-start(bf16[40,1152]{1,0:T(8,128)(2,1)S(1)} %get-tuple-element.41), channel_id=1, source_target_pairs={{0,2},{2,0},{4,6},{6,4},{1,3},{3,1},{5,7},{7,5},{8,10},{10,8},{12,... | collective-permute-start | bytes 276488 | tf_op jit(solution)/shard_map/ppermute | solution.py:356
  80.0 10.1 %collective-permute-start.12 = (bf16[40,1152]{1,0:T(8,128)(2,1)S(1)}, bf16[40,1152]{1,0:T(8,128)(2,1)S(1)}, u32[]{:S(2)}, u32[]{:S(2)}) collective-permute-start(bf16[40,1152]{1,0:T(8,128)(2,1)S(1)} %get-tuple-element.43), channel_id=1, source_target_pairs={{0,4},{2,6},{4,0},{6,2},{1,5},{3,7},{5,1},{7,3},{8,12},{10,14},{12... | collective-permute-start | bytes 276488 | tf_op jit(solution)/shard_map/ppermute | solution.py:356
  81.3 8.8 %collective-permute-start.13 = (bf16[40,1152]{1,0:T(8,128)(2,1)S(1)}, bf16[40,1152]{1,0:T(8,128)(2,1)S(1)}, u32[]{:S(2)}, u32[]{:S(2)}) collective-permute-start(bf16[40,1152]{1,0:T(8,128)(2,1)S(1)} %get-tuple-element.42), channel_id=1, source_target_pairs={{0,6},{2,4},{4,2},{6,0},{1,7},{3,5},{5,3},{7,1},{8,14},{10,12},{12... | collective-permute-start | bytes 276488 | tf_op jit(solution)/shard_map/ppermute | solution.py:356
  83.0 11.6 %collective-permute-start.18 = (bf16[4,40,1152]{2,1,0:T(8,128)(2,1)S(1)}, bf16[4,40,1152]{2,1,0:T(8,128)(2,1)S(1)}, u32[]{:S(2)}, u32[]{:S(2)}) collective-permute-start(bf16[4,40,1152]{2,1,0:T(8,128)(2,1)S(1)} %get-tuple-element.31), channel_id=1, source_target_pairs={{0,8},{8,0},{16,24},{24,16},{1,9},{9,1},{17,25},{25,17},{2,10},{10... | collective-permute-start | bytes 1105928 | tf_op jit(solution)/shard_map/ppermute | solution.py:356
  84.6 19.2 %collective-permute-start.19 = (bf16[4,40,1152]{2,1,0:T(8,128)(2,1)S(1)}, bf16[4,40,1152]{2,1,0:T(8,128)(2,1)S(1)}, u32[]{:S(2)}, u32[]{:S(2)}) collective-permute-start(bf16[4,40,1152]{2,1,0:T(8,128)(2,1)S(1)} %get-tuple-element.32), channel_id=1, source_target_pairs={{0,16},{8,24},{16,0},{24,8},{1,17},{9,25},{17,1},{25,9},{2,18},{10... | collective-permute-start | bytes 1105928 | tf_op jit(solution)/shard_map/ppermute | solution.py:356
  86.0 17.8 %collective-permute-start.20 = (bf16[4,40,1152]{2,1,0:T(8,128)(2,1)S(1)}, bf16[4,40,1152]{2,1,0:T(8,128)(2,1)S(1)}, u32[]{:S(2)}, u32[]{:S(2)}) collective-permute-start(bf16[4,40,1152]{2,1,0:T(8,128)(2,1)S(1)} %get-tuple-element.33), channel_id=1, source_target_pairs={{0,24},{8,16},{16,8},{24,0},{1,25},{9,17},{17,9},{25,1},{2,26},{10... | collective-permute-start | bytes 1105928 | tf_op jit(solution)/shard_map/ppermute | solution.py:356
  90.2 17.2 %collective-permute-start.14 = (bf16[40,1152]{1,0:T(8,128)(2,1)S(1)}, bf16[40,1152]{1,0:T(8,128)(2,1)S(1)}, u32[]{:S(2)}, u32[]{:S(2)}) collective-permute-start(bf16[40,1152]{1,0:T(8,128)(2,1)S(1)} %get-tuple-element.25), channel_id=1, source_target_pairs={{0,8},{8,0},{16,24},{24,16},{1,9},{9,1},{17,25},{25,17},{2,10},{10... | collective-permute-start | bytes 276488 | tf_op jit(solution)/shard_map/ppermute | solution.py:371
  91.7 23.3 %collective-permute-start.15 = (bf16[40,1152]{1,0:T(8,128)(2,1)S(1)}, bf16[40,1152]{1,0:T(8,128)(2,1)S(1)}, u32[]{:S(2)}, u32[]{:S(2)}) collective-permute-start(bf16[40,1152]{1,0:T(8,128)(2,1)S(1)} %get-tuple-element.25), channel_id=1, source_target_pairs={{0,16},{8,24},{16,0},{24,8},{1,17},{9,25},{17,1},{25,9},{2,18},{10... | collective-permute-start | bytes 276488 | tf_op jit(solution)/shard_map/ppermute | solution.py:371
  94.6 25.1 %collective-permute-start.16 = (bf16[40,1152]{1,0:T(8,128)(2,1)S(1)}, bf16[40,1152]{1,0:T(8,128)(2,1)S(1)}, u32[]{:S(2)}, u32[]{:S(2)}) collective-permute-start(bf16[40,1152]{1,0:T(8,128)(2,1)S(1)} %get-tuple-element.25), channel_id=1, source_target_pairs={{0,24},{8,16},{16,8},{24,0},{1,25},{9,17},{17,9},{25,1},{2,26},{10... | collective-permute-start | bytes 276488 | tf_op jit(solution)/shard_map/ppermute | solution.py:371
  104.1 5.2 %collective-permute-start.21 = (bf16[40,1152]{1,0:T(8,128)(2,1)S(1)}, bf16[40,1152]{1,0:T(8,128)(2,1)S(1)}, u32[]{:S(2)}, u32[]{:S(2)}) collective-permute-start(bf16[40,1152]{1,0:T(8,128)(2,1)S(1)} %get-tuple-element.47), channel_id=1, source_target_pairs={{0,2},{2,0},{4,6},{6,4},{1,3},{3,1},{5,7},{7,5},{8,10},{10,8},{12,... | collective-permute-start | bytes 276488 | tf_op jit(solution)/shard_map/ppermute | solution.py:356
  105.1 6.4 %collective-permute-start.22 = (bf16[40,1152]{1,0:T(8,128)(2,1)S(1)}, bf16[40,1152]{1,0:T(8,128)(2,1)S(1)}, u32[]{:S(2)}, u32[]{:S(2)}) collective-permute-start(bf16[40,1152]{1,0:T(8,128)(2,1)S(1)} %get-tuple-element.46), channel_id=1, source_target_pairs={{0,4},{2,6},{4,0},{6,2},{1,5},{3,7},{5,1},{7,3},{8,12},{10,14},{12... | collective-permute-start | bytes 276488 | tf_op jit(solution)/shard_map/ppermute | solution.py:356
  107.4 6.3 %collective-permute-start.23 = (bf16[40,1152]{1,0:T(8,128)(2,1)S(1)}, bf16[40,1152]{1,0:T(8,128)(2,1)S(1)}, u32[]{:S(2)}, u32[]{:S(2)}) collective-permute-start(bf16[40,1152]{1,0:T(8,128)(2,1)S(1)} %get-tuple-element.45), channel_id=1, source_target_pairs={{0,6},{2,4},{4,2},{6,0},{1,7},{3,5},{5,3},{7,1},{8,14},{10,12},{12... | collective-permute-start | bytes 276488 | tf_op jit(solution)/shard_map/ppermute | solution.py:356
  113.8 4.6 %collective-permute-start.24 = (bf16[40,1152]{1,0:T(8,128)(2,1)S(1)}, bf16[40,1152]{1,0:T(8,128)(2,1)S(1)}, u32[]{:S(2)}, u32[]{:S(2)}) collective-permute-start(bf16[40,1152]{1,0:T(8,128)(2,1)S(1)} %get-tuple-element.27), channel_id=1, source_target_pairs={{0,8},{8,0},{16,24},{24,16},{1,9},{9,1},{17,25},{25,17},{2,10},{10... | collective-permute-start | bytes 276488 | tf_op jit(solution)/shard_map/ppermute | solution.py:371
  115.1 4.6 %collective-permute-start.25 = (bf16[40,1152]{1,0:T(8,128)(2,1)S(1)}, bf16[40,1152]{1,0:T(8,128)(2,1)S(1)}, u32[]{:S(2)}, u32[]{:S(2)}) collective-permute-start(bf16[40,1152]{1,0:T(8,128)(2,1)S(1)} %get-tuple-element.27), channel_id=1, source_target_pairs={{0,16},{8,24},{16,0},{24,8},{1,17},{9,25},{17,1},{25,9},{2,18},{10... | collective-permute-start | bytes 276488 | tf_op jit(solution)/shard_map/ppermute | solution.py:371
  116.5 5.5 %collective-permute-start.26 = (bf16[40,1152]{1,0:T(8,128)(2,1)S(1)}, bf16[40,1152]{1,0:T(8,128)(2,1)S(1)}, u32[]{:S(2)}, u32[]{:S(2)}) collective-permute-start(bf16[40,1152]{1,0:T(8,128)(2,1)S(1)} %get-tuple-element.27), channel_id=1, source_target_pairs={{0,24},{8,16},{16,8},{24,0},{1,25},{9,17},{17,9},{25,1},{2,26},{10... | collective-permute-start | bytes 276488 | tf_op jit(solution)/shard_map/ppermute | solution.py:371

commit v5 on v4

--- a/solution.py
+++ b/solution.py
@@ -30,9 +30,69 @@
     return lax.dot_general(a, b, (((1,), (1,)), ((), ())), preferred_element_type=jnp.float32)
 
 
+def project_kernel(
+    own_ref, tokens_ref, weight_ref, qt_ref, kv_ref, top_ref, bottom_ref, near_ref, total
+):
+    step = pl.program_id(0)
+    part = dot(tokens_ref[...], weight_ref[...])
+
+    @pl.when(step == 0)
+    def _():
+        total[...] = part
+
+    @pl.when(step > 0)
+    def _():
+        total[...] += part
+
+    @pl.when(step == pl.num_programs(0) - 1)
+    def _():
+        count, edge = kv_ref.shape[0], top_ref.shape[0]
+        qt_ref[...] = total[:, : INNER + 64].astype(jnp.bfloat16).T
+        keyvals = total[:, INNER - 64 :].astype(jnp.bfloat16)[:, 64:]
+        kv_ref[...] = keyvals
+        top_ref[...] = keyvals[:edge]
+        bottom_ref[...] = keyvals[count - edge :]
+        grid = keyvals.astype(jnp.float32).reshape(-1, edge // SIDE, 2 * INNER)
+        is_right = own_ref[0].astype(jnp.float32)
+        near = grid[:, :REACH] * is_right + grid[:, -REACH:] * (1.0 - is_right)
+        near_ref[...] = near.reshape(near_ref.shape).astype(jnp.bfloat16)
+
+
+def project(token_rows, weight, tile_cols):
+    rows, width = token_rows.shape
+    steps = 3
+    depth = width // steps
+    chunk_own = SIDE * tile_cols
+    own = lax.axis_index("col").astype(jnp.int32).reshape(1)
+    shapes = [
+        (INNER + 64, rows),
+        (rows, 2 * INNER),
+        (chunk_own, 2 * INNER),
+        (chunk_own, 2 * INNER),
+        (rows // tile_cols * REACH, 2 * INNER),
+    ]
+    return pl.pallas_call(
+        project_kernel,
+        grid=(steps,),
+        out_shape=[jax.ShapeDtypeStruct(shape, jnp.bfloat16) for shape in shapes],
+        in_specs=[
+            pl.BlockSpec(memory_space=pltpu.SMEM),
+            pl.BlockSpec((rows, depth), lambda k: (0, k)),
+            pl.BlockSpec((depth, weight.shape[1]), lambda k: (k, 0)),
+        ],
+        out_specs=[pl.BlockSpec(shape, lambda k: (0, 0)) for shape in shapes],
+        scratch_shapes=[pltpu.VMEM((rows, weight.shape[1]), jnp.float32)],
+        compiler_params=pltpu.CompilerParams(vmem_limit_bytes=32 * 1024 * 1024),
+        cost_estimate=pl.CostEstimate(
+            flops=2 * rows * width * weight.shape[1], bytes_accessed=8 * 1024 * 1024, transcendentals=0
+        ),
+        name="project",
+    )(own, token_rows, weight)
+
+
 def attention_kernel(
     start_ref,
-    q_ref,
+    qt_ref,
     own_ref,
     g_ref,
     rows_ref,
@@ -41,11 +101,12 @@
     bias_ref,
     o_ref,
     dq_ref,
-    grad_ref,
+    inner_ref,
+    edge_ref,
+    side_ref,
     kv,
     kvt,
     acc,
-    qt,
     ot,
     dqt,
 ):
@@ -55,11 +116,8 @@
     chunk_side = chunk - chunk_own
     band = 3 * chunk
     token_count = own_ref.shape[0]
-    side_first = token_count + 2 * chunk_own
     last = strips + 1
-    own_at = [token_count] + [chunk_own * s for s in range(strips)] + [token_count + chunk_own]
     side_order = [strips] + list(range(strips)) + [strips + 1]
-    side_at = [side_first + chunk_side * s for s in side_order]
 
     def place(slot, first, part):
         count = part.shape[0]
@@ -69,7 +127,6 @@
             part = jnp.concatenate([part, filler], axis=0)
         kvt[slot, :, first : first + count] = part.T[:, :count]
 
-    qt[...] = q_ref[...].T
     dqt[INNER:, :] = jnp.zeros((64, chunk_own), jnp.float32)
     ot[:64, :] = jnp.zeros((64, chunk_own), jnp.float32)
     for s in range(strips):
@@ -118,7 +175,7 @@
                 got += dot(kvt[top + j, lines, :], weights[chunk * j : chunk * (j + 1)])
             return got
 
-        q2 = [pair_block(qt[heads[i], rows], 16 * i) for i in range(PAIRS)]
+        q2 = [pair_block(qt_ref[heads[i], rows], 16 * i) for i in range(PAIRS)]
         g2 = [pair_block(g_ref[heads[i], rows], V_SHIFT + 16 * i) for i in range(PAIRS)]
         prob, inv, row_dot, dscore = [], [], [], []
         for i in range(PAIRS):
@@ -160,25 +217,28 @@
         return carry
 
     lax.fori_loop(0, strips, strip, 0)
-    for slot in range(strips + 2):
-        grad_ref[own_at[slot] : own_at[slot] + chunk_own, :] = acc[slot, :chunk_own].astype(
+    for slot, at in enumerate(side_order):
+        own_grad = acc[slot, :chunk_own].astype(jnp.bfloat16)
+        if at < strips:
+            inner_ref[chunk_own * at : chunk_own * (at + 1), :] = own_grad
+        else:
+            edge_ref[chunk_own * (at - strips) : chunk_own * (at - strips + 1), :] = own_grad
+        side_ref[chunk_side * at : chunk_side * (at + 1), :] = acc[slot, chunk_own:].astype(
             jnp.bfloat16
         )
-        grad_ref[side_at[slot] : side_at[slot] + chunk_side, :] = acc[slot, chunk_own:].astype(
-            jnp.bfloat16
-        )
-
-
-def attention(start, projected, own, grads, rows, cols, corner, bias):
+
+
+def attention(start, queries, own, grads, rows, cols, corner, bias):
     strips, band, chunk_own = bias.shape
     chunk = band // 3
     token_count, width = own.shape
-    key_count = token_count + rows.shape[0] + cols.shape[0] + corner.shape[0]
     whole = lambda a: pl.BlockSpec(a.shape, lambda _: (0,) * a.ndim)
     outs = (
         jax.ShapeDtypeStruct((token_count, INNER + 64), jnp.bfloat16),
         jax.ShapeDtypeStruct((token_count, INNER + 64), jnp.bfloat16),
-        jax.ShapeDtypeStruct((key_count, width), jnp.bfloat16),
+        jax.ShapeDtypeStruct(own.shape, jnp.bfloat16),
+        jax.ShapeDtypeStruct(rows.shape, jnp.bfloat16),
+        jax.ShapeDtypeStruct((cols.shape[0] + corner.shape[0], width), jnp.bfloat16),
     )
     return pl.pallas_call(
         attention_kernel,
@@ -186,7 +246,7 @@
         out_shape=outs,
         in_specs=[
             pl.BlockSpec(memory_space=pltpu.SMEM),
-            pl.BlockSpec((token_count, 640), lambda _: (0, 0)),
+            whole(queries),
             whole(own),
             whole(grads),
             whole(rows),
@@ -199,18 +259,17 @@
             pltpu.VMEM((strips + 2, chunk, width), jnp.bfloat16),
             pltpu.VMEM((strips + 2, width, chunk), jnp.bfloat16),
             pltpu.VMEM((strips + 2, chunk, width), jnp.float32),
-            pltpu.VMEM((640, token_count), jnp.bfloat16),
             pltpu.VMEM((640, chunk_own), jnp.float32),
             pltpu.VMEM((640, chunk_own), jnp.float32),
         ],
-        compiler_params=pltpu.CompilerParams(vmem_limit_bytes=52 * 1024 * 1024),
+        compiler_params=pltpu.CompilerParams(vmem_limit_bytes=36 * 1024 * 1024),
         cost_estimate=pl.CostEstimate(
             flops=12 * token_count * band * 2 * INNER,
             bytes_accessed=16 * 1024 * 1024,
             transcendentals=token_count * band * H,
         ),
         name="window_attention",
-    )(start, projected, own, grads, rows, cols, corner, bias)
+    )(start, queries, own, grads, rows, cols, corner, bias)
 
 
 def outer_kernel(own_ref, *refs):
@@ -248,7 +307,7 @@
         in_specs=[pl.BlockSpec(memory_space=pltpu.SMEM)] + [whole(a) for a in operands],
         out_specs=(whole(out), whole(out)),
         scratch_shapes=[pltpu.VMEM((len(operands) // 2, width, rows), jnp.bfloat16)],
-        compiler_params=pltpu.CompilerParams(vmem_limit_bytes=40 * 1024 * 1024),
+        compiler_params=pltpu.CompilerParams(vmem_limit_bytes=28 * 1024 * 1024),
         cost_estimate=pl.CostEstimate(
             flops=2 * rows * width * 2 * INNER, bytes_accessed=5 * 1024 * 1024, transcendentals=0
         ),
@@ -258,7 +317,7 @@
 
 def late_kernel(
     own_ref, first, second, third, tokens_ref, inner_ref, side_ref, above_ref, below_ref,
-    sent_ref, kept_ref, grad_ref, turned,
+    dq_ref, o_ref, sent_ref, kept_ref, all_ref, att_ref, turned, grad_ref,
 ):
     own = own_ref[0]
     count = inner_ref.shape[0]
@@ -281,29 +340,36 @@
         ]
         product = dot(jnp.concatenate(picked, axis=0), grad_ref[...])
         out_ref[...] = product.astype(jnp.bfloat16)
-
-
-def late_halves(earlier, token_rows, ext_grad, side, above, below):
+    all_ref[...] = jnp.concatenate([dq_ref[:, :INNER], grad_ref[...]], axis=1)
+    att_ref[...] = o_ref[:, 64:]
+
+
+def late_halves(earlier, token_rows, inner, side, above, below, dquery, attended):
     rows, width = token_rows.shape
     whole = lambda a: pl.BlockSpec(a.shape, lambda _: (0,) * a.ndim)
     out = jax.ShapeDtypeStruct((width // 2, 2 * INNER), jnp.bfloat16)
-    grad = jax.ShapeDtypeStruct((rows, 2 * INNER), jnp.bfloat16)
+    grads = jax.ShapeDtypeStruct((rows, 3 * INNER), jnp.bfloat16)
+    att = jax.ShapeDtypeStruct((rows, INNER), jnp.bfloat16)
+    operands = (token_rows, inner, side, above, below, dquery, attended)
     own = lax.axis_index("col").astype(jnp.int32).reshape(1)
     return pl.pallas_call(
         late_kernel,
         grid=(1,),
-        out_shape=(out, out, grad),
+        out_shape=(out, out, grads, att),
         in_specs=[pl.BlockSpec(memory_space=pltpu.SMEM)]
         + [pl.BlockSpec(memory_space=pl.ANY)] * 3
-        + [whole(token_rows), whole(grad), whole(side), whole(above), whole(below)],
-        out_specs=(whole(out), whole(out), whole(grad)),
-        scratch_shapes=[pltpu.VMEM((width, rows), jnp.bfloat16)],
-        compiler_params=pltpu.CompilerParams(vmem_limit_bytes=40 * 1024 * 1024),
+        + [whole(a) for a in operands],
+        out_specs=(whole(out), whole(out), whole(grads), whole(att)),
+        scratch_shapes=[
+            pltpu.VMEM((width, rows), jnp.bfloat16),
+            pltpu.VMEM((rows, 2 * INNER), jnp.bfloat16),
+        ],
+        compiler_params=pltpu.CompilerParams(vmem_limit_bytes=28 * 1024 * 1024),
         cost_estimate=pl.CostEstimate(
             flops=2 * rows * width * 2 * INNER, bytes_accessed=7 * 1024 * 1024, transcendentals=0
         ),
         name="late_weight_grad_halves",
-    )(own, *earlier, token_rows, ext_grad, side, above, below)
+    )(own, *earlier, *operands)
 
 
 def window_starts(places, extent):
@@ -436,19 +502,21 @@
         got = got[0] if two_columns else jnp.concatenate(got, axis=1)
         return got.reshape(-1, 2 * INNER)
 
-    projected = dot(token_rows, qkv_weight).astype(jnp.bfloat16)
-    keyvals = projected[:, INNER:]
-    above = moved(keyvals[token_count - chunk_own :], 1)
-    below = moved(keyvals[:chunk_own], -1)
-    cols = side_of(keyvals)
+    queries, keyvals, top, bottom, near = project(token_rows, qkv_weight, tile_cols)
+    above = moved(bottom, 1)
+    below = moved(top, -1)
+    if two_columns:
+        cols = moved(near, 0, 0)
+    else:
+        cols = side_of(keyvals)
     rows = jnp.concatenate([above, below], axis=0)
     corner = side_of(rows)
     grad_att = lax.dot_general(
         out_weight, grad_rows, (((0,), (1,)), ((), ())), preferred_element_type=jnp.float32
     ).astype(jnp.bfloat16)
     start, bias = window_bias(tile_rows, tile_cols, two_columns)
-    attended, dquery, ext_grad = attention(
-        start, projected, keyvals, grad_att, rows, cols, corner, bias
+    attended, dquery, inner_grad, edge_grad, side_grad = attention(
+        start, queries, keyvals, grad_att, rows, cols, corner, bias
     )
 
     def outer(a, b):
@@ -459,17 +527,12 @@
     simple = two_columns and row_count == 4 and lax.axis_size("img") == 4
     if simple:
         early = image_parts(core_sum(*outer_halves(token_rows, dquery, grad_rows, attended)))
-    dquery, attended = dquery[:, :INNER], attended[:, 64:]
-    sublayer_out = nt_dot(attended, out_weight).astype(jnp.bfloat16)
-
     def spread(side, first):
         side = side.reshape(-1, SIDE, REACH, 2 * INNER).astype(jnp.float32)
         zeros = jnp.zeros((side.shape[0], SIDE, tile_cols - REACH, 2 * INNER), jnp.float32)
         order = [side, zeros] if first else [zeros, side]
         return jnp.concatenate(order, axis=2).reshape(-1, 2 * INNER)
 
-    side_first = token_count + 2 * chunk_own
-    side_grad = ext_grad[side_first:]
     if two_columns:
         got = moved(side_grad, 0, 0)
         returned = lambda part: jnp.where(col_id == 0, spread(part, False), spread(part, True))
@@ -478,19 +541,23 @@
         got = jnp.stack([moved(halves[:, 0], 0, -1), moved(halves[:, 1], 0, 1)], axis=1)
         returned = lambda part: spread(part[:, 0], False) + spread(part[:, 1], True)
     got = got.reshape(strips + 2, -1, SIDE * REACH, 2 * INNER)
-    outer_grad = ext_grad[token_count:side_first].astype(jnp.float32) + returned(got[strips:])
+    outer_grad = edge_grad.astype(jnp.float32) + returned(got[strips:])
     outer_grad = outer_grad.astype(jnp.bfloat16)
     from_below = moved(outer_grad[:chunk_own], -1)
     from_above = moved(outer_grad[chunk_own:], 1)
     if simple:
         side = got.reshape(-1, 2 * INNER)
-        sent, kept, dkv = late_halves(early[1:], token_rows, ext_grad, side, from_above, from_below)
+        sent, kept, dqkv, attended = late_halves(
+            early[1:], token_rows, inner_grad, side, from_above, from_below, dquery, attended
+        )
     else:
-        dkv = ext_grad[:token_count].astype(jnp.float32) + returned(got[:strips])
+        dquery, attended = dquery[:, :INNER], attended[:, 64:]
+        dkv = inner_grad.astype(jnp.float32) + returned(got[:strips])
         rest = jnp.zeros((token_count - chunk_own, 2 * INNER), jnp.float32)
         dkv = dkv + jnp.concatenate([from_above.astype(jnp.float32), rest], axis=0)
         dkv = dkv + jnp.concatenate([rest, from_below.astype(jnp.float32)], axis=0)
         dkv = dkv.astype(jnp.bfloat16)
+        dqkv = jnp.concatenate([dquery, dkv], axis=1)
     if simple:
         late = image_parts(core_sum(sent, kept))
         early = exchange_sum(early, "img")
@@ -502,7 +569,7 @@
     else:
         early = jnp.concatenate([outer(token_rows, dquery), outer(grad_rows, attended)], axis=1)
         early, late = plain_shares(early), plain_shares(outer(token_rows, dkv))
-    dqkv = jnp.concatenate([dquery, dkv], axis=1)
+    sublayer_out = nt_dot(attended, out_weight).astype(jnp.bfloat16)
     tokens_grad = nt_dot(dqkv, qkv_weight).astype(jnp.bfloat16)
     return (
         sublayer_out.reshape(tokens.shape),

time: 125 us -> 126 us (level)
  matrix products: 12 us -> 6.7 us
  Pallas kernels: 19.8 us -> 24.5 us
  local copies, waits for them, and re-layouts: 12.4 us -> 14.7 us
    unnamed x22 -> x41, local copies, waits for them, and re-layouts: 6.08 us -> 12.6 us
    pallas_call x1 -> x2, Pallas kernels: 2.11 us -> 8.08 us  [the longest x1 5.98 us: project(): pl.pallas_call(project_kernel, grid=(steps,), out_shape=[jax.ShapeDtypeSt...]
    dot_general x1 -> x0, matrix products: 5.15 us -> none  [dot(): return jnp.dot(a, b, preferred_element_type=jnp.float32)]
    slice x4 -> x1, local copies, waits for them, and re-layouts: 4.28 us -> 0.02 us  [local(): outer_grad = edge_grad.astype(jnp.float32) + returned(got[strips:])]
    pallas_call x1, Pallas kernels: 15.1 us -> 12.8 us  [attention(): pl.pallas_call(attention_kernel, grid=(1,), out_shape=outs, in_specs=[pl....]
    convert_element_type x2, other arithmetic: 0.65 us -> 2.07 us  [core_sum(): (kept.astype(jnp.float32) + got.astype(jnp.float32)).astype(jnp.bfloat16)]
  transfers between devices with their start and end apart: 27 -> 27, of which waited for: 15 -> 14; matrix products, arithmetic and copies ran while one was open for 10% -> 10% of each run, Pallas kernels for 4% -> 5%
where the time goes in v5:
time: 126 us
  starting transfers between devices  38.1 us (30%)
  waiting for transfers between devices  35.9 us (28%)
  Pallas kernels  24.5 us (19%)
  local copies, waits for them, and re-layouts  14.7 us (12%)
  matrix products  6.7 us (5%)
  other arithmetic  4.96 us (4%)
    ppermute x12, waiting for transfers between devices, exchange_sum(): got.append(lax.ppermute(part, axis, pairs))  21 us
    ppermute x12, starting transfers between devices, exchange_sum(): got.append(lax.ppermute(part, axis, pairs))  16.5 us
    pallas_call x1, Pallas kernels, attention(): pl.pallas_call(attention_kernel, grid=(1,), out_shape=outs, in_specs=[pl....  12.8 us
    unnamed x41, local copies, waits for them, and re-layouts  12.6 us
    ppermute x7, starting transfers between devices, moved(): return lax.ppermute(block, ('row', 'col'), pairs)  11.8 us
    ppermute x7, waiting for transfers between devices, moved(): return lax.ppermute(block, ('row', 'col'), pairs)  11.1 us
    ppermute x6, starting transfers between devices, gathered(): got = lax.ppermute(block, axis, [(i, i ^ step) for i in range(count)])  9.64 us
    pallas_call x1, Pallas kernels, project(): pl.pallas_call(project_kernel, grid=(steps,), out_shape=[jax.ShapeDtypeSt...  5.98 us
  transfers between devices with their start and end apart: 27, of which 14 were waited for; matrix products, arithmetic and copies ran while one was open for 10% of the time, Pallas kernels for 5%

profile of v5, /device:TPU:0, one launch (start us, length us, event | category | flops | bytes accessed | tf_op | source)
XLA Modules:
  0.0 126.0 jit_solution(14602135576163984964)
XLA Ops:
  0.7 6.6 %copy.8.weight_ref = bf16[1152,1728]{1,0:T(8,128)(2,1)} copy(bf16[1152,1728]{0,1:T(8,128)(2,1)} %param.5) | data formatting | bytes 7962624 | tf_op args[1]
  7.2 2.2 %copy-done.1 = bf16[1152,1728]{1,0:T(8,128)(2,1)S(1)} copy-done((bf16[1152,1728]{1,0:T(8,128)(2,1)S(1)}, bf16[1152,1728]{1,0:T(8,128)(2,1)}, u32[]{:S(2)}) %copy-start.1) | copy-done | bytes 3981336
  9.4 6.0 %project.1 = (bf16[640,512]{1,0:T(8,128)(2,1)S(1)}, bf16[512,1152]{1,0:T(8,128)(2,1)S(1)}, bf16[128,1152]{1,0:T(8,128)(2,1)S(1)}, bf16[128,1152]{1,0:T(8,128)(2,1)}, bf16[256,1152]{1,0:T(8,128)(2,1)S(1)}) custom-call(s32[1]{0:T(128)} %bitcast.own_ref, bf16[512,1152]{1,0:T(8,128)(2,1)S(1)} %bitcast.57, bf16[1152,1728]{1,0:T(8,128)(2,1)S(1)} %copy-done.1), custom_call_target="tpu_custom_call" | custom-call | flops 2038431744 | bytes 8388608 | tf_op jit(solution)/shard_map/project/pallas_call | solution.py:74
  15.4 1.0 copy-done.14
  16.4 0.8 copy-done.16
  17.2 5.6 %collective-permute-start = (bf16[128,1152]{1,0:T(8,128)(2,1)}, bf16[128,1152]{1,0:T(8,128)(2,1)}, u32[]{:S(2)}, u32[]{:S(2)}) collective-permute-start(bf16[128,1152]{1,0:T(8,128)(2,1)} %get-tuple-element.24), channel_id=1, source_target_pairs={{0,2},{1,3},{2,4},{3,5},{4,6},{5,7},{8,10},{9,11},{10,12},{11,13},... | collective-permute-start | bytes 884744 | tf_op jit(solution)/shard_map/ppermute | solution.py:491
  22.9 1.3 %collective-permute-start.1 = (bf16[128,1152]{1,0:T(8,128)(2,1)S(1)}, bf16[128,1152]{1,0:T(8,128)(2,1)S(1)}, u32[]{:S(2)}, u32[]{:S(2)}) collective-permute-start(bf16[128,1152]{1,0:T(8,128)(2,1)S(1)} %get-tuple-element.25), channel_id=1, source_target_pairs={{2,0},{3,1},{4,2},{5,3},{6,4},{7,5},{10,8},{11,9},{12,10},{13,11},... | collective-permute-start | bytes 884744 | tf_op jit(solution)/shard_map/ppermute | solution.py:491
  24.4 0.1 tile.11
  24.6 0.1 reshape.194
  24.9 0.1 fusion.4
  25.2 0.4 fusion.3.bias_ref
  25.6 3.1 %collective-permute-done = bf16[128,1152]{1,0:T(8,128)(2,1)} collective-permute-done((bf16[128,1152]{1,0:T(8,128)(2,1)}, bf16[128,1152]{1,0:T(8,128)(2,1)}, u32[]{:S(2)}, u32[]{:S(2)}) %collective-permute-start) | collective-permute-done | bytes 294944 | tf_op jit(solution)/shard_map/ppermute | solution.py:491
  28.7 1.0 constant_dynamic-update-slice_fusion.1
  29.7 3.5 %collective-permute-done.1 = bf16[128,1152]{1,0:T(8,128)(2,1)S(1)} collective-permute-done((bf16[128,1152]{1,0:T(8,128)(2,1)S(1)}, bf16[128,1152]{1,0:T(8,128)(2,1)S(1)}, u32[]{:S(2)}, u32[]{:S(2)}) %collective-permute-start.1) | collective-permute-done | bytes 294944 | tf_op jit(solution)/shard_map/ppermute | solution.py:491
  33.4 1.0 convolution_convert_fusion.2.g_ref
  34.4 0.6 collective-permute-done.3
  35.0 12.8 %window_attention.1 = (bf16[512,640]{1,0:T(8,128)(2,1)S(1)}, bf16[512,640]{1,0:T(8,128)(2,1)S(1)}, bf16[512,1152]{1,0:T(8,128)(2,1)S(1)}, bf16[256,1152]{1,0:T(8,128)(2,1)S(1)}, bf16[384,1152]{1,0:T(8,128)(2,1)}) custom-call(s32[4]{0:T(128)S(1)} %broadcast_subtract_fusion.start_ref, bf16[640,512]{1,0:T(8,128)(2,1)S(1)} %copy-done.17, ...), custom_call_target="tpu_custom_call" | custom-call | flops 4076863488 | bytes 16777216 | tf_op jit(solution)/shard_map/window_attention/pallas_call | solution.py:243
  47.8 0.4 collective-permute-start.5
  48.2 3.6 %weight_grad_halves.1 = (bf16[576,1152]{1,0:T(8,128)(2,1)}, bf16[576,1152]{1,0:T(8,128)(2,1)S(1)}) custom-call(s32[1]{0:T(128)} %bitcast.own_ref, bf16[512,1152]{1,0:T(8,128)(2,1)S(1)} %bitcast.58, bf16[512,640]{1,0:T(8,128)(2,1)S(1)} %get-tuple-element.27.refs_1_.dq_ref, bf16[512,1152]{1,0:T(8,128)(2,1)S(1)} %bitcast.62, ...), custom_call_target="tpu_custom_call" | custom-call | flops 1358954496 | bytes 5242880 | tf_op jit(solution)/shard_map/weight_grad_halves/pallas_call | solution.py:303
  51.9 0.2 collective-permute-start.4
  52.2 0.9 copy-done.12
  53.2 0.1 fusion
  53.3 2.8 %collective-permute-start.6 = (bf16[128,1152]{1,0:T(8,128)(2,1)S(1)}, bf16[128,1152]{1,0:T(8,128)(2,1)S(1)}, u32[]{:S(2)}, u32[]{:S(2)}) collective-permute-start(bf16[128,1152]{1,0:T(8,128)(2,1)S(1)} %get-tuple-element.54), channel_id=1, source_target_pairs={{0,2},{1,3},{2,4},{3,5},{4,6},{5,7},{8,10},{9,11},{10,12},{11,13},... | collective-permute-start | bytes 884744 | tf_op jit(solution)/shard_map/ppermute | solution.py:491
  56.1 1.5 %collective-permute-start.7 = (bf16[128,1152]{1,0:T(8,128)(2,1)S(1)}, bf16[128,1152]{1,0:T(8,128)(2,1)S(1)}, u32[]{:S(2)}, u32[]{:S(2)}) collective-permute-start(bf16[128,1152]{1,0:T(8,128)(2,1)S(1)} %get-tuple-element.53), channel_id=1, source_target_pairs={{2,0},{3,1},{4,2},{5,3},{6,4},{7,5},{10,8},{11,9},{12,10},{13,11},... | collective-permute-start | bytes 884744 | tf_op jit(solution)/shard_map/ppermute | solution.py:491
  57.7 1.7 %add_convert_fusion.1 = bf16[576,1152]{1,0:T(8,128)(2,1)S(1)} fusion(bf16[576,1152]{1,0:T(8,128)(2,1)} %collective-permute-done.4, bf16[576,1152]{1,0:T(8,128)(2,1)S(1)} %get-tuple-element.29), kind=kLoop, calls=%fused_computation.3 | loop fusion | flops 2654208 | bytes 3981312 | tf_op jit(solution)/shard_map/convert_element_type | solution.py:448
  59.4 0.2 pad_dynamic-slice_fusion.5
  59.6 2.5 %collective-permute-start.10 = (bf16[4,40,1152]{2,1,0:T(8,128)(2,1)S(1)}, bf16[4,40,1152]{2,1,0:T(8,128)(2,1)S(1)}, u32[]{:S(2)}, u32[]{:S(2)}) collective-permute-start(bf16[4,40,1152]{2,1,0:T(8,128)(2,1)S(1)} %get-tuple-element.48.third), channel_id=1, source_target_pairs={{0,24},{8,16},{16,8},{24,0},{1,25},{9,17},{17,9},{25,1},{2,26},{10... | collective-permute-start | bytes 1105928 | tf_op jit(solution)/shard_map/ppermute | solution.py:422
  62.1 0.5 collective-permute-start.8
  62.6 0.5 collective-permute-start.9
  63.1 3.9 %collective-permute-done.7.below_ref = bf16[128,1152]{1,0:T(8,128)(2,1)S(1)} collective-permute-done((bf16[128,1152]{1,0:T(8,128)(2,1)S(1)}, bf16[128,1152]{1,0:T(8,128)(2,1)S(1)}, u32[]{:S(2)}, u32[]{:S(2)}) %collective-permute-start.7) | collective-permute-done | bytes 294944 | tf_op jit(solution)/shard_map/ppermute | solution.py:491
  67.0 2.1 %late_weight_grad_halves.1 = (bf16[576,1152]{1,0:T(8,128)(2,1)S(1)}, bf16[576,1152]{1,0:T(8,128)(2,1)S(1)}, bf16[512,1728]{1,0:T(8,128)(2,1)S(1)}, bf16[512,576]{1,0:T(8,128)(2,1)S(1)}) custom-call(s32[1]{0:T(128)} %bitcast.own_ref, bf16[4,40,1152]{2,1,0:T(8,128)(2,1)S(1)} %get-tuple-element.50.first, bf16[4,40,1152]{2,1,0:T(8,128)(2,1)S(1)} %get-tuple-element.49.second, ...), custom_call_target="tpu_custom_call" | custom-call | flops 1358954496 | bytes 7340032 | tf_op jit(solution)/shard_map/late_weight_grad_halves/pallas_call | solution.py:355
  69.2 3.5 %convolution_convert_fusion = bf16[512,1152]{1,0:T(8,128)(2,1)} fusion(bf16[512,1728]{1,0:T(8,128)(2,1)S(1)} %get-tuple-element.35, bf16[1152,1728]{0,1:T(8,128)(2,1)S(1)} %copy-done.18), kind=kOutput, calls=%fused_computation | convolution fusion | flops 2039021568 | bytes 6930432 | tf_op jit(solution)/shard_map/dot_general | solution.py:30
  72.8 2.2 %convolution_convert_fusion.1 = bf16[512,1152]{1,0:T(8,128)(2,1)} fusion(bf16[512,576]{1,0:T(8,128)(2,1)S(1)} %get-tuple-element.34, bf16[1152,576]{0,1:T(8,128)(2,1)S(1)} %copy-done), kind=kOutput, calls=%fused_computation.1 | convolution fusion | flops 680067072 | bytes 3096576 | tf_op jit(solution)/shard_map/dot_general | solution.py:30
  75.0 4.1 %collective-permute-done.8 = bf16[4,40,1152]{2,1,0:T(8,128)(2,1)S(1)} collective-permute-done((bf16[4,40,1152]{2,1,0:T(8,128)(2,1)S(1)}, bf16[4,40,1152]{2,1,0:T(8,128)(2,1)S(1)}, u32[]{:S(2)}, u32[]{:S(2)}) %collective-permute-start.8) | collective-permute-done | bytes 368672 | tf_op jit(solution)/shard_map/ppermute | solution.py:422
  79.1 0.2 add_convert_fusion.3
  79.4 2.4 %collective-permute-start.11 = (bf16[40,1152]{1,0:T(8,128)(2,1)S(1)}, bf16[40,1152]{1,0:T(8,128)(2,1)S(1)}, u32[]{:S(2)}, u32[]{:S(2)}) collective-permute-start(bf16[40,1152]{1,0:T(8,128)(2,1)S(1)} %get-tuple-element.55), channel_id=1, source_target_pairs={{0,2},{2,0},{4,6},{6,4},{1,3},{3,1},{5,7},{7,5},{8,10},{10,8},{12,... | collective-permute-start | bytes 276488 | tf_op jit(solution)/shard_map/ppermute | solution.py:422
  81.8 1.3 %collective-permute-start.12 = (bf16[40,1152]{1,0:T(8,128)(2,1)S(1)}, bf16[40,1152]{1,0:T(8,128)(2,1)S(1)}, u32[]{:S(2)}, u32[]{:S(2)}) collective-permute-start(bf16[40,1152]{1,0:T(8,128)(2,1)S(1)} %get-tuple-element.57), channel_id=1, source_target_pairs={{0,4},{2,6},{4,0},{6,2},{1,5},{3,7},{5,1},{7,3},{8,12},{10,14},{12... | collective-permute-start | bytes 276488 | tf_op jit(solution)/shard_map/ppermute | solution.py:422
  83.1 1.2 collective-permute-start.13
  84.3 0.3 add_convert_fusion
  84.6 0.2 pad_dynamic-slice_fusion.3
  84.8 1.6 %collective-permute-start.18 = (bf16[4,40,1152]{2,1,0:T(8,128)(2,1)S(1)}, bf16[4,40,1152]{2,1,0:T(8,128)(2,1)S(1)}, u32[]{:S(2)}, u32[]{:S(2)}) collective-permute-start(bf16[4,40,1152]{2,1,0:T(8,128)(2,1)S(1)} %get-tuple-element.45), channel_id=1, source_target_pairs={{0,8},{8,0},{16,24},{24,16},{1,9},{9,1},{17,25},{25,17},{2,10},{10... | collective-permute-start | bytes 1105928 | tf_op jit(solution)/shard_map/ppermute | solution.py:422
  86.4 1.4 %collective-permute-start.19 = (bf16[4,40,1152]{2,1,0:T(8,128)(2,1)S(1)}, bf16[4,40,1152]{2,1,0:T(8,128)(2,1)S(1)}, u32[]{:S(2)}, u32[]{:S(2)}) collective-permute-start(bf16[4,40,1152]{2,1,0:T(8,128)(2,1)S(1)} %get-tuple-element.46), channel_id=1, source_target_pairs={{0,16},{8,24},{16,0},{24,8},{1,17},{9,25},{17,1},{25,9},{2,18},{10... | collective-permute-start | bytes 1105928 | tf_op jit(solution)/shard_map/ppermute | solution.py:422
  87.8 0.6 collective-permute-start.20
  88.4 3.5 %collective-permute-done.12 = bf16[40,1152]{1,0:T(8,128)(2,1)S(1)} collective-permute-done((bf16[40,1152]{1,0:T(8,128)(2,1)S(1)}, bf16[40,1152]{1,0:T(8,128)(2,1)S(1)}, u32[]{:S(2)}, u32[]{:S(2)}) %collective-permute-start.12) | collective-permute-done | bytes 92192 | tf_op jit(solution)/shard_map/ppermute | solution.py:422
  91.9 1.6 %collective-permute-start.14 = (bf16[40,1152]{1,0:T(8,128)(2,1)S(1)}, bf16[40,1152]{1,0:T(8,128)(2,1)S(1)}, u32[]{:S(2)}, u32[]{:S(2)}) collective-permute-start(bf16[40,1152]{1,0:T(8,128)(2,1)S(1)} %get-tuple-element.41), channel_id=1, source_target_pairs={{0,8},{8,0},{16,24},{24,16},{1,9},{9,1},{17,25},{25,17},{2,10},{10... | collective-permute-start | bytes 276488 | tf_op jit(solution)/shard_map/ppermute | solution.py:437
  93.5 1.5 %collective-permute-start.15 = (bf16[40,1152]{1,0:T(8,128)(2,1)S(1)}, bf16[40,1152]{1,0:T(8,128)(2,1)S(1)}, u32[]{:S(2)}, u32[]{:S(2)}) collective-permute-start(bf16[40,1152]{1,0:T(8,128)(2,1)S(1)} %get-tuple-element.41), channel_id=1, source_target_pairs={{0,16},{8,24},{16,0},{24,8},{1,17},{9,25},{17,1},{25,9},{2,18},{10... | collective-permute-start | bytes 276488 | tf_op jit(solution)/shard_map/ppermute | solution.py:437
  95.1 1.4 %collective-permute-done.18 = bf16[4,40,1152]{2,1,0:T(8,128)(2,1)S(1)} collective-permute-done((bf16[4,40,1152]{2,1,0:T(8,128)(2,1)S(1)}, bf16[4,40,1152]{2,1,0:T(8,128)(2,1)S(1)}, u32[]{:S(2)}, u32[]{:S(2)}) %collective-permute-start.18) | collective-permute-done | bytes 368672 | tf_op jit(solution)/shard_map/ppermute | solution.py:422
  96.4 2.3 %collective-permute-start.16 = (bf16[40,1152]{1,0:T(8,128)(2,1)S(1)}, bf16[40,1152]{1,0:T(8,128)(2,1)S(1)}, u32[]{:S(2)}, u32[]{:S(2)}) collective-permute-start(bf16[40,1152]{1,0:T(8,128)(2,1)S(1)} %get-tuple-element.41), channel_id=1, source_target_pairs={{0,24},{8,16},{16,8},{24,0},{1,25},{9,17},{17,9},{25,1},{2,26},{10... | collective-permute-start | bytes 276488 | tf_op jit(solution)/shard_map/ppermute | solution.py:437
  98.8 6.9 %collective-permute-done.19 = bf16[4,40,1152]{2,1,0:T(8,128)(2,1)S(1)} collective-permute-done((bf16[4,40,1152]{2,1,0:T(8,128)(2,1)S(1)}, bf16[4,40,1152]{2,1,0:T(8,128)(2,1)S(1)}, u32[]{:S(2)}, u32[]{:S(2)}) %collective-permute-start.19) | collective-permute-done | bytes 368672 | tf_op jit(solution)/shard_map/ppermute | solution.py:422
  105.6 0.2 add_convert_fusion.2
  105.9 1.0 collective-permute-start.21
  106.9 2.3 %collective-permute-start.22 = (bf16[40,1152]{1,0:T(8,128)(2,1)S(1)}, bf16[40,1152]{1,0:T(8,128)(2,1)S(1)}, u32[]{:S(2)}, u32[]{:S(2)}) collective-permute-start(bf16[40,1152]{1,0:T(8,128)(2,1)S(1)} %get-tuple-element.60), channel_id=1, source_target_pairs={{0,4},{2,6},{4,0},{6,2},{1,5},{3,7},{5,1},{7,3},{8,12},{10,14},{12... | collective-permute-start | bytes 276488 | tf_op jit(solution)/shard_map/ppermute | solution.py:422
  109.1 1.2 collective-permute-start.23
  110.4 0.8 collective-permute-done.21
  111.1 2.2 %collective-permute-done.22 = bf16[40,1152]{1,0:T(8,128)(2,1)S(1)} collective-permute-done((bf16[40,1152]{1,0:T(8,128)(2,1)S(1)}, bf16[40,1152]{1,0:T(8,128)(2,1)S(1)}, u32[]{:S(2)}, u32[]{:S(2)}) %collective-permute-start.22) | collective-permute-done | bytes 92192 | tf_op jit(solution)/shard_map/ppermute | solution.py:422
  113.3 2.2 %collective-permute-done.23 = bf16[40,1152]{1,0:T(8,128)(2,1)S(1)} collective-permute-done((bf16[40,1152]{1,0:T(8,128)(2,1)S(1)}, bf16[40,1152]{1,0:T(8,128)(2,1)S(1)}, u32[]{:S(2)}, u32[]{:S(2)}) %collective-permute-start.23) | collective-permute-done | bytes 92192 | tf_op jit(solution)/shard_map/ppermute | solution.py:422
  115.6 1.2 collective-permute-start.24
  116.9 1.4 %collective-permute-start.25 = (bf16[40,1152]{1,0:T(8,128)(2,1)S(1)}, bf16[40,1152]{1,0:T(8,128)(2,1)S(1)}, u32[]{:S(2)}, u32[]{:S(2)}) collective-permute-start(bf16[40,1152]{1,0:T(8,128)(2,1)S(1)} %get-tuple-element.43), channel_id=1, source_target_pairs={{0,16},{8,24},{16,0},{24,8},{1,17},{9,25},{17,1},{25,9},{2,18},{10... | collective-permute-start | bytes 276488 | tf_op jit(solution)/shard_map/ppermute | solution.py:437
  118.3 1.5 %collective-permute-start.26 = (bf16[40,1152]{1,0:T(8,128)(2,1)S(1)}, bf16[40,1152]{1,0:T(8,128)(2,1)S(1)}, u32[]{:S(2)}, u32[]{:S(2)}) collective-permute-start(bf16[40,1152]{1,0:T(8,128)(2,1)S(1)} %get-tuple-element.43), channel_id=1, source_target_pairs={{0,24},{8,16},{16,8},{24,0},{1,25},{9,17},{17,9},{25,1},{2,26},{10... | collective-permute-start | bytes 276488 | tf_op jit(solution)/shard_map/ppermute | solution.py:437
  119.8 0.4 collective-permute-done.24
  120.2 1.2 collective-permute-done.25
  121.5 2.3 %collective-permute-done.26 = bf16[40,1152]{1,0:T(8,128)(2,1)S(1)} collective-permute-done((bf16[40,1152]{1,0:T(8,128)(2,1)S(1)}, bf16[40,1152]{1,0:T(8,128)(2,1)S(1)}, u32[]{:S(2)}, u32[]{:S(2)}) %collective-permute-start.26) | collective-permute-done | bytes 92192 | tf_op jit(solution)/shard_map/ppermute | solution.py:437
  123.8 0.9 fusion.9
  124.8 1.2 pad_maximum_fusion
  (91 shorter events, 1.6 us)
Async XLA Ops:
  0.6 32.8 %copy-start = (bf16[1152,576]{0,1:T(8,128)(2,1)S(1)}, bf16[1152,576]{0,1:T(8,128)(2,1)}, u32[]{:S(2)}) copy-start(bf16[1152,576]{0,1:T(8,128)(2,1)} %param.6) | copy-start | bytes 3981316
  0.7 6.6 %copy-start.2 = (bf16[1,32,16,1152]{3,2,1,0:T(8,128)(2,1)S(1)}, bf16[1,32,16,1152]{3,2,1,0:T(8,128)(2,1)}, u32[]{:S(2)}) copy-start(bf16[1,32,16,1152]{3,2,1,0:T(8,128)(2,1)} %param.4) | copy-start | bytes 3538948
  7.2 2.2 %copy-start.1 = (bf16[1152,1728]{1,0:T(8,128)(2,1)S(1)}, bf16[1152,1728]{1,0:T(8,128)(2,1)}, u32[]{:S(2)}) copy-start(bf16[1152,1728]{1,0:T(8,128)(2,1)} %copy.8.weight_ref) | copy-start | bytes 11943940
  15.4 1.0 copy-start.14
  16.4 0.8 copy-start.16
  17.2 11.5 %collective-permute-start = (bf16[128,1152]{1,0:T(8,128)(2,1)}, bf16[128,1152]{1,0:T(8,128)(2,1)}, u32[]{:S(2)}, u32[]{:S(2)}) collective-permute-start(bf16[128,1152]{1,0:T(8,128)(2,1)} %get-tuple-element.24), channel_id=1, source_target_pairs={{0,2},{1,3},{2,4},{3,5},{4,6},{5,7},{8,10},{9,11},{10,12},{11,13},... | collective-permute-start | bytes 884744 | tf_op jit(solution)/shard_map/ppermute | solution.py:491
  22.9 10.3 %collective-permute-start.1 = (bf16[128,1152]{1,0:T(8,128)(2,1)S(1)}, bf16[128,1152]{1,0:T(8,128)(2,1)S(1)}, u32[]{:S(2)}, u32[]{:S(2)}) collective-permute-start(bf16[128,1152]{1,0:T(8,128)(2,1)S(1)} %get-tuple-element.25), channel_id=1, source_target_pairs={{2,0},{3,1},{4,2},{5,3},{6,4},{7,5},{10,8},{11,9},{12,10},{13,11},... | collective-permute-start | bytes 884744 | tf_op jit(solution)/shard_map/ppermute | solution.py:491
  24.2 10.8 %collective-permute-start.2 = (bf16[256,1152]{1,0:T(8,128)(2,1)S(1)}, bf16[256,1152]{1,0:T(8,128)(2,1)S(1)}, u32[]{:S(2)}, u32[]{:S(2)}) collective-permute-start(bf16[256,1152]{1,0:T(8,128)(2,1)S(1)} %get-tuple-element.26), channel_id=1, source_target_pairs={{0,1},{1,0},{2,3},{3,2},{4,5},{5,4},{6,7},{7,6},{8,9},{9,8},{10,11... | collective-permute-start | bytes 1769480 | tf_op jit(solution)/shard_map/ppermute | solution.py:491
  25.2 8.2 %copy-start.13 = (bf16[1,32,16,1152]{3,2,1,0:T(8,128)(2,1)S(1)}, bf16[1,32,16,1152]{3,2,1,0:T(8,128)(2,1)}, u32[]{:S(2)}) copy-start(bf16[1,32,16,1152]{3,2,1,0:T(8,128)(2,1)} %param.7) | copy-start | bytes 3538948
  33.3 1.6 %collective-permute-start.3 = (bf16[16,8,1152]{2,1,0:T(8,128)(2,1)S(1)}, bf16[16,8,1152]{2,1,0:T(8,128)(2,1)S(1)}, u32[]{:S(2)}, u32[]{:S(2)}) collective-permute-start(bf16[16,8,1152]{2,1,0:T(8,128)(2,1)S(1)} %constant_dynamic-slice_fusion), channel_id=1, source_target_pairs={{0,1},{1,0},{2,3},{3,2},{4,5},{5,4},{6,7},{7,6},{8,9},{9,8},{10,11... | collective-permute-start | bytes 884744 | tf_op jit(solution)/shard_map/ppermute | solution.py:491
  33.4 1.6 %copy-start.15 = (bf16[512,1152]{1,0:T(8,128)(2,1)S(1)}, bf16[512,1152]{1,0:T(8,128)(2,1)}, u32[]{:S(2)}) copy-start(bf16[512,1152]{1,0:T(8,128)(2,1)} %copy-done.14) | copy-start | bytes 3538948
  33.4 1.5 %copy-start.17 = (bf16[640,512]{1,0:T(8,128)(2,1)S(1)}, bf16[640,512]{1,0:T(8,128)(2,1)}, u32[]{:S(2)}) copy-start(bf16[640,512]{1,0:T(8,128)(2,1)} %copy-done.16) | copy-start | bytes 1966084
  35.0 13.2 %copy-start.3 = (bf16[1,32,16,1152]{3,2,1,0:T(8,128)(2,1)S(1)}, bf16[1,32,16,1152]{3,2,1,0:T(8,128)(2,1)}, u32[]{:S(2)}) copy-start(bf16[1,32,16,1152]{3,2,1,0:T(8,128)(2,1)} %param.4) | copy-start | bytes 3538948
  47.8 4.1 %copy-start.5 = (bf16[512,1152]{1,0:T(8,128)(2,1)}, bf16[512,1152]{1,0:T(8,128)(2,1)S(1)}, u32[]{:S(2)}) copy-start(bf16[512,1152]{1,0:T(8,128)(2,1)S(1)} %get-tuple-element.31.inner_ref) | copy-start | bytes 3538948
  47.8 4.1 %copy-start.7 = (bf16[512,640]{1,0:T(8,128)(2,1)}, bf16[512,640]{1,0:T(8,128)(2,1)S(1)}, u32[]{:S(2)}) copy-start(bf16[512,640]{1,0:T(8,128)(2,1)S(1)} %get-tuple-element.28.refs_3_.o_ref) | copy-start | bytes 1966084
  47.8 4.1 %copy-start.9 = (bf16[512,640]{1,0:T(8,128)(2,1)}, bf16[512,640]{1,0:T(8,128)(2,1)S(1)}, u32[]{:S(2)}) copy-start(bf16[512,640]{1,0:T(8,128)(2,1)S(1)} %get-tuple-element.27.refs_1_.dq_ref) | copy-start | bytes 1966084
  47.8 4.1 %copy-start.11 = (bf16[256,1152]{1,0:T(8,128)(2,1)}, bf16[256,1152]{1,0:T(8,128)(2,1)S(1)}, u32[]{:S(2)}) copy-start(bf16[256,1152]{1,0:T(8,128)(2,1)S(1)} %get-tuple-element.33) | copy-start | bytes 1769476
  47.8 4.3 %collective-permute-start.5 = (bf16[384,1152]{1,0:T(8,128)(2,1)}, bf16[384,1152]{1,0:T(8,128)(2,1)S(1)}, u32[]{:S(2)}, u32[]{:S(2)}) collective-permute-start(bf16[384,1152]{1,0:T(8,128)(2,1)} %get-tuple-element.32), channel_id=1, source_target_pairs={{0,1},{1,0},{2,3},{3,2},{4,5},{5,4},{6,7},{7,6},{8,9},{9,8},{10,11... | collective-permute-start | bytes 2654216 | tf_op jit(solution)/shard_map/ppermute | solution.py:491
  51.9 5.8 %collective-permute-start.4 = (bf16[576,1152]{1,0:T(8,128)(2,1)}, bf16[576,1152]{1,0:T(8,128)(2,1)}, u32[]{:S(2)}, u32[]{:S(2)}) collective-permute-start(bf16[576,1152]{1,0:T(8,128)(2,1)} %get-tuple-element.30), channel_id=1, source_target_pairs={{0,1},{1,0},{2,3},{3,2},{4,5},{5,4},{6,7},{7,6},{8,9},{9,8},{10,11... | collective-permute-start | bytes 3981320 | tf_op jit(solution)/shard_map/ppermute | solution.py:447
  52.1 1.1 copy-start.12
  53.3 9.8 %collective-permute-start.6 = (bf16[128,1152]{1,0:T(8,128)(2,1)S(1)}, bf16[128,1152]{1,0:T(8,128)(2,1)S(1)}, u32[]{:S(2)}, u32[]{:S(2)}) collective-permute-start(bf16[128,1152]{1,0:T(8,128)(2,1)S(1)} %get-tuple-element.54), channel_id=1, source_target_pairs={{0,2},{1,3},{2,4},{3,5},{4,6},{5,7},{8,10},{9,11},{10,12},{11,13},... | collective-permute-start | bytes 884744 | tf_op jit(solution)/shard_map/ppermute | solution.py:491
  56.1 10.9 %collective-permute-start.7 = (bf16[128,1152]{1,0:T(8,128)(2,1)S(1)}, bf16[128,1152]{1,0:T(8,128)(2,1)S(1)}, u32[]{:S(2)}, u32[]{:S(2)}) collective-permute-start(bf16[128,1152]{1,0:T(8,128)(2,1)S(1)} %get-tuple-element.53), channel_id=1, source_target_pairs={{2,0},{3,1},{4,2},{5,3},{6,4},{7,5},{10,8},{11,9},{12,10},{13,11},... | collective-permute-start | bytes 884744 | tf_op jit(solution)/shard_map/ppermute | solution.py:491
  57.6 9.4 %copy-start.8 = (bf16[512,640]{1,0:T(8,128)(2,1)S(1)}, bf16[512,640]{1,0:T(8,128)(2,1)}, u32[]{:S(2)}) copy-start(bf16[512,640]{1,0:T(8,128)(2,1)} %copy-done.7) | copy-start | bytes 1966084
  57.6 9.4 %copy-start.10 = (bf16[512,640]{1,0:T(8,128)(2,1)S(1)}, bf16[512,640]{1,0:T(8,128)(2,1)}, u32[]{:S(2)}) copy-start(bf16[512,640]{1,0:T(8,128)(2,1)} %copy-done.9) | copy-start | bytes 1966084
  59.4 7.6 %copy-start.4 = (bf16[1,32,16,1152]{3,2,1,0:T(8,128)(2,1)S(1)}, bf16[1,32,16,1152]{3,2,1,0:T(8,128)(2,1)}, u32[]{:S(2)}) copy-start(bf16[1,32,16,1152]{3,2,1,0:T(8,128)(2,1)} %param.4) | copy-start | bytes 3538948
  59.4 7.6 %copy-start.6 = (bf16[512,1152]{1,0:T(8,128)(2,1)S(1)}, bf16[512,1152]{1,0:T(8,128)(2,1)}, u32[]{:S(2)}) copy-start(bf16[512,1152]{1,0:T(8,128)(2,1)} %copy-done.5) | copy-start | bytes 3538948
  59.6 15.4 %collective-permute-start.10 = (bf16[4,40,1152]{2,1,0:T(8,128)(2,1)S(1)}, bf16[4,40,1152]{2,1,0:T(8,128)(2,1)S(1)}, u32[]{:S(2)}, u32[]{:S(2)}) collective-permute-start(bf16[4,40,1152]{2,1,0:T(8,128)(2,1)S(1)} %get-tuple-element.48.third), channel_id=1, source_target_pairs={{0,24},{8,16},{16,8},{24,0},{1,25},{9,17},{17,9},{25,1},{2,26},{10... | collective-permute-start | bytes 1105928 | tf_op jit(solution)/shard_map/ppermute | solution.py:422
  62.1 17.0 %collective-permute-start.8 = (bf16[4,40,1152]{2,1,0:T(8,128)(2,1)S(1)}, bf16[4,40,1152]{2,1,0:T(8,128)(2,1)S(1)}, u32[]{:S(2)}, u32[]{:S(2)}) collective-permute-start(bf16[4,40,1152]{2,1,0:T(8,128)(2,1)S(1)} %get-tuple-element.50.first), channel_id=1, source_target_pairs={{0,8},{8,0},{16,24},{24,16},{1,9},{9,1},{17,25},{25,17},{2,10},{10... | collective-permute-start | bytes 1105928 | tf_op jit(solution)/shard_map/ppermute | solution.py:422
  62.6 16.5 %collective-permute-start.9 = (bf16[4,40,1152]{2,1,0:T(8,128)(2,1)S(1)}, bf16[4,40,1152]{2,1,0:T(8,128)(2,1)S(1)}, u32[]{:S(2)}, u32[]{:S(2)}) collective-permute-start(bf16[4,40,1152]{2,1,0:T(8,128)(2,1)S(1)} %get-tuple-element.49.second), channel_id=1, source_target_pairs={{0,16},{8,24},{16,0},{24,8},{1,17},{9,25},{17,1},{25,9},{2,18},{10... | collective-permute-start | bytes 1105928 | tf_op jit(solution)/shard_map/ppermute | solution.py:422
  67.0 2.2 %copy-start.18 = (bf16[1152,1728]{0,1:T(8,128)(2,1)S(1)}, bf16[1152,1728]{0,1:T(8,128)(2,1)}, u32[]{:S(2)}) copy-start(bf16[1152,1728]{0,1:T(8,128)(2,1)} %param.5) | copy-start | bytes 11943940
  69.2 15.1 %collective-permute-start.17 = (bf16[576,1152]{1,0:T(8,128)(2,1)S(1)}, bf16[576,1152]{1,0:T(8,128)(2,1)S(1)}, u32[]{:S(2)}, u32[]{:S(2)}) collective-permute-start(bf16[576,1152]{1,0:T(8,128)(2,1)S(1)} %get-tuple-element.37), channel_id=1, source_target_pairs={{0,1},{1,0},{2,3},{3,2},{4,5},{5,4},{6,7},{7,6},{8,9},{9,8},{10,11... | collective-permute-start | bytes 3981320 | tf_op jit(solution)/shard_map/ppermute | solution.py:447
  79.4 8.4 %collective-permute-start.11 = (bf16[40,1152]{1,0:T(8,128)(2,1)S(1)}, bf16[40,1152]{1,0:T(8,128)(2,1)S(1)}, u32[]{:S(2)}, u32[]{:S(2)}) collective-permute-start(bf16[40,1152]{1,0:T(8,128)(2,1)S(1)} %get-tuple-element.55), channel_id=1, source_target_pairs={{0,2},{2,0},{4,6},{6,4},{1,3},{3,1},{5,7},{7,5},{8,10},{10,8},{12,... | collective-permute-start | bytes 276488 | tf_op jit(solution)/shard_map/ppermute | solution.py:422
  81.8 10.0 %collective-permute-start.12 = (bf16[40,1152]{1,0:T(8,128)(2,1)S(1)}, bf16[40,1152]{1,0:T(8,128)(2,1)S(1)}, u32[]{:S(2)}, u32[]{:S(2)}) collective-permute-start(bf16[40,1152]{1,0:T(8,128)(2,1)S(1)} %get-tuple-element.57), channel_id=1, source_target_pairs={{0,4},{2,6},{4,0},{6,2},{1,5},{3,7},{5,1},{7,3},{8,12},{10,14},{12... | collective-permute-start | bytes 276488 | tf_op jit(solution)/shard_map/ppermute | solution.py:422
  83.1 8.7 %collective-permute-start.13 = (bf16[40,1152]{1,0:T(8,128)(2,1)S(1)}, bf16[40,1152]{1,0:T(8,128)(2,1)S(1)}, u32[]{:S(2)}, u32[]{:S(2)}) collective-permute-start(bf16[40,1152]{1,0:T(8,128)(2,1)S(1)} %get-tuple-element.56), channel_id=1, source_target_pairs={{0,6},{2,4},{4,2},{6,0},{1,7},{3,5},{5,3},{7,1},{8,14},{10,12},{12... | collective-permute-start | bytes 276488 | tf_op jit(solution)/shard_map/ppermute | solution.py:422
  84.8 11.6 %collective-permute-start.18 = (bf16[4,40,1152]{2,1,0:T(8,128)(2,1)S(1)}, bf16[4,40,1152]{2,1,0:T(8,128)(2,1)S(1)}, u32[]{:S(2)}, u32[]{:S(2)}) collective-permute-start(bf16[4,40,1152]{2,1,0:T(8,128)(2,1)S(1)} %get-tuple-element.45), channel_id=1, source_target_pairs={{0,8},{8,0},{16,24},{24,16},{1,9},{9,1},{17,25},{25,17},{2,10},{10... | collective-permute-start | bytes 1105928 | tf_op jit(solution)/shard_map/ppermute | solution.py:422
  86.4 19.2 %collective-permute-start.19 = (bf16[4,40,1152]{2,1,0:T(8,128)(2,1)S(1)}, bf16[4,40,1152]{2,1,0:T(8,128)(2,1)S(1)}, u32[]{:S(2)}, u32[]{:S(2)}) collective-permute-start(bf16[4,40,1152]{2,1,0:T(8,128)(2,1)S(1)} %get-tuple-element.46), channel_id=1, source_target_pairs={{0,16},{8,24},{16,0},{24,8},{1,17},{9,25},{17,1},{25,9},{2,18},{10... | collective-permute-start | bytes 1105928 | tf_op jit(solution)/shard_map/ppermute | solution.py:422
  87.8 17.8 %collective-permute-start.20 = (bf16[4,40,1152]{2,1,0:T(8,128)(2,1)S(1)}, bf16[4,40,1152]{2,1,0:T(8,128)(2,1)S(1)}, u32[]{:S(2)}, u32[]{:S(2)}) collective-permute-start(bf16[4,40,1152]{2,1,0:T(8,128)(2,1)S(1)} %get-tuple-element.47), channel_id=1, source_target_pairs={{0,24},{8,16},{16,8},{24,0},{1,25},{9,17},{17,9},{25,1},{2,26},{10... | collective-permute-start | bytes 1105928 | tf_op jit(solution)/shard_map/ppermute | solution.py:422
  91.9 17.2 %collective-permute-start.14 = (bf16[40,1152]{1,0:T(8,128)(2,1)S(1)}, bf16[40,1152]{1,0:T(8,128)(2,1)S(1)}, u32[]{:S(2)}, u32[]{:S(2)}) collective-permute-start(bf16[40,1152]{1,0:T(8,128)(2,1)S(1)} %get-tuple-element.41), channel_id=1, source_target_pairs={{0,8},{8,0},{16,24},{24,16},{1,9},{9,1},{17,25},{25,17},{2,10},{10... | collective-permute-start | bytes 276488 | tf_op jit(solution)/shard_map/ppermute | solution.py:437
  93.5 23.3 %collective-permute-start.15 = (bf16[40,1152]{1,0:T(8,128)(2,1)S(1)}, bf16[40,1152]{1,0:T(8,128)(2,1)S(1)}, u32[]{:S(2)}, u32[]{:S(2)}) collective-permute-start(bf16[40,1152]{1,0:T(8,128)(2,1)S(1)} %get-tuple-element.41), channel_id=1, source_target_pairs={{0,16},{8,24},{16,0},{24,8},{1,17},{9,25},{17,1},{25,9},{2,18},{10... | collective-permute-start | bytes 276488 | tf_op jit(solution)/shard_map/ppermute | solution.py:437
  96.4 25.1 %collective-permute-start.16 = (bf16[40,1152]{1,0:T(8,128)(2,1)S(1)}, bf16[40,1152]{1,0:T(8,128)(2,1)S(1)}, u32[]{:S(2)}, u32[]{:S(2)}) collective-permute-start(bf16[40,1152]{1,0:T(8,128)(2,1)S(1)} %get-tuple-element.41), channel_id=1, source_target_pairs={{0,24},{8,16},{16,8},{24,0},{1,25},{9,17},{17,9},{25,1},{2,26},{10... | collective-permute-start | bytes 276488 | tf_op jit(solution)/shard_map/ppermute | solution.py:437
  105.9 5.2 %collective-permute-start.21 = (bf16[40,1152]{1,0:T(8,128)(2,1)S(1)}, bf16[40,1152]{1,0:T(8,128)(2,1)S(1)}, u32[]{:S(2)}, u32[]{:S(2)}) collective-permute-start(bf16[40,1152]{1,0:T(8,128)(2,1)S(1)} %get-tuple-element.61), channel_id=1, source_target_pairs={{0,2},{2,0},{4,6},{6,4},{1,3},{3,1},{5,7},{7,5},{8,10},{10,8},{12,... | collective-permute-start | bytes 276488 | tf_op jit(solution)/shard_map/ppermute | solution.py:422
  106.9 6.4 %collective-permute-start.22 = (bf16[40,1152]{1,0:T(8,128)(2,1)S(1)}, bf16[40,1152]{1,0:T(8,128)(2,1)S(1)}, u32[]{:S(2)}, u32[]{:S(2)}) collective-permute-start(bf16[40,1152]{1,0:T(8,128)(2,1)S(1)} %get-tuple-element.60), channel_id=1, source_target_pairs={{0,4},{2,6},{4,0},{6,2},{1,5},{3,7},{5,1},{7,3},{8,12},{10,14},{12... | collective-permute-start | bytes 276488 | tf_op jit(solution)/shard_map/ppermute | solution.py:422
  109.1 6.3 %collective-permute-start.23 = (bf16[40,1152]{1,0:T(8,128)(2,1)S(1)}, bf16[40,1152]{1,0:T(8,128)(2,1)S(1)}, u32[]{:S(2)}, u32[]{:S(2)}) collective-permute-start(bf16[40,1152]{1,0:T(8,128)(2,1)S(1)} %get-tuple-element.59), channel_id=1, source_target_pairs={{0,6},{2,4},{4,2},{6,0},{1,7},{3,5},{5,3},{7,1},{8,14},{10,12},{12... | collective-permute-start | bytes 276488 | tf_op jit(solution)/shard_map/ppermute | solution.py:422
  115.6 4.6 %collective-permute-start.24 = (bf16[40,1152]{1,0:T(8,128)(2,1)S(1)}, bf16[40,1152]{1,0:T(8,128)(2,1)S(1)}, u32[]{:S(2)}, u32[]{:S(2)}) collective-permute-start(bf16[40,1152]{1,0:T(8,128)(2,1)S(1)} %get-tuple-element.43), channel_id=1, source_target_pairs={{0,8},{8,0},{16,24},{24,16},{1,9},{9,1},{17,25},{25,17},{2,10},{10... | collective-permute-start | bytes 276488 | tf_op jit(solution)/shard_map/ppermute | solution.py:437
  116.9 4.6 %collective-permute-start.25 = (bf16[40,1152]{1,0:T(8,128)(2,1)S(1)}, bf16[40,1152]{1,0:T(8,128)(2,1)S(1)}, u32[]{:S(2)}, u32[]{:S(2)}) collective-permute-start(bf16[40,1152]{1,0:T(8,128)(2,1)S(1)} %get-tuple-element.43), channel_id=1, source_target_pairs={{0,16},{8,24},{16,0},{24,8},{1,17},{9,25},{17,1},{25,9},{2,18},{10... | collective-permute-start | bytes 276488 | tf_op jit(solution)/shard_map/ppermute | solution.py:437
  118.3 5.5 %collective-permute-start.26 = (bf16[40,1152]{1,0:T(8,128)(2,1)S(1)}, bf16[40,1152]{1,0:T(8,128)(2,1)S(1)}, u32[]{:S(2)}, u32[]{:S(2)}) collective-permute-start(bf16[40,1152]{1,0:T(8,128)(2,1)S(1)} %get-tuple-element.43), channel_id=1, source_target_pairs={{0,24},{8,16},{16,8},{24,0},{1,25},{9,17},{17,9},{25,1},{2,26},{10... | collective-permute-start | bytes 276488 | tf_op jit(solution)/shard_map/ppermute | solution.py:437

commit v6 on v5

--- a/solution.py
+++ b/solution.py
@@ -16,6 +16,7 @@
 V_SHIFT = 64
 MASKED = -1e30
 SCALE = DH ** (-0.5)
+LIGHT = pl.CostEstimate(flops=1, bytes_accessed=1, transcendentals=0)
 
 
 def shifted_pairs(count, by):
@@ -30,42 +31,43 @@
     return lax.dot_general(a, b, (((1,), (1,)), ((), ())), preferred_element_type=jnp.float32)
 
 
+PIECE = 384
+
+
 def project_kernel(
-    own_ref, tokens_ref, weight_ref, qt_ref, kv_ref, top_ref, bottom_ref, near_ref, total
+    own_ref, tokens_ref, weight_ref, qt_ref, kv_ref, top_ref, bottom_ref, near_ref, tokens, weight, sems
 ):
-    step = pl.program_id(0)
-    part = dot(tokens_ref[...], weight_ref[...])
-
-    @pl.when(step == 0)
-    def _():
-        total[...] = part
-
-    @pl.when(step > 0)
-    def _():
-        total[...] += part
-
-    @pl.when(step == pl.num_programs(0) - 1)
-    def _():
-        count, edge = kv_ref.shape[0], top_ref.shape[0]
-        qt_ref[...] = total[:, : INNER + 64].astype(jnp.bfloat16).T
-        keyvals = total[:, INNER - 64 :].astype(jnp.bfloat16)[:, 64:]
-        kv_ref[...] = keyvals
-        top_ref[...] = keyvals[:edge]
-        bottom_ref[...] = keyvals[count - edge :]
-        grid = keyvals.astype(jnp.float32).reshape(-1, edge // SIDE, 2 * INNER)
-        is_right = own_ref[0].astype(jnp.float32)
-        near = grid[:, :REACH] * is_right + grid[:, -REACH:] * (1.0 - is_right)
-        near_ref[...] = near.reshape(near_ref.shape).astype(jnp.bfloat16)
+    rows = [(INNER + PIECE * p, PIECE) for p in range(2 * INNER // PIECE)] + [(0, INNER)]
+    whole = pltpu.make_async_copy(tokens_ref, tokens, sems.at[len(rows)])
+    whole.start()
+    copies = []
+    for n, (first, count) in enumerate(rows):
+        part = pl.ds(first, count)
+        copies.append(pltpu.make_async_copy(weight_ref.at[part], weight.at[part], sems.at[n]))
+        copies[-1].start()
+    whole.wait()
+    for p in range(2 * INNER // PIECE):
+        copies[p].wait()
+        lines = weight[INNER + PIECE * p : INNER + PIECE * (p + 1)]
+        kv_ref[:, PIECE * p : PIECE * (p + 1)] = nt_dot(tokens[...], lines).astype(jnp.bfloat16)
+    count, edge = kv_ref.shape[0], top_ref.shape[0]
+    keyvals = kv_ref[...]
+    top_ref[...] = keyvals[:edge]
+    bottom_ref[...] = keyvals[count - edge :]
+    grid = keyvals.astype(jnp.float32).reshape(-1, edge // SIDE, 2 * INNER)
+    is_right = own_ref[0].astype(jnp.float32)
+    near = grid[:, :REACH] * is_right + grid[:, -REACH:] * (1.0 - is_right)
+    near_ref[...] = near.reshape(near_ref.shape).astype(jnp.bfloat16)
+    copies[-1].wait()
+    qt_ref[...] = nt_dot(weight[:INNER], tokens[...]).astype(jnp.bfloat16)
 
 
 def project(token_rows, weight, tile_cols):
     rows, width = token_rows.shape
-    steps = 3
-    depth = width // steps
     chunk_own = SIDE * tile_cols
     own = lax.axis_index("col").astype(jnp.int32).reshape(1)
     shapes = [
-        (INNER + 64, rows),
+        (INNER, rows),
         (rows, 2 * INNER),
         (chunk_own, 2 * INNER),
         (chunk_own, 2 * INNER),
@@ -73,21 +75,25 @@
     ]
     return pl.pallas_call(
         project_kernel,
-        grid=(steps,),
+        grid=(1,),
         out_shape=[jax.ShapeDtypeStruct(shape, jnp.bfloat16) for shape in shapes],
         in_specs=[
             pl.BlockSpec(memory_space=pltpu.SMEM),
-            pl.BlockSpec((rows, depth), lambda k: (0, k)),
-            pl.BlockSpec((depth, weight.shape[1]), lambda k: (k, 0)),
+            pl.BlockSpec(memory_space=pl.ANY),
+            pl.BlockSpec(memory_space=pl.ANY),
         ],
         out_specs=[pl.BlockSpec(shape, lambda k: (0, 0)) for shape in shapes],
-        scratch_shapes=[pltpu.VMEM((rows, weight.shape[1]), jnp.float32)],
-        compiler_params=pltpu.CompilerParams(vmem_limit_bytes=32 * 1024 * 1024),
+        scratch_shapes=[
+            pltpu.VMEM((rows, width), jnp.bfloat16),
+            pltpu.VMEM((3 * INNER, width), jnp.bfloat16),
+            pltpu.SemaphoreType.DMA((2 * INNER // PIECE + 2,)),
+        ],
+        compiler_params=pltpu.CompilerParams(vmem_limit_bytes=56 * 1024 * 1024),
         cost_estimate=pl.CostEstimate(
-            flops=2 * rows * width * weight.shape[1], bytes_accessed=8 * 1024 * 1024, transcendentals=0
+            flops=6 * rows * width * INNER, bytes_accessed=8 * 1024 * 1024, transcendentals=0
         ),
         name="project",
-    )(own, token_rows, weight)
+    )(own, token_rows, weight.T)
 
 
 def attention_kernel(
@@ -95,7 +101,8 @@
     qt_ref,
     own_ref,
     g_ref,
-    rows_ref,
+    above_ref,
+    below_ref,
     cols_ref,
     corner_ref,
     bias_ref,
@@ -133,8 +140,9 @@
         place(s + 1, 0, own_ref[chunk_own * s : chunk_own * (s + 1)])
     for s in range(strips):
         place(s + 1, chunk_own, cols_ref[chunk_side * s : chunk_side * (s + 1)])
+    place(0, 0, above_ref[...])
+    place(last, 0, below_ref[...])
     for slot, at in ((0, 0), (last, 1)):
-        place(slot, 0, rows_ref[chunk_own * at : chunk_own * (at + 1)])
         place(slot, chunk_own, corner_ref[chunk_side * at : chunk_side * (at + 1)])
     acc[...] = jnp.zeros_like(acc)
 
@@ -228,7 +236,7 @@
         )
 
 
-def attention(start, queries, own, grads, rows, cols, corner, bias):
+def attention(start, queries, own, grads, above, below, cols, corner, bias):
     strips, band, chunk_own = bias.shape
     chunk = band // 3
     token_count, width = own.shape
@@ -237,7 +245,7 @@
         jax.ShapeDtypeStruct((token_count, INNER + 64), jnp.bfloat16),
         jax.ShapeDtypeStruct((token_count, INNER + 64), jnp.bfloat16),
         jax.ShapeDtypeStruct(own.shape, jnp.bfloat16),
-        jax.ShapeDtypeStruct(rows.shape, jnp.bfloat16),
+        jax.ShapeDtypeStruct((2 * chunk_own, width), jnp.bfloat16),
         jax.ShapeDtypeStruct((cols.shape[0] + corner.shape[0], width), jnp.bfloat16),
     )
     return pl.pallas_call(
@@ -249,7 +257,8 @@
             whole(queries),
             whole(own),
             whole(grads),
-            whole(rows),
+            whole(above),
+            whole(below),
             whole(cols),
             whole(corner),
             whole(bias),
@@ -269,7 +278,7 @@
             transcendentals=token_count * band * H,
         ),
         name="window_attention",
-    )(start, queries, own, grads, rows, cols, corner, bias)
+    )(start, queries, own, grads, above, below, cols, corner, bias)
 
 
 def outer_kernel(own_ref, *refs):
@@ -308,9 +317,7 @@
         out_specs=(whole(out), whole(out)),
         scratch_shapes=[pltpu.VMEM((len(operands) // 2, width, rows), jnp.bfloat16)],
         compiler_params=pltpu.CompilerParams(vmem_limit_bytes=28 * 1024 * 1024),
-        cost_estimate=pl.CostEstimate(
-            flops=2 * rows * width * 2 * INNER, bytes_accessed=5 * 1024 * 1024, transcendentals=0
-        ),
+        cost_estimate=LIGHT,
         name="weight_grad_halves",
     )(own, *operands)
 
@@ -365,9 +372,7 @@
             pltpu.VMEM((rows, 2 * INNER), jnp.bfloat16),
         ],
         compiler_params=pltpu.CompilerParams(vmem_limit_bytes=28 * 1024 * 1024),
-        cost_estimate=pl.CostEstimate(
-            flops=2 * rows * width * 2 * INNER, bytes_accessed=7 * 1024 * 1024, transcendentals=0
-        ),
+        cost_estimate=LIGHT,
         name="late_weight_grad_halves",
     )(own, *earlier, *operands)
 
@@ -495,10 +500,12 @@
             return lax.dynamic_slice_in_dim(block, (1 - col_id) * (tile_cols - REACH), REACH, 1)
         return block[:, tile_cols - REACH :] if turn == 1 else block[:, :REACH]
 
-    def side_of(block):
-        block = block.reshape(-1, tile_cols, 2 * INNER)
-        got = [moved(edge(block, t), 0, t) for t in sorted(turns, reverse=True)]
-        got = [g.reshape(-1, SIDE * REACH, 2 * INNER) for g in got]
+    def side_of(*blocks):
+        got = []
+        for turn in sorted(turns, reverse=True):
+            near = [edge(block.reshape(-1, tile_cols, 2 * INNER), turn) for block in blocks]
+            near = jnp.concatenate(near, axis=0) if len(near) > 1 else near[0]
+            got.append(moved(near, 0, turn).reshape(-1, SIDE * REACH, 2 * INNER))
         got = got[0] if two_columns else jnp.concatenate(got, axis=1)
         return got.reshape(-1, 2 * INNER)
 
@@ -509,14 +516,13 @@
         cols = moved(near, 0, 0)
     else:
         cols = side_of(keyvals)
-    rows = jnp.concatenate([above, below], axis=0)
-    corner = side_of(rows)
+    corner = side_of(above, below)
     grad_att = lax.dot_general(
         out_weight, grad_rows, (((0,), (1,)), ((), ())), preferred_element_type=jnp.float32
     ).astype(jnp.bfloat16)
     start, bias = window_bias(tile_rows, tile_cols, two_columns)
     attended, dquery, inner_grad, edge_grad, side_grad = attention(
-        start, queries, keyvals, grad_att, rows, cols, corner, bias
+        start, queries, keyvals, grad_att, above, below, cols, corner, bias
     )
 
     def outer(a, b):

time: 126 us -> 120 us (0.952)
  local copies, waits for them, and re-layouts: 14.7 us -> 6.01 us
  Pallas kernels: 24.5 us -> 26.9 us
  starting transfers between devices: 38.1 us -> 39.7 us
  waiting for transfers between devices: 35.9 us -> 34.3 us
    unnamed x41 -> x35, local copies, waits for them, and re-layouts: 12.6 us -> 3.03 us
    ppermute x7, starting transfers between devices: 11.8 us -> 13.2 us  [moved(): return lax.ppermute(block, ('row', 'col'), pairs)]
    ppermute x7, waiting for transfers between devices: 11.1 us -> 9.59 us  [moved(): return lax.ppermute(block, ('row', 'col'), pairs)]
    pallas_call x1, Pallas kernels: 2.1 us -> 3.45 us  [late_halves(): pl.pallas_call(late_kernel, grid=(1,), out_shape=(out, out, grads, att),...]
  transfers between devices with their start and end apart: 27 -> 27, of which waited for: 14 -> 14; matrix products, arithmetic and copies ran while one was open for 10% -> 10% of each run, Pallas kernels for 5% -> 6%
where the time goes in v6:
time: 120 us
  starting transfers between devices  39.7 us (33%)
  waiting for transfers between devices  34.3 us (29%)
  Pallas kernels  26.9 us (22%)
  matrix products  6.74 us (6%)
  local copies, waits for them, and re-layouts  6.01 us (5%)
  other arithmetic  4.9 us (4%)
    ppermute x12, waiting for transfers between devices, exchange_sum(): got.append(lax.ppermute(part, axis, pairs))  20.8 us
    ppermute x12, starting transfers between devices, exchange_sum(): got.append(lax.ppermute(part, axis, pairs))  16.6 us
    pallas_call x1, Pallas kernels, attention(): pl.pallas_call(attention_kernel, grid=(1,), out_shape=outs, in_specs=[pl....  13.5 us
    ppermute x7, starting transfers between devices, moved(): return lax.ppermute(block, ('row', 'col'), pairs)  13.2 us
    ppermute x6, starting transfers between devices, gathered(): got = lax.ppermute(block, axis, [(i, i ^ step) for i in range(count)])  9.64 us
    ppermute x7, waiting for transfers between devices, moved(): return lax.ppermute(block, ('row', 'col'), pairs)  9.59 us
    pallas_call x1, Pallas kernels, project(): pl.pallas_call(project_kernel, grid=(1,), out_shape=[jax.ShapeDtypeStruct...  6.32 us
    dot_general x2, matrix products, nt_dot(): lax.dot_general(a, b, (((1,), (1,)), ((), ())), preferred_element_type=jn...  5.78 us
  transfers between devices with their start and end apart: 27, of which 14 were waited for; matrix products, arithmetic and copies ran while one was open for 10% of the time, Pallas kernels for 6%

profile of v6, /device:TPU:0, one launch (start us, length us, event | category | flops | bytes accessed | tf_op | source)
XLA Modules:
  0.0 119.6 jit_solution(10590892901752229332)
XLA Ops:
  0.7 6.3 %project.1 = (bf16[576,512]{1,0:T(8,128)(2,1)}, bf16[512,1152]{1,0:T(8,128)(2,1)}, bf16[128,1152]{1,0:T(8,128)(2,1)}, bf16[128,1152]{1,0:T(8,128)(2,1)}, bf16[256,1152]{1,0:T(8,128)(2,1)}) custom-call(s32[1]{0:T(128)} %bitcast.own_ref, bf16[512,1152]{1,0:T(8,128)(2,1)} %bitcast.59, bf16[1728,1152]{1,0:T(8,128)(2,1)} %bitcast.73), custom_call_target="tpu_custom_call" | custom-call | flops 2038431744 | bytes 8388608 | tf_op jit(solution)/shard_map/project/pallas_call | solution.py:76
  7.0 1.3 %collective-permute-start.1 = (bf16[128,1152]{1,0:T(8,128)(2,1)}, bf16[128,1152]{1,0:T(8,128)(2,1)S(1)}, u32[]{:S(2)}, u32[]{:S(2)}) collective-permute-start(bf16[128,1152]{1,0:T(8,128)(2,1)} %get-tuple-element.25), channel_id=1, source_target_pairs={{2,0},{3,1},{4,2},{5,3},{6,4},{7,5},{10,8},{11,9},{12,10},{13,11},... | collective-permute-start | bytes 884744 | tf_op jit(solution)/shard_map/ppermute | solution.py:496
  8.3 5.6 %collective-permute-start = (bf16[128,1152]{1,0:T(8,128)(2,1)}, bf16[128,1152]{1,0:T(8,128)(2,1)S(1)}, u32[]{:S(2)}, u32[]{:S(2)}) collective-permute-start(bf16[128,1152]{1,0:T(8,128)(2,1)} %get-tuple-element.24), channel_id=1, source_target_pairs={{0,2},{1,3},{2,4},{3,5},{4,6},{5,7},{8,10},{9,11},{10,12},{11,13},... | collective-permute-start | bytes 884744 | tf_op jit(solution)/shard_map/ppermute | solution.py:496
  14.0 0.1 tile.13
  14.1 0.1 tile.11
  14.3 0.1 reshape.198
  14.4 0.1 reshape.199
  14.6 0.1 fusion.4
  14.9 0.4 fusion.3.bias_ref
  15.3 3.8 %collective-permute-done.1.below_ref = bf16[128,1152]{1,0:T(8,128)(2,1)S(1)} collective-permute-done((bf16[128,1152]{1,0:T(8,128)(2,1)}, bf16[128,1152]{1,0:T(8,128)(2,1)S(1)}, u32[]{:S(2)}, u32[]{:S(2)}) %collective-permute-start.1) | collective-permute-done | bytes 294944 | tf_op jit(solution)/shard_map/ppermute | solution.py:496
  19.1 1.3 %collective-permute-done.above_ref = bf16[128,1152]{1,0:T(8,128)(2,1)S(1)} collective-permute-done((bf16[128,1152]{1,0:T(8,128)(2,1)}, bf16[128,1152]{1,0:T(8,128)(2,1)S(1)}, u32[]{:S(2)}, u32[]{:S(2)}) %collective-permute-start) | collective-permute-done | bytes 294944 | tf_op jit(solution)/shard_map/ppermute | solution.py:496
  20.6 1.0 convolution_convert_fusion.2.g_ref
  21.6 0.5 collective-permute-done.3
  22.1 1.0 copy-done.13
  23.1 13.5 %window_attention.1 = (bf16[512,640]{1,0:T(8,128)(2,1)S(1)}, bf16[512,640]{1,0:T(8,128)(2,1)S(1)}, bf16[512,1152]{1,0:T(8,128)(2,1)S(1)}, bf16[256,1152]{1,0:T(8,128)(2,1)S(1)}, bf16[384,1152]{1,0:T(8,128)(2,1)}) custom-call(s32[4]{0:T(128)S(1)} %broadcast_subtract_fusion.start_ref, bf16[576,512]{1,0:T(8,128)(2,1)S(1)} %copy-done.15, ...), custom_call_target="tpu_custom_call" | custom-call | flops 4076863488 | bytes 16777216 | tf_op jit(solution)/shard_map/window_attention/pallas_call | solution.py:251
  36.6 0.3 collective-permute-start.5
  36.9 3.6 %weight_grad_halves.1 = (bf16[576,1152]{1,0:T(8,128)(2,1)}, bf16[576,1152]{1,0:T(8,128)(2,1)S(1)}) custom-call(s32[1]{0:T(128)} %bitcast.own_ref, bf16[512,1152]{1,0:T(8,128)(2,1)S(1)} %bitcast.60, bf16[512,640]{1,0:T(8,128)(2,1)S(1)} %get-tuple-element.27.refs_1_.dq_ref, bf16[512,1152]{1,0:T(8,128)(2,1)S(1)} %bitcast.63, ...), custom_call_target="tpu_custom_call" | custom-call | flops 1 | bytes 1 | tf_op jit(solution)/shard_map/weight_grad_halves/pallas_call | solution.py:312
  40.5 1.1 copy-done.4
  41.6 0.2 collective-permute-start.4
  41.8 1.0 slice.29
  42.8 0.1 pad_select_fusion
  42.9 0.9 copy-done.11
  43.8 0.1 fusion
  44.0 4.4 %collective-permute-start.6 = (bf16[128,1152]{1,0:T(8,128)(2,1)S(1)}, bf16[128,1152]{1,0:T(8,128)(2,1)S(1)}, u32[]{:S(2)}, u32[]{:S(2)}) collective-permute-start(bf16[128,1152]{1,0:T(8,128)(2,1)S(1)} %get-tuple-element.54), channel_id=1, source_target_pairs={{0,2},{1,3},{2,4},{3,5},{4,6},{5,7},{8,10},{9,11},{10,12},{11,13},... | collective-permute-start | bytes 884744 | tf_op jit(solution)/shard_map/ppermute | solution.py:496
  48.4 1.5 %collective-permute-start.7 = (bf16[128,1152]{1,0:T(8,128)(2,1)S(1)}, bf16[128,1152]{1,0:T(8,128)(2,1)S(1)}, u32[]{:S(2)}, u32[]{:S(2)}) collective-permute-start(bf16[128,1152]{1,0:T(8,128)(2,1)S(1)} %get-tuple-element.53), channel_id=1, source_target_pairs={{2,0},{3,1},{4,2},{5,3},{6,4},{7,5},{10,8},{11,9},{12,10},{13,11},... | collective-permute-start | bytes 884744 | tf_op jit(solution)/shard_map/ppermute | solution.py:496
  49.9 1.7 %add_convert_fusion.1 = bf16[576,1152]{1,0:T(8,128)(2,1)S(1)} fusion(bf16[576,1152]{1,0:T(8,128)(2,1)} %collective-permute-done.4, bf16[576,1152]{1,0:T(8,128)(2,1)S(1)} %copy-done.5), kind=kLoop, calls=%fused_computation.3 | loop fusion | flops 2654208 | bytes 3981312 | tf_op jit(solution)/shard_map/convert_element_type | solution.py:453
  51.6 0.2 pad_dynamic-slice_fusion.5
  51.8 2.7 %collective-permute-start.10 = (bf16[4,40,1152]{2,1,0:T(8,128)(2,1)S(1)}, bf16[4,40,1152]{2,1,0:T(8,128)(2,1)S(1)}, u32[]{:S(2)}, u32[]{:S(2)}) collective-permute-start(bf16[4,40,1152]{2,1,0:T(8,128)(2,1)S(1)} %get-tuple-element.48.third), channel_id=1, source_target_pairs={{0,24},{8,16},{16,8},{24,0},{1,25},{9,17},{17,9},{25,1},{2,26},{10... | collective-permute-start | bytes 1105928 | tf_op jit(solution)/shard_map/ppermute | solution.py:427
  54.5 0.5 collective-permute-start.8
  55.0 0.4 collective-permute-start.9
  55.3 4.0 %collective-permute-done.7.below_ref = bf16[128,1152]{1,0:T(8,128)(2,1)S(1)} collective-permute-done((bf16[128,1152]{1,0:T(8,128)(2,1)S(1)}, bf16[128,1152]{1,0:T(8,128)(2,1)S(1)}, u32[]{:S(2)}, u32[]{:S(2)}) %collective-permute-start.7) | collective-permute-done | bytes 294944 | tf_op jit(solution)/shard_map/ppermute | solution.py:496
  59.3 3.4 %late_weight_grad_halves.1 = (bf16[576,1152]{1,0:T(8,128)(2,1)S(1)}, bf16[576,1152]{1,0:T(8,128)(2,1)S(1)}, bf16[512,1728]{1,0:T(8,128)(2,1)S(1)}, bf16[512,576]{1,0:T(8,128)(2,1)S(1)}) custom-call(s32[1]{0:T(128)} %bitcast.own_ref, bf16[4,40,1152]{2,1,0:T(8,128)(2,1)S(1)} %get-tuple-element.50.first, bf16[4,40,1152]{2,1,0:T(8,128)(2,1)S(1)} %get-tuple-element.49.second, ...), custom_call_target="tpu_custom_call" | custom-call | flops 1 | bytes 1 | tf_op jit(solution)/shard_map/late_weight_grad_halves/pallas_call | solution.py:362
  62.9 3.6 %convolution_convert_fusion = bf16[512,1152]{1,0:T(8,128)(2,1)} fusion(bf16[512,1728]{1,0:T(8,128)(2,1)S(1)} %get-tuple-element.35, bf16[1152,1728]{0,1:T(8,128)(2,1)S(1)} %copy-done.16), kind=kOutput, calls=%fused_computation | convolution fusion | flops 2039021568 | bytes 6930432 | tf_op jit(solution)/shard_map/dot_general | solution.py:31
  66.4 2.2 %convolution_convert_fusion.1 = bf16[512,1152]{1,0:T(8,128)(2,1)} fusion(bf16[512,576]{1,0:T(8,128)(2,1)S(1)} %get-tuple-element.34, bf16[1152,576]{0,1:T(8,128)(2,1)S(1)} %copy-done), kind=kOutput, calls=%fused_computation.1 | convolution fusion | flops 680067072 | bytes 3096576 | tf_op jit(solution)/shard_map/dot_general | solution.py:31
  68.6 2.8 %collective-permute-done.8 = bf16[4,40,1152]{2,1,0:T(8,128)(2,1)S(1)} collective-permute-done((bf16[4,40,1152]{2,1,0:T(8,128)(2,1)S(1)}, bf16[4,40,1152]{2,1,0:T(8,128)(2,1)S(1)}, u32[]{:S(2)}, u32[]{:S(2)}) %collective-permute-start.8) | collective-permute-done | bytes 368672 | tf_op jit(solution)/shard_map/ppermute | solution.py:427
  71.5 0.2 add_convert_fusion.3
  71.7 2.4 %collective-permute-start.11 = (bf16[40,1152]{1,0:T(8,128)(2,1)S(1)}, bf16[40,1152]{1,0:T(8,128)(2,1)S(1)}, u32[]{:S(2)}, u32[]{:S(2)}) collective-permute-start(bf16[40,1152]{1,0:T(8,128)(2,1)S(1)} %get-tuple-element.55), channel_id=1, source_target_pairs={{0,2},{2,0},{4,6},{6,4},{1,3},{3,1},{5,7},{7,5},{8,10},{10,8},{12,... | collective-permute-start | bytes 276488 | tf_op jit(solution)/shard_map/ppermute | solution.py:427
  74.1 2.6 %collective-permute-start.12 = (bf16[40,1152]{1,0:T(8,128)(2,1)S(1)}, bf16[40,1152]{1,0:T(8,128)(2,1)S(1)}, u32[]{:S(2)}, u32[]{:S(2)}) collective-permute-start(bf16[40,1152]{1,0:T(8,128)(2,1)S(1)} %get-tuple-element.57), channel_id=1, source_target_pairs={{0,4},{2,6},{4,0},{6,2},{1,5},{3,7},{5,1},{7,3},{8,12},{10,14},{12... | collective-permute-start | bytes 276488 | tf_op jit(solution)/shard_map/ppermute | solution.py:427
  76.8 0.3 add_convert_fusion
  77.1 0.2 pad_dynamic-slice_fusion.3
  77.3 1.6 %collective-permute-start.18 = (bf16[4,40,1152]{2,1,0:T(8,128)(2,1)S(1)}, bf16[4,40,1152]{2,1,0:T(8,128)(2,1)S(1)}, u32[]{:S(2)}, u32[]{:S(2)}) collective-permute-start(bf16[4,40,1152]{2,1,0:T(8,128)(2,1)S(1)} %get-tuple-element.45), channel_id=1, source_target_pairs={{0,8},{8,0},{16,24},{24,16},{1,9},{9,1},{17,25},{25,17},{2,10},{10... | collective-permute-start | bytes 1105928 | tf_op jit(solution)/shard_map/ppermute | solution.py:427
  78.9 1.4 %collective-permute-start.19 = (bf16[4,40,1152]{2,1,0:T(8,128)(2,1)S(1)}, bf16[4,40,1152]{2,1,0:T(8,128)(2,1)S(1)}, u32[]{:S(2)}, u32[]{:S(2)}) collective-permute-start(bf16[4,40,1152]{2,1,0:T(8,128)(2,1)S(1)} %get-tuple-element.46), channel_id=1, source_target_pairs={{0,16},{8,24},{16,0},{24,8},{1,17},{9,25},{17,1},{25,9},{2,18},{10... | collective-permute-start | bytes 1105928 | tf_op jit(solution)/shard_map/ppermute | solution.py:427
  80.3 0.6 collective-permute-start.20
  80.9 3.4 %collective-permute-done.12 = bf16[40,1152]{1,0:T(8,128)(2,1)S(1)} collective-permute-done((bf16[40,1152]{1,0:T(8,128)(2,1)S(1)}, bf16[40,1152]{1,0:T(8,128)(2,1)S(1)}, u32[]{:S(2)}, u32[]{:S(2)}) %collective-permute-start.12) | collective-permute-done | bytes 92192 | tf_op jit(solution)/shard_map/ppermute | solution.py:427
  84.3 1.5 %collective-permute-start.14 = (bf16[40,1152]{1,0:T(8,128)(2,1)S(1)}, bf16[40,1152]{1,0:T(8,128)(2,1)S(1)}, u32[]{:S(2)}, u32[]{:S(2)}) collective-permute-start(bf16[40,1152]{1,0:T(8,128)(2,1)S(1)} %get-tuple-element.41), channel_id=1, source_target_pairs={{0,8},{8,0},{16,24},{24,16},{1,9},{9,1},{17,25},{25,17},{2,10},{10... | collective-permute-start | bytes 276488 | tf_op jit(solution)/shard_map/ppermute | solution.py:442
  85.9 1.6 %collective-permute-start.15 = (bf16[40,1152]{1,0:T(8,128)(2,1)S(1)}, bf16[40,1152]{1,0:T(8,128)(2,1)S(1)}, u32[]{:S(2)}, u32[]{:S(2)}) collective-permute-start(bf16[40,1152]{1,0:T(8,128)(2,1)S(1)} %get-tuple-element.41), channel_id=1, source_target_pairs={{0,16},{8,24},{16,0},{24,8},{1,17},{9,25},{17,1},{25,9},{2,18},{10... | collective-permute-start | bytes 276488 | tf_op jit(solution)/shard_map/ppermute | solution.py:442
  87.4 1.5 %collective-permute-done.18 = bf16[4,40,1152]{2,1,0:T(8,128)(2,1)S(1)} collective-permute-done((bf16[4,40,1152]{2,1,0:T(8,128)(2,1)S(1)}, bf16[4,40,1152]{2,1,0:T(8,128)(2,1)S(1)}, u32[]{:S(2)}, u32[]{:S(2)}) %collective-permute-start.18) | collective-permute-done | bytes 368672 | tf_op jit(solution)/shard_map/ppermute | solution.py:427
  88.9 2.4 %collective-permute-start.16 = (bf16[40,1152]{1,0:T(8,128)(2,1)S(1)}, bf16[40,1152]{1,0:T(8,128)(2,1)S(1)}, u32[]{:S(2)}, u32[]{:S(2)}) collective-permute-start(bf16[40,1152]{1,0:T(8,128)(2,1)S(1)} %get-tuple-element.41), channel_id=1, source_target_pairs={{0,24},{8,16},{16,8},{24,0},{1,25},{9,17},{17,9},{25,1},{2,26},{10... | collective-permute-start | bytes 276488 | tf_op jit(solution)/shard_map/ppermute | solution.py:442
  91.2 6.9 %collective-permute-done.19 = bf16[4,40,1152]{2,1,0:T(8,128)(2,1)S(1)} collective-permute-done((bf16[4,40,1152]{2,1,0:T(8,128)(2,1)S(1)}, bf16[4,40,1152]{2,1,0:T(8,128)(2,1)S(1)}, u32[]{:S(2)}, u32[]{:S(2)}) %collective-permute-start.19) | collective-permute-done | bytes 368672 | tf_op jit(solution)/shard_map/ppermute | solution.py:427
  98.1 0.2 add_convert_fusion.2
  98.4 0.9 collective-permute-start.21
  99.3 3.4 %collective-permute-start.22 = (bf16[40,1152]{1,0:T(8,128)(2,1)S(1)}, bf16[40,1152]{1,0:T(8,128)(2,1)S(1)}, u32[]{:S(2)}, u32[]{:S(2)}) collective-permute-start(bf16[40,1152]{1,0:T(8,128)(2,1)S(1)} %get-tuple-element.60), channel_id=1, source_target_pairs={{0,4},{2,6},{4,0},{6,2},{1,5},{3,7},{5,1},{7,3},{8,12},{10,14},{12... | collective-permute-start | bytes 276488 | tf_op jit(solution)/shard_map/ppermute | solution.py:427
  102.7 0.1 collective-permute-start.23
  102.8 1.1 collective-permute-done.21
  104.0 2.3 %collective-permute-done.22 = bf16[40,1152]{1,0:T(8,128)(2,1)S(1)} collective-permute-done((bf16[40,1152]{1,0:T(8,128)(2,1)S(1)}, bf16[40,1152]{1,0:T(8,128)(2,1)S(1)}, u32[]{:S(2)}, u32[]{:S(2)}) %collective-permute-start.22) | collective-permute-done | bytes 92192 | tf_op jit(solution)/shard_map/ppermute | solution.py:427
  106.2 2.8 %collective-permute-done.23 = bf16[40,1152]{1,0:T(8,128)(2,1)S(1)} collective-permute-done((bf16[40,1152]{1,0:T(8,128)(2,1)S(1)}, bf16[40,1152]{1,0:T(8,128)(2,1)S(1)}, u32[]{:S(2)}, u32[]{:S(2)}) %collective-permute-start.23) | collective-permute-done | bytes 92192 | tf_op jit(solution)/shard_map/ppermute | solution.py:427
  109.2 1.3 %collective-permute-start.24 = (bf16[40,1152]{1,0:T(8,128)(2,1)S(1)}, bf16[40,1152]{1,0:T(8,128)(2,1)S(1)}, u32[]{:S(2)}, u32[]{:S(2)}) collective-permute-start(bf16[40,1152]{1,0:T(8,128)(2,1)S(1)} %get-tuple-element.43), channel_id=1, source_target_pairs={{0,8},{8,0},{16,24},{24,16},{1,9},{9,1},{17,25},{25,17},{2,10},{10... | collective-permute-start | bytes 276488 | tf_op jit(solution)/shard_map/ppermute | solution.py:442
  110.5 1.4 %collective-permute-start.25 = (bf16[40,1152]{1,0:T(8,128)(2,1)S(1)}, bf16[40,1152]{1,0:T(8,128)(2,1)S(1)}, u32[]{:S(2)}, u32[]{:S(2)}) collective-permute-start(bf16[40,1152]{1,0:T(8,128)(2,1)S(1)} %get-tuple-element.43), channel_id=1, source_target_pairs={{0,16},{8,24},{16,0},{24,8},{1,17},{9,25},{17,1},{25,9},{2,18},{10... | collective-permute-start | bytes 276488 | tf_op jit(solution)/shard_map/ppermute | solution.py:442
  111.9 1.5 %collective-permute-start.26 = (bf16[40,1152]{1,0:T(8,128)(2,1)S(1)}, bf16[40,1152]{1,0:T(8,128)(2,1)S(1)}, u32[]{:S(2)}, u32[]{:S(2)}) collective-permute-start(bf16[40,1152]{1,0:T(8,128)(2,1)S(1)} %get-tuple-element.43), channel_id=1, source_target_pairs={{0,24},{8,16},{16,8},{24,0},{1,25},{9,17},{17,9},{25,1},{2,26},{10... | collective-permute-start | bytes 276488 | tf_op jit(solution)/shard_map/ppermute | solution.py:442
  113.4 0.4 collective-permute-done.24
  113.8 1.3 %collective-permute-done.25 = bf16[40,1152]{1,0:T(8,128)(2,1)S(1)} collective-permute-done((bf16[40,1152]{1,0:T(8,128)(2,1)S(1)}, bf16[40,1152]{1,0:T(8,128)(2,1)S(1)}, u32[]{:S(2)}, u32[]{:S(2)}) %collective-permute-start.25) | collective-permute-done | bytes 92192 | tf_op jit(solution)/shard_map/ppermute | solution.py:442
  115.1 2.2 %collective-permute-done.26 = bf16[40,1152]{1,0:T(8,128)(2,1)S(1)} collective-permute-done((bf16[40,1152]{1,0:T(8,128)(2,1)S(1)}, bf16[40,1152]{1,0:T(8,128)(2,1)S(1)}, u32[]{:S(2)}, u32[]{:S(2)}) %collective-permute-start.26) | collective-permute-done | bytes 92192 | tf_op jit(solution)/shard_map/ppermute | solution.py:442
  117.4 0.9 fusion.9
  118.4 1.2 %pad_maximum_fusion = f32[144,1728]{1,0:T(8,128)} fusion(f32[144,1152]{1,0:T(8,128)S(1)} %slice_convert_fusion, f32[144,576]{1,0:T(8,128)S(1)} %get-tuple-element.52), kind=kLoop, calls=%fused_computation.21 | loop fusion | flops 248832 | bytes 1990656 | tf_op jit(solution)/shard_map/concatenate | solution.py:583
  (86 shorter events, 1.3 us)
Async XLA Ops:
  0.6 19.9 %copy-start = (bf16[1152,576]{0,1:T(8,128)(2,1)S(1)}, bf16[1152,576]{0,1:T(8,128)(2,1)}, u32[]{:S(2)}) copy-start(bf16[1152,576]{0,1:T(8,128)(2,1)} %param.6) | copy-start | bytes 3981316
  7.0 12.1 %collective-permute-start.1 = (bf16[128,1152]{1,0:T(8,128)(2,1)}, bf16[128,1152]{1,0:T(8,128)(2,1)S(1)}, u32[]{:S(2)}, u32[]{:S(2)}) collective-permute-start(bf16[128,1152]{1,0:T(8,128)(2,1)} %get-tuple-element.25), channel_id=1, source_target_pairs={{2,0},{3,1},{4,2},{5,3},{6,4},{7,5},{10,8},{11,9},{12,10},{13,11},... | collective-permute-start | bytes 884744 | tf_op jit(solution)/shard_map/ppermute | solution.py:496
  8.3 12.1 %collective-permute-start = (bf16[128,1152]{1,0:T(8,128)(2,1)}, bf16[128,1152]{1,0:T(8,128)(2,1)S(1)}, u32[]{:S(2)}, u32[]{:S(2)}) collective-permute-start(bf16[128,1152]{1,0:T(8,128)(2,1)} %get-tuple-element.24), channel_id=1, source_target_pairs={{0,2},{1,3},{2,4},{3,5},{4,6},{5,7},{8,10},{9,11},{10,12},{11,13},... | collective-permute-start | bytes 884744 | tf_op jit(solution)/shard_map/ppermute | solution.py:496
  13.9 8.3 %collective-permute-start.2 = (bf16[256,1152]{1,0:T(8,128)(2,1)}, bf16[256,1152]{1,0:T(8,128)(2,1)}, u32[]{:S(2)}, u32[]{:S(2)}) collective-permute-start(bf16[256,1152]{1,0:T(8,128)(2,1)} %get-tuple-element.26), channel_id=1, source_target_pairs={{0,1},{1,0},{2,3},{3,2},{4,5},{5,4},{6,7},{7,6},{8,9},{9,8},{10,11... | collective-permute-start | bytes 1769480 | tf_op jit(solution)/shard_map/ppermute | solution.py:496
  13.9 6.6 %copy-start.8 = (bf16[1,32,16,1152]{3,2,1,0:T(8,128)(2,1)S(1)}, bf16[1,32,16,1152]{3,2,1,0:T(8,128)(2,1)}, u32[]{:S(2)}) copy-start(bf16[1,32,16,1152]{3,2,1,0:T(8,128)(2,1)} %param.7) | copy-start | bytes 3538948
  20.4 1.1 copy-start.12
  20.5 1.6 %collective-permute-start.3 = (bf16[16,8,1152]{2,1,0:T(8,128)(2,1)S(1)}, bf16[16,8,1152]{2,1,0:T(8,128)(2,1)S(1)}, u32[]{:S(2)}, u32[]{:S(2)}) collective-permute-start(bf16[16,8,1152]{2,1,0:T(8,128)(2,1)S(1)} %pad_maximum_fusion.1), channel_id=1, source_target_pairs={{0,1},{1,0},{2,3},{3,2},{4,5},{5,4},{6,7},{7,6},{8,9},{9,8},{10,11... | collective-permute-start | bytes 884744 | tf_op jit(solution)/shard_map/ppermute | solution.py:496
  20.6 1.6 %copy-start.14 = (bf16[512,1152]{1,0:T(8,128)(2,1)S(1)}, bf16[512,1152]{1,0:T(8,128)(2,1)}, u32[]{:S(2)}) copy-start(bf16[512,1152]{1,0:T(8,128)(2,1)} %get-tuple-element.23.own_ref) | copy-start | bytes 3538948
  20.6 1.5 %copy-start.15 = (bf16[576,512]{1,0:T(8,128)(2,1)S(1)}, bf16[576,512]{1,0:T(8,128)(2,1)}, u32[]{:S(2)}) copy-start(bf16[576,512]{1,0:T(8,128)(2,1)} %get-tuple-element.22.qt_ref) | copy-start | bytes 1769476
  22.1 1.0 copy-start.13
  23.1 13.8 %copy-start.1 = (bf16[1,32,16,1152]{3,2,1,0:T(8,128)(2,1)S(1)}, bf16[1,32,16,1152]{3,2,1,0:T(8,128)(2,1)}, u32[]{:S(2)}) copy-start(bf16[1,32,16,1152]{3,2,1,0:T(8,128)(2,1)} %param.4) | copy-start | bytes 3538948
  23.1 13.8 %copy-start.9 = (bf16[1,32,16,1152]{3,2,1,0:T(8,128)(2,1)S(1)}, bf16[1,32,16,1152]{3,2,1,0:T(8,128)(2,1)}, u32[]{:S(2)}) copy-start(bf16[1,32,16,1152]{3,2,1,0:T(8,128)(2,1)} %param.7) | copy-start | bytes 3538948
  36.6 4.0 %copy-start.2 = (bf16[512,640]{1,0:T(8,128)(2,1)}, bf16[512,640]{1,0:T(8,128)(2,1)S(1)}, u32[]{:S(2)}) copy-start(bf16[512,640]{1,0:T(8,128)(2,1)S(1)} %get-tuple-element.27.refs_1_.dq_ref) | copy-start | bytes 1966084
  36.6 4.0 %copy-start.6 = (bf16[512,1152]{1,0:T(8,128)(2,1)}, bf16[512,1152]{1,0:T(8,128)(2,1)S(1)}, u32[]{:S(2)}) copy-start(bf16[512,1152]{1,0:T(8,128)(2,1)S(1)} %get-tuple-element.31.inner_ref) | copy-start | bytes 3538948
  36.6 4.0 %copy-start.10 = (bf16[256,1152]{1,0:T(8,128)(2,1)}, bf16[256,1152]{1,0:T(8,128)(2,1)S(1)}, u32[]{:S(2)}) copy-start(bf16[256,1152]{1,0:T(8,128)(2,1)S(1)} %get-tuple-element.33) | copy-start | bytes 1769476
  36.6 5.2 %collective-permute-start.5 = (bf16[384,1152]{1,0:T(8,128)(2,1)}, bf16[384,1152]{1,0:T(8,128)(2,1)}, u32[]{:S(2)}, u32[]{:S(2)}) collective-permute-start(bf16[384,1152]{1,0:T(8,128)(2,1)} %get-tuple-element.32), channel_id=1, source_target_pairs={{0,1},{1,0},{2,3},{3,2},{4,5},{5,4},{6,7},{7,6},{8,9},{9,8},{10,11... | collective-permute-start | bytes 2654216 | tf_op jit(solution)/shard_map/ppermute | solution.py:496
  40.5 1.1 copy-start.4
  41.6 8.3 %collective-permute-start.4 = (bf16[576,1152]{1,0:T(8,128)(2,1)}, bf16[576,1152]{1,0:T(8,128)(2,1)}, u32[]{:S(2)}, u32[]{:S(2)}) collective-permute-start(bf16[576,1152]{1,0:T(8,128)(2,1)} %get-tuple-element.30), channel_id=1, source_target_pairs={{0,1},{1,0},{2,3},{3,2},{4,5},{5,4},{6,7},{7,6},{8,9},{9,8},{10,11... | collective-permute-start | bytes 3981320 | tf_op jit(solution)/shard_map/ppermute | solution.py:452
  42.8 1.1 copy-start.11
  43.8 6.1 %copy-start.5 = (bf16[576,1152]{1,0:T(8,128)(2,1)S(1)}, bf16[576,1152]{1,0:T(8,128)(2,1)}, u32[]{:S(2)}) copy-start(bf16[576,1152]{1,0:T(8,128)(2,1)} %copy-done.4) | copy-start | bytes 3981316
  44.0 11.3 %collective-permute-start.6 = (bf16[128,1152]{1,0:T(8,128)(2,1)S(1)}, bf16[128,1152]{1,0:T(8,128)(2,1)S(1)}, u32[]{:S(2)}, u32[]{:S(2)}) collective-permute-start(bf16[128,1152]{1,0:T(8,128)(2,1)S(1)} %get-tuple-element.54), channel_id=1, source_target_pairs={{0,2},{1,3},{2,4},{3,5},{4,6},{5,7},{8,10},{9,11},{10,12},{11,13},... | collective-permute-start | bytes 884744 | tf_op jit(solution)/shard_map/ppermute | solution.py:496
  48.4 10.9 %collective-permute-start.7 = (bf16[128,1152]{1,0:T(8,128)(2,1)S(1)}, bf16[128,1152]{1,0:T(8,128)(2,1)S(1)}, u32[]{:S(2)}, u32[]{:S(2)}) collective-permute-start(bf16[128,1152]{1,0:T(8,128)(2,1)S(1)} %get-tuple-element.53), channel_id=1, source_target_pairs={{2,0},{3,1},{4,2},{5,3},{6,4},{7,5},{10,8},{11,9},{12,10},{13,11},... | collective-permute-start | bytes 884744 | tf_op jit(solution)/shard_map/ppermute | solution.py:496
  51.6 7.7 %copy-start.3 = (bf16[512,640]{1,0:T(8,128)(2,1)S(1)}, bf16[512,640]{1,0:T(8,128)(2,1)}, u32[]{:S(2)}) copy-start(bf16[512,640]{1,0:T(8,128)(2,1)} %copy-done.2) | copy-start | bytes 1966084
  51.6 7.7 %copy-start.7 = (bf16[512,1152]{1,0:T(8,128)(2,1)S(1)}, bf16[512,1152]{1,0:T(8,128)(2,1)}, u32[]{:S(2)}) copy-start(bf16[512,1152]{1,0:T(8,128)(2,1)} %copy-done.6) | copy-start | bytes 3538948
  51.8 16.9 %collective-permute-start.10 = (bf16[4,40,1152]{2,1,0:T(8,128)(2,1)S(1)}, bf16[4,40,1152]{2,1,0:T(8,128)(2,1)S(1)}, u32[]{:S(2)}, u32[]{:S(2)}) collective-permute-start(bf16[4,40,1152]{2,1,0:T(8,128)(2,1)S(1)} %get-tuple-element.48.third), channel_id=1, source_target_pairs={{0,24},{8,16},{16,8},{24,0},{1,25},{9,17},{17,9},{25,1},{2,26},{10... | collective-permute-start | bytes 1105928 | tf_op jit(solution)/shard_map/ppermute | solution.py:427
  54.5 17.0 %collective-permute-start.8 = (bf16[4,40,1152]{2,1,0:T(8,128)(2,1)S(1)}, bf16[4,40,1152]{2,1,0:T(8,128)(2,1)S(1)}, u32[]{:S(2)}, u32[]{:S(2)}) collective-permute-start(bf16[4,40,1152]{2,1,0:T(8,128)(2,1)S(1)} %get-tuple-element.50.first), channel_id=1, source_target_pairs={{0,8},{8,0},{16,24},{24,16},{1,9},{9,1},{17,25},{25,17},{2,10},{10... | collective-permute-start | bytes 1105928 | tf_op jit(solution)/shard_map/ppermute | solution.py:427
  55.0 16.5 %collective-permute-start.9 = (bf16[4,40,1152]{2,1,0:T(8,128)(2,1)S(1)}, bf16[4,40,1152]{2,1,0:T(8,128)(2,1)S(1)}, u32[]{:S(2)}, u32[]{:S(2)}) collective-permute-start(bf16[4,40,1152]{2,1,0:T(8,128)(2,1)S(1)} %get-tuple-element.49.second), channel_id=1, source_target_pairs={{0,16},{8,24},{16,0},{24,8},{1,17},{9,25},{17,1},{25,9},{2,18},{10... | collective-permute-start | bytes 1105928 | tf_op jit(solution)/shard_map/ppermute | solution.py:427
  59.3 3.5 %copy-start.16 = (bf16[1152,1728]{0,1:T(8,128)(2,1)S(1)}, bf16[1152,1728]{0,1:T(8,128)(2,1)}, u32[]{:S(2)}) copy-start(bf16[1152,1728]{0,1:T(8,128)(2,1)} %param.5) | copy-start | bytes 11943940
  62.8 14.0 %collective-permute-start.17 = (bf16[576,1152]{1,0:T(8,128)(2,1)S(1)}, bf16[576,1152]{1,0:T(8,128)(2,1)S(1)}, u32[]{:S(2)}, u32[]{:S(2)}) collective-permute-start(bf16[576,1152]{1,0:T(8,128)(2,1)S(1)} %get-tuple-element.37), channel_id=1, source_target_pairs={{0,1},{1,0},{2,3},{3,2},{4,5},{5,4},{6,7},{7,6},{8,9},{9,8},{10,11... | collective-permute-start | bytes 3981320 | tf_op jit(solution)/shard_map/ppermute | solution.py:452
  71.7 8.6 %collective-permute-start.11 = (bf16[40,1152]{1,0:T(8,128)(2,1)S(1)}, bf16[40,1152]{1,0:T(8,128)(2,1)S(1)}, u32[]{:S(2)}, u32[]{:S(2)}) collective-permute-start(bf16[40,1152]{1,0:T(8,128)(2,1)S(1)} %get-tuple-element.55), channel_id=1, source_target_pairs={{0,2},{2,0},{4,6},{6,4},{1,3},{3,1},{5,7},{7,5},{8,10},{10,8},{12,... | collective-permute-start | bytes 276488 | tf_op jit(solution)/shard_map/ppermute | solution.py:427
  74.1 10.1 %collective-permute-start.12 = (bf16[40,1152]{1,0:T(8,128)(2,1)S(1)}, bf16[40,1152]{1,0:T(8,128)(2,1)S(1)}, u32[]{:S(2)}, u32[]{:S(2)}) collective-permute-start(bf16[40,1152]{1,0:T(8,128)(2,1)S(1)} %get-tuple-element.57), channel_id=1, source_target_pairs={{0,4},{2,6},{4,0},{6,2},{1,5},{3,7},{5,1},{7,3},{8,12},{10,14},{12... | collective-permute-start | bytes 276488 | tf_op jit(solution)/shard_map/ppermute | solution.py:427
  76.7 7.5 %collective-permute-start.13 = (bf16[40,1152]{1,0:T(8,128)(2,1)S(1)}, bf16[40,1152]{1,0:T(8,128)(2,1)S(1)}, u32[]{:S(2)}, u32[]{:S(2)}) collective-permute-start(bf16[40,1152]{1,0:T(8,128)(2,1)S(1)} %get-tuple-element.56), channel_id=1, source_target_pairs={{0,6},{2,4},{4,2},{6,0},{1,7},{3,5},{5,3},{7,1},{8,14},{10,12},{12... | collective-permute-start | bytes 276488 | tf_op jit(solution)/shard_map/ppermute | solution.py:427
  77.3 11.6 %collective-permute-start.18 = (bf16[4,40,1152]{2,1,0:T(8,128)(2,1)S(1)}, bf16[4,40,1152]{2,1,0:T(8,128)(2,1)S(1)}, u32[]{:S(2)}, u32[]{:S(2)}) collective-permute-start(bf16[4,40,1152]{2,1,0:T(8,128)(2,1)S(1)} %get-tuple-element.45), channel_id=1, source_target_pairs={{0,8},{8,0},{16,24},{24,16},{1,9},{9,1},{17,25},{25,17},{2,10},{10... | collective-permute-start | bytes 1105928 | tf_op jit(solution)/shard_map/ppermute | solution.py:427
  78.9 19.2 %collective-permute-start.19 = (bf16[4,40,1152]{2,1,0:T(8,128)(2,1)S(1)}, bf16[4,40,1152]{2,1,0:T(8,128)(2,1)S(1)}, u32[]{:S(2)}, u32[]{:S(2)}) collective-permute-start(bf16[4,40,1152]{2,1,0:T(8,128)(2,1)S(1)} %get-tuple-element.46), channel_id=1, source_target_pairs={{0,16},{8,24},{16,0},{24,8},{1,17},{9,25},{17,1},{25,9},{2,18},{10... | collective-permute-start | bytes 1105928 | tf_op jit(solution)/shard_map/ppermute | solution.py:427
  80.3 17.8 %collective-permute-start.20 = (bf16[4,40,1152]{2,1,0:T(8,128)(2,1)S(1)}, bf16[4,40,1152]{2,1,0:T(8,128)(2,1)S(1)}, u32[]{:S(2)}, u32[]{:S(2)}) collective-permute-start(bf16[4,40,1152]{2,1,0:T(8,128)(2,1)S(1)} %get-tuple-element.47), channel_id=1, source_target_pairs={{0,24},{8,16},{16,8},{24,0},{1,25},{9,17},{17,9},{25,1},{2,26},{10... | collective-permute-start | bytes 1105928 | tf_op jit(solution)/shard_map/ppermute | solution.py:427
  84.3 18.4 %collective-permute-start.14 = (bf16[40,1152]{1,0:T(8,128)(2,1)S(1)}, bf16[40,1152]{1,0:T(8,128)(2,1)S(1)}, u32[]{:S(2)}, u32[]{:S(2)}) collective-permute-start(bf16[40,1152]{1,0:T(8,128)(2,1)S(1)} %get-tuple-element.41), channel_id=1, source_target_pairs={{0,8},{8,0},{16,24},{24,16},{1,9},{9,1},{17,25},{25,17},{2,10},{10... | collective-permute-start | bytes 276488 | tf_op jit(solution)/shard_map/ppermute | solution.py:442
  85.9 24.6 %collective-permute-start.15 = (bf16[40,1152]{1,0:T(8,128)(2,1)S(1)}, bf16[40,1152]{1,0:T(8,128)(2,1)S(1)}, u32[]{:S(2)}, u32[]{:S(2)}) collective-permute-start(bf16[40,1152]{1,0:T(8,128)(2,1)S(1)} %get-tuple-element.41), channel_id=1, source_target_pairs={{0,16},{8,24},{16,0},{24,8},{1,17},{9,25},{17,1},{25,9},{2,18},{10... | collective-permute-start | bytes 276488 | tf_op jit(solution)/shard_map/ppermute | solution.py:442
  88.9 26.2 %collective-permute-start.16 = (bf16[40,1152]{1,0:T(8,128)(2,1)S(1)}, bf16[40,1152]{1,0:T(8,128)(2,1)S(1)}, u32[]{:S(2)}, u32[]{:S(2)}) collective-permute-start(bf16[40,1152]{1,0:T(8,128)(2,1)S(1)} %get-tuple-element.41), channel_id=1, source_target_pairs={{0,24},{8,16},{16,8},{24,0},{1,25},{9,17},{17,9},{25,1},{2,26},{10... | collective-permute-start | bytes 276488 | tf_op jit(solution)/shard_map/ppermute | solution.py:442
  98.4 5.6 %collective-permute-start.21 = (bf16[40,1152]{1,0:T(8,128)(2,1)S(1)}, bf16[40,1152]{1,0:T(8,128)(2,1)S(1)}, u32[]{:S(2)}, u32[]{:S(2)}) collective-permute-start(bf16[40,1152]{1,0:T(8,128)(2,1)S(1)} %get-tuple-element.61), channel_id=1, source_target_pairs={{0,2},{2,0},{4,6},{6,4},{1,3},{3,1},{5,7},{7,5},{8,10},{10,8},{12,... | collective-permute-start | bytes 276488 | tf_op jit(solution)/shard_map/ppermute | solution.py:427
  99.3 6.9 %collective-permute-start.22 = (bf16[40,1152]{1,0:T(8,128)(2,1)S(1)}, bf16[40,1152]{1,0:T(8,128)(2,1)S(1)}, u32[]{:S(2)}, u32[]{:S(2)}) collective-permute-start(bf16[40,1152]{1,0:T(8,128)(2,1)S(1)} %get-tuple-element.60), channel_id=1, source_target_pairs={{0,4},{2,6},{4,0},{6,2},{1,5},{3,7},{5,1},{7,3},{8,12},{10,14},{12... | collective-permute-start | bytes 276488 | tf_op jit(solution)/shard_map/ppermute | solution.py:427
  102.7 6.3 %collective-permute-start.23 = (bf16[40,1152]{1,0:T(8,128)(2,1)S(1)}, bf16[40,1152]{1,0:T(8,128)(2,1)S(1)}, u32[]{:S(2)}, u32[]{:S(2)}) collective-permute-start(bf16[40,1152]{1,0:T(8,128)(2,1)S(1)} %get-tuple-element.59), channel_id=1, source_target_pairs={{0,6},{2,4},{4,2},{6,0},{1,7},{3,5},{5,3},{7,1},{8,14},{10,12},{12... | collective-permute-start | bytes 276488 | tf_op jit(solution)/shard_map/ppermute | solution.py:427
  109.2 4.6 %collective-permute-start.24 = (bf16[40,1152]{1,0:T(8,128)(2,1)S(1)}, bf16[40,1152]{1,0:T(8,128)(2,1)S(1)}, u32[]{:S(2)}, u32[]{:S(2)}) collective-permute-start(bf16[40,1152]{1,0:T(8,128)(2,1)S(1)} %get-tuple-element.43), channel_id=1, source_target_pairs={{0,8},{8,0},{16,24},{24,16},{1,9},{9,1},{17,25},{25,17},{2,10},{10... | collective-permute-start | bytes 276488 | tf_op jit(solution)/shard_map/ppermute | solution.py:442
  110.5 4.6 %collective-permute-start.25 = (bf16[40,1152]{1,0:T(8,128)(2,1)S(1)}, bf16[40,1152]{1,0:T(8,128)(2,1)S(1)}, u32[]{:S(2)}, u32[]{:S(2)}) collective-permute-start(bf16[40,1152]{1,0:T(8,128)(2,1)S(1)} %get-tuple-element.43), channel_id=1, source_target_pairs={{0,16},{8,24},{16,0},{24,8},{1,17},{9,25},{17,1},{25,9},{2,18},{10... | collective-permute-start | bytes 276488 | tf_op jit(solution)/shard_map/ppermute | solution.py:442
  111.9 5.5 %collective-permute-start.26 = (bf16[40,1152]{1,0:T(8,128)(2,1)S(1)}, bf16[40,1152]{1,0:T(8,128)(2,1)S(1)}, u32[]{:S(2)}, u32[]{:S(2)}) collective-permute-start(bf16[40,1152]{1,0:T(8,128)(2,1)S(1)} %get-tuple-element.43), channel_id=1, source_target_pairs={{0,24},{8,16},{16,8},{24,0},{1,25},{9,17},{17,9},{25,1},{2,26},{10... | collective-permute-start | bytes 276488 | tf_op jit(solution)/shard_map/ppermute | solution.py:442

commit v7 on v6

--- a/solution.py
+++ b/solution.py
@@ -32,68 +32,91 @@
 
 
 PIECE = 384
-
-
-def project_kernel(
-    own_ref, tokens_ref, weight_ref, qt_ref, kv_ref, top_ref, bottom_ref, near_ref, tokens, weight, sems
-):
-    rows = [(INNER + PIECE * p, PIECE) for p in range(2 * INNER // PIECE)] + [(0, INNER)]
-    whole = pltpu.make_async_copy(tokens_ref, tokens, sems.at[len(rows)])
-    whole.start()
-    copies = []
-    for n, (first, count) in enumerate(rows):
-        part = pl.ds(first, count)
-        copies.append(pltpu.make_async_copy(weight_ref.at[part], weight.at[part], sems.at[n]))
-        copies[-1].start()
-    whole.wait()
-    for p in range(2 * INNER // PIECE):
-        copies[p].wait()
-        lines = weight[INNER + PIECE * p : INNER + PIECE * (p + 1)]
-        kv_ref[:, PIECE * p : PIECE * (p + 1)] = nt_dot(tokens[...], lines).astype(jnp.bfloat16)
-    count, edge = kv_ref.shape[0], top_ref.shape[0]
-    keyvals = kv_ref[...]
-    top_ref[...] = keyvals[:edge]
-    bottom_ref[...] = keyvals[count - edge :]
-    grid = keyvals.astype(jnp.float32).reshape(-1, edge // SIDE, 2 * INNER)
-    is_right = own_ref[0].astype(jnp.float32)
-    near = grid[:, :REACH] * is_right + grid[:, -REACH:] * (1.0 - is_right)
-    near_ref[...] = near.reshape(near_ref.shape).astype(jnp.bfloat16)
-    copies[-1].wait()
-    qt_ref[...] = nt_dot(weight[:INNER], tokens[...]).astype(jnp.bfloat16)
+PIECES = 2 * INNER // PIECE
+
+
+def fetch(pairs, sems):
+    copies = [pltpu.make_async_copy(*pair, sems.at[n]) for n, pair in enumerate(pairs)]
+    for copy in copies:
+        copy.start()
+    return copies
+
+
+def weight_pieces(weight_ref, weight):
+    return [
+        (weight_ref.at[pl.ds(INNER + PIECE * p, PIECE)], weight.at[pl.ds(PIECE * p, PIECE)])
+        for p in range(PIECES)
+    ]
+
+
+def edges_kernel(tokens_ref, weight_ref, top_ref, bottom_ref, tokens, weight, sems):
+    edge = top_ref.shape[0]
+    ends = [(0, 0), (edge, tokens_ref.shape[0] - edge)]
+    token_pairs = [
+        (tokens_ref.at[pl.ds(there, edge)], tokens.at[pl.ds(here, edge)]) for here, there in ends
+    ]
+    copies = fetch(token_pairs + weight_pieces(weight_ref, weight), sems)
+    copies[0].wait()
+    copies[1].wait()
+    for p in range(PIECES):
+        copies[2 + p].wait()
+        lanes = slice(PIECE * p, PIECE * (p + 1))
+        part = nt_dot(tokens[...], weight[lanes]).astype(jnp.bfloat16)
+        top_ref[:, lanes] = part[:edge]
+        bottom_ref[:, lanes] = part[edge:]
+
+
+def project_kernel(own_ref, top_ref, tokens_ref, weight_ref, kv_ref, near_ref, tokens, weight, sems):
+    copies = fetch([(tokens_ref, tokens)] + weight_pieces(weight_ref, weight), sems)
+    copies[0].wait()
+    for p in range(PIECES):
+        copies[1 + p].wait()
+        lanes = slice(PIECE * p, PIECE * (p + 1))
+        part = nt_dot(tokens[...], weight[lanes])
+        kv_ref[:, lanes] = part.astype(jnp.bfloat16)
+        grid = part.reshape(near_ref.shape[0] // REACH, -1, PIECE)
+        is_right = own_ref[0].astype(jnp.float32)
+        near = grid[:, :REACH] * is_right + grid[:, -REACH:] * (1.0 - is_right)
+        near_ref[:, lanes] = near.reshape(-1, PIECE).astype(jnp.bfloat16)
 
 
 def project(token_rows, weight, tile_cols):
     rows, width = token_rows.shape
-    chunk_own = SIDE * tile_cols
+    edge = SIDE * tile_cols
     own = lax.axis_index("col").astype(jnp.int32).reshape(1)
-    shapes = [
-        (INNER, rows),
-        (rows, 2 * INNER),
-        (chunk_own, 2 * INNER),
-        (chunk_own, 2 * INNER),
-        (rows // tile_cols * REACH, 2 * INNER),
+    shape = lambda count: jax.ShapeDtypeStruct((count, 2 * INNER), jnp.bfloat16)
+    block = lambda count: pl.BlockSpec((count, 2 * INNER), lambda _: (0, 0))
+    anywhere = pl.BlockSpec(memory_space=pl.ANY)
+    params = pltpu.CompilerParams(vmem_limit_bytes=56 * 1024 * 1024)
+    scratch = lambda count, copies: [
+        pltpu.VMEM((count, width), jnp.bfloat16),
+        pltpu.VMEM((2 * INNER, width), jnp.bfloat16),
+        pltpu.SemaphoreType.DMA((copies,)),
     ]
-    return pl.pallas_call(
+    top, bottom = pl.pallas_call(
+        edges_kernel,
+        grid=(1,),
+        out_shape=[shape(edge)] * 2,
+        in_specs=[anywhere] * 2,
+        out_specs=[block(edge)] * 2,
+        scratch_shapes=scratch(2 * edge, PIECES + 2),
+        compiler_params=params,
+        cost_estimate=LIGHT,
+        name="project_edges",
+    )(token_rows, weight.T)
+    near = rows // tile_cols * REACH
+    keyvals, near = pl.pallas_call(
         project_kernel,
         grid=(1,),
-        out_shape=[jax.ShapeDtypeStruct(shape, jnp.bfloat16) for shape in shapes],
-        in_specs=[
-            pl.BlockSpec(memory_space=pltpu.SMEM),
-            pl.BlockSpec(memory_space=pl.ANY),
-            pl.BlockSpec(memory_space=pl.ANY),
-        ],
-        out_specs=[pl.BlockSpec(shape, lambda k: (0, 0)) for shape in shapes],
-        scratch_shapes=[
-            pltpu.VMEM((rows, width), jnp.bfloat16),
-            pltpu.VMEM((3 * INNER, width), jnp.bfloat16),
-            pltpu.SemaphoreType.DMA((2 * INNER // PIECE + 2,)),
-        ],
-        compiler_params=pltpu.CompilerParams(vmem_limit_bytes=56 * 1024 * 1024),
-        cost_estimate=pl.CostEstimate(
-            flops=6 * rows * width * INNER, bytes_accessed=8 * 1024 * 1024, transcendentals=0
-        ),
+        out_shape=[shape(rows), shape(near)],
+        in_specs=[pl.BlockSpec(memory_space=pltpu.SMEM)] + [anywhere] * 3,
+        out_specs=[block(rows), block(near)],
+        scratch_shapes=scratch(rows, PIECES + 1),
+        compiler_params=params,
+        cost_estimate=LIGHT,
         name="project",
-    )(own, token_rows, weight.T)
+    )(own, top, token_rows, weight.T)
+    return keyvals, top, bottom, near
 
 
 def attention_kernel(
@@ -316,15 +339,15 @@
         in_specs=[pl.BlockSpec(memory_space=pltpu.SMEM)] + [whole(a) for a in operands],
         out_specs=(whole(out), whole(out)),
         scratch_shapes=[pltpu.VMEM((len(operands) // 2, width, rows), jnp.bfloat16)],
-        compiler_params=pltpu.CompilerParams(vmem_limit_bytes=28 * 1024 * 1024),
+        compiler_params=pltpu.CompilerParams(vmem_limit_bytes=22 * 1024 * 1024),
         cost_estimate=LIGHT,
         name="weight_grad_halves",
     )(own, *operands)
 
 
 def late_kernel(
-    own_ref, first, second, third, tokens_ref, inner_ref, side_ref, above_ref, below_ref,
-    dq_ref, o_ref, sent_ref, kept_ref, all_ref, att_ref, turned, grad_ref,
+    own_ref, earlier_ref, tokens_ref, inner_ref, side_ref, above_ref, below_ref,
+    o_ref, sent_ref, kept_ref, grad_ref, att_ref, turned,
 ):
     own = own_ref[0]
     count = inner_ref.shape[0]
@@ -347,34 +370,59 @@
         ]
         product = dot(jnp.concatenate(picked, axis=0), grad_ref[...])
         out_ref[...] = product.astype(jnp.bfloat16)
-    all_ref[...] = jnp.concatenate([dq_ref[:, :INNER], grad_ref[...]], axis=1)
     att_ref[...] = o_ref[:, 64:]
 
 
-def late_halves(earlier, token_rows, inner, side, above, below, dquery, attended):
+def late_halves(earlier, token_rows, inner, side, above, below, attended):
     rows, width = token_rows.shape
     whole = lambda a: pl.BlockSpec(a.shape, lambda _: (0,) * a.ndim)
     out = jax.ShapeDtypeStruct((width // 2, 2 * INNER), jnp.bfloat16)
-    grads = jax.ShapeDtypeStruct((rows, 3 * INNER), jnp.bfloat16)
+    grads = jax.ShapeDtypeStruct((rows, 2 * INNER), jnp.bfloat16)
     att = jax.ShapeDtypeStruct((rows, INNER), jnp.bfloat16)
-    operands = (token_rows, inner, side, above, below, dquery, attended)
+    operands = (token_rows, inner, side, above, below, attended)
     own = lax.axis_index("col").astype(jnp.int32).reshape(1)
     return pl.pallas_call(
         late_kernel,
         grid=(1,),
         out_shape=(out, out, grads, att),
         in_specs=[pl.BlockSpec(memory_space=pltpu.SMEM)]
-        + [pl.BlockSpec(memory_space=pl.ANY)] * 3
+        + [pl.BlockSpec(memory_space=pl.ANY)]
         + [whole(a) for a in operands],
         out_specs=(whole(out), whole(out), whole(grads), whole(att)),
-        scratch_shapes=[
-            pltpu.VMEM((width, rows), jnp.bfloat16),
-            pltpu.VMEM((rows, 2 * INNER), jnp.bfloat16),
-        ],
-        compiler_params=pltpu.CompilerParams(vmem_limit_bytes=28 * 1024 * 1024),
+        scratch_shapes=[pltpu.VMEM((width, rows), jnp.bfloat16)],
+        compiler_params=pltpu.CompilerParams(vmem_limit_bytes=22 * 1024 * 1024),
         cost_estimate=LIGHT,
         name="late_weight_grad_halves",
-    )(own, *earlier, *operands)
+    )(own, earlier, *operands)
+
+
+def row_parts_kernel(own_ref, held, dq_ref, dkv_ref, *refs):
+    for step, out in enumerate(refs[-5:-1]):
+        out[...] = held[own_ref[0] ^ step]
+    refs[-1][...] = jnp.concatenate([dq_ref[:, :INNER], dkv_ref[...]], axis=1)
+
+
+def row_parts(held, dquery, dkv, *earlier):
+    rows, small, width = held.shape
+    own = lax.axis_index("row").astype(jnp.int32).reshape(1)
+    return pl.pallas_call(
+        row_parts_kernel,
+        grid=(1,),
+        out_shape=[jax.ShapeDtypeStruct((small, width), jnp.bfloat16)] * 4
+        + [jax.ShapeDtypeStruct((dkv.shape[0], 3 * INNER), jnp.bfloat16)],
+        in_specs=[
+            pl.BlockSpec(memory_space=pltpu.SMEM),
+            pl.BlockSpec((rows, small, width), lambda _: (0, 0, 0)),
+            pl.BlockSpec(dquery.shape, lambda _: (0, 0)),
+            pl.BlockSpec(dkv.shape, lambda _: (0, 0)),
+        ]
+        + [pl.BlockSpec(memory_space=pl.ANY)] * len(earlier),
+        out_specs=[pl.BlockSpec((small, width), lambda _: (0, 0))] * 4
+        + [pl.BlockSpec((dkv.shape[0], 3 * INNER), lambda _: (0, 0))],
+        compiler_params=pltpu.CompilerParams(vmem_limit_bytes=16 * 1024 * 1024),
+        cost_estimate=LIGHT,
+        name="row_parts",
+    )(own, held, dquery, dkv, *earlier)
 
 
 def window_starts(places, extent):
@@ -420,11 +468,15 @@
     return [take(block, own ^ step) for step in range(lax.axis_size(axis))]
 
 
-def exchange_sum(parts, axis, *earlier):
-    kept, got = parts[0], []
+def exchanged(parts, axis):
+    got = []
     for step, part in enumerate(parts[1:], 1):
         pairs = [(i, i ^ step) for i in range(lax.axis_size(axis))]
         got.append(lax.ppermute(part, axis, pairs))
+    return got
+
+
+def added(kept, got, *earlier):
     if earlier:
         kept = after(kept, *earlier)
     total = kept.astype(jnp.float32)
@@ -460,8 +512,20 @@
     return cut(held, "img", lambda h, j: lax.dynamic_slice_in_dim(h, small * j, small, 1))
 
 
-def row_parts(held):
-    return cut(held, "row", lambda h, r: lax.dynamic_index_in_dim(h, r, 0, keepdims=False))
+def row_sum_in_steps(held):
+    own = lax.axis_index("row")
+    count = lax.axis_size("row")
+    bit = 1
+    while bit < count:
+        parts = held.reshape((-1, 2) + held.shape[1:])
+        mine = (own // bit) % 2
+        kept = lax.dynamic_index_in_dim(parts, mine, 1, keepdims=False)
+        sent = lax.dynamic_index_in_dim(parts, 1 - mine, 1, keepdims=False)
+        got = lax.ppermute(sent, "row", [(i, i ^ bit) for i in range(count)])
+        total = kept.astype(jnp.float32) + got.astype(jnp.float32)
+        held = total.astype(jnp.bfloat16)
+        bit *= 2
+    return held[0]
 
 
 def whole_share(held, share):
@@ -509,7 +573,10 @@
         got = got[0] if two_columns else jnp.concatenate(got, axis=1)
         return got.reshape(-1, 2 * INNER)
 
-    queries, keyvals, top, bottom, near = project(token_rows, qkv_weight, tile_cols)
+    keyvals, top, bottom, near = project(token_rows, qkv_weight, tile_cols)
+    queries = lax.dot_general(
+        qkv_weight[:, :INNER], token_rows, (((0,), (1,)), ((), ())), preferred_element_type=jnp.float32
+    ).astype(jnp.bfloat16)
     above = moved(bottom, 1)
     below = moved(top, -1)
     if two_columns:
@@ -533,6 +600,7 @@
     simple = two_columns and row_count == 4 and lax.axis_size("img") == 4
     if simple:
         early = image_parts(core_sum(*outer_halves(token_rows, dquery, grad_rows, attended)))
+        early_got = exchanged(early, "img")
     def spread(side, first):
         side = side.reshape(-1, SIDE, REACH, 2 * INNER).astype(jnp.float32)
         zeros = jnp.zeros((side.shape[0], SIDE, tile_cols - REACH, 2 * INNER), jnp.float32)
@@ -553,8 +621,8 @@
     from_above = moved(outer_grad[chunk_own:], 1)
     if simple:
         side = got.reshape(-1, 2 * INNER)
-        sent, kept, dqkv, attended = late_halves(
-            early[1:], token_rows, inner_grad, side, from_above, from_below, dquery, attended
+        sent, kept, dkv, attended = late_halves(
+            early_got[-1], token_rows, inner_grad, side, from_above, from_below, attended
         )
     else:
         dquery, attended = dquery[:, :INNER], attended[:, 64:]
@@ -564,18 +632,21 @@
         dkv = dkv + jnp.concatenate([rest, from_below.astype(jnp.float32)], axis=0)
         dkv = dkv.astype(jnp.bfloat16)
         dqkv = jnp.concatenate([dquery, dkv], axis=1)
+        sublayer_out = nt_dot(attended, out_weight).astype(jnp.bfloat16)
     if simple:
         late = image_parts(core_sum(sent, kept))
-        early = exchange_sum(early, "img")
-        late = exchange_sum(late, "img", early)
-        early = exchange_sum(row_parts(early), "row")
-        late = exchange_sum(row_parts(late), "row", early)
+        late_got = exchanged(late, "img")
+        early = added(early[0], early_got)
+        late = added(late[0], late_got, early)
+        sublayer_out = nt_dot(attended, out_weight).astype(jnp.bfloat16)
+        *early, dqkv = row_parts(early, dquery, dkv, late_got[-1])
+        early = added(early[0], exchanged(early, "row"))
+        late = row_sum_in_steps(late)
         share = width // (row_count * col_count)
         early, late = whole_share(early, share), whole_share(late, share)
     else:
         early = jnp.concatenate([outer(token_rows, dquery), outer(grad_rows, attended)], axis=1)
         early, late = plain_shares(early), plain_shares(outer(token_rows, dkv))
-    sublayer_out = nt_dot(attended, out_weight).astype(jnp.bfloat16)
     tokens_grad = nt_dot(dqkv, qkv_weight).astype(jnp.bfloat16)
     return (
         sublayer_out.reshape(tokens.shape),

time: 120 us -> 126 us (1.050)
  waiting for transfers between devices: 34.3 us -> 29.1 us
  local copies, waits for them, and re-layouts: 6.01 us -> 10 us
  Pallas kernels: 26.9 us -> 30.7 us
  matrix products: 6.74 us -> 9.8 us
  other arithmetic: 4.9 us -> 6.72 us
  starting transfers between devices: 39.7 us -> 38.3 us
    ppermute x12 -> x11, waiting for transfers between devices: 20.8 us -> 15.9 us  [the longest x9 13.4 us: exchanged(): got.append(lax.ppermute(part, axis, pairs))]
    pallas_call x1 -> x3, Pallas kernels: 6.32 us -> 9.7 us  [the longest x1 5.46 us: project(): pl.pallas_call(project_kernel, grid=(1,), out_shape=[shape(rows), shape(n...]
    ppermute x2, waiting for transfers between devices: 0.01 us -> 3.38 us  [core_sum(): lax.ppermute(sent, 'col', [(0, 1), (1, 0)]).reshape(rows, share, width)]
    ppermute x7, waiting for transfers between devices: 9.59 us -> 6.31 us  [moved(): return lax.ppermute(block, ('row', 'col'), pairs)]
    unnamed x35 -> x47, local copies, waits for them, and re-layouts: 3.03 us -> 6.19 us
    dot_general x0 -> x1, matrix products: none -> 3.1 us  [local(): lax.dot_general(qkv_weight[:, :INNER], token_rows, (((0,), (1,)), ((), ()...]
    ppermute x6, starting transfers between devices: 9.64 us -> 7.48 us  [gathered(): got = lax.ppermute(block, axis, [(i, i ^ step) for i in range(count)])]
    convert_element_type x2, other arithmetic: 1.97 us -> 3.69 us  [core_sum(): (kept.astype(jnp.float32) + got.astype(jnp.float32)).astype(jnp.bfloat16)]
  transfers between devices with their start and end apart: 27 -> 26, of which waited for: 14 -> 10; matrix products, arithmetic and copies ran while one was open for 10% -> 12% of each run, Pallas kernels for 6% -> 8%
where the time goes in v7:
time: 126 us
  starting transfers between devices  38.3 us (30%)
  Pallas kernels  30.7 us (24%)
  waiting for transfers between devices  29.1 us (23%)
  local copies, waits for them, and re-layouts  10 us (8%)
  matrix products  9.8 us (8%)
  other arithmetic  6.72 us (5%)
    ppermute x7, starting transfers between devices, moved(): return lax.ppermute(block, ('row', 'col'), pairs)  13.8 us
    ppermute x9, waiting for transfers between devices, exchanged(): got.append(lax.ppermute(part, axis, pairs))  13.4 us
    pallas_call x1, Pallas kernels, attention(): pl.pallas_call(attention_kernel, grid=(1,), out_shape=outs, in_specs=[pl....  13.2 us
    ppermute x9, starting transfers between devices, exchanged(): got.append(lax.ppermute(part, axis, pairs))  11.4 us
    ppermute x6, starting transfers between devices, gathered(): got = lax.ppermute(block, axis, [(i, i ^ step) for i in range(count)])  7.48 us
    ppermute x7, waiting for transfers between devices, moved(): return lax.ppermute(block, ('row', 'col'), pairs)  6.31 us
    unnamed x47, local copies, waits for them, and re-layouts  6.19 us
    dot_general x2, matrix products, nt_dot(): lax.dot_general(a, b, (((1,), (1,)), ((), ())), preferred_element_type=jn...  5.75 us
  transfers between devices with their start and end apart: 26, of which 10 were waited for; matrix products, arithmetic and copies ran while one was open for 12% of the time, Pallas kernels for 8%

profile of v7, /device:TPU:0, one launch (start us, length us, event | category | flops | bytes accessed | tf_op | source)
XLA Modules:
  0.0 125.9 jit_solution(7809315800541061520)
XLA Ops:
  0.6 3.9 %project_edges.1 = (bf16[128,1152]{1,0:T(8,128)(2,1)}, bf16[128,1152]{1,0:T(8,128)(2,1)}) custom-call(bf16[512,1152]{1,0:T(8,128)(2,1)} %bitcast.49, bf16[1728,1152]{1,0:T(8,128)(2,1)} %bitcast.59), custom_call_target="tpu_custom_call" | custom-call | flops 1 | bytes 1 | tf_op jit(solution)/shard_map/project_edges/pallas_call | solution.py:96
  4.5 4.9 %collective-permute-start = (bf16[128,1152]{1,0:T(8,128)(2,1)}, bf16[128,1152]{1,0:T(8,128)(2,1)S(1)}, u32[]{:S(2)}, u32[]{:S(2)}) collective-permute-start(bf16[128,1152]{1,0:T(8,128)(2,1)} %get-tuple-element.27), channel_id=1, source_target_pairs={{0,2},{1,3},{2,4},{3,5},{4,6},{5,7},{8,10},{9,11},{10,12},{11,13},... | collective-permute-start | bytes 884744 | tf_op jit(solution)/shard_map/ppermute | solution.py:560
  9.5 1.3 %collective-permute-start.1 = (bf16[128,1152]{1,0:T(8,128)(2,1)}, bf16[128,1152]{1,0:T(8,128)(2,1)S(1)}, u32[]{:S(2)}, u32[]{:S(2)}) collective-permute-start(bf16[128,1152]{1,0:T(8,128)(2,1)} %get-tuple-element.25.top_ref), channel_id=1, source_target_pairs={{2,0},{3,1},{4,2},{5,3},{6,4},{7,5},{10,8},{11,9},{12,10},{13,11},... | collective-permute-start | bytes 884744 | tf_op jit(solution)/shard_map/ppermute | solution.py:560
  10.8 5.5 %project.1 = (bf16[512,1152]{1,0:T(8,128)(2,1)}, bf16[256,1152]{1,0:T(8,128)(2,1)}) custom-call(s32[1]{0:T(128)} %bitcast.own_ref, bf16[128,1152]{1,0:T(8,128)(2,1)} %get-tuple-element.25.top_ref, bf16[512,1152]{1,0:T(8,128)(2,1)} %bitcast.50, bf16[1728,1152]{1,0:T(8,128)(2,1)} %bitcast.60), custom_call_target="tpu_custom_call" | custom-call | flops 1 | bytes 1 | tf_op jit(solution)/shard_map/project/pallas_call | solution.py:108
  16.4 3.1 %fusion.2.qt_ref = bf16[576,512]{1,0:T(8,128)(2,1)} fusion(bf16[512,1152]{1,0:T(8,128)(2,1)S(1)} %bitcast.51, bf16[1152,1728]{0,1:T(8,128)(2,1)} %param.5), kind=kOutput, calls=%fused_computation.8 | convolution fusion | flops 679772160 | bytes 3096576 | tf_op jit(solution)/shard_map/dot_general | solution.py:577
  19.8 0.1 reshape.212
  19.9 0.1 reshape.211
  20.2 0.1 fusion.10
  20.4 0.4 fusion.8.bias_ref
  20.9 0.5 collective-permute-start.3
  21.5 1.0 convolution_convert_fusion.2.g_ref
  22.4 0.2 collective-permute-done.3
  22.7 0.1 copy-done.19
  22.9 1.0 copy-done.15
  23.8 13.2 %window_attention.1 = (bf16[512,640]{1,0:T(8,128)(2,1)S(1)}, bf16[512,640]{1,0:T(8,128)(2,1)S(1)}, bf16[512,1152]{1,0:T(8,128)(2,1)S(1)}, bf16[256,1152]{1,0:T(8,128)(2,1)S(1)}, bf16[384,1152]{1,0:T(8,128)(2,1)}) custom-call(s32[4]{0:T(128)S(1)} %broadcast_subtract_fusion.start_ref, bf16[576,512]{1,0:T(8,128)(2,1)S(1)} %copy-done.19, ...), custom_call_target="tpu_custom_call" | custom-call | flops 4076863488 | bytes 16777216 | tf_op jit(solution)/shard_map/window_attention/pallas_call | solution.py:274
  37.0 0.4 collective-permute-start.6
  37.4 3.6 %weight_grad_halves.1 = (bf16[576,1152]{1,0:T(8,128)(2,1)}, bf16[576,1152]{1,0:T(8,128)(2,1)S(1)}) custom-call(s32[1]{0:T(128)} %bitcast.own_ref, bf16[512,1152]{1,0:T(8,128)(2,1)S(1)} %bitcast.52, bf16[512,640]{1,0:T(8,128)(2,1)S(1)} %get-tuple-element.29.refs_1_.dq_ref, bf16[512,1152]{1,0:T(8,128)(2,1)S(1)} %bitcast.55, ...), custom_call_target="tpu_custom_call" | custom-call | flops 1 | bytes 1 | tf_op jit(solution)/shard_map/weight_grad_halves/pallas_call | solution.py:335
  41.1 1.1 copy-done.5
  42.1 0.1 collective-permute-start.4
  42.3 1.0 slice.33
  43.4 0.9 copy-done.13
  44.3 0.1 fusion.5
  44.5 1.1 collective-permute-done.4
  45.5 1.7 %add_convert_fusion.1 = bf16[576,1152]{1,0:T(8,128)(2,1)S(1)} fusion(bf16[576,1152]{1,0:T(8,128)(2,1)} %collective-permute-done.4, bf16[576,1152]{1,0:T(8,128)(2,1)S(1)} %copy-done.6), kind=kLoop, calls=%fused_computation.3 | loop fusion | flops 2654208 | bytes 3981312 | tf_op jit(solution)/shard_map/convert_element_type | solution.py:505
  47.2 1.0 pad_dynamic-slice_fusion.5
  48.2 2.5 %collective-permute-start.5 = (bf16[4,40,1152]{2,1,0:T(8,128)(2,1)S(1)}, bf16[4,40,1152]{2,1,0:T(8,128)(2,1)S(1)}, u32[]{:S(2)}, u32[]{:S(2)}) collective-permute-start(bf16[4,40,1152]{2,1,0:T(8,128)(2,1)S(1)} %get-tuple-element.54), channel_id=1, source_target_pairs={{0,24},{8,16},{16,8},{24,0},{1,25},{9,17},{17,9},{25,1},{2,26},{10... | collective-permute-start | bytes 1105928 | tf_op jit(solution)/shard_map/ppermute | solution.py:475
  50.7 1.3 %collective-permute-start.8 = (bf16[128,1152]{1,0:T(8,128)(2,1)S(1)}, bf16[128,1152]{1,0:T(8,128)(2,1)S(1)}, u32[]{:S(2)}, u32[]{:S(2)}) collective-permute-start(bf16[128,1152]{1,0:T(8,128)(2,1)S(1)} %get-tuple-element.57), channel_id=1, source_target_pairs={{2,0},{3,1},{4,2},{5,3},{6,4},{7,5},{10,8},{11,9},{12,10},{13,11},... | collective-permute-start | bytes 884744 | tf_op jit(solution)/shard_map/ppermute | solution.py:560
  52.0 5.4 %collective-permute-start.7 = (bf16[128,1152]{1,0:T(8,128)(2,1)S(1)}, bf16[128,1152]{1,0:T(8,128)(2,1)S(1)}, u32[]{:S(2)}, u32[]{:S(2)}) collective-permute-start(bf16[128,1152]{1,0:T(8,128)(2,1)S(1)} %get-tuple-element.58), channel_id=1, source_target_pairs={{0,2},{1,3},{2,4},{3,5},{4,6},{5,7},{8,10},{9,11},{10,12},{11,13},... | collective-permute-start | bytes 884744 | tf_op jit(solution)/shard_map/ppermute | solution.py:560
  57.4 4.9 %collective-permute-done.8.below_ref = bf16[128,1152]{1,0:T(8,128)(2,1)S(1)} collective-permute-done((bf16[128,1152]{1,0:T(8,128)(2,1)S(1)}, bf16[128,1152]{1,0:T(8,128)(2,1)S(1)}, u32[]{:S(2)}, u32[]{:S(2)}) %collective-permute-start.8) | collective-permute-done | bytes 294944 | tf_op jit(solution)/shard_map/ppermute | solution.py:560
  62.3 1.2 collective-permute-done.7.above_ref
  63.5 4.2 %late_weight_grad_halves.1 = (bf16[576,1152]{1,0:T(8,128)(2,1)}, bf16[576,1152]{1,0:T(8,128)(2,1)S(1)}, bf16[512,1152]{1,0:T(8,128)(2,1)S(1)}, bf16[512,576]{1,0:T(8,128)(2,1)S(1)}) custom-call(s32[1]{0:T(128)} %bitcast.own_ref, bf16[4,40,1152]{2,1,0:T(8,128)(2,1)S(1)} %collective-permute-done.5.earlier_ref, bf16[512,1152]{1,0:T(8,128)(2,1)S(1)} %bitcast.53, ...), custom_call_target="tpu_custom_call" | custom-call | flops 1 | bytes 1 | tf_op jit(solution)/shard_map/late_weight_grad_halves/pallas_call | solution.py:384
  67.7 1.1 copy-done.4
  68.7 1.0 copy-done.10
  69.8 0.8 copy-done.17
  70.6 0.5 collective-permute-start.9
  71.1 0.6 collective-permute-start.10
  71.7 2.3 %collective-permute-done.11 = bf16[576,1152]{1,0:T(8,128)(2,1)} collective-permute-done((bf16[576,1152]{1,0:T(8,128)(2,1)}, bf16[576,1152]{1,0:T(8,128)(2,1)}, u32[]{:S(2)}, u32[]{:S(2)}) %collective-permute-start.11) | collective-permute-done | bytes 1327136 | tf_op jit(solution)/shard_map/ppermute | solution.py:504
  74.0 2.0 %add_convert_fusion = bf16[576,1152]{1,0:T(8,128)(2,1)S(1)} fusion(bf16[576,1152]{1,0:T(8,128)(2,1)} %collective-permute-done.11, bf16[576,1152]{1,0:T(8,128)(2,1)} %copy-done.4), kind=kLoop, calls=%fused_computation.2 | loop fusion | flops 2654208 | bytes 3981312 | tf_op jit(solution)/shard_map/convert_element_type | solution.py:505
  76.0 0.2 pad_dynamic-slice_fusion.2
  76.3 0.6 collective-permute-start.12
  76.9 5.3 %collective-permute-done.9 = bf16[4,40,1152]{2,1,0:T(8,128)(2,1)S(1)} collective-permute-done((bf16[4,40,1152]{2,1,0:T(8,128)(2,1)}, bf16[4,40,1152]{2,1,0:T(8,128)(2,1)S(1)}, u32[]{:S(2)}, u32[]{:S(2)}) %collective-permute-start.9) | collective-permute-done | bytes 368672 | tf_op jit(solution)/shard_map/ppermute | solution.py:475
  82.2 7.8 %collective-permute-done.10 = bf16[4,40,1152]{2,1,0:T(8,128)(2,1)S(1)} collective-permute-done((bf16[4,40,1152]{2,1,0:T(8,128)(2,1)}, bf16[4,40,1152]{2,1,0:T(8,128)(2,1)S(1)}, u32[]{:S(2)}, u32[]{:S(2)}) %collective-permute-start.10) | collective-permute-done | bytes 368672 | tf_op jit(solution)/shard_map/ppermute | solution.py:475
  90.0 0.2 add_convert_fusion.3.held
  90.2 2.2 %convolution_convert_fusion.1 = bf16[512,1152]{1,0:T(8,128)(2,1)} fusion(bf16[512,576]{1,0:T(8,128)(2,1)S(1)} %copy-done.18, bf16[1152,576]{0,1:T(8,128)(2,1)S(1)} %copy-done), kind=kOutput, calls=%fused_computation.1 | convolution fusion | flops 680067072 | bytes 3096576 | tf_op jit(solution)/shard_map/dot_general | solution.py:31
  92.4 1.5 %collective-permute-start.19 = (bf16[4,40,1152]{2,1,0:T(8,128)(2,1)S(1)}, bf16[4,40,1152]{2,1,0:T(8,128)(2,1)S(1)}, u32[]{:S(2)}, u32[]{:S(2)}) collective-permute-start(bf16[4,40,1152]{2,1,0:T(8,128)(2,1)S(1)} %get-tuple-element.49), channel_id=1, source_target_pairs={{0,8},{8,0},{16,24},{24,16},{1,9},{9,1},{17,25},{25,17},{2,10},{10... | collective-permute-start | bytes 1105928 | tf_op jit(solution)/shard_map/ppermute | solution.py:475
  93.9 0.5 collective-permute-start.20
  94.4 0.4 row_parts.1
  94.8 2.5 %collective-permute-start.13 = (bf16[40,1152]{1,0:T(8,128)(2,1)S(1)}, bf16[40,1152]{1,0:T(8,128)(2,1)S(1)}, u32[]{:S(2)}, u32[]{:S(2)}) collective-permute-start(bf16[40,1152]{1,0:T(8,128)(2,1)S(1)} %get-tuple-element.42), channel_id=1, source_target_pairs={{0,2},{2,0},{4,6},{6,4},{1,3},{3,1},{5,7},{7,5},{8,10},{10,8},{12,... | collective-permute-start | bytes 276488 | tf_op jit(solution)/shard_map/ppermute | solution.py:475
  97.4 2.8 %collective-permute-start.14 = (bf16[40,1152]{1,0:T(8,128)(2,1)S(1)}, bf16[40,1152]{1,0:T(8,128)(2,1)S(1)}, u32[]{:S(2)}, u32[]{:S(2)}) collective-permute-start(bf16[40,1152]{1,0:T(8,128)(2,1)S(1)} %get-tuple-element.43), channel_id=1, source_target_pairs={{0,4},{2,6},{4,0},{6,2},{1,5},{3,7},{5,1},{7,3},{8,12},{10,14},{12... | collective-permute-start | bytes 276488 | tf_op jit(solution)/shard_map/ppermute | solution.py:475
  100.1 3.6 %convolution_convert_fusion = bf16[512,1152]{1,0:T(8,128)(2,1)} fusion(bf16[512,1728]{1,0:T(8,128)(2,1)S(1)} %get-tuple-element.40, bf16[1152,1728]{0,1:T(8,128)(2,1)S(1)} %copy-done.20), kind=kOutput, calls=%fused_computation | convolution fusion | flops 2039021568 | bytes 6930432 | tf_op jit(solution)/shard_map/dot_general | solution.py:31
  103.7 0.2 add_convert_fusion.2
  103.9 2.4 %collective-permute-start.21 = (bf16[2,40,1152]{2,1,0:T(8,128)(2,1)S(1)}, bf16[2,40,1152]{2,1,0:T(8,128)(2,1)S(1)}, u32[]{:S(2)}, u32[]{:S(2)}) collective-permute-start(bf16[2,40,1152]{2,1,0:T(8,128)(2,1)S(1)} %dynamic-slice_bitcast_fusion), channel_id=1, source_target_pairs={{0,2},{2,0},{4,6},{6,4},{1,3},{3,1},{5,7},{7,5},{8,10},{10,8},{12,... | collective-permute-start | bytes 552968 | tf_op jit(solution)/shard_map/ppermute | solution.py:524
  106.3 0.3 collective-permute-done.15
  106.7 1.6 %collective-permute-start.17 = (bf16[40,1152]{1,0:T(8,128)(2,1)S(1)}, bf16[40,1152]{1,0:T(8,128)(2,1)S(1)}, u32[]{:S(2)}, u32[]{:S(2)}) collective-permute-start(bf16[40,1152]{1,0:T(8,128)(2,1)S(1)} %get-tuple-element.47), channel_id=1, source_target_pairs={{0,16},{8,24},{16,0},{24,8},{1,17},{9,25},{17,1},{25,9},{2,18},{10... | collective-permute-start | bytes 276488 | tf_op jit(solution)/shard_map/ppermute | solution.py:494
  108.3 0.5 collective-permute-start.16
  108.8 1.4 %collective-permute-start.18 = (bf16[40,1152]{1,0:T(8,128)(2,1)S(1)}, bf16[40,1152]{1,0:T(8,128)(2,1)S(1)}, u32[]{:S(2)}, u32[]{:S(2)}) collective-permute-start(bf16[40,1152]{1,0:T(8,128)(2,1)S(1)} %get-tuple-element.47), channel_id=1, source_target_pairs={{0,24},{8,16},{16,8},{24,0},{1,25},{9,17},{17,9},{25,1},{2,26},{10... | collective-permute-start | bytes 276488 | tf_op jit(solution)/shard_map/ppermute | solution.py:494
  110.4 3.1 %collective-permute-start.22 = (bf16[1,40,1152]{2,1,0:T(8,128)(2,1)S(1)}, bf16[1,40,1152]{2,1,0:T(8,128)(2,1)S(1)}, u32[]{:S(2)}, u32[]{:S(2)}) collective-permute-start(bf16[1,40,1152]{2,1,0:T(8,128)(2,1)S(1)} %constant_dynamic-slice_fusion), channel_id=1, source_target_pairs={{0,4},{2,6},{4,0},{6,2},{1,5},{3,7},{5,1},{7,3},{8,12},{10,14},{12... | collective-permute-start | bytes 276488 | tf_op jit(solution)/shard_map/ppermute | solution.py:524
  113.5 2.5 %collective-permute-done.22 = bf16[1,40,1152]{2,1,0:T(8,128)(2,1)S(1)} collective-permute-done((bf16[1,40,1152]{2,1,0:T(8,128)(2,1)S(1)}, bf16[1,40,1152]{2,1,0:T(8,128)(2,1)S(1)}, u32[]{:S(2)}, u32[]{:S(2)}) %collective-permute-start.22) | collective-permute-done | bytes 92192 | tf_op jit(solution)/shard_map/ppermute | solution.py:524
  116.0 2.4 %collective-permute-start.25 = (bf16[40,1152]{1,0:T(8,128)(2,1)S(1)}, bf16[40,1152]{1,0:T(8,128)(2,1)S(1)}, u32[]{:S(2)}, u32[]{:S(2)}) collective-permute-start(bf16[40,1152]{1,0:T(8,128)(2,1)S(1)} %fusion.11), channel_id=1, source_target_pairs={{0,24},{8,16},{16,8},{24,0},{1,25},{9,17},{17,9},{25,1},{2,26},{10... | collective-permute-start | bytes 276488 | tf_op jit(solution)/shard_map/ppermute | solution.py:494
  118.4 0.1 collective-permute-start.24
  118.6 1.4 %collective-permute-start.23 = (bf16[40,1152]{1,0:T(8,128)(2,1)S(1)}, bf16[40,1152]{1,0:T(8,128)(2,1)S(1)}, u32[]{:S(2)}, u32[]{:S(2)}) collective-permute-start(bf16[40,1152]{1,0:T(8,128)(2,1)S(1)} %fusion.11), channel_id=1, source_target_pairs={{0,8},{8,0},{16,24},{24,16},{1,9},{9,1},{17,25},{25,17},{2,10},{10... | collective-permute-start | bytes 276488 | tf_op jit(solution)/shard_map/ppermute | solution.py:494
  120.0 3.5 %collective-permute-done.23 = bf16[40,1152]{1,0:T(8,128)(2,1)S(1)} collective-permute-done((bf16[40,1152]{1,0:T(8,128)(2,1)S(1)}, bf16[40,1152]{1,0:T(8,128)(2,1)S(1)}, u32[]{:S(2)}, u32[]{:S(2)}) %collective-permute-start.23) | collective-permute-done | bytes 92192 | tf_op jit(solution)/shard_map/ppermute | solution.py:494
  123.7 0.9 fusion.13
  124.6 1.2 pad_maximum_fusion
  (101 shorter events, 1.6 us)
Async XLA Ops:
  0.6 20.8 %copy-start = (bf16[1152,576]{0,1:T(8,128)(2,1)S(1)}, bf16[1152,576]{0,1:T(8,128)(2,1)}, u32[]{:S(2)}) copy-start(bf16[1152,576]{0,1:T(8,128)(2,1)} %param.6) | copy-start | bytes 3981316
  4.5 16.3 %collective-permute-start = (bf16[128,1152]{1,0:T(8,128)(2,1)}, bf16[128,1152]{1,0:T(8,128)(2,1)S(1)}, u32[]{:S(2)}, u32[]{:S(2)}) collective-permute-start(bf16[128,1152]{1,0:T(8,128)(2,1)} %get-tuple-element.27), channel_id=1, source_target_pairs={{0,2},{1,3},{2,4},{3,5},{4,6},{5,7},{8,10},{9,11},{10,12},{11,13},... | collective-permute-start | bytes 884744 | tf_op jit(solution)/shard_map/ppermute | solution.py:560
  9.5 11.4 %collective-permute-start.1 = (bf16[128,1152]{1,0:T(8,128)(2,1)}, bf16[128,1152]{1,0:T(8,128)(2,1)S(1)}, u32[]{:S(2)}, u32[]{:S(2)}) collective-permute-start(bf16[128,1152]{1,0:T(8,128)(2,1)} %get-tuple-element.25.top_ref), channel_id=1, source_target_pairs={{2,0},{3,1},{4,2},{5,3},{6,4},{7,5},{10,8},{11,9},{12,10},{13,11},... | collective-permute-start | bytes 884744 | tf_op jit(solution)/shard_map/ppermute | solution.py:560
  10.8 5.6 %copy-start.1 = (bf16[1,32,16,1152]{3,2,1,0:T(8,128)(2,1)S(1)}, bf16[1,32,16,1152]{3,2,1,0:T(8,128)(2,1)}, u32[]{:S(2)}) copy-start(bf16[1,32,16,1152]{3,2,1,0:T(8,128)(2,1)} %param.4) | copy-start | bytes 3538948
  16.2 6.4 %collective-permute-start.2 = (bf16[256,1152]{1,0:T(8,128)(2,1)}, bf16[256,1152]{1,0:T(8,128)(2,1)}, u32[]{:S(2)}, u32[]{:S(2)}) collective-permute-start(bf16[256,1152]{1,0:T(8,128)(2,1)} %get-tuple-element.28), channel_id=1, source_target_pairs={{0,1},{1,0},{2,3},{3,2},{4,5},{5,4},{6,7},{7,6},{8,9},{9,8},{10,11... | collective-permute-start | bytes 1769480 | tf_op jit(solution)/shard_map/ppermute | solution.py:560
  20.1 1.4 %copy-start.9 = (bf16[1,32,16,1152]{3,2,1,0:T(8,128)(2,1)S(1)}, bf16[1,32,16,1152]{3,2,1,0:T(8,128)(2,1)}, u32[]{:S(2)}) copy-start(bf16[1,32,16,1152]{3,2,1,0:T(8,128)(2,1)} %param.7) | copy-start | bytes 3538948
  20.8 1.6 %copy-start.14 = (bf16[128,1152]{1,0:T(8,128)(2,1)}, bf16[128,1152]{1,0:T(8,128)(2,1)S(1)}, u32[]{:S(2)}) copy-start(bf16[128,1152]{1,0:T(8,128)(2,1)S(1)} %collective-permute-done.1.below_ref) | copy-start | bytes 884740
  20.9 1.7 %collective-permute-start.3 = (bf16[16,8,1152]{2,1,0:T(8,128)(2,1)S(1)}, bf16[16,8,1152]{2,1,0:T(8,128)(2,1)S(1)}, u32[]{:S(2)}, u32[]{:S(2)}) collective-permute-start(bf16[16,8,1152]{2,1,0:T(8,128)(2,1)S(1)} %pad_maximum_fusion.1), channel_id=1, source_target_pairs={{0,1},{1,0},{2,3},{3,2},{4,5},{5,4},{6,7},{7,6},{8,9},{9,8},{10,11... | collective-permute-start | bytes 884744 | tf_op jit(solution)/shard_map/ppermute | solution.py:560
  21.5 1.3 %copy-start.16 = (bf16[512,1152]{1,0:T(8,128)(2,1)S(1)}, bf16[512,1152]{1,0:T(8,128)(2,1)}, u32[]{:S(2)}) copy-start(bf16[512,1152]{1,0:T(8,128)(2,1)} %get-tuple-element.26.own_ref) | copy-start | bytes 3538948
  21.5 1.4 %copy-start.19 = (bf16[576,512]{1,0:T(8,128)(2,1)S(1)}, bf16[576,512]{1,0:T(8,128)(2,1)}, u32[]{:S(2)}) copy-start(bf16[576,512]{1,0:T(8,128)(2,1)} %fusion.2.qt_ref) | copy-start | bytes 1769476
  22.9 1.0 copy-start.15
  37.0 4.0 %copy-start.2 = (bf16[512,640]{1,0:T(8,128)(2,1)}, bf16[512,640]{1,0:T(8,128)(2,1)S(1)}, u32[]{:S(2)}) copy-start(bf16[512,640]{1,0:T(8,128)(2,1)S(1)} %get-tuple-element.29.refs_1_.dq_ref) | copy-start | bytes 1966084
  37.0 4.0 %copy-start.7 = (bf16[512,1152]{1,0:T(8,128)(2,1)}, bf16[512,1152]{1,0:T(8,128)(2,1)S(1)}, u32[]{:S(2)}) copy-start(bf16[512,1152]{1,0:T(8,128)(2,1)S(1)} %get-tuple-element.33.inner_ref) | copy-start | bytes 3538948
  37.0 4.0 %copy-start.12 = (bf16[256,1152]{1,0:T(8,128)(2,1)}, bf16[256,1152]{1,0:T(8,128)(2,1)S(1)}, u32[]{:S(2)}) copy-start(bf16[256,1152]{1,0:T(8,128)(2,1)S(1)} %get-tuple-element.35) | copy-start | bytes 1769476
  37.0 5.2 %collective-permute-start.6 = (bf16[384,1152]{1,0:T(8,128)(2,1)}, bf16[384,1152]{1,0:T(8,128)(2,1)}, u32[]{:S(2)}, u32[]{:S(2)}) collective-permute-start(bf16[384,1152]{1,0:T(8,128)(2,1)} %get-tuple-element.34), channel_id=1, source_target_pairs={{0,1},{1,0},{2,3},{3,2},{4,5},{5,4},{6,7},{7,6},{8,9},{9,8},{10,11... | collective-permute-start | bytes 2654216 | tf_op jit(solution)/shard_map/ppermute | solution.py:560
  41.0 1.1 copy-start.5
  42.1 3.4 %collective-permute-start.4 = (bf16[576,1152]{1,0:T(8,128)(2,1)}, bf16[576,1152]{1,0:T(8,128)(2,1)}, u32[]{:S(2)}, u32[]{:S(2)}) collective-permute-start(bf16[576,1152]{1,0:T(8,128)(2,1)} %get-tuple-element.32), channel_id=1, source_target_pairs={{0,1},{1,0},{2,3},{3,2},{4,5},{5,4},{6,7},{7,6},{8,9},{9,8},{10,11... | collective-permute-start | bytes 3981320 | tf_op jit(solution)/shard_map/ppermute | solution.py:504
  43.3 1.1 copy-start.13
  43.4 2.1 %copy-start.6 = (bf16[576,1152]{1,0:T(8,128)(2,1)S(1)}, bf16[576,1152]{1,0:T(8,128)(2,1)}, u32[]{:S(2)}) copy-start(bf16[576,1152]{1,0:T(8,128)(2,1)} %copy-done.5) | copy-start | bytes 3981316
  47.2 3.5 %copy-start.21 = (bf16[576,1152]{1,0:T(8,128)(2,1)}, bf16[576,1152]{1,0:T(8,128)(2,1)S(1)}, u32[]{:S(2)}) copy-start(bf16[576,1152]{1,0:T(8,128)(2,1)S(1)} %add_convert_fusion.1) | copy-start | bytes 3981316
  47.2 16.3 %copy-start.8 = (bf16[512,1152]{1,0:T(8,128)(2,1)S(1)}, bf16[512,1152]{1,0:T(8,128)(2,1)}, u32[]{:S(2)}) copy-start(bf16[512,1152]{1,0:T(8,128)(2,1)} %copy-done.7) | copy-start | bytes 3538948
  48.2 15.3 %collective-permute-start.5 = (bf16[4,40,1152]{2,1,0:T(8,128)(2,1)S(1)}, bf16[4,40,1152]{2,1,0:T(8,128)(2,1)S(1)}, u32[]{:S(2)}, u32[]{:S(2)}) collective-permute-start(bf16[4,40,1152]{2,1,0:T(8,128)(2,1)S(1)} %get-tuple-element.54), channel_id=1, source_target_pairs={{0,24},{8,16},{16,8},{24,0},{1,25},{9,17},{17,9},{25,1},{2,26},{10... | collective-permute-start | bytes 1105928 | tf_op jit(solution)/shard_map/ppermute | solution.py:475
  50.7 11.6 %collective-permute-start.8 = (bf16[128,1152]{1,0:T(8,128)(2,1)S(1)}, bf16[128,1152]{1,0:T(8,128)(2,1)S(1)}, u32[]{:S(2)}, u32[]{:S(2)}) collective-permute-start(bf16[128,1152]{1,0:T(8,128)(2,1)S(1)} %get-tuple-element.57), channel_id=1, source_target_pairs={{2,0},{3,1},{4,2},{5,3},{6,4},{7,5},{10,8},{11,9},{12,10},{13,11},... | collective-permute-start | bytes 884744 | tf_op jit(solution)/shard_map/ppermute | solution.py:560
  52.0 11.5 %collective-permute-start.7 = (bf16[128,1152]{1,0:T(8,128)(2,1)S(1)}, bf16[128,1152]{1,0:T(8,128)(2,1)S(1)}, u32[]{:S(2)}, u32[]{:S(2)}) collective-permute-start(bf16[128,1152]{1,0:T(8,128)(2,1)S(1)} %get-tuple-element.58), channel_id=1, source_target_pairs={{0,2},{1,3},{2,4},{3,5},{4,6},{5,7},{8,10},{9,11},{10,12},{11,13},... | collective-permute-start | bytes 884744 | tf_op jit(solution)/shard_map/ppermute | solution.py:560
  67.7 1.1 copy-start.4
  68.7 1.0 copy-start.10
  69.8 0.8 copy-start.17
  70.6 3.4 %collective-permute-start.11 = (bf16[576,1152]{1,0:T(8,128)(2,1)}, bf16[576,1152]{1,0:T(8,128)(2,1)}, u32[]{:S(2)}, u32[]{:S(2)}) collective-permute-start(bf16[576,1152]{1,0:T(8,128)(2,1)} %get-tuple-element.39), channel_id=1, source_target_pairs={{0,1},{1,0},{2,3},{3,2},{4,5},{5,4},{6,7},{7,6},{8,9},{9,8},{10,11... | collective-permute-start | bytes 3981320 | tf_op jit(solution)/shard_map/ppermute | solution.py:504
  70.6 11.6 %collective-permute-start.9 = (bf16[4,40,1152]{2,1,0:T(8,128)(2,1)}, bf16[4,40,1152]{2,1,0:T(8,128)(2,1)S(1)}, u32[]{:S(2)}, u32[]{:S(2)}) collective-permute-start(bf16[4,40,1152]{2,1,0:T(8,128)(2,1)} %get-tuple-element.52), channel_id=1, source_target_pairs={{0,8},{8,0},{16,24},{24,16},{1,9},{9,1},{17,25},{25,17},{2,10},{10... | collective-permute-start | bytes 1105928 | tf_op jit(solution)/shard_map/ppermute | solution.py:475
  71.1 18.8 %collective-permute-start.10 = (bf16[4,40,1152]{2,1,0:T(8,128)(2,1)}, bf16[4,40,1152]{2,1,0:T(8,128)(2,1)S(1)}, u32[]{:S(2)}, u32[]{:S(2)}) collective-permute-start(bf16[4,40,1152]{2,1,0:T(8,128)(2,1)} %get-tuple-element.53), channel_id=1, source_target_pairs={{0,16},{8,24},{16,0},{24,8},{1,17},{9,25},{17,1},{25,9},{2,18},{10... | collective-permute-start | bytes 1105928 | tf_op jit(solution)/shard_map/ppermute | solution.py:475
  76.0 13.9 %copy-start.22 = (bf16[576,1152]{1,0:T(8,128)(2,1)S(1)}, bf16[576,1152]{1,0:T(8,128)(2,1)}, u32[]{:S(2)}) copy-start(bf16[576,1152]{1,0:T(8,128)(2,1)} %copy-done.21) | copy-start | bytes 3981316
  76.3 13.9 %copy-start.18 = (bf16[512,576]{1,0:T(8,128)(2,1)S(1)}, bf16[512,576]{1,0:T(8,128)(2,1)}, u32[]{:S(2)}) copy-start(bf16[512,576]{1,0:T(8,128)(2,1)} %copy-done.17) | copy-start | bytes 1769476
  76.3 18.1 %collective-permute-start.12 = (bf16[4,40,1152]{2,1,0:T(8,128)(2,1)S(1)}, bf16[4,40,1152]{2,1,0:T(8,128)(2,1)S(1)}, u32[]{:S(2)}, u32[]{:S(2)}) collective-permute-start(bf16[4,40,1152]{2,1,0:T(8,128)(2,1)S(1)} %get-tuple-element.51), channel_id=1, source_target_pairs={{0,24},{8,16},{16,8},{24,0},{1,25},{9,17},{17,9},{25,1},{2,26},{10... | collective-permute-start | bytes 1105928 | tf_op jit(solution)/shard_map/ppermute | solution.py:475
  90.2 4.2 %copy-start.3 = (bf16[512,640]{1,0:T(8,128)(2,1)S(1)}, bf16[512,640]{1,0:T(8,128)(2,1)}, u32[]{:S(2)}) copy-start(bf16[512,640]{1,0:T(8,128)(2,1)} %copy-done.2) | copy-start | bytes 1966084
  90.2 4.2 %copy-start.11 = (bf16[512,1152]{1,0:T(8,128)(2,1)S(1)}, bf16[512,1152]{1,0:T(8,128)(2,1)}, u32[]{:S(2)}) copy-start(bf16[512,1152]{1,0:T(8,128)(2,1)} %copy-done.10) | copy-start | bytes 3538948
  90.2 9.9 %copy-start.20 = (bf16[1152,1728]{0,1:T(8,128)(2,1)S(1)}, bf16[1152,1728]{0,1:T(8,128)(2,1)}, u32[]{:S(2)}) copy-start(bf16[1152,1728]{0,1:T(8,128)(2,1)} %param.5) | copy-start | bytes 11943940
  92.4 11.3 %collective-permute-start.19 = (bf16[4,40,1152]{2,1,0:T(8,128)(2,1)S(1)}, bf16[4,40,1152]{2,1,0:T(8,128)(2,1)S(1)}, u32[]{:S(2)}, u32[]{:S(2)}) collective-permute-start(bf16[4,40,1152]{2,1,0:T(8,128)(2,1)S(1)} %get-tuple-element.49), channel_id=1, source_target_pairs={{0,8},{8,0},{16,24},{24,16},{1,9},{9,1},{17,25},{25,17},{2,10},{10... | collective-permute-start | bytes 1105928 | tf_op jit(solution)/shard_map/ppermute | solution.py:475
  93.9 9.8 %collective-permute-start.20 = (bf16[4,40,1152]{2,1,0:T(8,128)(2,1)S(1)}, bf16[4,40,1152]{2,1,0:T(8,128)(2,1)S(1)}, u32[]{:S(2)}, u32[]{:S(2)}) collective-permute-start(bf16[4,40,1152]{2,1,0:T(8,128)(2,1)S(1)} %get-tuple-element.50), channel_id=1, source_target_pairs={{0,16},{8,24},{16,0},{24,8},{1,17},{9,25},{17,1},{25,9},{2,18},{10... | collective-permute-start | bytes 1105928 | tf_op jit(solution)/shard_map/ppermute | solution.py:475
  94.8 11.5 %collective-permute-start.13 = (bf16[40,1152]{1,0:T(8,128)(2,1)S(1)}, bf16[40,1152]{1,0:T(8,128)(2,1)S(1)}, u32[]{:S(2)}, u32[]{:S(2)}) collective-permute-start(bf16[40,1152]{1,0:T(8,128)(2,1)S(1)} %get-tuple-element.42), channel_id=1, source_target_pairs={{0,2},{2,0},{4,6},{6,4},{1,3},{3,1},{5,7},{7,5},{8,10},{10,8},{12,... | collective-permute-start | bytes 276488 | tf_op jit(solution)/shard_map/ppermute | solution.py:475
  97.4 9.0 %collective-permute-start.14 = (bf16[40,1152]{1,0:T(8,128)(2,1)S(1)}, bf16[40,1152]{1,0:T(8,128)(2,1)S(1)}, u32[]{:S(2)}, u32[]{:S(2)}) collective-permute-start(bf16[40,1152]{1,0:T(8,128)(2,1)S(1)} %get-tuple-element.43), channel_id=1, source_target_pairs={{0,4},{2,6},{4,0},{6,2},{1,5},{3,7},{5,1},{7,3},{8,12},{10,14},{12... | collective-permute-start | bytes 276488 | tf_op jit(solution)/shard_map/ppermute | solution.py:475
  100.1 6.5 %collective-permute-start.15 = (bf16[40,1152]{1,0:T(8,128)(2,1)S(1)}, bf16[40,1152]{1,0:T(8,128)(2,1)S(1)}, u32[]{:S(2)}, u32[]{:S(2)}) collective-permute-start(bf16[40,1152]{1,0:T(8,128)(2,1)S(1)} %get-tuple-element.44), channel_id=1, source_target_pairs={{0,6},{2,4},{4,2},{6,0},{1,7},{3,5},{5,3},{7,1},{8,14},{10,12},{12... | collective-permute-start | bytes 276488 | tf_op jit(solution)/shard_map/ppermute | solution.py:475
  103.9 6.4 %collective-permute-start.21 = (bf16[2,40,1152]{2,1,0:T(8,128)(2,1)S(1)}, bf16[2,40,1152]{2,1,0:T(8,128)(2,1)S(1)}, u32[]{:S(2)}, u32[]{:S(2)}) collective-permute-start(bf16[2,40,1152]{2,1,0:T(8,128)(2,1)S(1)} %dynamic-slice_bitcast_fusion), channel_id=1, source_target_pairs={{0,2},{2,0},{4,6},{6,4},{1,3},{3,1},{5,7},{7,5},{8,10},{10,8},{12,... | collective-permute-start | bytes 552968 | tf_op jit(solution)/shard_map/ppermute | solution.py:524
  106.7 6.8 %collective-permute-start.17 = (bf16[40,1152]{1,0:T(8,128)(2,1)S(1)}, bf16[40,1152]{1,0:T(8,128)(2,1)S(1)}, u32[]{:S(2)}, u32[]{:S(2)}) collective-permute-start(bf16[40,1152]{1,0:T(8,128)(2,1)S(1)} %get-tuple-element.47), channel_id=1, source_target_pairs={{0,16},{8,24},{16,0},{24,8},{1,17},{9,25},{17,1},{25,9},{2,18},{10... | collective-permute-start | bytes 276488 | tf_op jit(solution)/shard_map/ppermute | solution.py:494
  108.3 5.2 %collective-permute-start.16 = (bf16[40,1152]{1,0:T(8,128)(2,1)S(1)}, bf16[40,1152]{1,0:T(8,128)(2,1)S(1)}, u32[]{:S(2)}, u32[]{:S(2)}) collective-permute-start(bf16[40,1152]{1,0:T(8,128)(2,1)S(1)} %get-tuple-element.47), channel_id=1, source_target_pairs={{0,8},{8,0},{16,24},{24,16},{1,9},{9,1},{17,25},{25,17},{2,10},{10... | collective-permute-start | bytes 276488 | tf_op jit(solution)/shard_map/ppermute | solution.py:494
  108.8 14.7 %collective-permute-start.18 = (bf16[40,1152]{1,0:T(8,128)(2,1)S(1)}, bf16[40,1152]{1,0:T(8,128)(2,1)S(1)}, u32[]{:S(2)}, u32[]{:S(2)}) collective-permute-start(bf16[40,1152]{1,0:T(8,128)(2,1)S(1)} %get-tuple-element.47), channel_id=1, source_target_pairs={{0,24},{8,16},{16,8},{24,0},{1,25},{9,17},{17,9},{25,1},{2,26},{10... | collective-permute-start | bytes 276488 | tf_op jit(solution)/shard_map/ppermute | solution.py:494
  110.4 5.6 %collective-permute-start.22 = (bf16[1,40,1152]{2,1,0:T(8,128)(2,1)S(1)}, bf16[1,40,1152]{2,1,0:T(8,128)(2,1)S(1)}, u32[]{:S(2)}, u32[]{:S(2)}) collective-permute-start(bf16[1,40,1152]{2,1,0:T(8,128)(2,1)S(1)} %constant_dynamic-slice_fusion), channel_id=1, source_target_pairs={{0,4},{2,6},{4,0},{6,2},{1,5},{3,7},{5,1},{7,3},{8,12},{10,14},{12... | collective-permute-start | bytes 276488 | tf_op jit(solution)/shard_map/ppermute | solution.py:524
  116.0 7.5 %collective-permute-start.25 = (bf16[40,1152]{1,0:T(8,128)(2,1)S(1)}, bf16[40,1152]{1,0:T(8,128)(2,1)S(1)}, u32[]{:S(2)}, u32[]{:S(2)}) collective-permute-start(bf16[40,1152]{1,0:T(8,128)(2,1)S(1)} %fusion.11), channel_id=1, source_target_pairs={{0,24},{8,16},{16,8},{24,0},{1,25},{9,17},{17,9},{25,1},{2,26},{10... | collective-permute-start | bytes 276488 | tf_op jit(solution)/shard_map/ppermute | solution.py:494
  118.4 5.1 %collective-permute-start.24 = (bf16[40,1152]{1,0:T(8,128)(2,1)S(1)}, bf16[40,1152]{1,0:T(8,128)(2,1)S(1)}, u32[]{:S(2)}, u32[]{:S(2)}) collective-permute-start(bf16[40,1152]{1,0:T(8,128)(2,1)S(1)} %fusion.11), channel_id=1, source_target_pairs={{0,16},{8,24},{16,0},{24,8},{1,17},{9,25},{17,1},{25,9},{2,18},{10... | collective-permute-start | bytes 276488 | tf_op jit(solution)/shard_map/ppermute | solution.py:494
  118.6 4.9 %collective-permute-start.23 = (bf16[40,1152]{1,0:T(8,128)(2,1)S(1)}, bf16[40,1152]{1,0:T(8,128)(2,1)S(1)}, u32[]{:S(2)}, u32[]{:S(2)}) collective-permute-start(bf16[40,1152]{1,0:T(8,128)(2,1)S(1)} %fusion.11), channel_id=1, source_target_pairs={{0,8},{8,0},{16,24},{24,16},{1,9},{9,1},{17,25},{25,17},{2,10},{10... | collective-permute-start | bytes 276488 | tf_op jit(solution)/shard_map/ppermute | solution.py:494

commit v8 on v7

--- a/solution.py
+++ b/solution.py
@@ -66,8 +66,11 @@
         bottom_ref[:, lanes] = part[edge:]
 
 
-def project_kernel(own_ref, top_ref, tokens_ref, weight_ref, kv_ref, near_ref, tokens, weight, sems):
-    copies = fetch([(tokens_ref, tokens)] + weight_pieces(weight_ref, weight), sems)
+def project_kernel(
+    own_ref, top_ref, tokens_ref, weight_ref, qt_ref, kv_ref, near_ref, tokens, weight, q_weight, sems
+):
+    pairs = [(tokens_ref, tokens)] + weight_pieces(weight_ref, weight)
+    copies = fetch(pairs + [(weight_ref.at[pl.ds(0, INNER)], q_weight)], sems)
     copies[0].wait()
     for p in range(PIECES):
         copies[1 + p].wait()
@@ -78,6 +81,8 @@
         is_right = own_ref[0].astype(jnp.float32)
         near = grid[:, :REACH] * is_right + grid[:, -REACH:] * (1.0 - is_right)
         near_ref[:, lanes] = near.reshape(-1, PIECE).astype(jnp.bfloat16)
+    copies[1 + PIECES].wait()
+    qt_ref[...] = nt_dot(q_weight[...], tokens[...]).astype(jnp.bfloat16)
 
 
 def project(token_rows, weight, tile_cols):
@@ -87,36 +92,39 @@
     shape = lambda count: jax.ShapeDtypeStruct((count, 2 * INNER), jnp.bfloat16)
     block = lambda count: pl.BlockSpec((count, 2 * INNER), lambda _: (0, 0))
     anywhere = pl.BlockSpec(memory_space=pl.ANY)
-    params = pltpu.CompilerParams(vmem_limit_bytes=56 * 1024 * 1024)
-    scratch = lambda count, copies: [
-        pltpu.VMEM((count, width), jnp.bfloat16),
-        pltpu.VMEM((2 * INNER, width), jnp.bfloat16),
-        pltpu.SemaphoreType.DMA((copies,)),
-    ]
     top, bottom = pl.pallas_call(
         edges_kernel,
         grid=(1,),
         out_shape=[shape(edge)] * 2,
         in_specs=[anywhere] * 2,
         out_specs=[block(edge)] * 2,
-        scratch_shapes=scratch(2 * edge, PIECES + 2),
-        compiler_params=params,
+        scratch_shapes=[
+            pltpu.VMEM((2 * edge, width), jnp.bfloat16),
+            pltpu.VMEM((2 * INNER, width), jnp.bfloat16),
+            pltpu.SemaphoreType.DMA((PIECES + 2,)),
+        ],
+        compiler_params=pltpu.CompilerParams(vmem_limit_bytes=56 * 1024 * 1024),
         cost_estimate=LIGHT,
         name="project_edges",
     )(token_rows, weight.T)
     near = rows // tile_cols * REACH
-    keyvals, near = pl.pallas_call(
+    queries, keyvals, near = pl.pallas_call(
         project_kernel,
         grid=(1,),
-        out_shape=[shape(rows), shape(near)],
+        out_shape=[jax.ShapeDtypeStruct((INNER, rows), jnp.bfloat16), shape(rows), shape(near)],
         in_specs=[pl.BlockSpec(memory_space=pltpu.SMEM)] + [anywhere] * 3,
-        out_specs=[block(rows), block(near)],
-        scratch_shapes=scratch(rows, PIECES + 1),
-        compiler_params=params,
+        out_specs=[pl.BlockSpec((INNER, rows), lambda _: (0, 0)), block(rows), block(near)],
+        scratch_shapes=[
+            pltpu.VMEM((rows, width), jnp.bfloat16),
+            pltpu.VMEM((2 * INNER, width), jnp.bfloat16),
+            pltpu.VMEM((INNER, width), jnp.bfloat16),
+            pltpu.SemaphoreType.DMA((PIECES + 2,)),
+        ],
+        compiler_params=pltpu.CompilerParams(vmem_limit_bytes=24 * 1024 * 1024),
         cost_estimate=LIGHT,
         name="project",
     )(own, top, token_rows, weight.T)
-    return keyvals, top, bottom, near
+    return queries, keyvals, top, bottom, near
 
 
 def attention_kernel(
@@ -134,6 +142,7 @@
     inner_ref,
     edge_ref,
     side_ref,
+    corner_grad_ref,
     kv,
     kvt,
     acc,
@@ -254,9 +263,12 @@
             inner_ref[chunk_own * at : chunk_own * (at + 1), :] = own_grad
         else:
             edge_ref[chunk_own * (at - strips) : chunk_own * (at - strips + 1), :] = own_grad
-        side_ref[chunk_side * at : chunk_side * (at + 1), :] = acc[slot, chunk_own:].astype(
-            jnp.bfloat16
-        )
+        side_grad = acc[slot, chunk_own:].astype(jnp.bfloat16)
+        if at < strips:
+            side_ref[chunk_side * at : chunk_side * (at + 1), :] = side_grad
+        else:
+            at -= strips
+            corner_grad_ref[chunk_side * at : chunk_side * (at + 1), :] = side_grad
 
 
 def attention(start, queries, own, grads, above, below, cols, corner, bias):
@@ -269,7 +281,8 @@
         jax.ShapeDtypeStruct((token_count, INNER + 64), jnp.bfloat16),
         jax.ShapeDtypeStruct(own.shape, jnp.bfloat16),
         jax.ShapeDtypeStruct((2 * chunk_own, width), jnp.bfloat16),
-        jax.ShapeDtypeStruct((cols.shape[0] + corner.shape[0], width), jnp.bfloat16),
+        jax.ShapeDtypeStruct(cols.shape, jnp.bfloat16),
+        jax.ShapeDtypeStruct(corner.shape, jnp.bfloat16),
     )
     return pl.pallas_call(
         attention_kernel,
@@ -346,8 +359,8 @@
 
 
 def late_kernel(
-    own_ref, earlier_ref, tokens_ref, inner_ref, side_ref, above_ref, below_ref,
-    o_ref, sent_ref, kept_ref, grad_ref, att_ref, turned,
+    own_ref, first, second, third, tokens_ref, inner_ref, side_ref, above_ref, below_ref,
+    dq_ref, o_ref, sent_ref, kept_ref, all_ref, att_ref, turned, grad_ref,
 ):
     own = own_ref[0]
     count = inner_ref.shape[0]
@@ -370,59 +383,89 @@
         ]
         product = dot(jnp.concatenate(picked, axis=0), grad_ref[...])
         out_ref[...] = product.astype(jnp.bfloat16)
+    all_ref[...] = jnp.concatenate([dq_ref[:, :INNER], grad_ref[...]], axis=1)
     att_ref[...] = o_ref[:, 64:]
 
 
-def late_halves(earlier, token_rows, inner, side, above, below, attended):
+def late_halves(earlier, token_rows, inner, side, above, below, dquery, attended):
     rows, width = token_rows.shape
     whole = lambda a: pl.BlockSpec(a.shape, lambda _: (0,) * a.ndim)
     out = jax.ShapeDtypeStruct((width // 2, 2 * INNER), jnp.bfloat16)
-    grads = jax.ShapeDtypeStruct((rows, 2 * INNER), jnp.bfloat16)
+    grads = jax.ShapeDtypeStruct((rows, 3 * INNER), jnp.bfloat16)
     att = jax.ShapeDtypeStruct((rows, INNER), jnp.bfloat16)
-    operands = (token_rows, inner, side, above, below, attended)
+    operands = (token_rows, inner, side, above, below, dquery, attended)
     own = lax.axis_index("col").astype(jnp.int32).reshape(1)
     return pl.pallas_call(
         late_kernel,
         grid=(1,),
         out_shape=(out, out, grads, att),
         in_specs=[pl.BlockSpec(memory_space=pltpu.SMEM)]
-        + [pl.BlockSpec(memory_space=pl.ANY)]
+        + [pl.BlockSpec(memory_space=pl.ANY)] * 3
         + [whole(a) for a in operands],
         out_specs=(whole(out), whole(out), whole(grads), whole(att)),
-        scratch_shapes=[pltpu.VMEM((width, rows), jnp.bfloat16)],
+        scratch_shapes=[
+            pltpu.VMEM((width, rows), jnp.bfloat16),
+            pltpu.VMEM((rows, 2 * INNER), jnp.bfloat16),
+        ],
         compiler_params=pltpu.CompilerParams(vmem_limit_bytes=22 * 1024 * 1024),
         cost_estimate=LIGHT,
         name="late_weight_grad_halves",
-    )(own, earlier, *operands)
-
-
-def row_parts_kernel(own_ref, held, dq_ref, dkv_ref, *refs):
-    for step, out in enumerate(refs[-5:-1]):
-        out[...] = held[own_ref[0] ^ step]
-    refs[-1][...] = jnp.concatenate([dq_ref[:, :INNER], dkv_ref[...]], axis=1)
-
-
-def row_parts(held, dquery, dkv, *earlier):
-    rows, small, width = held.shape
-    own = lax.axis_index("row").astype(jnp.int32).reshape(1)
+    )(own, *earlier, *operands)
+
+
+def core_parts_kernel(own_ref, kept_ref, got_ref, *refs):
+    outs, total = refs[-5:-1], refs[-1]
+    rows, padded, _ = total.shape
+    share, small = kept_ref.shape[0] // rows, padded // 4
+    for r in range(rows):
+        part = slice(share * r, share * (r + 1))
+        total[r, :share] = kept_ref[part].astype(jnp.float32) + got_ref[part].astype(jnp.float32)
+        total[r, share:] = jnp.zeros((padded - share, total.shape[2]), jnp.float32)
+    for step, out in enumerate(outs):
+        first = pl.multiple_of((own_ref[0] ^ step) * small, 8)
+        out[...] = total[:, pl.ds(first, small), :].astype(jnp.bfloat16)
+
+
+def core_parts(sent, kept, *earlier):
+    got = lax.ppermute(sent, "col", [(0, 1), (1, 0)])
+    rows, images = lax.axis_size("row"), lax.axis_size("img")
+    width = kept.shape[1]
+    small = -(-kept.shape[0] // rows // (8 * images)) * 8
+    own = lax.axis_index("img").astype(jnp.int32).reshape(1)
     return pl.pallas_call(
-        row_parts_kernel,
+        core_parts_kernel,
         grid=(1,),
-        out_shape=[jax.ShapeDtypeStruct((small, width), jnp.bfloat16)] * 4
-        + [jax.ShapeDtypeStruct((dkv.shape[0], 3 * INNER), jnp.bfloat16)],
-        in_specs=[
-            pl.BlockSpec(memory_space=pltpu.SMEM),
-            pl.BlockSpec((rows, small, width), lambda _: (0, 0, 0)),
-            pl.BlockSpec(dquery.shape, lambda _: (0, 0)),
-            pl.BlockSpec(dkv.shape, lambda _: (0, 0)),
-        ]
+        out_shape=[jax.ShapeDtypeStruct((rows, small, width), jnp.bfloat16)] * images,
+        in_specs=[pl.BlockSpec(memory_space=pltpu.SMEM)]
+        + [pl.BlockSpec(kept.shape, lambda _: (0, 0))] * 2
         + [pl.BlockSpec(memory_space=pl.ANY)] * len(earlier),
-        out_specs=[pl.BlockSpec((small, width), lambda _: (0, 0))] * 4
-        + [pl.BlockSpec((dkv.shape[0], 3 * INNER), lambda _: (0, 0))],
-        compiler_params=pltpu.CompilerParams(vmem_limit_bytes=16 * 1024 * 1024),
+        out_specs=[pl.BlockSpec((rows, small, width), lambda _: (0, 0, 0))] * images,
+        scratch_shapes=[pltpu.VMEM((rows, images * small, width), jnp.float32)],
+        compiler_params=pltpu.CompilerParams(vmem_limit_bytes=20 * 1024 * 1024),
         cost_estimate=LIGHT,
-        name="row_parts",
-    )(own, held, dquery, dkv, *earlier)
+        name="core_parts",
+    )(own, kept, got, *earlier)
+
+
+def row_sum_kernel(kept, first, second, third, *refs):
+    total = kept[...].astype(jnp.float32) + first[...].astype(jnp.float32)
+    total += second[...].astype(jnp.float32)
+    refs[-1][...] = (total + third[...].astype(jnp.float32)).astype(jnp.bfloat16)
+
+
+def row_sum_after(parts, earlier):
+    parts = [parts[0]] + exchanged(parts, "row")
+    shape = parts[0].shape
+    return pl.pallas_call(
+        row_sum_kernel,
+        grid=(1,),
+        out_shape=jax.ShapeDtypeStruct(shape, jnp.bfloat16),
+        in_specs=[pl.BlockSpec(shape, lambda _: (0, 0))] * 4 + [pl.BlockSpec(memory_space=pl.ANY)],
+        out_specs=pl.BlockSpec(shape, lambda _: (0, 0)),
+        compiler_params=pltpu.CompilerParams(vmem_limit_bytes=8 * 1024 * 1024),
+        cost_estimate=LIGHT,
+        name="row_sum",
+    )(*parts, earlier)
 
 
 def window_starts(places, extent):
@@ -496,36 +539,8 @@
     return whole
 
 
-def core_sum(sent, kept):
-    rows, images = lax.axis_size("row"), lax.axis_size("img")
-    width = sent.shape[1]
-    share = sent.shape[0] // rows
-    kept = kept.reshape(rows, share, width)
-    got = lax.ppermute(sent, "col", [(0, 1), (1, 0)]).reshape(rows, share, width)
-    held = (kept.astype(jnp.float32) + got.astype(jnp.float32)).astype(jnp.bfloat16)
-    small = -(-share // (8 * images)) * 8
-    return jnp.pad(held, ((0, 0), (0, images * small - share), (0, 0)))
-
-
-def image_parts(held):
-    small = held.shape[1] // lax.axis_size("img")
-    return cut(held, "img", lambda h, j: lax.dynamic_slice_in_dim(h, small * j, small, 1))
-
-
-def row_sum_in_steps(held):
-    own = lax.axis_index("row")
-    count = lax.axis_size("row")
-    bit = 1
-    while bit < count:
-        parts = held.reshape((-1, 2) + held.shape[1:])
-        mine = (own // bit) % 2
-        kept = lax.dynamic_index_in_dim(parts, mine, 1, keepdims=False)
-        sent = lax.dynamic_index_in_dim(parts, 1 - mine, 1, keepdims=False)
-        got = lax.ppermute(sent, "row", [(i, i ^ bit) for i in range(count)])
-        total = kept.astype(jnp.float32) + got.astype(jnp.float32)
-        held = total.astype(jnp.bfloat16)
-        bit *= 2
-    return held[0]
+def row_parts(held):
+    return cut(held, "row", lambda h, r: lax.dynamic_index_in_dim(h, r, 0, keepdims=False))
 
 
 def whole_share(held, share):
@@ -573,10 +588,7 @@
         got = got[0] if two_columns else jnp.concatenate(got, axis=1)
         return got.reshape(-1, 2 * INNER)
 
-    keyvals, top, bottom, near = project(token_rows, qkv_weight, tile_cols)
-    queries = lax.dot_general(
-        qkv_weight[:, :INNER], token_rows, (((0,), (1,)), ((), ())), preferred_element_type=jnp.float32
-    ).astype(jnp.bfloat16)
+    queries, keyvals, top, bottom, near = project(token_rows, qkv_weight, tile_cols)
     above = moved(bottom, 1)
     below = moved(top, -1)
     if two_columns:
@@ -588,7 +600,7 @@
         out_weight, grad_rows, (((0,), (1,)), ((), ())), preferred_element_type=jnp.float32
     ).astype(jnp.bfloat16)
     start, bias = window_bias(tile_rows, tile_cols, two_columns)
-    attended, dquery, inner_grad, edge_grad, side_grad = attention(
+    attended, dquery, inner_grad, edge_grad, side_grad, corner_grad = attention(
         start, queries, keyvals, grad_att, above, below, cols, corner, bias
     )
 
@@ -599,55 +611,60 @@
 
     simple = two_columns and row_count == 4 and lax.axis_size("img") == 4
     if simple:
-        early = image_parts(core_sum(*outer_halves(token_rows, dquery, grad_rows, attended)))
-        early_got = exchanged(early, "img")
+        early = core_parts(*outer_halves(token_rows, dquery, grad_rows, attended))
+    def outputs(attended, dqkv):
+        sublayer_out = nt_dot(attended, out_weight).astype(jnp.bfloat16)
+        return sublayer_out, nt_dot(dqkv, qkv_weight).astype(jnp.bfloat16)
+
     def spread(side, first):
         side = side.reshape(-1, SIDE, REACH, 2 * INNER).astype(jnp.float32)
         zeros = jnp.zeros((side.shape[0], SIDE, tile_cols - REACH, 2 * INNER), jnp.float32)
         order = [side, zeros] if first else [zeros, side]
         return jnp.concatenate(order, axis=2).reshape(-1, 2 * INNER)
 
-    if two_columns:
-        got = moved(side_grad, 0, 0)
-        returned = lambda part: jnp.where(col_id == 0, spread(part, False), spread(part, True))
-    else:
-        halves = side_grad.reshape(strips + 2, 2, SIDE * REACH, 2 * INNER)
-        got = jnp.stack([moved(halves[:, 0], 0, -1), moved(halves[:, 1], 0, 1)], axis=1)
-        returned = lambda part: spread(part[:, 0], False) + spread(part[:, 1], True)
-    got = got.reshape(strips + 2, -1, SIDE * REACH, 2 * INNER)
-    outer_grad = edge_grad.astype(jnp.float32) + returned(got[strips:])
+    def sides_back(part):
+        if two_columns:
+            return moved(part, 0, 0).reshape(-1, SIDE * REACH, 2 * INNER)
+        halves = part.reshape(-1, 2, SIDE * REACH, 2 * INNER)
+        return jnp.stack([moved(halves[:, 0], 0, -1), moved(halves[:, 1], 0, 1)], axis=1)
+
+    def returned(part):
+        if two_columns:
+            return jnp.where(col_id == 0, spread(part, False), spread(part, True))
+        return spread(part[:, 0], False) + spread(part[:, 1], True)
+
+    side, corner = sides_back(side_grad), sides_back(corner_grad)
+    outer_grad = edge_grad.astype(jnp.float32) + returned(corner)
     outer_grad = outer_grad.astype(jnp.bfloat16)
     from_below = moved(outer_grad[:chunk_own], -1)
     from_above = moved(outer_grad[chunk_own:], 1)
     if simple:
-        side = got.reshape(-1, 2 * INNER)
-        sent, kept, dkv, attended = late_halves(
-            early_got[-1], token_rows, inner_grad, side, from_above, from_below, attended
+        side = side.reshape(-1, 2 * INNER)
+        sent, kept, dqkv, attended = late_halves(
+            early[1:], token_rows, inner_grad, side, from_above, from_below, dquery, attended
         )
     else:
         dquery, attended = dquery[:, :INNER], attended[:, 64:]
-        dkv = inner_grad.astype(jnp.float32) + returned(got[:strips])
+        dkv = inner_grad.astype(jnp.float32) + returned(side)
         rest = jnp.zeros((token_count - chunk_own, 2 * INNER), jnp.float32)
         dkv = dkv + jnp.concatenate([from_above.astype(jnp.float32), rest], axis=0)
         dkv = dkv + jnp.concatenate([rest, from_below.astype(jnp.float32)], axis=0)
         dkv = dkv.astype(jnp.bfloat16)
         dqkv = jnp.concatenate([dquery, dkv], axis=1)
-        sublayer_out = nt_dot(attended, out_weight).astype(jnp.bfloat16)
+        sublayer_out, tokens_grad = outputs(attended, dqkv)
     if simple:
-        late = image_parts(core_sum(sent, kept))
-        late_got = exchanged(late, "img")
-        early = added(early[0], early_got)
-        late = added(late[0], late_got, early)
-        sublayer_out = nt_dot(attended, out_weight).astype(jnp.bfloat16)
-        *early, dqkv = row_parts(early, dquery, dkv, late_got[-1])
-        early = added(early[0], exchanged(early, "row"))
-        late = row_sum_in_steps(late)
+        early = added(early[0], exchanged(early, "img"))
+        sublayer_out, tokens_grad = outputs(attended, dqkv)
+        late = core_parts(sent, kept, early, sublayer_out, tokens_grad)
+        late = added(late[0], exchanged(late, "img"), early)
+        early = row_sum_after(row_parts(early), late)
+        late = row_parts(late)
+        late = added(late[0], exchanged(late, "row"), early)
         share = width // (row_count * col_count)
         early, late = whole_share(early, share), whole_share(late, share)
     else:
         early = jnp.concatenate([outer(token_rows, dquery), outer(grad_rows, attended)], axis=1)
         early, late = plain_shares(early), plain_shares(outer(token_rows, dkv))
-    tokens_grad = nt_dot(dqkv, qkv_weight).astype(jnp.bfloat16)
     return (
         sublayer_out.reshape(tokens.shape),
         tokens_grad.reshape(tokens.shape),

time: 126 us -> 118 us (0.937)
  waiting for transfers between devices: 29.1 us -> 23.8 us
  matrix products: 9.8 us -> 4.67 us
  other arithmetic: 6.72 us -> 3.88 us
  starting transfers between devices: 38.3 us -> 40.9 us
  Pallas kernels: 30.7 us -> 32.1 us
    ppermute x9 -> x12, starting transfers between devices: 11.4 us -> 19.9 us  [exchanged(): got.append(lax.ppermute(part, axis, pairs))]
    ppermute x4 -> x2, waiting for transfers between devices: 5.91 us -> 0.01 us  [core_parts(): got = lax.ppermute(sent, 'col', [(0, 1), (1, 0)])]
    ppermute x4 -> x2, starting transfers between devices: 5.59 us -> 0.08 us  [core_parts(): got = lax.ppermute(sent, 'col', [(0, 1), (1, 0)])]
    ppermute x9 -> x12, waiting for transfers between devices: 13.4 us -> 17.2 us  [exchanged(): got.append(lax.ppermute(part, axis, pairs))]
    convert_element_type x3 -> x0, other arithmetic: 3.74 us -> none  [the longest x2 3.69 us: core_sum(): (kept.astype(jnp.float32) + got.astype(jnp.float32)).astype(jnp.bfloat16)]
    ppermute x7 -> x8, waiting for transfers between devices: 6.31 us -> 2.74 us  [moved(): return lax.ppermute(block, ('row', 'col'), pairs)]
    dot_general x1 -> x0, matrix products: 3.1 us -> none  [local(): lax.dot_general(qkv_weight[:, :INNER], token_rows, (((0,), (1,)), ((), ()...]
    pallas_call x2 -> x4, Pallas kernels: 5.84 us -> 8 us  [the longest x1 4.52 us: project(): pl.pallas_call(project_kernel, grid=(1,), out_shape=[jax.ShapeDtypeStruct...]
  transfers between devices with their start and end apart: 26 -> 28, of which waited for: 10 -> 12; matrix products, arithmetic and copies ran while one was open for 12% -> 8% of each run, Pallas kernels for 8% -> 12%
where the time goes in v8:
time: 118 us; the launch traced here: 117 us
  starting transfers between devices  40.9 us (35%)
  Pallas kernels  32.1 us (27%)
  waiting for transfers between devices  23.8 us (20%)
  local copies, waits for them, and re-layouts  10.7 us (9%)
  matrix products  4.67 us (4%)
  other arithmetic  3.88 us (3%)
    ppermute x12, starting transfers between devices, exchanged(): got.append(lax.ppermute(part, axis, pairs))  19.9 us
    ppermute x12, waiting for transfers between devices, exchanged(): got.append(lax.ppermute(part, axis, pairs))  17.2 us
    ppermute x8, starting transfers between devices, moved(): return lax.ppermute(block, ('row', 'col'), pairs)  13.8 us
    pallas_call x1, Pallas kernels, attention(): pl.pallas_call(attention_kernel, grid=(1,), out_shape=outs, in_specs=[pl....  13.2 us
    unnamed x41, local copies, waits for them, and re-layouts  8.2 us
    ppermute x6, starting transfers between devices, gathered(): got = lax.ppermute(block, axis, [(i, i ^ step) for i in range(count)])  7.12 us
    pallas_call x1, Pallas kernels, project(): pl.pallas_call(project_kernel, grid=(1,), out_shape=[jax.ShapeDtypeStruct...  4.52 us
    pallas_call x1, Pallas kernels, project(): pl.pallas_call(edges_kernel, grid=(1,), out_shape=[shape(edge)] * 2, in_s...  3.9 us
  transfers between devices with their start and end apart: 28, of which 12 were waited for; matrix products, arithmetic and copies ran while one was open for 8% of the time, Pallas kernels for 12%

profile of v8, /device:TPU:0, one launch (start us, length us, event | category | flops | bytes accessed | tf_op | source)
XLA Modules:
  0.0 117.2 jit_solution(10458064256906881163)
XLA Ops:
  0.7 3.9 %project_edges.1 = (bf16[128,1152]{1,0:T(8,128)(2,1)}, bf16[128,1152]{1,0:T(8,128)(2,1)}) custom-call(bf16[512,1152]{1,0:T(8,128)(2,1)} %bitcast.56, bf16[1728,1152]{1,0:T(8,128)(2,1)} %bitcast.60), custom_call_target="tpu_custom_call" | custom-call | flops 1 | bytes 1 | tf_op jit(solution)/shard_map/project_edges/pallas_call | solution.py:95
  4.6 1.3 %collective-permute-start.1 = (bf16[128,1152]{1,0:T(8,128)(2,1)}, bf16[128,1152]{1,0:T(8,128)(2,1)S(1)}, u32[]{:S(2)}, u32[]{:S(2)}) collective-permute-start(bf16[128,1152]{1,0:T(8,128)(2,1)} %get-tuple-element.31.top_ref), channel_id=1, source_target_pairs={{2,0},{3,1},{4,2},{5,3},{6,4},{7,5},{10,8},{11,9},{12,10},{13,11},... | collective-permute-start | bytes 884744 | tf_op jit(solution)/shard_map/ppermute | solution.py:575
  5.9 5.6 %collective-permute-start = (bf16[128,1152]{1,0:T(8,128)(2,1)}, bf16[128,1152]{1,0:T(8,128)(2,1)S(1)}, u32[]{:S(2)}, u32[]{:S(2)}) collective-permute-start(bf16[128,1152]{1,0:T(8,128)(2,1)} %get-tuple-element.34), channel_id=1, source_target_pairs={{0,2},{1,3},{2,4},{3,5},{4,6},{5,7},{8,10},{9,11},{10,12},{11,13},... | collective-permute-start | bytes 884744 | tf_op jit(solution)/shard_map/ppermute | solution.py:575
  11.5 2.1 %copy-done.2 = bf16[1152,1728]{0,1:T(8,128)(2,1)S(1)} copy-done((bf16[1152,1728]{0,1:T(8,128)(2,1)S(1)}, bf16[1152,1728]{0,1:T(8,128)(2,1)}, u32[]{:S(2)}) %copy-start.2) | copy-done | bytes 3981336
  13.6 1.0 copy-done.13
  14.6 4.5 %project.1 = (bf16[576,512]{1,0:T(8,128)(2,1)S(1)}, bf16[512,1152]{1,0:T(8,128)(2,1)S(1)}, bf16[256,1152]{1,0:T(8,128)(2,1)}) custom-call(s32[1]{0:T(128)} %bitcast.own_ref, bf16[128,1152]{1,0:T(8,128)(2,1)S(1)} %copy-done.13, bf16[512,1152]{1,0:T(8,128)(2,1)S(1)} %bitcast.57, bf16[1728,1152]{1,0:T(8,128)(2,1)S(1)} %bitcast.61), custom_call_target="tpu_custom_call" | custom-call | flops 1 | bytes 1 | tf_op jit(solution)/shard_map/project/pallas_call | solution.py:111
  19.1 1.0 copy-done.16
  20.1 0.8 copy-done.18
  21.0 0.1 tile.11
  21.5 0.1 fusion.4
  21.8 0.4 fusion.3.bias_ref
  22.4 0.6 collective-permute-start.3
  23.0 0.2 copy-done.8
  23.1 1.0 convolution_convert_fusion.2.g_ref
  24.2 0.2 copy-done.17
  24.4 0.1 copy-done.19
  24.5 1.0 copy-done.15
  25.5 13.2 %window_attention.1 = (bf16[512,640]{1,0:T(8,128)(2,1)S(1)}, bf16[512,640]{1,0:T(8,128)(2,1)S(1)}, bf16[512,1152]{1,0:T(8,128)(2,1)S(1)}, bf16[256,1152]{1,0:T(8...) custom-call(s32[4]{0:T(128)S(1)} %broadcast_subtract_fusion.start_ref, ...), custom_call_target="tpu_custom_call" | custom-call | flops 4076863488 | bytes 16777216 | tf_op jit(solution)/shard_map/window_attention/pallas_call | solution.py:287
  38.7 0.5 collective-permute-start.6
  39.2 3.6 %weight_grad_halves.1 = (bf16[576,1152]{1,0:T(8,128)(2,1)}, bf16[576,1152]{1,0:T(8,128)(2,1)S(1)}) custom-call(s32[1]{0:T(128)} %bitcast.own_ref, bf16[512,1152]{1,0:T(8,128)(2,1)S(1)} %bitcast.58, bf16[512,640]{1,0:T(8,128)(2,1)S(1)} %get-tuple-element.36.refs_1_.dq_ref, bf16[512,1152]{1,0:T(8,128)(2,1)S(1)} %bitcast.63, ...), custom_call_target="tpu_custom_call" | custom-call | flops 1 | bytes 1 | tf_op jit(solution)/shard_map/weight_grad_halves/pallas_call | solution.py:348
  42.9 0.5 collective-permute-start.5
  43.5 0.4 copy-done.6
  43.9 0.1 fusion
  44.0 0.9 fusion.6
  44.9 3.9 %collective-permute-start.7 = (bf16[128,1152]{1,0:T(8,128)(2,1)}, bf16[128,1152]{1,0:T(8,128)(2,1)S(1)}, u32[]{:S(2)}, u32[]{:S(2)}) collective-permute-start(bf16[128,1152]{1,0:T(8,128)(2,1)} %get-tuple-element.63), channel_id=1, source_target_pairs={{0,2},{1,3},{2,4},{3,5},{4,6},{5,7},{8,10},{9,11},{10,12},{11,13},... | collective-permute-start | bytes 884744 | tf_op jit(solution)/shard_map/ppermute | solution.py:575
  48.8 1.5 %collective-permute-start.8 = (bf16[128,1152]{1,0:T(8,128)(2,1)}, bf16[128,1152]{1,0:T(8,128)(2,1)}, u32[]{:S(2)}, u32[]{:S(2)}) collective-permute-start(bf16[128,1152]{1,0:T(8,128)(2,1)} %get-tuple-element.62), channel_id=1, source_target_pairs={{2,0},{3,1},{4,2},{5,3},{6,4},{7,5},{10,8},{11,9},{12,10},{13,11},... | collective-permute-start | bytes 884744 | tf_op jit(solution)/shard_map/ppermute | solution.py:575
  50.3 1.3 %copy-done.7 = bf16[576,1152]{1,0:T(8,128)(2,1)S(1)} copy-done((bf16[576,1152]{1,0:T(8,128)(2,1)S(1)}, bf16[576,1152]{1,0:T(8,128)(2,1)}, u32[]{:S(2)}) %copy-start.7) | copy-done | bytes 1327128
  51.6 2.0 %core_parts.2 = (bf16[4,40,1152]{2,1,0:T(8,128)(2,1)S(1)}, bf16[4,40,1152]{2,1,0:T(8,128)(2,1)S(1)}, bf16[4,40,1152]{2,1,0:T(8,128)(2,1)S(1)}, bf16[4,40,1152]{2,1,0:T(8,128)(2,1)S(1)}) custom-call(s32[1]{0:T(128)} %bitcast.1.own_ref, bf16[576,1152]{1,0:T(8,128)(2,1)S(1)} %copy-done.7, bf16[576,1152]{1,0:T(8,128)(2,1)} %collective-permute-done.4.got_ref), custom_call_target="tpu_custom_call" | custom-call | flops 1 | bytes 1 | tf_op jit(solution)/shard_map/core_parts/pallas_call | solution.py:435
  53.6 1.6 %collective-permute-start.10 = (bf16[4,40,1152]{2,1,0:T(8,128)(2,1)S(1)}, bf16[4,40,1152]{2,1,0:T(8,128)(2,1)S(1)}, u32[]{:S(2)}, u32[]{:S(2)}) collective-permute-start(bf16[4,40,1152]{2,1,0:T(8,128)(2,1)S(1)} %get-tuple-element.41.second), channel_id=1, source_target_pairs={{0,16},{8,24},{16,0},{24,8},{1,17},{9,25},{17,1},{25,9},{2,18},{10... | collective-permute-start | bytes 1105928 | tf_op jit(solution)/shard_map/ppermute | solution.py:518
  55.2 1.4 %collective-permute-start.11 = (bf16[4,40,1152]{2,1,0:T(8,128)(2,1)S(1)}, bf16[4,40,1152]{2,1,0:T(8,128)(2,1)S(1)}, u32[]{:S(2)}, u32[]{:S(2)}) collective-permute-start(bf16[4,40,1152]{2,1,0:T(8,128)(2,1)S(1)} %get-tuple-element.42.third), channel_id=1, source_target_pairs={{0,24},{8,16},{16,8},{24,0},{1,25},{9,17},{17,9},{25,1},{2,26},{10... | collective-permute-start | bytes 1105928 | tf_op jit(solution)/shard_map/ppermute | solution.py:518
  56.7 0.5 collective-permute-start.9
  57.2 2.7 %collective-permute-done.8.below_ref = bf16[128,1152]{1,0:T(8,128)(2,1)} collective-permute-done((bf16[128,1152]{1,0:T(8,128)(2,1)}, bf16[128,1152]{1,0:T(8,128)(2,1)}, u32[]{:S(2)}, u32[]{:S(2)}) %collective-permute-start.8) | collective-permute-done | bytes 294944 | tf_op jit(solution)/shard_map/ppermute | solution.py:575
  59.9 3.4 %late_weight_grad_halves.1 = (bf16[576,1152]{1,0:T(8,128)(2,1)S(1)}, bf16[576,1152]{1,0:T(8,128)(2,1)S(1)}, bf16[512,1728]{1,0:T(8,128)(2,1)S(1)}, bf16[512,576]{1,0:T(8,128)(2,1)S(1)}) custom-call(s32[1]{0:T(128)} %bitcast.own_ref, bf16[4,40,1152]{2,1,0:T(8,128)(2,1)S(1)} %get-tuple-element.40.first, bf16[4,40,1152]{2,1,0:T(8,128)(2,1)S(1)} %get-tuple-element.41.second, ...), custom_call_target="tpu_custom_call" | custom-call | flops 1 | bytes 1 | tf_op jit(solution)/shard_map/late_weight_grad_halves/pallas_call | solution.py:398
  63.4 2.5 %convolution_convert_fusion.refs_2_ = bf16[512,1152]{1,0:T(8,128)(2,1)S(1)} fusion(bf16[512,1728]{1,0:T(8,128)(2,1)S(1)} %get-tuple-element.48, bf16[1152,1728]{0,1:T(8,128)(2,1)S(1)} %copy-done.3), kind=kOutput, calls=%fused_computation | convolution fusion | flops 2039021568 | bytes 6930432 | tf_op jit(solution)/shard_map/dot_general | solution.py:31
  65.9 1.2 %convolution_convert_fusion.1.refs_1_ = bf16[512,1152]{1,0:T(8,128)(2,1)S(1)} fusion(bf16[512,576]{1,0:T(8,128)(2,1)S(1)} %get-tuple-element.47, bf16[1152,576]{0,1:T(8,128)(2,1)S(1)} %copy-done), kind=kOutput, calls=%fused_computation.1 | convolution fusion | flops 680067072 | bytes 3096576 | tf_op jit(solution)/shard_map/dot_general | solution.py:31
  67.1 4.7 %collective-permute-done.10 = bf16[4,40,1152]{2,1,0:T(8,128)(2,1)S(1)} collective-permute-done((bf16[4,40,1152]{2,1,0:T(8,128)(2,1)S(1)}, bf16[4,40,1152]{2,1,0:T(8,128)(2,1)S(1)}, u32[]{:S(2)}, u32[]{:S(2)}) %collective-permute-start.10) | collective-permute-done | bytes 368672 | tf_op jit(solution)/shard_map/ppermute | solution.py:518
  71.8 1.2 %collective-permute-done.9 = bf16[4,40,1152]{2,1,0:T(8,128)(2,1)S(1)} collective-permute-done((bf16[4,40,1152]{2,1,0:T(8,128)(2,1)S(1)}, bf16[4,40,1152]{2,1,0:T(8,128)(2,1)S(1)}, u32[]{:S(2)}, u32[]{:S(2)}) %collective-permute-start.9) | collective-permute-done | bytes 368672 | tf_op jit(solution)/shard_map/ppermute | solution.py:518
  73.0 0.2 add_convert_fusion.1.refs_0_
  73.3 1.4 %core_parts.3 = (bf16[4,40,1152]{2,1,0:T(8,128)(2,1)S(1)}, bf16[4,40,1152]{2,1,0:T(8,128)(2,1)}, bf16[4,40,1152]{2,1,0:T(8,128)(2,1)}, bf16[4,40,1152]{2,1,0:T(8,128)(2,1)}) custom-call(s32[1]{0:T(128)} %bitcast.1.own_ref, bf16[576,1152]{1,0:T(8,128)(2,1)S(1)} %get-tuple-element.50.kept_ref, bf16[576,1152]{1,0:T(8,128)(2,1)S(1)} %collective-permute-done.15.got_ref, ...), custom_call_target="tpu_custom_call" | custom-call | flops 1 | bytes 1 | tf_op jit(solution)/shard_map/core_parts/pallas_call | solution.py:435
  74.7 1.5 %collective-permute-start.16 = (bf16[4,40,1152]{2,1,0:T(8,128)(2,1)}, bf16[4,40,1152]{2,1,0:T(8,128)(2,1)S(1)}, u32[]{:S(2)}, u32[]{:S(2)}) collective-permute-start(bf16[4,40,1152]{2,1,0:T(8,128)(2,1)} %get-tuple-element.54), channel_id=1, source_target_pairs={{0,8},{8,0},{16,24},{24,16},{1,9},{9,1},{17,25},{25,17},{2,10},{10... | collective-permute-start | bytes 1105928 | tf_op jit(solution)/shard_map/ppermute | solution.py:518
  76.2 1.5 %collective-permute-start.17 = (bf16[4,40,1152]{2,1,0:T(8,128)(2,1)}, bf16[4,40,1152]{2,1,0:T(8,128)(2,1)S(1)}, u32[]{:S(2)}, u32[]{:S(2)}) collective-permute-start(bf16[4,40,1152]{2,1,0:T(8,128)(2,1)} %get-tuple-element.55), channel_id=1, source_target_pairs={{0,16},{8,24},{16,0},{24,8},{1,17},{9,25},{17,1},{25,9},{2,18},{10... | collective-permute-start | bytes 1105928 | tf_op jit(solution)/shard_map/ppermute | solution.py:518
  77.7 0.5 collective-permute-start.18
  78.2 2.4 %collective-permute-start.12 = (bf16[40,1152]{1,0:T(8,128)(2,1)S(1)}, bf16[40,1152]{1,0:T(8,128)(2,1)S(1)}, u32[]{:S(2)}, u32[]{:S(2)}) collective-permute-start(bf16[40,1152]{1,0:T(8,128)(2,1)S(1)} %get-tuple-element.66), channel_id=1, source_target_pairs={{0,2},{2,0},{4,6},{6,4},{1,3},{3,1},{5,7},{7,5},{8,10},{10,8},{12,... | collective-permute-start | bytes 276488 | tf_op jit(solution)/shard_map/ppermute | solution.py:518
  80.7 2.0 %collective-permute-start.13 = (bf16[40,1152]{1,0:T(8,128)(2,1)S(1)}, bf16[40,1152]{1,0:T(8,128)(2,1)S(1)}, u32[]{:S(2)}, u32[]{:S(2)}) collective-permute-start(bf16[40,1152]{1,0:T(8,128)(2,1)S(1)} %get-tuple-element.65), channel_id=1, source_target_pairs={{0,4},{2,6},{4,0},{6,2},{1,5},{3,7},{5,1},{7,3},{8,12},{10,14},{12... | collective-permute-start | bytes 276488 | tf_op jit(solution)/shard_map/ppermute | solution.py:518
  82.7 3.8 %collective-permute-done.16 = bf16[4,40,1152]{2,1,0:T(8,128)(2,1)S(1)} collective-permute-done((bf16[4,40,1152]{2,1,0:T(8,128)(2,1)}, bf16[4,40,1152]{2,1,0:T(8,128)(2,1)S(1)}, u32[]{:S(2)}, u32[]{:S(2)}) %collective-permute-start.16) | collective-permute-done | bytes 368672 | tf_op jit(solution)/shard_map/ppermute | solution.py:518
  86.5 3.8 %collective-permute-start.14 = (bf16[40,1152]{1,0:T(8,128)(2,1)S(1)}, bf16[40,1152]{1,0:T(8,128)(2,1)S(1)}, u32[]{:S(2)}, u32[]{:S(2)}) collective-permute-start(bf16[40,1152]{1,0:T(8,128)(2,1)S(1)} %get-tuple-element.64), channel_id=1, source_target_pairs={{0,6},{2,4},{4,2},{6,0},{1,7},{3,5},{5,3},{7,1},{8,14},{10,12},{12... | collective-permute-start | bytes 276488 | tf_op jit(solution)/shard_map/ppermute | solution.py:518
  90.3 2.8 %collective-permute-done.17 = bf16[4,40,1152]{2,1,0:T(8,128)(2,1)S(1)} collective-permute-done((bf16[4,40,1152]{2,1,0:T(8,128)(2,1)}, bf16[4,40,1152]{2,1,0:T(8,128)(2,1)S(1)}, u32[]{:S(2)}, u32[]{:S(2)}) %collective-permute-start.17) | collective-permute-done | bytes 368672 | tf_op jit(solution)/shard_map/ppermute | solution.py:518
  93.1 1.2 %add_convert_fusion.refs_0_ = bf16[4,40,1152]{2,1,0:T(8,128)(2,1)S(1)} fusion(bf16[4,40,1152]{2,1,0:T(8,128)(2,1)} %collective-permute-done.18, bf16[4,40,1152]{2,1,0:T(8,128)(2,1)S(1)} %collective-permute-done.17, bf16[4,40,1152]{2,1,0:T(8,128)(2,1)S(1)} %collective-permute-done.16, bf16[4,40,1152]{2,1,0:T(8,128)(2,1)S(1)} %get-tuple-element.53), kind=kLoop, calls=%fused_computation.12 | loop fusion | flops 1474560 | bytes 1843200 | tf_op jit(solution)/shard_map/convert_element_type | solution.py:528
  94.4 1.4 %collective-permute-start.19 = (bf16[40,1152]{1,0:T(8,128)(2,1)S(1)}, bf16[40,1152]{1,0:T(8,128)(2,1)S(1)}, u32[]{:S(2)}, u32[]{:S(2)}) collective-permute-start(bf16[40,1152]{1,0:T(8,128)(2,1)S(1)} %row_sum.1), channel_id=1, source_target_pairs={{0,8},{8,0},{16,24},{24,16},{1,9},{9,1},{17,25},{25,17},{2,10},{10... | collective-permute-start | bytes 276488 | tf_op jit(solution)/shard_map/ppermute | solution.py:537
  95.8 0.7 collective-permute-start.20
  96.6 2.2 %collective-permute-start.22 = (bf16[40,1152]{1,0:T(8,128)(2,1)S(1)}, bf16[40,1152]{1,0:T(8,128)(2,1)S(1)}, u32[]{:S(2)}, u32[]{:S(2)}) collective-permute-start(bf16[40,1152]{1,0:T(8,128)(2,1)S(1)} %get-tuple-element.71), channel_id=1, source_target_pairs={{0,2},{2,0},{4,6},{6,4},{1,3},{3,1},{5,7},{7,5},{8,10},{10,8},{12,... | collective-permute-start | bytes 276488 | tf_op jit(solution)/shard_map/ppermute | solution.py:518
  98.7 2.3 %collective-permute-start.23 = (bf16[40,1152]{1,0:T(8,128)(2,1)S(1)}, bf16[40,1152]{1,0:T(8,128)(2,1)S(1)}, u32[]{:S(2)}, u32[]{:S(2)}) collective-permute-start(bf16[40,1152]{1,0:T(8,128)(2,1)S(1)} %get-tuple-element.70), channel_id=1, source_target_pairs={{0,4},{2,6},{4,0},{6,2},{1,5},{3,7},{5,1},{7,3},{8,12},{10,14},{12... | collective-permute-start | bytes 276488 | tf_op jit(solution)/shard_map/ppermute | solution.py:518
  101.0 0.2 collective-permute-start.24
  101.3 1.4 %collective-permute-start.21 = (bf16[40,1152]{1,0:T(8,128)(2,1)S(1)}, bf16[40,1152]{1,0:T(8,128)(2,1)S(1)}, u32[]{:S(2)}, u32[]{:S(2)}) collective-permute-start(bf16[40,1152]{1,0:T(8,128)(2,1)S(1)} %row_sum.1), channel_id=1, source_target_pairs={{0,24},{8,16},{16,8},{24,0},{1,25},{9,17},{17,9},{25,1},{2,26},{10... | collective-permute-start | bytes 276488 | tf_op jit(solution)/shard_map/ppermute | solution.py:537
  102.8 2.4 %collective-permute-done.23 = bf16[40,1152]{1,0:T(8,128)(2,1)S(1)} collective-permute-done((bf16[40,1152]{1,0:T(8,128)(2,1)S(1)}, bf16[40,1152]{1,0:T(8,128)(2,1)S(1)}, u32[]{:S(2)}, u32[]{:S(2)}) %collective-permute-start.23) | collective-permute-done | bytes 92192 | tf_op jit(solution)/shard_map/ppermute | solution.py:518
  105.2 2.2 %collective-permute-done.24 = bf16[40,1152]{1,0:T(8,128)(2,1)S(1)} collective-permute-done((bf16[40,1152]{1,0:T(8,128)(2,1)S(1)}, bf16[40,1152]{1,0:T(8,128)(2,1)S(1)}, u32[]{:S(2)}, u32[]{:S(2)}) %collective-permute-start.24) | collective-permute-done | bytes 92192 | tf_op jit(solution)/shard_map/ppermute | solution.py:518
  107.5 1.6 %collective-permute-start.25 = (bf16[40,1152]{1,0:T(8,128)(2,1)S(1)}, bf16[40,1152]{1,0:T(8,128)(2,1)S(1)}, u32[]{:S(2)}, u32[]{:S(2)}) collective-permute-start(bf16[40,1152]{1,0:T(8,128)(2,1)S(1)} %get-tuple-element.59), channel_id=1, source_target_pairs={{0,8},{8,0},{16,24},{24,16},{1,9},{9,1},{17,25},{25,17},{2,10},{10... | collective-permute-start | bytes 276488 | tf_op jit(solution)/shard_map/ppermute | solution.py:537
  109.0 0.5 collective-permute-start.26
  109.5 1.5 %collective-permute-start.27 = (bf16[40,1152]{1,0:T(8,128)(2,1)S(1)}, bf16[40,1152]{1,0:T(8,128)(2,1)S(1)}, u32[]{:S(2)}, u32[]{:S(2)}) collective-permute-start(bf16[40,1152]{1,0:T(8,128)(2,1)S(1)} %get-tuple-element.59), channel_id=1, source_target_pairs={{0,24},{8,16},{16,8},{24,0},{1,25},{9,17},{17,9},{25,1},{2,26},{10... | collective-permute-start | bytes 276488 | tf_op jit(solution)/shard_map/ppermute | solution.py:537
  111.1 1.0 collective-permute-done.25
  112.1 1.5 %collective-permute-done.26 = bf16[40,1152]{1,0:T(8,128)(2,1)S(1)} collective-permute-done((bf16[40,1152]{1,0:T(8,128)(2,1)S(1)}, bf16[40,1152]{1,0:T(8,128)(2,1)S(1)}, u32[]{:S(2)}, u32[]{:S(2)}) %collective-permute-start.26) | collective-permute-done | bytes 92192 | tf_op jit(solution)/shard_map/ppermute | solution.py:537
  113.6 1.4 %collective-permute-done.27 = bf16[40,1152]{1,0:T(8,128)(2,1)S(1)} collective-permute-done((bf16[40,1152]{1,0:T(8,128)(2,1)S(1)}, bf16[40,1152]{1,0:T(8,128)(2,1)S(1)}, u32[]{:S(2)}, u32[]{:S(2)}) %collective-permute-start.27) | collective-permute-done | bytes 92192 | tf_op jit(solution)/shard_map/ppermute | solution.py:537
  115.1 0.9 fusion.5
  116.0 1.2 %pad_maximum_fusion = f32[144,1728]{1,0:T(8,128)} fusion(f32[144,1152]{1,0:T(8,128)S(1)} %slice_convert_fusion, f32[144,576]{1,0:T(8,128)S(1)} %get-tuple-element.61), kind=kLoop, calls=%fused_computation.11 | loop fusion | flops 248832 | bytes 1990656 | tf_op jit(solution)/shard_map/concatenate | solution.py:671
  (93 shorter events, 1.6 us)
Async XLA Ops:
  0.6 22.3 %copy-start = (bf16[1152,576]{0,1:T(8,128)(2,1)S(1)}, bf16[1152,576]{0,1:T(8,128)(2,1)}, u32[]{:S(2)}) copy-start(bf16[1152,576]{0,1:T(8,128)(2,1)} %param.6) | copy-start | bytes 3981316
  0.6 10.8 %copy-start.1 = (bf16[1,32,16,1152]{3,2,1,0:T(8,128)(2,1)S(1)}, bf16[1,32,16,1152]{3,2,1,0:T(8,128)(2,1)}, u32[]{:S(2)}) copy-start(bf16[1,32,16,1152]{3,2,1,0:T(8,128)(2,1)} %param.4) | copy-start | bytes 3538948
  4.6 17.7 %collective-permute-start.1 = (bf16[128,1152]{1,0:T(8,128)(2,1)}, bf16[128,1152]{1,0:T(8,128)(2,1)S(1)}, u32[]{:S(2)}, u32[]{:S(2)}) collective-permute-start(bf16[128,1152]{1,0:T(8,128)(2,1)} %get-tuple-element.31.top_ref), channel_id=1, source_target_pairs={{2,0},{3,1},{4,2},{5,3},{6,4},{7,5},{10,8},{11,9},{12,10},{13,11},... | collective-permute-start | bytes 884744 | tf_op jit(solution)/shard_map/ppermute | solution.py:575
  5.9 16.4 %collective-permute-start = (bf16[128,1152]{1,0:T(8,128)(2,1)}, bf16[128,1152]{1,0:T(8,128)(2,1)S(1)}, u32[]{:S(2)}, u32[]{:S(2)}) collective-permute-start(bf16[128,1152]{1,0:T(8,128)(2,1)} %get-tuple-element.34), channel_id=1, source_target_pairs={{0,2},{1,3},{2,4},{3,5},{4,6},{5,7},{8,10},{9,11},{10,12},{11,13},... | collective-permute-start | bytes 884744 | tf_op jit(solution)/shard_map/ppermute | solution.py:575
  11.5 2.1 %copy-start.2 = (bf16[1152,1728]{0,1:T(8,128)(2,1)S(1)}, bf16[1152,1728]{0,1:T(8,128)(2,1)}, u32[]{:S(2)}) copy-start(bf16[1152,1728]{0,1:T(8,128)(2,1)} %param.5) | copy-start | bytes 11943940
  13.6 1.0 copy-start.13
  19.1 1.0 copy-start.16
  20.1 0.8 copy-start.18
  20.9 3.2 %collective-permute-start.2 = (bf16[256,1152]{1,0:T(8,128)(2,1)}, bf16[256,1152]{1,0:T(8,128)(2,1)}, u32[]{:S(2)}, u32[]{:S(2)}) collective-permute-start(bf16[256,1152]{1,0:T(8,128)(2,1)} %get-tuple-element.35), channel_id=1, source_target_pairs={{0,1},{1,0},{2,3},{3,2},{4,5},{5,4},{6,7},{7,6},{8,9},{9,8},{10,11... | collective-permute-start | bytes 1769480 | tf_op jit(solution)/shard_map/ppermute | solution.py:575
  21.8 1.3 %copy-start.8 = (bf16[1,32,16,1152]{3,2,1,0:T(8,128)(2,1)S(1)}, bf16[1,32,16,1152]{3,2,1,0:T(8,128)(2,1)}, u32[]{:S(2)}) copy-start(bf16[1,32,16,1152]{3,2,1,0:T(8,128)(2,1)} %param.7) | copy-start | bytes 3538948
  22.3 1.8 %copy-start.14 = (bf16[128,1152]{1,0:T(8,128)(2,1)}, bf16[128,1152]{1,0:T(8,128)(2,1)S(1)}, u32[]{:S(2)}) copy-start(bf16[128,1152]{1,0:T(8,128)(2,1)S(1)} %collective-permute-done.above_ref) | copy-start | bytes 884740
  22.4 1.8 %collective-permute-start.3 = (bf16[16,8,1152]{2,1,0:T(8,128)(2,1)S(1)}, bf16[16,8,1152]{2,1,0:T(8,128)(2,1)S(1)}, u32[]{:S(2)}, u32[]{:S(2)}) collective-permute-start(bf16[16,8,1152]{2,1,0:T(8,128)(2,1)S(1)} %pad_maximum_fusion.1), channel_id=1, source_target_pairs={{0,1},{1,0},{2,3},{3,2},{4,5},{5,4},{6,7},{7,6},{8,9},{9,8},{10,11... | collective-permute-start | bytes 884744 | tf_op jit(solution)/shard_map/ppermute | solution.py:575
  23.1 1.3 %copy-start.17 = (bf16[512,1152]{1,0:T(8,128)(2,1)S(1)}, bf16[512,1152]{1,0:T(8,128)(2,1)}, u32[]{:S(2)}) copy-start(bf16[512,1152]{1,0:T(8,128)(2,1)} %copy-done.16) | copy-start | bytes 3538948
  23.1 1.4 %copy-start.19 = (bf16[576,512]{1,0:T(8,128)(2,1)S(1)}, bf16[576,512]{1,0:T(8,128)(2,1)}, u32[]{:S(2)}) copy-start(bf16[576,512]{1,0:T(8,128)(2,1)} %copy-done.18) | copy-start | bytes 1769476
  24.5 1.0 copy-start.15
  38.7 4.1 %copy-start.4 = (bf16[512,640]{1,0:T(8,128)(2,1)}, bf16[512,640]{1,0:T(8,128)(2,1)S(1)}, u32[]{:S(2)}) copy-start(bf16[512,640]{1,0:T(8,128)(2,1)S(1)} %get-tuple-element.36.refs_1_.dq_ref) | copy-start | bytes 1966084
  38.7 4.1 %copy-start.11 = (bf16[512,1152]{1,0:T(8,128)(2,1)}, bf16[512,1152]{1,0:T(8,128)(2,1)S(1)}, u32[]{:S(2)}) copy-start(bf16[512,1152]{1,0:T(8,128)(2,1)S(1)} %get-tuple-element.43.inner_ref) | copy-start | bytes 3538948
  38.7 4.7 %collective-permute-start.6 = (bf16[128,1152]{1,0:T(8,128)(2,1)S(1)}, bf16[128,1152]{1,0:T(8,128)(2,1)S(1)}, u32[]{:S(2)}, u32[]{:S(2)}) collective-permute-start(bf16[128,1152]{1,0:T(8,128)(2,1)S(1)} %get-tuple-element.46), channel_id=1, source_target_pairs={{0,1},{1,0},{2,3},{3,2},{4,5},{5,4},{6,7},{7,6},{8,9},{9,8},{10,11... | collective-permute-start | bytes 884744 | tf_op jit(solution)/shard_map/ppermute | solution.py:575
  42.8 1.1 copy-start.6
  42.8 7.4 %collective-permute-start.4 = (bf16[576,1152]{1,0:T(8,128)(2,1)}, bf16[576,1152]{1,0:T(8,128)(2,1)}, u32[]{:S(2)}, u32[]{:S(2)}) collective-permute-start(bf16[576,1152]{1,0:T(8,128)(2,1)} %get-tuple-element.39), channel_id=1, source_target_pairs={{0,1},{1,0},{2,3},{3,2},{4,5},{5,4},{6,7},{7,6},{8,9},{9,8},{10,11... | collective-permute-start | bytes 3981320 | tf_op jit(solution)/shard_map/ppermute | solution.py:430
  42.9 17.0 %collective-permute-start.5 = (bf16[256,1152]{1,0:T(8,128)(2,1)}, bf16[256,1152]{1,0:T(8,128)(2,1)}, u32[]{:S(2)}, u32[]{:S(2)}) collective-permute-start(bf16[256,1152]{1,0:T(8,128)(2,1)} %get-tuple-element.44), channel_id=1, source_target_pairs={{0,1},{1,0},{2,3},{3,2},{4,5},{5,4},{6,7},{7,6},{8,9},{9,8},{10,11... | collective-permute-start | bytes 1769480 | tf_op jit(solution)/shard_map/ppermute | solution.py:575
  44.9 11.8 %collective-permute-start.7 = (bf16[128,1152]{1,0:T(8,128)(2,1)}, bf16[128,1152]{1,0:T(8,128)(2,1)S(1)}, u32[]{:S(2)}, u32[]{:S(2)}) collective-permute-start(bf16[128,1152]{1,0:T(8,128)(2,1)} %get-tuple-element.63), channel_id=1, source_target_pairs={{0,2},{1,3},{2,4},{3,5},{4,6},{5,7},{8,10},{9,11},{10,12},{11,13},... | collective-permute-start | bytes 884744 | tf_op jit(solution)/shard_map/ppermute | solution.py:575
  48.8 11.0 %collective-permute-start.8 = (bf16[128,1152]{1,0:T(8,128)(2,1)}, bf16[128,1152]{1,0:T(8,128)(2,1)}, u32[]{:S(2)}, u32[]{:S(2)}) collective-permute-start(bf16[128,1152]{1,0:T(8,128)(2,1)} %get-tuple-element.62), channel_id=1, source_target_pairs={{2,0},{3,1},{4,2},{5,3},{6,4},{7,5},{10,8},{11,9},{12,10},{13,11},... | collective-permute-start | bytes 884744 | tf_op jit(solution)/shard_map/ppermute | solution.py:575
  50.3 1.3 %copy-start.7 = (bf16[576,1152]{1,0:T(8,128)(2,1)S(1)}, bf16[576,1152]{1,0:T(8,128)(2,1)}, u32[]{:S(2)}) copy-start(bf16[576,1152]{1,0:T(8,128)(2,1)} %copy-done.6) | copy-start | bytes 3981316
  51.6 8.2 %copy-start.5 = (bf16[512,640]{1,0:T(8,128)(2,1)S(1)}, bf16[512,640]{1,0:T(8,128)(2,1)}, u32[]{:S(2)}) copy-start(bf16[512,640]{1,0:T(8,128)(2,1)} %copy-done.4) | copy-start | bytes 1966084
  51.6 8.2 %copy-start.12 = (bf16[512,1152]{1,0:T(8,128)(2,1)S(1)}, bf16[512,1152]{1,0:T(8,128)(2,1)}, u32[]{:S(2)}) copy-start(bf16[512,1152]{1,0:T(8,128)(2,1)} %copy-done.11) | copy-start | bytes 3538948
  53.6 18.2 %collective-permute-start.10 = (bf16[4,40,1152]{2,1,0:T(8,128)(2,1)S(1)}, bf16[4,40,1152]{2,1,0:T(8,128)(2,1)S(1)}, u32[]{:S(2)}, u32[]{:S(2)}) collective-permute-start(bf16[4,40,1152]{2,1,0:T(8,128)(2,1)S(1)} %get-tuple-element.41.second), channel_id=1, source_target_pairs={{0,16},{8,24},{16,0},{24,8},{1,17},{9,25},{17,1},{25,9},{2,18},{10... | collective-permute-start | bytes 1105928 | tf_op jit(solution)/shard_map/ppermute | solution.py:518
  55.2 16.6 %collective-permute-start.11 = (bf16[4,40,1152]{2,1,0:T(8,128)(2,1)S(1)}, bf16[4,40,1152]{2,1,0:T(8,128)(2,1)S(1)}, u32[]{:S(2)}, u32[]{:S(2)}) collective-permute-start(bf16[4,40,1152]{2,1,0:T(8,128)(2,1)S(1)} %get-tuple-element.42.third), channel_id=1, source_target_pairs={{0,24},{8,16},{16,8},{24,0},{1,25},{9,17},{17,9},{25,1},{2,26},{10... | collective-permute-start | bytes 1105928 | tf_op jit(solution)/shard_map/ppermute | solution.py:518
  56.7 16.4 %collective-permute-start.9 = (bf16[4,40,1152]{2,1,0:T(8,128)(2,1)S(1)}, bf16[4,40,1152]{2,1,0:T(8,128)(2,1)S(1)}, u32[]{:S(2)}, u32[]{:S(2)}) collective-permute-start(bf16[4,40,1152]{2,1,0:T(8,128)(2,1)S(1)} %get-tuple-element.40.first), channel_id=1, source_target_pairs={{0,8},{8,0},{16,24},{24,16},{1,9},{9,1},{17,25},{25,17},{2,10},{10... | collective-permute-start | bytes 1105928 | tf_op jit(solution)/shard_map/ppermute | solution.py:518
  59.9 3.5 %copy-start.3 = (bf16[1152,1728]{0,1:T(8,128)(2,1)S(1)}, bf16[1152,1728]{0,1:T(8,128)(2,1)}, u32[]{:S(2)}) copy-start(bf16[1152,1728]{0,1:T(8,128)(2,1)} %param.5) | copy-start | bytes 11943940
  63.3 10.0 %collective-permute-start.15 = (bf16[576,1152]{1,0:T(8,128)(2,1)S(1)}, bf16[576,1152]{1,0:T(8,128)(2,1)S(1)}, u32[]{:S(2)}, u32[]{:S(2)}) collective-permute-start(bf16[576,1152]{1,0:T(8,128)(2,1)S(1)} %get-tuple-element.51), channel_id=1, source_target_pairs={{0,1},{1,0},{2,3},{3,2},{4,5},{5,4},{6,7},{7,6},{8,9},{9,8},{10,11... | collective-permute-start | bytes 3981320 | tf_op jit(solution)/shard_map/ppermute | solution.py:430
  65.9 7.4 %copy-start.9 = (bf16[512,1152]{1,0:T(8,128)(2,1)}, bf16[512,1152]{1,0:T(8,128)(2,1)S(1)}, u32[]{:S(2)}) copy-start(bf16[512,1152]{1,0:T(8,128)(2,1)S(1)} %convolution_convert_fusion.refs_2_) | copy-start | bytes 3538948
  67.1 7.6 %copy-start.10 = (bf16[512,1152]{1,0:T(8,128)(2,1)}, bf16[512,1152]{1,0:T(8,128)(2,1)S(1)}, u32[]{:S(2)}) copy-start(bf16[512,1152]{1,0:T(8,128)(2,1)S(1)} %convolution_convert_fusion.1.refs_1_) | copy-start | bytes 3538948
  74.7 11.7 %collective-permute-start.16 = (bf16[4,40,1152]{2,1,0:T(8,128)(2,1)}, bf16[4,40,1152]{2,1,0:T(8,128)(2,1)S(1)}, u32[]{:S(2)}, u32[]{:S(2)}) collective-permute-start(bf16[4,40,1152]{2,1,0:T(8,128)(2,1)} %get-tuple-element.54), channel_id=1, source_target_pairs={{0,8},{8,0},{16,24},{24,16},{1,9},{9,1},{17,25},{25,17},{2,10},{10... | collective-permute-start | bytes 1105928 | tf_op jit(solution)/shard_map/ppermute | solution.py:518
  76.2 16.9 %collective-permute-start.17 = (bf16[4,40,1152]{2,1,0:T(8,128)(2,1)}, bf16[4,40,1152]{2,1,0:T(8,128)(2,1)S(1)}, u32[]{:S(2)}, u32[]{:S(2)}) collective-permute-start(bf16[4,40,1152]{2,1,0:T(8,128)(2,1)} %get-tuple-element.55), channel_id=1, source_target_pairs={{0,16},{8,24},{16,0},{24,8},{1,17},{9,25},{17,1},{25,9},{2,18},{10... | collective-permute-start | bytes 1105928 | tf_op jit(solution)/shard_map/ppermute | solution.py:518
  77.7 15.4 %collective-permute-start.18 = (bf16[4,40,1152]{2,1,0:T(8,128)(2,1)}, bf16[4,40,1152]{2,1,0:T(8,128)(2,1)}, u32[]{:S(2)}, u32[]{:S(2)}) collective-permute-start(bf16[4,40,1152]{2,1,0:T(8,128)(2,1)} %get-tuple-element.56), channel_id=1, source_target_pairs={{0,24},{8,16},{16,8},{24,0},{1,25},{9,17},{17,9},{25,1},{2,26},{10... | collective-permute-start | bytes 1105928 | tf_op jit(solution)/shard_map/ppermute | solution.py:518
  78.2 16.1 %collective-permute-start.12 = (bf16[40,1152]{1,0:T(8,128)(2,1)S(1)}, bf16[40,1152]{1,0:T(8,128)(2,1)S(1)}, u32[]{:S(2)}, u32[]{:S(2)}) collective-permute-start(bf16[40,1152]{1,0:T(8,128)(2,1)S(1)} %get-tuple-element.66), channel_id=1, source_target_pairs={{0,2},{2,0},{4,6},{6,4},{1,3},{3,1},{5,7},{7,5},{8,10},{10,8},{12,... | collective-permute-start | bytes 276488 | tf_op jit(solution)/shard_map/ppermute | solution.py:518
  80.7 13.7 %collective-permute-start.13 = (bf16[40,1152]{1,0:T(8,128)(2,1)S(1)}, bf16[40,1152]{1,0:T(8,128)(2,1)S(1)}, u32[]{:S(2)}, u32[]{:S(2)}) collective-permute-start(bf16[40,1152]{1,0:T(8,128)(2,1)S(1)} %get-tuple-element.65), channel_id=1, source_target_pairs={{0,4},{2,6},{4,0},{6,2},{1,5},{3,7},{5,1},{7,3},{8,12},{10,14},{12... | collective-permute-start | bytes 276488 | tf_op jit(solution)/shard_map/ppermute | solution.py:518
  86.5 7.9 %collective-permute-start.14 = (bf16[40,1152]{1,0:T(8,128)(2,1)S(1)}, bf16[40,1152]{1,0:T(8,128)(2,1)S(1)}, u32[]{:S(2)}, u32[]{:S(2)}) collective-permute-start(bf16[40,1152]{1,0:T(8,128)(2,1)S(1)} %get-tuple-element.64), channel_id=1, source_target_pairs={{0,6},{2,4},{4,2},{6,0},{1,7},{3,5},{5,3},{7,1},{8,14},{10,12},{12... | collective-permute-start | bytes 276488 | tf_op jit(solution)/shard_map/ppermute | solution.py:518
  94.4 15.1 %collective-permute-start.19 = (bf16[40,1152]{1,0:T(8,128)(2,1)S(1)}, bf16[40,1152]{1,0:T(8,128)(2,1)S(1)}, u32[]{:S(2)}, u32[]{:S(2)}) collective-permute-start(bf16[40,1152]{1,0:T(8,128)(2,1)S(1)} %row_sum.1), channel_id=1, source_target_pairs={{0,8},{8,0},{16,24},{24,16},{1,9},{9,1},{17,25},{25,17},{2,10},{10... | collective-permute-start | bytes 276488 | tf_op jit(solution)/shard_map/ppermute | solution.py:537
  95.8 15.2 %collective-permute-start.20 = (bf16[40,1152]{1,0:T(8,128)(2,1)S(1)}, bf16[40,1152]{1,0:T(8,128)(2,1)S(1)}, u32[]{:S(2)}, u32[]{:S(2)}) collective-permute-start(bf16[40,1152]{1,0:T(8,128)(2,1)S(1)} %row_sum.1), channel_id=1, source_target_pairs={{0,16},{8,24},{16,0},{24,8},{1,17},{9,25},{17,1},{25,9},{2,18},{10... | collective-permute-start | bytes 276488 | tf_op jit(solution)/shard_map/ppermute | solution.py:537
  96.6 4.8 %collective-permute-start.22 = (bf16[40,1152]{1,0:T(8,128)(2,1)S(1)}, bf16[40,1152]{1,0:T(8,128)(2,1)S(1)}, u32[]{:S(2)}, u32[]{:S(2)}) collective-permute-start(bf16[40,1152]{1,0:T(8,128)(2,1)S(1)} %get-tuple-element.71), channel_id=1, source_target_pairs={{0,2},{2,0},{4,6},{6,4},{1,3},{3,1},{5,7},{7,5},{8,10},{10,8},{12,... | collective-permute-start | bytes 276488 | tf_op jit(solution)/shard_map/ppermute | solution.py:518
  98.7 6.4 %collective-permute-start.23 = (bf16[40,1152]{1,0:T(8,128)(2,1)S(1)}, bf16[40,1152]{1,0:T(8,128)(2,1)S(1)}, u32[]{:S(2)}, u32[]{:S(2)}) collective-permute-start(bf16[40,1152]{1,0:T(8,128)(2,1)S(1)} %get-tuple-element.70), channel_id=1, source_target_pairs={{0,4},{2,6},{4,0},{6,2},{1,5},{3,7},{5,1},{7,3},{8,12},{10,14},{12... | collective-permute-start | bytes 276488 | tf_op jit(solution)/shard_map/ppermute | solution.py:518
  101.0 6.3 %collective-permute-start.24 = (bf16[40,1152]{1,0:T(8,128)(2,1)S(1)}, bf16[40,1152]{1,0:T(8,128)(2,1)S(1)}, u32[]{:S(2)}, u32[]{:S(2)}) collective-permute-start(bf16[40,1152]{1,0:T(8,128)(2,1)S(1)} %get-tuple-element.69), channel_id=1, source_target_pairs={{0,6},{2,4},{4,2},{6,0},{1,7},{3,5},{5,3},{7,1},{8,14},{10,12},{12... | collective-permute-start | bytes 276488 | tf_op jit(solution)/shard_map/ppermute | solution.py:518
  101.3 12.3 %collective-permute-start.21 = (bf16[40,1152]{1,0:T(8,128)(2,1)S(1)}, bf16[40,1152]{1,0:T(8,128)(2,1)S(1)}, u32[]{:S(2)}, u32[]{:S(2)}) collective-permute-start(bf16[40,1152]{1,0:T(8,128)(2,1)S(1)} %row_sum.1), channel_id=1, source_target_pairs={{0,24},{8,16},{16,8},{24,0},{1,25},{9,17},{17,9},{25,1},{2,26},{10... | collective-permute-start | bytes 276488 | tf_op jit(solution)/shard_map/ppermute | solution.py:537
  107.5 4.6 %collective-permute-start.25 = (bf16[40,1152]{1,0:T(8,128)(2,1)S(1)}, bf16[40,1152]{1,0:T(8,128)(2,1)S(1)}, u32[]{:S(2)}, u32[]{:S(2)}) collective-permute-start(bf16[40,1152]{1,0:T(8,128)(2,1)S(1)} %get-tuple-element.59), channel_id=1, source_target_pairs={{0,8},{8,0},{16,24},{24,16},{1,9},{9,1},{17,25},{25,17},{2,10},{10... | collective-permute-start | bytes 276488 | tf_op jit(solution)/shard_map/ppermute | solution.py:537
  109.0 4.6 %collective-permute-start.26 = (bf16[40,1152]{1,0:T(8,128)(2,1)S(1)}, bf16[40,1152]{1,0:T(8,128)(2,1)S(1)}, u32[]{:S(2)}, u32[]{:S(2)}) collective-permute-start(bf16[40,1152]{1,0:T(8,128)(2,1)S(1)} %get-tuple-element.59), channel_id=1, source_target_pairs={{0,16},{8,24},{16,0},{24,8},{1,17},{9,25},{17,1},{25,9},{2,18},{10... | collective-permute-start | bytes 276488 | tf_op jit(solution)/shard_map/ppermute | solution.py:537
  109.5 5.5 %collective-permute-start.27 = (bf16[40,1152]{1,0:T(8,128)(2,1)S(1)}, bf16[40,1152]{1,0:T(8,128)(2,1)S(1)}, u32[]{:S(2)}, u32[]{:S(2)}) collective-permute-start(bf16[40,1152]{1,0:T(8,128)(2,1)S(1)} %get-tuple-element.59), channel_id=1, source_target_pairs={{0,24},{8,16},{16,8},{24,0},{1,25},{9,17},{17,9},{25,1},{2,26},{10... | collective-permute-start | bytes 276488 | tf_op jit(solution)/shard_map/ppermute | solution.py:537

commit v9 on v8

--- a/solution.py
+++ b/solution.py
@@ -33,6 +33,7 @@
 
 PIECE = 384
 PIECES = 2 * INNER // PIECE
+CUTS = 3
 
 
 def fetch(pairs, sems):
@@ -43,9 +44,10 @@
 
 
 def weight_pieces(weight_ref, weight):
+    part = PIECE // CUTS
     return [
-        (weight_ref.at[pl.ds(INNER + PIECE * p, PIECE)], weight.at[pl.ds(PIECE * p, PIECE)])
-        for p in range(PIECES)
+        (weight_ref.at[pl.ds(INNER + part * p, part)], weight.at[pl.ds(part * p, part)])
+        for p in range(PIECES * CUTS)
     ]
 
 
@@ -59,7 +61,8 @@
     copies[0].wait()
     copies[1].wait()
     for p in range(PIECES):
-        copies[2 + p].wait()
+        for copy in copies[2 + CUTS * p : 2 + CUTS * (p + 1)]:
+            copy.wait()
         lanes = slice(PIECE * p, PIECE * (p + 1))
         part = nt_dot(tokens[...], weight[lanes]).astype(jnp.bfloat16)
         top_ref[:, lanes] = part[:edge]
@@ -73,7 +76,8 @@
     copies = fetch(pairs + [(weight_ref.at[pl.ds(0, INNER)], q_weight)], sems)
     copies[0].wait()
     for p in range(PIECES):
-        copies[1 + p].wait()
+        for copy in copies[1 + CUTS * p : 1 + CUTS * (p + 1)]:
+            copy.wait()
         lanes = slice(PIECE * p, PIECE * (p + 1))
         part = nt_dot(tokens[...], weight[lanes])
         kv_ref[:, lanes] = part.astype(jnp.bfloat16)
@@ -81,7 +85,7 @@
         is_right = own_ref[0].astype(jnp.float32)
         near = grid[:, :REACH] * is_right + grid[:, -REACH:] * (1.0 - is_right)
         near_ref[:, lanes] = near.reshape(-1, PIECE).astype(jnp.bfloat16)
-    copies[1 + PIECES].wait()
+    copies[-1].wait()
     qt_ref[...] = nt_dot(q_weight[...], tokens[...]).astype(jnp.bfloat16)
 
 
@@ -101,7 +105,7 @@
         scratch_shapes=[
             pltpu.VMEM((2 * edge, width), jnp.bfloat16),
             pltpu.VMEM((2 * INNER, width), jnp.bfloat16),
-            pltpu.SemaphoreType.DMA((PIECES + 2,)),
+            pltpu.SemaphoreType.DMA((PIECES * CUTS + 2,)),
         ],
         compiler_params=pltpu.CompilerParams(vmem_limit_bytes=56 * 1024 * 1024),
         cost_estimate=LIGHT,
@@ -118,9 +122,9 @@
             pltpu.VMEM((rows, width), jnp.bfloat16),
             pltpu.VMEM((2 * INNER, width), jnp.bfloat16),
             pltpu.VMEM((INNER, width), jnp.bfloat16),
-            pltpu.SemaphoreType.DMA((PIECES + 2,)),
+            pltpu.SemaphoreType.DMA((PIECES * CUTS + 2,)),
         ],
-        compiler_params=pltpu.CompilerParams(vmem_limit_bytes=24 * 1024 * 1024),
+        compiler_params=pltpu.CompilerParams(vmem_limit_bytes=56 * 1024 * 1024),
         cost_estimate=LIGHT,
         name="project",
     )(own, top, token_rows, weight.T)
@@ -129,6 +133,9 @@
 
 def attention_kernel(
     start_ref,
+    core_ref,
+    tokens_ref,
+    upstream_ref,
     qt_ref,
     own_ref,
     g_ref,
@@ -143,11 +150,16 @@
     edge_ref,
     side_ref,
     corner_grad_ref,
+    sent_ref,
+    kept_ref,
     kv,
     kvt,
     acc,
     ot,
     dqt,
+    left,
+    turned,
+    sems,
 ):
     strips = bias_ref.shape[0]
     chunk = kv.shape[1]
@@ -166,6 +178,7 @@
             part = jnp.concatenate([part, filler], axis=0)
         kvt[slot, :, first : first + count] = part.T[:, :count]
 
+    copies = fetch([(tokens_ref, left.at[0]), (upstream_ref, left.at[1])], sems)
     dqt[INNER:, :] = jnp.zeros((64, chunk_own), jnp.float32)
     ot[:64, :] = jnp.zeros((64, chunk_own), jnp.float32)
     for s in range(strips):
@@ -254,9 +267,26 @@
             acc[pl.ds(top, 3), :, k_lanes[i]] += dk.reshape(3, chunk, SLAB)
         o_ref[rows, :] = ot[...].T.astype(jnp.bfloat16)
         dq_ref[rows, :] = dqt[...].T.astype(jnp.bfloat16)
+        for side in range(2):
+            turned[side, :, rows] = left[side, rows, :].T
         return carry
 
+    for copy in copies:
+        copy.wait()
     lax.fori_loop(0, strips, strip, 0)
+    share = sent_ref.shape[0] // 4
+    for out_ref, half in ((sent_ref, 1 - core_ref[0]), (kept_ref, core_ref[0])):
+        products = []
+        for side, right in enumerate((dq_ref, o_ref)):
+            picked = [
+                turned[side, pl.ds(pl.multiple_of((2 * r + half) * share, 16), share), :]
+                for r in range(4)
+            ]
+            products.append(dot(jnp.concatenate(picked, axis=0), right[...]))
+        first, second = products
+        out_ref[:, :512] = first[:, :512].astype(jnp.bfloat16)
+        out_ref[:, 512:640] = (first[:, 512:] + second[:, :128]).astype(jnp.bfloat16)
+        out_ref[:, 640:] = second[:, 128:].astype(jnp.bfloat16)
     for slot, at in enumerate(side_order):
         own_grad = acc[slot, :chunk_own].astype(jnp.bfloat16)
         if at < strips:
@@ -271,11 +301,13 @@
             corner_grad_ref[chunk_side * at : chunk_side * (at + 1), :] = side_grad
 
 
-def attention(start, queries, own, grads, above, below, cols, corner, bias):
+def attention(start, token_rows, grad_rows, queries, own, grads, above, below, cols, corner, bias):
     strips, band, chunk_own = bias.shape
     chunk = band // 3
     token_count, width = own.shape
-    whole = lambda a: pl.BlockSpec(a.shape, lambda _: (0,) * a.ndim)
+    whole = lambda a: pl.BlockSpec(
+        a.shape, lambda _: (0,) * a.ndim, pipeline_mode=pl.Buffered(1)
+    )
     outs = (
         jax.ShapeDtypeStruct((token_count, INNER + 64), jnp.bfloat16),
         jax.ShapeDtypeStruct((token_count, INNER + 64), jnp.bfloat16),
@@ -283,13 +315,19 @@
         jax.ShapeDtypeStruct((2 * chunk_own, width), jnp.bfloat16),
         jax.ShapeDtypeStruct(cols.shape, jnp.bfloat16),
         jax.ShapeDtypeStruct(corner.shape, jnp.bfloat16),
+        jax.ShapeDtypeStruct((token_rows.shape[1] // 2, width), jnp.bfloat16),
+        jax.ShapeDtypeStruct((token_rows.shape[1] // 2, width), jnp.bfloat16),
     )
+    core = lax.axis_index("col").astype(jnp.int32).reshape(1) % 2
     return pl.pallas_call(
         attention_kernel,
         grid=(1,),
         out_shape=outs,
         in_specs=[
             pl.BlockSpec(memory_space=pltpu.SMEM),
+            pl.BlockSpec(memory_space=pltpu.SMEM),
+            pl.BlockSpec(memory_space=pl.ANY),
+            pl.BlockSpec(memory_space=pl.ANY),
             whole(queries),
             whole(own),
             whole(grads),
@@ -306,56 +344,18 @@
             pltpu.VMEM((strips + 2, chunk, width), jnp.float32),
             pltpu.VMEM((640, chunk_own), jnp.float32),
             pltpu.VMEM((640, chunk_own), jnp.float32),
+            pltpu.VMEM((2,) + token_rows.shape, jnp.bfloat16),
+            pltpu.VMEM((2,) + token_rows.shape[::-1], jnp.bfloat16),
+            pltpu.SemaphoreType.DMA((2,)),
         ],
-        compiler_params=pltpu.CompilerParams(vmem_limit_bytes=36 * 1024 * 1024),
+        compiler_params=pltpu.CompilerParams(vmem_limit_bytes=34 * 1024 * 1024),
         cost_estimate=pl.CostEstimate(
             flops=12 * token_count * band * 2 * INNER,
             bytes_accessed=16 * 1024 * 1024,
             transcendentals=token_count * band * H,
         ),
         name="window_attention",
-    )(start, queries, own, grads, above, below, cols, corner, bias)
-
-
-def outer_kernel(own_ref, *refs):
-    pairs = (len(refs) - 3) // 2
-    operands, (sent_ref, kept_ref, turned) = refs[: 2 * pairs], refs[2 * pairs :]
-    share = sent_ref.shape[0] // 4
-    for p in range(pairs):
-        turned[p] = operands[2 * p][...].T
-    for out_ref, half in ((sent_ref, 1 - own_ref[0]), (kept_ref, own_ref[0])):
-        products = []
-        for p in range(pairs):
-            picked = [
-                turned[p, pl.ds(pl.multiple_of((2 * r + half) * share, 16), share), :]
-                for r in range(4)
-            ]
-            products.append(dot(jnp.concatenate(picked, axis=0), operands[2 * p + 1][...]))
-        if pairs == 1:
-            out_ref[...] = products[0].astype(jnp.bfloat16)
-        else:
-            first, second = products
-            out_ref[:, :512] = first[:, :512].astype(jnp.bfloat16)
-            out_ref[:, 512:640] = (first[:, 512:] + second[:, :128]).astype(jnp.bfloat16)
-            out_ref[:, 640:] = second[:, 128:].astype(jnp.bfloat16)
-
-
-def outer_halves(*operands):
-    rows, width = operands[0].shape
-    whole = lambda a: pl.BlockSpec(a.shape, lambda _: (0,) * a.ndim)
-    out = jax.ShapeDtypeStruct((width // 2, 2 * INNER), jnp.bfloat16)
-    own = lax.axis_index("col").astype(jnp.int32).reshape(1)
-    return pl.pallas_call(
-        outer_kernel,
-        grid=(1,),
-        out_shape=(out, out),
-        in_specs=[pl.BlockSpec(memory_space=pltpu.SMEM)] + [whole(a) for a in operands],
-        out_specs=(whole(out), whole(out)),
-        scratch_shapes=[pltpu.VMEM((len(operands) // 2, width, rows), jnp.bfloat16)],
-        compiler_params=pltpu.CompilerParams(vmem_limit_bytes=22 * 1024 * 1024),
-        cost_estimate=LIGHT,
-        name="weight_grad_halves",
-    )(own, *operands)
+    )(start, core, token_rows, grad_rows, queries, own, grads, above, below, cols, corner, bias)
 
 
 def late_kernel(
@@ -466,6 +466,37 @@
         cost_estimate=LIGHT,
         name="row_sum",
     )(*parts, earlier)
+
+
+def outputs_kernel(own_ref, *refs):
+    parts, (qkv_ref, out_ref, early, late) = refs[:8], refs[8:]
+    share = qkv_ref.shape[0]
+    small = parts[0].shape[0]
+    for step in range(4):
+        first = pl.multiple_of((own_ref[0] ^ step) * small, 8)
+        early[pl.ds(first, small), :] = parts[step][...].astype(jnp.float32)
+        late[pl.ds(first, small), :] = parts[4 + step][...].astype(jnp.float32)
+    qkv_ref[...] = jnp.concatenate([early[:share, :INNER], late[:share]], axis=1)
+    out_ref[...] = early[:share, INNER:]
+
+
+def written_outputs(early, late, share):
+    small, width = early[0].shape
+    parts = early + late
+    own = lax.axis_index("img").astype(jnp.int32).reshape(1)
+    shapes = [(share, 3 * INNER), (share, INNER)]
+    return pl.pallas_call(
+        outputs_kernel,
+        grid=(1,),
+        out_shape=[jax.ShapeDtypeStruct(shape, jnp.float32) for shape in shapes],
+        in_specs=[pl.BlockSpec(memory_space=pltpu.SMEM)]
+        + [pl.BlockSpec((small, width), lambda _: (0, 0))] * len(parts),
+        out_specs=[pl.BlockSpec(shape, lambda _: (0, 0)) for shape in shapes],
+        scratch_shapes=[pltpu.VMEM((len(early) * small, width), jnp.float32)] * 2,
+        compiler_params=pltpu.CompilerParams(vmem_limit_bytes=16 * 1024 * 1024),
+        cost_estimate=LIGHT,
+        name="weight_grads",
+    )(own, *parts)
 
 
 def window_starts(places, extent):
@@ -528,24 +559,8 @@
     return total.astype(jnp.bfloat16)
 
 
-def gathered(block, axis):
-    own = lax.axis_index(axis)
-    count = lax.axis_size(axis)
-    whole = jnp.zeros((count,) + block.shape, block.dtype)
-    whole = lax.dynamic_update_index_in_dim(whole, block, own, 0)
-    for step in range(1, count):
-        got = lax.ppermute(block, axis, [(i, i ^ step) for i in range(count)])
-        whole = lax.dynamic_update_index_in_dim(whole, got, own ^ step, 0)
-    return whole
-
-
 def row_parts(held):
     return cut(held, "row", lambda h, r: lax.dynamic_index_in_dim(h, r, 0, keepdims=False))
-
-
-def whole_share(held, share):
-    whole = gathered(held, "img")
-    return whole.reshape(-1, held.shape[1])[:share].astype(jnp.float32)
 
 
 def plain_shares(part):
@@ -600,8 +615,8 @@
         out_weight, grad_rows, (((0,), (1,)), ((), ())), preferred_element_type=jnp.float32
     ).astype(jnp.bfloat16)
     start, bias = window_bias(tile_rows, tile_cols, two_columns)
-    attended, dquery, inner_grad, edge_grad, side_grad, corner_grad = attention(
-        start, queries, keyvals, grad_att, above, below, cols, corner, bias
+    attended, dquery, inner_grad, edge_grad, side_grad, corner_grad, sent, kept = attention(
+        start, token_rows, grad_rows, queries, keyvals, grad_att, above, below, cols, corner, bias
     )
 
     def outer(a, b):
@@ -611,7 +626,7 @@
 
     simple = two_columns and row_count == 4 and lax.axis_size("img") == 4
     if simple:
-        early = core_parts(*outer_halves(token_rows, dquery, grad_rows, attended))
+        early = core_parts(sent, kept)
     def outputs(attended, dqkv):
         sublayer_out = nt_dot(attended, out_weight).astype(jnp.bfloat16)
         return sublayer_out, nt_dot(dqkv, qkv_weight).astype(jnp.bfloat16)
@@ -656,20 +671,25 @@
         early = added(early[0], exchanged(early, "img"))
         sublayer_out, tokens_grad = outputs(attended, dqkv)
         late = core_parts(sent, kept, early, sublayer_out, tokens_grad)
-        late = added(late[0], exchanged(late, "img"), early)
-        early = row_sum_after(row_parts(early), late)
+        late_got = exchanged(late, "img")
+        late = added(late[0], late_got, early)
+        early = row_sum_after(row_parts(early), late_got[0])
         late = row_parts(late)
         late = added(late[0], exchanged(late, "row"), early)
         share = width // (row_count * col_count)
-        early, late = whole_share(early, share), whole_share(late, share)
+        early = [early] + exchanged([early] * 4, "img")
+        late = [late] + exchanged([late] * 4, "img")
+        qkv_grad, out_grad = written_outputs(early, late, share)
     else:
         early = jnp.concatenate([outer(token_rows, dquery), outer(grad_rows, attended)], axis=1)
         early, late = plain_shares(early), plain_shares(outer(token_rows, dkv))
+        qkv_grad = jnp.concatenate([early[:, :INNER], late], axis=1)
+        out_grad = early[:, INNER:]
     return (
         sublayer_out.reshape(tokens.shape),
         tokens_grad.reshape(tokens.shape),
-        jnp.concatenate([early[:, :INNER], late], axis=1),
-        early[:, INNER:],
+        qkv_grad,
+        out_grad,
     )
 
 

time: 118 us -> 113 us (0.958)
  local copies, waits for them, and re-layouts: 10.7 us -> 6.49 us
  waiting for transfers between devices: 23.8 us -> 22.4 us
  Pallas kernels: 32.1 us -> 33.5 us
  other arithmetic: 3.88 us -> 2.55 us
    ppermute x12 -> x18, starting transfers between devices: 19.9 us -> 27.7 us  [exchanged(): got.append(lax.ppermute(part, axis, pairs))]
    ppermute x6 -> x0, starting transfers between devices: 7.12 us -> none  [gathered(): got = lax.ppermute(block, axis, [(i, i ^ step) for i in range(count)])]
    ppermute x6 -> x0, waiting for transfers between devices: 3.86 us -> none  [gathered(): got = lax.ppermute(block, axis, [(i, i ^ step) for i in range(count)])]
    unnamed x41 -> x39, local copies, waits for them, and re-layouts: 8.2 us -> 5.08 us
    pallas_call x1, Pallas kernels: 3.63 us -> 1.41 us  [written_outputs(): pl.pallas_call(outputs_kernel, grid=(1,), out_shape=[jax.ShapeDtypeStruct...]
    pallas_call x1, Pallas kernels: 13.2 us -> 15.4 us  [attention(): pl.pallas_call(attention_kernel, grid=(1,), out_shape=outs, in_specs=[pl....]
    ppermute x12 -> x18, waiting for transfers between devices: 17.2 us -> 19 us  [exchanged(): got.append(lax.ppermute(part, axis, pairs))]
    pallas_call x1, Pallas kernels: 4.52 us -> 5.99 us  [project(): pl.pallas_call(project_kernel, grid=(1,), out_shape=[jax.ShapeDtypeStruct...]
  transfers between devices with their start and end apart: 28 -> 28, of which waited for: 12 -> 11; matrix products, arithmetic and copies ran while one was open for 8% -> 8% of each run, Pallas kernels for 12% -> 10%
where the time goes in v9:
time: 113 us; the launch traced here: 112 us
  starting transfers between devices  41.6 us (37%)
  Pallas kernels  33.5 us (30%)
  waiting for transfers between devices  22.4 us (20%)
  local copies, waits for them, and re-layouts  6.49 us (6%)
  matrix products  4.67 us (4%)
  other arithmetic  2.55 us (2%)
    ppermute x18, starting transfers between devices, exchanged(): got.append(lax.ppermute(part, axis, pairs))  27.7 us
    ppermute x18, waiting for transfers between devices, exchanged(): got.append(lax.ppermute(part, axis, pairs))  19 us
    pallas_call x1, Pallas kernels, attention(): pl.pallas_call(attention_kernel, grid=(1,), out_shape=outs, in_specs=[pl....  15.4 us
    ppermute x8, starting transfers between devices, moved(): return lax.ppermute(block, ('row', 'col'), pairs)  13.8 us
    pallas_call x1, Pallas kernels, project(): pl.pallas_call(project_kernel, grid=(1,), out_shape=[jax.ShapeDtypeStruct...  5.99 us
    unnamed x39, local copies, waits for them, and re-layouts  5.08 us
    pallas_call x1, Pallas kernels, project(): pl.pallas_call(edges_kernel, grid=(1,), out_shape=[shape(edge)] * 2, in_s...  3.88 us
    dot_general x2, matrix products, nt_dot(): lax.dot_general(a, b, (((1,), (1,)), ((), ())), preferred_element_type=jn...  3.71 us
  transfers between devices with their start and end apart: 28, of which 11 were waited for; matrix products, arithmetic and copies ran while one was open for 8% of the time, Pallas kernels for 10%

profile of v9, /device:TPU:0, one launch (start us, length us, event | category | flops | bytes accessed | tf_op | source)
XLA Modules:
  0.0 112.3 jit_solution(6307021283371492676)
XLA Ops:
  0.6 3.9 %project_edges.1 = (bf16[128,1152]{1,0:T(8,128)(2,1)}, bf16[128,1152]{1,0:T(8,128)(2,1)}) custom-call(bf16[512,1152]{1,0:T(8,128)(2,1)} %bitcast.38, bf16[1728,1152]{1,0:T(8,128)(2,1)} %bitcast.49), custom_call_target="tpu_custom_call" | custom-call | flops 1 | bytes 1 | tf_op jit(solution)/shard_map/project_edges/pallas_call | solution.py:99
  4.5 1.3 %collective-permute-start.1 = (bf16[128,1152]{1,0:T(8,128)(2,1)}, bf16[128,1152]{1,0:T(8,128)(2,1)S(1)}, u32[]{:S(2)}, u32[]{:S(2)}) collective-permute-start(bf16[128,1152]{1,0:T(8,128)(2,1)} %get-tuple-element.33.top_ref), channel_id=1, source_target_pairs={{2,0},{3,1},{4,2},{5,3},{6,4},{7,5},{10,8},{11,9},{12,10},{13,11},... | collective-permute-start | bytes 884744 | tf_op jit(solution)/shard_map/ppermute | solution.py:590
  5.8 5.6 %collective-permute-start = (bf16[128,1152]{1,0:T(8,128)(2,1)}, bf16[128,1152]{1,0:T(8,128)(2,1)S(1)}, u32[]{:S(2)}, u32[]{:S(2)}) collective-permute-start(bf16[128,1152]{1,0:T(8,128)(2,1)} %get-tuple-element.36), channel_id=1, source_target_pairs={{0,2},{1,3},{2,4},{3,5},{4,6},{5,7},{8,10},{9,11},{10,12},{11,13},... | collective-permute-start | bytes 884744 | tf_op jit(solution)/shard_map/ppermute | solution.py:590
  11.4 6.0 %project.1 = (bf16[576,512]{1,0:T(8,128)(2,1)}, bf16[512,1152]{1,0:T(8,128)(2,1)}, bf16[256,1152]{1,0:T(8,128)(2,1)}) custom-call(s32[1]{0:T(128)} %bitcast.own_ref, bf16[128,1152]{1,0:T(8,128)(2,1)} %get-tuple-element.33.top_ref, bf16[512,1152]{1,0:T(8,128)(2,1)} %bitcast.39, bf16[1728,1152]{1,0:T(8,128)(2,1)} %bitcast.50), custom_call_target="tpu_custom_call" | custom-call | flops 1 | bytes 1 | tf_op jit(solution)/shard_map/project/pallas_call | solution.py:115
  17.6 0.1 tile.13
  17.6 0.1 tile.11
  17.8 0.1 reshape.181
  17.9 0.1 reshape.182
  18.1 0.1 fusion.4
  18.5 0.4 fusion.3.bias_ref
  19.0 0.5 collective-permute-start.3
  19.5 0.1 copy-done.11
  19.6 0.1 copy-done.13
  19.7 1.0 convolution_convert_fusion.2.g_ref
  20.7 0.8 copy-done.16
  21.6 1.1 copy-done.17
  22.7 15.4 %window_attention.1 = (bf16[512,640]{1,0:T(8,128)(2,1)S(1)}, bf16[512,640]{1,0:T(8,128)(2,1)S(1)}, bf16[512,1152]{1,0:T(8,128)(2,1)S(1)}, bf16[256,1152]{1,0:T(8...) custom-call(s32[4]{0:T(128)S(1)} %broadcast_subtract_fusion.start_re, ...), custom_call_target="tpu_custom_call" | custom-call | flops 4076863488 | bytes 16777216 | tf_op jit(solution)/shard_map/window_attention/pallas_call | solution.py:322
  38.0 0.8 copy-done.8
  38.9 0.5 collective-permute-start.6
  39.4 0.5 collective-permute-start.5
  39.8 0.7 collective-permute-done.6
  40.6 0.1 pad_select_fusion
  40.7 0.1 fusion
  40.8 0.9 fusion.5
  41.7 3.9 %collective-permute-start.7 = (bf16[128,1152]{1,0:T(8,128)(2,1)}, bf16[128,1152]{1,0:T(8,128)(2,1)S(1)}, u32[]{:S(2)}, u32[]{:S(2)}) collective-permute-start(bf16[128,1152]{1,0:T(8,128)(2,1)} %get-tuple-element.63), channel_id=1, source_target_pairs={{0,2},{1,3},{2,4},{3,5},{4,6},{5,7},{8,10},{9,11},{10,12},{11,13},... | collective-permute-start | bytes 884744 | tf_op jit(solution)/shard_map/ppermute | solution.py:590
  45.6 1.5 %collective-permute-start.8 = (bf16[128,1152]{1,0:T(8,128)(2,1)}, bf16[128,1152]{1,0:T(8,128)(2,1)}, u32[]{:S(2)}, u32[]{:S(2)}) collective-permute-start(bf16[128,1152]{1,0:T(8,128)(2,1)} %get-tuple-element.62), channel_id=1, source_target_pairs={{2,0},{3,1},{4,2},{5,3},{6,4},{7,5},{10,8},{11,9},{12,10},{13,11},... | collective-permute-start | bytes 884744 | tf_op jit(solution)/shard_map/ppermute | solution.py:590
  47.1 1.3 %copy-done.3 = bf16[576,1152]{1,0:T(8,128)(2,1)S(1)} copy-done((bf16[576,1152]{1,0:T(8,128)(2,1)S(1)}, bf16[576,1152]{1,0:T(8,128)(2,1)}, u32[]{:S(2)}) %copy-start.3) | copy-done | bytes 1327128
  48.4 2.0 %core_parts.2 = (bf16[4,40,1152]{2,1,0:T(8,128)(2,1)S(1)}, bf16[4,40,1152]{2,1,0:T(8,128)(2,1)S(1)}, bf16[4,40,1152]{2,1,0:T(8,128)(2,1)S(1)}, bf16[4,40,1152]{2,1,0:T(8,128)(2,1)S(1)}) custom-call(s32[1]{0:T(128)} %bitcast.1.own_ref, bf16[576,1152]{1,0:T(8,128)(2,1)S(1)} %copy-done.3, bf16[576,1152]{1,0:T(8,128)(2,1)} %collective-permute-done.4.got_ref), custom_call_target="tpu_custom_call" | custom-call | flops 1 | bytes 1 | tf_op jit(solution)/shard_map/core_parts/pallas_call | solution.py:435
  50.4 1.6 %collective-permute-start.10 = (bf16[4,40,1152]{2,1,0:T(8,128)(2,1)S(1)}, bf16[4,40,1152]{2,1,0:T(8,128)(2,1)S(1)}, u32[]{:S(2)}, u32[]{:S(2)}) collective-permute-start(bf16[4,40,1152]{2,1,0:T(8,128)(2,1)S(1)} %get-tuple-element.41.second), channel_id=1, source_target_pairs={{0,16},{8,24},{16,0},{24,8},{1,17},{9,25},{17,1},{25,9},{2,18},{10... | collective-permute-start | bytes 1105928 | tf_op jit(solution)/shard_map/ppermute | solution.py:549
  52.0 1.4 %collective-permute-start.11 = (bf16[4,40,1152]{2,1,0:T(8,128)(2,1)S(1)}, bf16[4,40,1152]{2,1,0:T(8,128)(2,1)S(1)}, u32[]{:S(2)}, u32[]{:S(2)}) collective-permute-start(bf16[4,40,1152]{2,1,0:T(8,128)(2,1)S(1)} %get-tuple-element.42.third), channel_id=1, source_target_pairs={{0,24},{8,16},{16,8},{24,0},{1,25},{9,17},{17,9},{25,1},{2,26},{10... | collective-permute-start | bytes 1105928 | tf_op jit(solution)/shard_map/ppermute | solution.py:549
  53.5 0.7 collective-permute-start.9
  54.2 2.6 %collective-permute-done.8.below_ref = bf16[128,1152]{1,0:T(8,128)(2,1)} collective-permute-done((bf16[128,1152]{1,0:T(8,128)(2,1)}, bf16[128,1152]{1,0:T(8,128)(2,1)}, u32[]{:S(2)}, u32[]{:S(2)}) %collective-permute-start.8) | collective-permute-done | bytes 294944 | tf_op jit(solution)/shard_map/ppermute | solution.py:590
  56.8 3.4 %late_weight_grad_halves.1 = (bf16[576,1152]{1,0:T(8,128)(2,1)S(1)}, bf16[576,1152]{1,0:T(8,128)(2,1)S(1)}, bf16[512,1728]{1,0:T(8,128)(2,1)S(1)}, bf16[512,576]{1,0:T(8,128)(2,1)S(1)}) custom-call(s32[1]{0:T(128)} %bitcast.own_ref, bf16[4,40,1152]{2,1,0:T(8,128)(2,1)S(1)} %get-tuple-element.40.first, bf16[4,40,1152]{2,1,0:T(8,128)(2,1)S(1)} %get-tuple-element.41.second, ...), custom_call_target="tpu_custom_call" | custom-call | flops 1 | bytes 1 | tf_op jit(solution)/shard_map/late_weight_grad_halves/pallas_call | solution.py:398
  60.3 2.5 %convolution_convert_fusion.refs_2_ = bf16[512,1152]{1,0:T(8,128)(2,1)S(1)} fusion(bf16[512,1728]{1,0:T(8,128)(2,1)S(1)} %get-tuple-element.50, bf16[1152,1728]{0,1:T(8,128)(2,1)S(1)} %copy-done.18), kind=kOutput, calls=%fused_computation | convolution fusion | flops 2039021568 | bytes 6930432 | tf_op jit(solution)/shard_map/dot_general | solution.py:31
  62.9 1.2 %convolution_convert_fusion.1.refs_1_ = bf16[512,1152]{1,0:T(8,128)(2,1)S(1)} fusion(bf16[512,576]{1,0:T(8,128)(2,1)S(1)} %get-tuple-element.49, bf16[1152,576]{0,1:T(8,128)(2,1)S(1)} %copy-done), kind=kOutput, calls=%fused_computation.1 | convolution fusion | flops 680067072 | bytes 3096576 | tf_op jit(solution)/shard_map/dot_general | solution.py:31
  64.1 4.9 %collective-permute-done.10 = bf16[4,40,1152]{2,1,0:T(8,128)(2,1)S(1)} collective-permute-done((bf16[4,40,1152]{2,1,0:T(8,128)(2,1)S(1)}, bf16[4,40,1152]{2,1,0:T(8,128)(2,1)S(1)}, u32[]{:S(2)}, u32[]{:S(2)}) %collective-permute-start.10) | collective-permute-done | bytes 368672 | tf_op jit(solution)/shard_map/ppermute | solution.py:549
  69.0 1.2 %collective-permute-done.9 = bf16[4,40,1152]{2,1,0:T(8,128)(2,1)S(1)} collective-permute-done((bf16[4,40,1152]{2,1,0:T(8,128)(2,1)S(1)}, bf16[4,40,1152]{2,1,0:T(8,128)(2,1)S(1)}, u32[]{:S(2)}, u32[]{:S(2)}) %collective-permute-start.9) | collective-permute-done | bytes 368672 | tf_op jit(solution)/shard_map/ppermute | solution.py:549
  70.2 0.2 add_convert_fusion.1.refs_0_
  70.4 1.4 %core_parts.3 = (bf16[4,40,1152]{2,1,0:T(8,128)(2,1)S(1)}, bf16[4,40,1152]{2,1,0:T(8,128)(2,1)}, bf16[4,40,1152]{2,1,0:T(8,128)(2,1)}, bf16[4,40,1152]{2,1,0:T(8,128)(2,1)}) custom-call(s32[1]{0:T(128)} %bitcast.1.own_ref, bf16[576,1152]{1,0:T(8,128)(2,1)S(1)} %get-tuple-element.52.kept_ref, bf16[576,1152]{1,0:T(8,128)(2,1)S(1)} %collective-permute-done.15.got_ref, ...), custom_call_target="tpu_custom_call" | custom-call | flops 1 | bytes 1 | tf_op jit(solution)/shard_map/core_parts/pallas_call | solution.py:435
  71.9 0.7 copy-done.10
  72.6 1.5 %collective-permute-start.16 = (bf16[4,40,1152]{2,1,0:T(8,128)(2,1)}, bf16[4,40,1152]{2,1,0:T(8,128)(2,1)S(1)}, u32[]{:S(2)}, u32[]{:S(2)}) collective-permute-start(bf16[4,40,1152]{2,1,0:T(8,128)(2,1)} %get-tuple-element.54), channel_id=1, source_target_pairs={{0,8},{8,0},{16,24},{24,16},{1,9},{9,1},{17,25},{25,17},{2,10},{10... | collective-permute-start | bytes 1105928 | tf_op jit(solution)/shard_map/ppermute | solution.py:549
  74.1 1.5 %collective-permute-start.20 = (bf16[4,40,1152]{2,1,0:T(8,128)(2,1)}, bf16[4,40,1152]{2,1,0:T(8,128)(2,1)S(1)}, u32[]{:S(2)}, u32[]{:S(2)}) collective-permute-start(bf16[4,40,1152]{2,1,0:T(8,128)(2,1)} %get-tuple-element.57), channel_id=1, source_target_pairs={{0,16},{8,24},{16,0},{24,8},{1,17},{9,25},{17,1},{25,9},{2,18},{10... | collective-permute-start | bytes 1105928 | tf_op jit(solution)/shard_map/ppermute | solution.py:549
  75.6 0.5 collective-permute-start.21
  76.2 2.4 %collective-permute-start.12 = (bf16[40,1152]{1,0:T(8,128)(2,1)S(1)}, bf16[40,1152]{1,0:T(8,128)(2,1)S(1)}, u32[]{:S(2)}, u32[]{:S(2)}) collective-permute-start(bf16[40,1152]{1,0:T(8,128)(2,1)S(1)} %get-tuple-element.70), channel_id=1, source_target_pairs={{0,2},{2,0},{4,6},{6,4},{1,3},{3,1},{5,7},{7,5},{8,10},{10,8},{12,... | collective-permute-start | bytes 276488 | tf_op jit(solution)/shard_map/ppermute | solution.py:549
  78.6 2.3 %collective-permute-start.13 = (bf16[40,1152]{1,0:T(8,128)(2,1)S(1)}, bf16[40,1152]{1,0:T(8,128)(2,1)S(1)}, u32[]{:S(2)}, u32[]{:S(2)}) collective-permute-start(bf16[40,1152]{1,0:T(8,128)(2,1)S(1)} %get-tuple-element.69), channel_id=1, source_target_pairs={{0,4},{2,6},{4,0},{6,2},{1,5},{3,7},{5,1},{7,3},{8,12},{10,14},{12... | collective-permute-start | bytes 276488 | tf_op jit(solution)/shard_map/ppermute | solution.py:549
  80.9 3.5 %collective-permute-done.16.refs_0_ = bf16[4,40,1152]{2,1,0:T(8,128)(2,1)S(1)} collective-permute-done((bf16[4,40,1152]{2,1,0:T(8,128)(2,1)}, bf16[4,40,1152]{2,1,0:T(8,128)(2,1)S(1)}, u32[]{:S(2)}, u32[]{:S(2)}) %collective-permute-start.16) | collective-permute-done | bytes 368672 | tf_op jit(solution)/shard_map/ppermute | solution.py:549
  84.4 4.1 %collective-permute-start.14 = (bf16[40,1152]{1,0:T(8,128)(2,1)S(1)}, bf16[40,1152]{1,0:T(8,128)(2,1)S(1)}, u32[]{:S(2)}, u32[]{:S(2)}) collective-permute-start(bf16[40,1152]{1,0:T(8,128)(2,1)S(1)} %get-tuple-element.68), channel_id=1, source_target_pairs={{0,6},{2,4},{4,2},{6,0},{1,7},{3,5},{5,3},{7,1},{8,14},{10,12},{12... | collective-permute-start | bytes 276488 | tf_op jit(solution)/shard_map/ppermute | solution.py:549
  88.5 3.0 %collective-permute-done.20 = bf16[4,40,1152]{2,1,0:T(8,128)(2,1)S(1)} collective-permute-done((bf16[4,40,1152]{2,1,0:T(8,128)(2,1)}, bf16[4,40,1152]{2,1,0:T(8,128)(2,1)S(1)}, u32[]{:S(2)}, u32[]{:S(2)}) %collective-permute-start.20) | collective-permute-done | bytes 368672 | tf_op jit(solution)/shard_map/ppermute | solution.py:549
  91.4 1.2 %add_convert_fusion = bf16[4,40,1152]{2,1,0:T(8,128)(2,1)S(1)} fusion(bf16[4,40,1152]{2,1,0:T(8,128)(2,1)S(1)} %collective-permute-done.21, bf16[4,40,1152]{2,1,0:T(8,128)(2,1)S(1)} %collective-permute-done.20, bf16[4,40,1152]{2,1,0:T(8,128)(2,1)S(1)} %collective-permute-done.16.refs_0_, bf16[4,40,1152]{2,1,0:T(8,128)(2,1)} %copy-done.10), kind=kLoop, calls=%fused_computation.11 | loop fusion | flops 1474560 | bytes 1843200 | tf_op jit(solution)/shard_map/convert_element_type | solution.py:559
  92.7 2.1 %collective-permute-start.22 = (bf16[40,1152]{1,0:T(8,128)(2,1)S(1)}, bf16[40,1152]{1,0:T(8,128)(2,1)S(1)}, u32[]{:S(2)}, u32[]{:S(2)}) collective-permute-start(bf16[40,1152]{1,0:T(8,128)(2,1)S(1)} %get-tuple-element.67), channel_id=1, source_target_pairs={{0,2},{2,0},{4,6},{6,4},{1,3},{3,1},{5,7},{7,5},{8,10},{10,8},{12,... | collective-permute-start | bytes 276488 | tf_op jit(solution)/shard_map/ppermute | solution.py:549
  94.8 2.1 %collective-permute-start.23 = (bf16[40,1152]{1,0:T(8,128)(2,1)S(1)}, bf16[40,1152]{1,0:T(8,128)(2,1)S(1)}, u32[]{:S(2)}, u32[]{:S(2)}) collective-permute-start(bf16[40,1152]{1,0:T(8,128)(2,1)S(1)} %get-tuple-element.66), channel_id=1, source_target_pairs={{0,4},{2,6},{4,0},{6,2},{1,5},{3,7},{5,1},{7,3},{8,12},{10,14},{12... | collective-permute-start | bytes 276488 | tf_op jit(solution)/shard_map/ppermute | solution.py:549
  96.8 0.4 collective-permute-start.24
  97.3 1.3 %collective-permute-start.17 = (bf16[40,1152]{1,0:T(8,128)(2,1)S(1)}, bf16[40,1152]{1,0:T(8,128)(2,1)S(1)}, u32[]{:S(2)}, u32[]{:S(2)}) collective-permute-start(bf16[40,1152]{1,0:T(8,128)(2,1)S(1)} %row_sum.1.refs_0_), channel_id=1, source_target_pairs={{0,8},{8,0},{16,24},{24,16},{1,9},{9,1},{17,25},{25,17},{2,10},{10... | collective-permute-start | bytes 276488 | tf_op jit(solution)/shard_map/ppermute | solution.py:549
  98.6 0.8 collective-permute-start.18
  99.4 1.4 %collective-permute-start.19 = (bf16[40,1152]{1,0:T(8,128)(2,1)S(1)}, bf16[40,1152]{1,0:T(8,128)(2,1)S(1)}, u32[]{:S(2)}, u32[]{:S(2)}) collective-permute-start(bf16[40,1152]{1,0:T(8,128)(2,1)S(1)} %row_sum.1.refs_0_), channel_id=1, source_target_pairs={{0,24},{8,16},{16,8},{24,0},{1,25},{9,17},{17,9},{25,1},{2,26},{10... | collective-permute-start | bytes 276488 | tf_op jit(solution)/shard_map/ppermute | solution.py:549
  100.9 0.6 collective-permute-done.23
  101.4 1.9 %collective-permute-done.24 = bf16[40,1152]{1,0:T(8,128)(2,1)S(1)} collective-permute-done((bf16[40,1152]{1,0:T(8,128)(2,1)S(1)}, bf16[40,1152]{1,0:T(8,128)(2,1)S(1)}, u32[]{:S(2)}, u32[]{:S(2)}) %collective-permute-start.24) | collective-permute-done | bytes 92192 | tf_op jit(solution)/shard_map/ppermute | solution.py:549
  103.4 1.3 %collective-permute-start.25 = (bf16[40,1152]{1,0:T(8,128)(2,1)S(1)}, bf16[40,1152]{1,0:T(8,128)(2,1)S(1)}, u32[]{:S(2)}, u32[]{:S(2)}) collective-permute-start(bf16[40,1152]{1,0:T(8,128)(2,1)S(1)} %add_convert_fusion.2.refs_4_), channel_id=1, source_target_pairs={{0,8},{8,0},{16,24},{24,16},{1,9},{9,1},{17,25},{25,17},{2,10},{10... | collective-permute-start | bytes 276488 | tf_op jit(solution)/shard_map/ppermute | solution.py:549
  104.7 0.8 collective-permute-start.26
  105.5 1.4 %collective-permute-start.27 = (bf16[40,1152]{1,0:T(8,128)(2,1)S(1)}, bf16[40,1152]{1,0:T(8,128)(2,1)S(1)}, u32[]{:S(2)}, u32[]{:S(2)}) collective-permute-start(bf16[40,1152]{1,0:T(8,128)(2,1)S(1)} %add_convert_fusion.2.refs_4_), channel_id=1, source_target_pairs={{0,24},{8,16},{16,8},{24,0},{1,25},{9,17},{17,9},{25,1},{2,26},{10... | collective-permute-start | bytes 276488 | tf_op jit(solution)/shard_map/ppermute | solution.py:549
  106.9 1.1 collective-permute-done.25.refs_5_
  108.0 1.2 %collective-permute-done.26.refs_6_ = bf16[40,1152]{1,0:T(8,128)(2,1)S(1)} collective-permute-done((bf16[40,1152]{1,0:T(8,128)(2,1)S(1)}, bf16[40,1152]{1,0:T(8,128)(2,1)S(1)}, u32[]{:S(2)}, u32[]{:S(2)}) %collective-permute-start.26) | collective-permute-done | bytes 92192 | tf_op jit(solution)/shard_map/ppermute | solution.py:549
  109.2 1.7 %collective-permute-done.27.refs_7_ = bf16[40,1152]{1,0:T(8,128)(2,1)S(1)} collective-permute-done((bf16[40,1152]{1,0:T(8,128)(2,1)S(1)}, bf16[40,1152]{1,0:T(8,128)(2,1)S(1)}, u32[]{:S(2)}, u32[]{:S(2)}) %collective-permute-start.27) | collective-permute-done | bytes 92192 | tf_op jit(solution)/shard_map/ppermute | solution.py:549
  110.9 1.4 %weight_grads.1 = (f32[144,1728]{1,0:T(8,128)}, f32[144,576]{1,0:T(8,128)}) custom-call(s32[1]{0:T(128)} %bitcast.1.own_ref, bf16[40,1152]{1,0:T(8,128)(2,1)S(1)} %row_sum.1.refs_0_, bf16[40,1152]{1,0:T(8,128)(2,1)S(1)} %collective-permute-done.17.refs_1_, bf16[40,1152]{1,0:T(8,128)(2,1)S(1)} %collective-permute-done.18.refs_2_, ...), custom_call_target="tpu_custom_call" | custom-call | flops 1 | bytes 1 | tf_op jit(solution)/shard_map/weight_grads/pallas_call | solution.py:488
  (79 shorter events, 1.1 us)
Async XLA Ops:
  0.6 19.0 %copy-start = (bf16[1152,576]{0,1:T(8,128)(2,1)S(1)}, bf16[1152,576]{0,1:T(8,128)(2,1)}, u32[]{:S(2)}) copy-start(bf16[1152,576]{0,1:T(8,128)(2,1)} %param.6) | copy-start | bytes 3981316
  4.5 14.3 %collective-permute-start.1 = (bf16[128,1152]{1,0:T(8,128)(2,1)}, bf16[128,1152]{1,0:T(8,128)(2,1)S(1)}, u32[]{:S(2)}, u32[]{:S(2)}) collective-permute-start(bf16[128,1152]{1,0:T(8,128)(2,1)} %get-tuple-element.33.top_ref), channel_id=1, source_target_pairs={{2,0},{3,1},{4,2},{5,3},{6,4},{7,5},{10,8},{11,9},{12,10},{13,11},... | collective-permute-start | bytes 884744 | tf_op jit(solution)/shard_map/ppermute | solution.py:590
  5.8 13.1 %collective-permute-start = (bf16[128,1152]{1,0:T(8,128)(2,1)}, bf16[128,1152]{1,0:T(8,128)(2,1)S(1)}, u32[]{:S(2)}, u32[]{:S(2)}) collective-permute-start(bf16[128,1152]{1,0:T(8,128)(2,1)} %get-tuple-element.36), channel_id=1, source_target_pairs={{0,2},{1,3},{2,4},{3,5},{4,6},{5,7},{8,10},{9,11},{10,12},{11,13},... | collective-permute-start | bytes 884744 | tf_op jit(solution)/shard_map/ppermute | solution.py:590
  17.4 3.3 %collective-permute-start.2 = (bf16[256,1152]{1,0:T(8,128)(2,1)}, bf16[256,1152]{1,0:T(8,128)(2,1)S(1)}, u32[]{:S(2)}, u32[]{:S(2)}) collective-permute-start(bf16[256,1152]{1,0:T(8,128)(2,1)} %get-tuple-element.37), channel_id=1, source_target_pairs={{0,1},{1,0},{2,3},{3,2},{4,5},{5,4},{6,7},{7,6},{8,9},{9,8},{10,11... | collective-permute-start | bytes 1769480 | tf_op jit(solution)/shard_map/ppermute | solution.py:590
  18.5 1.3 %copy-start.13 = (bf16[1,32,16,1152]{3,2,1,0:T(8,128)(2,1)S(1)}, bf16[1,32,16,1152]{3,2,1,0:T(8,128)(2,1)}, u32[]{:S(2)}) copy-start(bf16[1,32,16,1152]{3,2,1,0:T(8,128)(2,1)} %param.7) | copy-start | bytes 3538948
  18.9 0.7 copy-start.11
  19.0 1.7 %collective-permute-start.3 = (bf16[16,8,1152]{2,1,0:T(8,128)(2,1)S(1)}, bf16[16,8,1152]{2,1,0:T(8,128)(2,1)S(1)}, u32[]{:S(2)}, u32[]{:S(2)}) collective-permute-start(bf16[16,8,1152]{2,1,0:T(8,128)(2,1)S(1)} %pad_maximum_fusion), channel_id=1, source_target_pairs={{0,1},{1,0},{2,3},{3,2},{4,5},{5,4},{6,7},{7,6},{8,9},{9,8},{10,11... | collective-permute-start | bytes 884744 | tf_op jit(solution)/shard_map/ppermute | solution.py:590
  19.7 1.8 %copy-start.1 = (bf16[1,32,16,1152]{3,2,1,0:T(8,128)(2,1)S(1)}, bf16[1,32,16,1152]{3,2,1,0:T(8,128)(2,1)}, u32[]{:S(2)}) copy-start(bf16[1,32,16,1152]{3,2,1,0:T(8,128)(2,1)} %param.4) | copy-start | bytes 3538948
  19.7 1.8 %copy-start.12 = (bf16[128,1152]{1,0:T(8,128)(2,1)S(1)}, bf16[128,1152]{1,0:T(8,128)(2,1)}, u32[]{:S(2)}) copy-start(bf16[128,1152]{1,0:T(8,128)(2,1)} %copy-done.11) | copy-start | bytes 884740
  19.7 1.8 %copy-start.14 = (bf16[512,1152]{1,0:T(8,128)(2,1)S(1)}, bf16[512,1152]{1,0:T(8,128)(2,1)}, u32[]{:S(2)}) copy-start(bf16[512,1152]{1,0:T(8,128)(2,1)} %get-tuple-element.35.own_ref) | copy-start | bytes 3538948
  19.7 1.9 %copy-start.15 = (bf16[576,512]{1,0:T(8,128)(2,1)S(1)}, bf16[576,512]{1,0:T(8,128)(2,1)}, u32[]{:S(2)}) copy-start(bf16[576,512]{1,0:T(8,128)(2,1)} %get-tuple-element.34.qt_ref) | copy-start | bytes 1769476
  20.7 0.8 copy-start.16
  21.6 1.1 copy-start.17
  38.0 0.8 copy-start.8
  38.9 1.8 %copy-start.2 = (bf16[576,1152]{1,0:T(8,128)(2,1)}, bf16[576,1152]{1,0:T(8,128)(2,1)S(1)}, u32[]{:S(2)}) copy-start(bf16[576,1152]{1,0:T(8,128)(2,1)S(1)} %get-tuple-element.38.kept_ref) | copy-start | bytes 3981316
  38.9 1.8 %copy-start.6 = (bf16[512,1152]{1,0:T(8,128)(2,1)}, bf16[512,1152]{1,0:T(8,128)(2,1)S(1)}, u32[]{:S(2)}) copy-start(bf16[512,1152]{1,0:T(8,128)(2,1)S(1)} %get-tuple-element.43.inner_ref) | copy-start | bytes 3538948
  38.9 1.7 %collective-permute-start.6 = (bf16[128,1152]{1,0:T(8,128)(2,1)S(1)}, bf16[128,1152]{1,0:T(8,128)(2,1)S(1)}, u32[]{:S(2)}, u32[]{:S(2)}) collective-permute-start(bf16[128,1152]{1,0:T(8,128)(2,1)S(1)} %get-tuple-element.46), channel_id=1, source_target_pairs={{0,1},{1,0},{2,3},{3,2},{4,5},{5,4},{6,7},{7,6},{8,9},{9,8},{10,11... | collective-permute-start | bytes 884744 | tf_op jit(solution)/shard_map/ppermute | solution.py:590
  39.3 7.8 %collective-permute-start.4 = (bf16[576,1152]{1,0:T(8,128)(2,1)}, bf16[576,1152]{1,0:T(8,128)(2,1)}, u32[]{:S(2)}, u32[]{:S(2)}) collective-permute-start(bf16[576,1152]{1,0:T(8,128)(2,1)} %get-tuple-element.39), channel_id=1, source_target_pairs={{0,1},{1,0},{2,3},{3,2},{4,5},{5,4},{6,7},{7,6},{8,9},{9,8},{10,11... | collective-permute-start | bytes 3981320 | tf_op jit(solution)/shard_map/ppermute | solution.py:430
  39.4 17.4 %collective-permute-start.5 = (bf16[256,1152]{1,0:T(8,128)(2,1)}, bf16[256,1152]{1,0:T(8,128)(2,1)}, u32[]{:S(2)}, u32[]{:S(2)}) collective-permute-start(bf16[256,1152]{1,0:T(8,128)(2,1)} %get-tuple-element.44), channel_id=1, source_target_pairs={{0,1},{1,0},{2,3},{3,2},{4,5},{5,4},{6,7},{7,6},{8,9},{9,8},{10,11... | collective-permute-start | bytes 1769480 | tf_op jit(solution)/shard_map/ppermute | solution.py:590
  41.7 11.8 %collective-permute-start.7 = (bf16[128,1152]{1,0:T(8,128)(2,1)}, bf16[128,1152]{1,0:T(8,128)(2,1)S(1)}, u32[]{:S(2)}, u32[]{:S(2)}) collective-permute-start(bf16[128,1152]{1,0:T(8,128)(2,1)} %get-tuple-element.63), channel_id=1, source_target_pairs={{0,2},{1,3},{2,4},{3,5},{4,6},{5,7},{8,10},{9,11},{10,12},{11,13},... | collective-permute-start | bytes 884744 | tf_op jit(solution)/shard_map/ppermute | solution.py:590
  45.6 11.2 %collective-permute-start.8 = (bf16[128,1152]{1,0:T(8,128)(2,1)}, bf16[128,1152]{1,0:T(8,128)(2,1)}, u32[]{:S(2)}, u32[]{:S(2)}) collective-permute-start(bf16[128,1152]{1,0:T(8,128)(2,1)} %get-tuple-element.62), channel_id=1, source_target_pairs={{2,0},{3,1},{4,2},{5,3},{6,4},{7,5},{10,8},{11,9},{12,10},{13,11},... | collective-permute-start | bytes 884744 | tf_op jit(solution)/shard_map/ppermute | solution.py:590
  47.1 1.3 %copy-start.3 = (bf16[576,1152]{1,0:T(8,128)(2,1)S(1)}, bf16[576,1152]{1,0:T(8,128)(2,1)}, u32[]{:S(2)}) copy-start(bf16[576,1152]{1,0:T(8,128)(2,1)} %copy-done.2) | copy-start | bytes 3981316
  48.4 8.4 %copy-start.7 = (bf16[512,1152]{1,0:T(8,128)(2,1)S(1)}, bf16[512,1152]{1,0:T(8,128)(2,1)}, u32[]{:S(2)}) copy-start(bf16[512,1152]{1,0:T(8,128)(2,1)} %copy-done.6) | copy-start | bytes 3538948
  48.4 8.4 %copy-start.9 = (bf16[512,640]{1,0:T(8,128)(2,1)S(1)}, bf16[512,640]{1,0:T(8,128)(2,1)}, u32[]{:S(2)}) copy-start(bf16[512,640]{1,0:T(8,128)(2,1)} %copy-done.8) | copy-start | bytes 1966084
  50.4 18.5 %collective-permute-start.10 = (bf16[4,40,1152]{2,1,0:T(8,128)(2,1)S(1)}, bf16[4,40,1152]{2,1,0:T(8,128)(2,1)S(1)}, u32[]{:S(2)}, u32[]{:S(2)}) collective-permute-start(bf16[4,40,1152]{2,1,0:T(8,128)(2,1)S(1)} %get-tuple-element.41.second), channel_id=1, source_target_pairs={{0,16},{8,24},{16,0},{24,8},{1,17},{9,25},{17,1},{25,9},{2,18},{10... | collective-permute-start | bytes 1105928 | tf_op jit(solution)/shard_map/ppermute | solution.py:549
  52.0 17.0 %collective-permute-start.11 = (bf16[4,40,1152]{2,1,0:T(8,128)(2,1)S(1)}, bf16[4,40,1152]{2,1,0:T(8,128)(2,1)S(1)}, u32[]{:S(2)}, u32[]{:S(2)}) collective-permute-start(bf16[4,40,1152]{2,1,0:T(8,128)(2,1)S(1)} %get-tuple-element.42.third), channel_id=1, source_target_pairs={{0,24},{8,16},{16,8},{24,0},{1,25},{9,17},{17,9},{25,1},{2,26},{10... | collective-permute-start | bytes 1105928 | tf_op jit(solution)/shard_map/ppermute | solution.py:549
  53.5 16.7 %collective-permute-start.9 = (bf16[4,40,1152]{2,1,0:T(8,128)(2,1)S(1)}, bf16[4,40,1152]{2,1,0:T(8,128)(2,1)S(1)}, u32[]{:S(2)}, u32[]{:S(2)}) collective-permute-start(bf16[4,40,1152]{2,1,0:T(8,128)(2,1)S(1)} %get-tuple-element.40.first), channel_id=1, source_target_pairs={{0,8},{8,0},{16,24},{24,16},{1,9},{9,1},{17,25},{25,17},{2,10},{10... | collective-permute-start | bytes 1105928 | tf_op jit(solution)/shard_map/ppermute | solution.py:549
  56.8 3.5 %copy-start.18 = (bf16[1152,1728]{0,1:T(8,128)(2,1)S(1)}, bf16[1152,1728]{0,1:T(8,128)(2,1)}, u32[]{:S(2)}) copy-start(bf16[1152,1728]{0,1:T(8,128)(2,1)} %param.5) | copy-start | bytes 11943940
  60.2 10.2 %collective-permute-start.15 = (bf16[576,1152]{1,0:T(8,128)(2,1)S(1)}, bf16[576,1152]{1,0:T(8,128)(2,1)S(1)}, u32[]{:S(2)}, u32[]{:S(2)}) collective-permute-start(bf16[576,1152]{1,0:T(8,128)(2,1)S(1)} %get-tuple-element.53), channel_id=1, source_target_pairs={{0,1},{1,0},{2,3},{3,2},{4,5},{5,4},{6,7},{7,6},{8,9},{9,8},{10,11... | collective-permute-start | bytes 3981320 | tf_op jit(solution)/shard_map/ppermute | solution.py:430
  62.9 7.6 %copy-start.4 = (bf16[512,1152]{1,0:T(8,128)(2,1)}, bf16[512,1152]{1,0:T(8,128)(2,1)S(1)}, u32[]{:S(2)}) copy-start(bf16[512,1152]{1,0:T(8,128)(2,1)S(1)} %convolution_convert_fusion.refs_2_) | copy-start | bytes 3538948
  64.1 7.8 %copy-start.5 = (bf16[512,1152]{1,0:T(8,128)(2,1)}, bf16[512,1152]{1,0:T(8,128)(2,1)S(1)}, u32[]{:S(2)}) copy-start(bf16[512,1152]{1,0:T(8,128)(2,1)S(1)} %convolution_convert_fusion.1.refs_1_) | copy-start | bytes 3538948
  71.9 0.7 copy-start.10
  72.6 11.7 %collective-permute-start.16 = (bf16[4,40,1152]{2,1,0:T(8,128)(2,1)}, bf16[4,40,1152]{2,1,0:T(8,128)(2,1)S(1)}, u32[]{:S(2)}, u32[]{:S(2)}) collective-permute-start(bf16[4,40,1152]{2,1,0:T(8,128)(2,1)} %get-tuple-element.54), channel_id=1, source_target_pairs={{0,8},{8,0},{16,24},{24,16},{1,9},{9,1},{17,25},{25,17},{2,10},{10... | collective-permute-start | bytes 1105928 | tf_op jit(solution)/shard_map/ppermute | solution.py:549
  74.1 17.3 %collective-permute-start.20 = (bf16[4,40,1152]{2,1,0:T(8,128)(2,1)}, bf16[4,40,1152]{2,1,0:T(8,128)(2,1)S(1)}, u32[]{:S(2)}, u32[]{:S(2)}) collective-permute-start(bf16[4,40,1152]{2,1,0:T(8,128)(2,1)} %get-tuple-element.57), channel_id=1, source_target_pairs={{0,16},{8,24},{16,0},{24,8},{1,17},{9,25},{17,1},{25,9},{2,18},{10... | collective-permute-start | bytes 1105928 | tf_op jit(solution)/shard_map/ppermute | solution.py:549
  75.6 15.8 %collective-permute-start.21 = (bf16[4,40,1152]{2,1,0:T(8,128)(2,1)}, bf16[4,40,1152]{2,1,0:T(8,128)(2,1)S(1)}, u32[]{:S(2)}, u32[]{:S(2)}) collective-permute-start(bf16[4,40,1152]{2,1,0:T(8,128)(2,1)} %get-tuple-element.58), channel_id=1, source_target_pairs={{0,24},{8,16},{16,8},{24,0},{1,25},{9,17},{17,9},{25,1},{2,26},{10... | collective-permute-start | bytes 1105928 | tf_op jit(solution)/shard_map/ppermute | solution.py:549
  76.2 20.7 %collective-permute-start.12 = (bf16[40,1152]{1,0:T(8,128)(2,1)S(1)}, bf16[40,1152]{1,0:T(8,128)(2,1)S(1)}, u32[]{:S(2)}, u32[]{:S(2)}) collective-permute-start(bf16[40,1152]{1,0:T(8,128)(2,1)S(1)} %get-tuple-element.70), channel_id=1, source_target_pairs={{0,2},{2,0},{4,6},{6,4},{1,3},{3,1},{5,7},{7,5},{8,10},{10,8},{12,... | collective-permute-start | bytes 276488 | tf_op jit(solution)/shard_map/ppermute | solution.py:549
  78.6 18.7 %collective-permute-start.13 = (bf16[40,1152]{1,0:T(8,128)(2,1)S(1)}, bf16[40,1152]{1,0:T(8,128)(2,1)S(1)}, u32[]{:S(2)}, u32[]{:S(2)}) collective-permute-start(bf16[40,1152]{1,0:T(8,128)(2,1)S(1)} %get-tuple-element.69), channel_id=1, source_target_pairs={{0,4},{2,6},{4,0},{6,2},{1,5},{3,7},{5,1},{7,3},{8,12},{10,14},{12... | collective-permute-start | bytes 276488 | tf_op jit(solution)/shard_map/ppermute | solution.py:549
  84.4 12.9 %collective-permute-start.14 = (bf16[40,1152]{1,0:T(8,128)(2,1)S(1)}, bf16[40,1152]{1,0:T(8,128)(2,1)S(1)}, u32[]{:S(2)}, u32[]{:S(2)}) collective-permute-start(bf16[40,1152]{1,0:T(8,128)(2,1)S(1)} %get-tuple-element.68), channel_id=1, source_target_pairs={{0,6},{2,4},{4,2},{6,0},{1,7},{3,5},{5,3},{7,1},{8,14},{10,12},{12... | collective-permute-start | bytes 276488 | tf_op jit(solution)/shard_map/ppermute | solution.py:549
  92.7 6.8 %collective-permute-start.22 = (bf16[40,1152]{1,0:T(8,128)(2,1)S(1)}, bf16[40,1152]{1,0:T(8,128)(2,1)S(1)}, u32[]{:S(2)}, u32[]{:S(2)}) collective-permute-start(bf16[40,1152]{1,0:T(8,128)(2,1)S(1)} %get-tuple-element.67), channel_id=1, source_target_pairs={{0,2},{2,0},{4,6},{6,4},{1,3},{3,1},{5,7},{7,5},{8,10},{10,8},{12,... | collective-permute-start | bytes 276488 | tf_op jit(solution)/shard_map/ppermute | solution.py:549
  94.8 6.6 %collective-permute-start.23 = (bf16[40,1152]{1,0:T(8,128)(2,1)S(1)}, bf16[40,1152]{1,0:T(8,128)(2,1)S(1)}, u32[]{:S(2)}, u32[]{:S(2)}) collective-permute-start(bf16[40,1152]{1,0:T(8,128)(2,1)S(1)} %get-tuple-element.66), channel_id=1, source_target_pairs={{0,4},{2,6},{4,0},{6,2},{1,5},{3,7},{5,1},{7,3},{8,12},{10,14},{12... | collective-permute-start | bytes 276488 | tf_op jit(solution)/shard_map/ppermute | solution.py:549
  96.8 6.5 %collective-permute-start.24 = (bf16[40,1152]{1,0:T(8,128)(2,1)S(1)}, bf16[40,1152]{1,0:T(8,128)(2,1)S(1)}, u32[]{:S(2)}, u32[]{:S(2)}) collective-permute-start(bf16[40,1152]{1,0:T(8,128)(2,1)S(1)} %get-tuple-element.65), channel_id=1, source_target_pairs={{0,6},{2,4},{4,2},{6,0},{1,7},{3,5},{5,3},{7,1},{8,14},{10,12},{12... | collective-permute-start | bytes 276488 | tf_op jit(solution)/shard_map/ppermute | solution.py:549
  97.3 8.2 %collective-permute-start.17 = (bf16[40,1152]{1,0:T(8,128)(2,1)S(1)}, bf16[40,1152]{1,0:T(8,128)(2,1)S(1)}, u32[]{:S(2)}, u32[]{:S(2)}) collective-permute-start(bf16[40,1152]{1,0:T(8,128)(2,1)S(1)} %row_sum.1.refs_0_), channel_id=1, source_target_pairs={{0,8},{8,0},{16,24},{24,16},{1,9},{9,1},{17,25},{25,17},{2,10},{10... | collective-permute-start | bytes 276488 | tf_op jit(solution)/shard_map/ppermute | solution.py:549
  98.6 8.3 %collective-permute-start.18 = (bf16[40,1152]{1,0:T(8,128)(2,1)S(1)}, bf16[40,1152]{1,0:T(8,128)(2,1)S(1)}, u32[]{:S(2)}, u32[]{:S(2)}) collective-permute-start(bf16[40,1152]{1,0:T(8,128)(2,1)S(1)} %row_sum.1.refs_0_), channel_id=1, source_target_pairs={{0,16},{8,24},{16,0},{24,8},{1,17},{9,25},{17,1},{25,9},{2,18},{10... | collective-permute-start | bytes 276488 | tf_op jit(solution)/shard_map/ppermute | solution.py:549
  99.4 7.5 %collective-permute-start.19 = (bf16[40,1152]{1,0:T(8,128)(2,1)S(1)}, bf16[40,1152]{1,0:T(8,128)(2,1)S(1)}, u32[]{:S(2)}, u32[]{:S(2)}) collective-permute-start(bf16[40,1152]{1,0:T(8,128)(2,1)S(1)} %row_sum.1.refs_0_), channel_id=1, source_target_pairs={{0,24},{8,16},{16,8},{24,0},{1,25},{9,17},{17,9},{25,1},{2,26},{10... | collective-permute-start | bytes 276488 | tf_op jit(solution)/shard_map/ppermute | solution.py:549
  103.4 4.6 %collective-permute-start.25 = (bf16[40,1152]{1,0:T(8,128)(2,1)S(1)}, bf16[40,1152]{1,0:T(8,128)(2,1)S(1)}, u32[]{:S(2)}, u32[]{:S(2)}) collective-permute-start(bf16[40,1152]{1,0:T(8,128)(2,1)S(1)} %add_convert_fusion.2.refs_4_), channel_id=1, source_target_pairs={{0,8},{8,0},{16,24},{24,16},{1,9},{9,1},{17,25},{25,17},{2,10},{10... | collective-permute-start | bytes 276488 | tf_op jit(solution)/shard_map/ppermute | solution.py:549
  104.7 4.6 %collective-permute-start.26 = (bf16[40,1152]{1,0:T(8,128)(2,1)S(1)}, bf16[40,1152]{1,0:T(8,128)(2,1)S(1)}, u32[]{:S(2)}, u32[]{:S(2)}) collective-permute-start(bf16[40,1152]{1,0:T(8,128)(2,1)S(1)} %add_convert_fusion.2.refs_4_), channel_id=1, source_target_pairs={{0,16},{8,24},{16,0},{24,8},{1,17},{9,25},{17,1},{25,9},{2,18},{10... | collective-permute-start | bytes 276488 | tf_op jit(solution)/shard_map/ppermute | solution.py:549
  105.5 5.5 %collective-permute-start.27 = (bf16[40,1152]{1,0:T(8,128)(2,1)S(1)}, bf16[40,1152]{1,0:T(8,128)(2,1)S(1)}, u32[]{:S(2)}, u32[]{:S(2)}) collective-permute-start(bf16[40,1152]{1,0:T(8,128)(2,1)S(1)} %add_convert_fusion.2.refs_4_), channel_id=1, source_target_pairs={{0,24},{8,16},{16,8},{24,0},{1,25},{9,17},{17,9},{25,1},{2,26},{10... | collective-permute-start | bytes 276488 | tf_op jit(solution)/shard_map/ppermute | solution.py:549

commit v10 on v9

--- a/solution.py
+++ b/solution.py
@@ -124,10 +124,10 @@
             pltpu.VMEM((INNER, width), jnp.bfloat16),
             pltpu.SemaphoreType.DMA((PIECES * CUTS + 2,)),
         ],
-        compiler_params=pltpu.CompilerParams(vmem_limit_bytes=56 * 1024 * 1024),
+        compiler_params=pltpu.CompilerParams(vmem_limit_bytes=50 * 1024 * 1024),
         cost_estimate=LIGHT,
         name="project",
-    )(own, top, token_rows, weight.T)
+    )(own, top[:16, :128], token_rows, weight.T)
     return queries, keyvals, top, bottom, near
 
 
@@ -273,7 +273,7 @@
 
     for copy in copies:
         copy.wait()
-    lax.fori_loop(0, strips, strip, 0)
+    lax.fori_loop(0, strips, strip, 0, unroll=2)
     share = sent_ref.shape[0] // 4
     for out_ref, half in ((sent_ref, 1 - core_ref[0]), (kept_ref, core_ref[0])):
         products = []
@@ -348,7 +348,7 @@
             pltpu.VMEM((2,) + token_rows.shape[::-1], jnp.bfloat16),
             pltpu.SemaphoreType.DMA((2,)),
         ],
-        compiler_params=pltpu.CompilerParams(vmem_limit_bytes=34 * 1024 * 1024),
+        compiler_params=pltpu.CompilerParams(vmem_limit_bytes=30 * 1024 * 1024),
         cost_estimate=pl.CostEstimate(
             flops=12 * token_count * band * 2 * INNER,
             bytes_accessed=16 * 1024 * 1024,

time: 113 us -> 115 us (1.018)
  local copies, waits for them, and re-layouts: 6.49 us -> 8.37 us
    unnamed x39, local copies, waits for them, and re-layouts: 5.08 us -> 6.26 us
  transfers between devices with their start and end apart: 28 -> 28, of which waited for: 11 -> 12; matrix products, arithmetic and copies ran while one was open for 8% -> 8% of each run, Pallas kernels for 10% -> 9%
where the time goes in v10:
time: 115 us; the launch traced here: 114 us
  starting transfers between devices  41.2 us (36%)
  Pallas kernels  33.2 us (29%)
  waiting for transfers between devices  23.4 us (20%)
  local copies, waits for them, and re-layouts  8.37 us (7%)
  matrix products  4.67 us (4%)
  other arithmetic  2.54 us (2%)
    ppermute x18, starting transfers between devices, exchanged(): got.append(lax.ppermute(part, axis, pairs))  27.4 us
    ppermute x18, waiting for transfers between devices, exchanged(): got.append(lax.ppermute(part, axis, pairs))  19.6 us
    pallas_call x1, Pallas kernels, attention(): pl.pallas_call(attention_kernel, grid=(1,), out_shape=outs, in_specs=[pl....  15.9 us
    ppermute x8, starting transfers between devices, moved(): return lax.ppermute(block, ('row', 'col'), pairs)  13.7 us
    unnamed x39, local copies, waits for them, and re-layouts  6.26 us
    pallas_call x1, Pallas kernels, project(): pl.pallas_call(project_kernel, grid=(1,), out_shape=[jax.ShapeDtypeStruct...  5.06 us
    pallas_call x1, Pallas kernels, project(): pl.pallas_call(edges_kernel, grid=(1,), out_shape=[shape(edge)] * 2, in_s...  3.92 us
    ppermute x8, waiting for transfers between devices, moved(): return lax.ppermute(block, ('row', 'col'), pairs)  3.75 us
  transfers between devices with their start and end apart: 28, of which 12 were waited for; matrix products, arithmetic and copies ran while one was open for 8% of the time, Pallas kernels for 9%

profile of v10, /device:TPU:0, one launch (start us, length us, event | category | flops | bytes accessed | tf_op | source)
XLA Modules:
  0.0 114.3 jit_solution(7395323138467237007)
XLA Ops:
  0.7 3.9 %project_edges.1 = (bf16[128,1152]{1,0:T(8,128)(2,1)}, bf16[128,1152]{1,0:T(8,128)(2,1)}) custom-call(bf16[512,1152]{1,0:T(8,128)(2,1)} %bitcast.38, bf16[1728,1152]{1,0:T(8,128)(2,1)} %bitcast.49), custom_call_target="tpu_custom_call" | custom-call | flops 1 | bytes 1 | tf_op jit(solution)/shard_map/project_edges/pallas_call | solution.py:99
  4.6 1.3 %collective-permute-start.1 = (bf16[128,1152]{1,0:T(8,128)(2,1)}, bf16[128,1152]{1,0:T(8,128)(2,1)S(1)}, u32[]{:S(2)}, u32[]{:S(2)}) collective-permute-start(bf16[128,1152]{1,0:T(8,128)(2,1)} %get-tuple-element.33), channel_id=1, source_target_pairs={{2,0},{3,1},{4,2},{5,3},{6,4},{7,5},{10,8},{11,9},{12,10},{13,11},... | collective-permute-start | bytes 884744 | tf_op jit(solution)/shard_map/ppermute | solution.py:590
  5.9 5.6 %collective-permute-start = (bf16[128,1152]{1,0:T(8,128)(2,1)}, bf16[128,1152]{1,0:T(8,128)(2,1)S(1)}, u32[]{:S(2)}, u32[]{:S(2)}) collective-permute-start(bf16[128,1152]{1,0:T(8,128)(2,1)} %get-tuple-element.36), channel_id=1, source_target_pairs={{0,2},{1,3},{2,4},{3,5},{4,6},{5,7},{8,10},{9,11},{10,12},{11,13},... | collective-permute-start | bytes 884744 | tf_op jit(solution)/shard_map/ppermute | solution.py:590
  11.5 0.7 slice.9.top_ref
  12.2 5.1 %project.1 = (bf16[576,512]{1,0:T(8,128)(2,1)S(1)}, bf16[512,1152]{1,0:T(8,128)(2,1)S(1)}, bf16[256,1152]{1,0:T(8,128)(2,1)}) custom-call(s32[1]{0:T(128)} %bitcast.own_ref, bf16[16,128]{1,0:T(8,128)(2,1)S(1)} %slice.9.top_ref, bf16[512,1152]{1,0:T(8,128)(2,1)S(1)} %bitcast.39, bf16[1728,1152]{1,0:T(8,128)(2,1)} %bitcast.50), custom_call_target="tpu_custom_call" | custom-call | flops 1 | bytes 1 | tf_op jit(solution)/shard_map/project/pallas_call | solution.py:115
  17.3 1.0 copy-done.14
  18.3 0.8 copy-done.16
  19.2 0.1 tile.11
  19.4 0.1 reshape.181
  19.7 0.1 fusion.4
  20.0 0.4 fusion.3.bias_ref
  20.5 0.6 collective-permute-start.3
  21.1 0.2 copy-done.13
  21.3 1.0 convolution_convert_fusion.2.g_ref
  22.3 0.2 copy-done.15
  22.5 0.1 copy-done.17
  22.7 1.0 copy-done.12
  23.6 15.9 %window_attention.1 = (bf16[512,640]{1,0:T(8,128)(2,1)S(1)}, bf16[512,640]{1,0:T(8,128)(2,1)S(1)}, bf16[512,1152]{1,0:T(8,128)(2,1)S(1)}, bf16[256,1152]{1,0:T(8...) custom-call(s32[4]{0:T(128)S(1)} %broadcast_subtract_fusion.start_re, ...), custom_call_target="tpu_custom_call" | custom-call | flops 4076863488 | bytes 16777216 | tf_op jit(solution)/shard_map/window_attention/pallas_call | solution.py:322
  39.6 0.8 copy-done.8
  40.4 0.5 collective-permute-start.6
  40.9 0.5 collective-permute-start.5
  41.4 1.0 collective-permute-done.6
  42.6 0.1 fusion
  42.7 0.9 fusion.5
  43.6 3.9 %collective-permute-start.7 = (bf16[128,1152]{1,0:T(8,128)(2,1)}, bf16[128,1152]{1,0:T(8,128)(2,1)S(1)}, u32[]{:S(2)}, u32[]{:S(2)}) collective-permute-start(bf16[128,1152]{1,0:T(8,128)(2,1)} %get-tuple-element.63), channel_id=1, source_target_pairs={{0,2},{1,3},{2,4},{3,5},{4,6},{5,7},{8,10},{9,11},{10,12},{11,13},... | collective-permute-start | bytes 884744 | tf_op jit(solution)/shard_map/ppermute | solution.py:590
  47.5 1.3 %collective-permute-start.8 = (bf16[128,1152]{1,0:T(8,128)(2,1)}, bf16[128,1152]{1,0:T(8,128)(2,1)}, u32[]{:S(2)}, u32[]{:S(2)}) collective-permute-start(bf16[128,1152]{1,0:T(8,128)(2,1)} %get-tuple-element.62), channel_id=1, source_target_pairs={{2,0},{3,1},{4,2},{5,3},{6,4},{7,5},{10,8},{11,9},{12,10},{13,11},... | collective-permute-start | bytes 884744 | tf_op jit(solution)/shard_map/ppermute | solution.py:590
  48.8 1.3 %copy-done.3 = bf16[576,1152]{1,0:T(8,128)(2,1)S(1)} copy-done((bf16[576,1152]{1,0:T(8,128)(2,1)S(1)}, bf16[576,1152]{1,0:T(8,128)(2,1)}, u32[]{:S(2)}) %copy-start.3) | copy-done | bytes 1327128
  50.1 2.0 %core_parts.2 = (bf16[4,40,1152]{2,1,0:T(8,128)(2,1)S(1)}, bf16[4,40,1152]{2,1,0:T(8,128)(2,1)S(1)}, bf16[4,40,1152]{2,1,0:T(8,128)(2,1)S(1)}, bf16[4,40,1152]{2,1,0:T(8,128)(2,1)S(1)}) custom-call(s32[1]{0:T(128)} %bitcast.1.own_ref, bf16[576,1152]{1,0:T(8,128)(2,1)S(1)} %copy-done.3, bf16[576,1152]{1,0:T(8,128)(2,1)} %collective-permute-done.4.got_ref), custom_call_target="tpu_custom_call" | custom-call | flops 1 | bytes 1 | tf_op jit(solution)/shard_map/core_parts/pallas_call | solution.py:435
  52.1 1.6 %collective-permute-start.10 = (bf16[4,40,1152]{2,1,0:T(8,128)(2,1)S(1)}, bf16[4,40,1152]{2,1,0:T(8,128)(2,1)S(1)}, u32[]{:S(2)}, u32[]{:S(2)}) collective-permute-start(bf16[4,40,1152]{2,1,0:T(8,128)(2,1)S(1)} %get-tuple-element.41.second), channel_id=1, source_target_pairs={{0,16},{8,24},{16,0},{24,8},{1,17},{9,25},{17,1},{25,9},{2,18},{10... | collective-permute-start | bytes 1105928 | tf_op jit(solution)/shard_map/ppermute | solution.py:549
  53.7 1.4 %collective-permute-start.11 = (bf16[4,40,1152]{2,1,0:T(8,128)(2,1)S(1)}, bf16[4,40,1152]{2,1,0:T(8,128)(2,1)S(1)}, u32[]{:S(2)}, u32[]{:S(2)}) collective-permute-start(bf16[4,40,1152]{2,1,0:T(8,128)(2,1)S(1)} %get-tuple-element.42.third), channel_id=1, source_target_pairs={{0,24},{8,16},{16,8},{24,0},{1,25},{9,17},{17,9},{25,1},{2,26},{10... | collective-permute-start | bytes 1105928 | tf_op jit(solution)/shard_map/ppermute | solution.py:549
  55.2 0.9 collective-permute-start.9
  56.1 2.6 %collective-permute-done.8.below_ref = bf16[128,1152]{1,0:T(8,128)(2,1)} collective-permute-done((bf16[128,1152]{1,0:T(8,128)(2,1)}, bf16[128,1152]{1,0:T(8,128)(2,1)}, u32[]{:S(2)}, u32[]{:S(2)}) %collective-permute-start.8) | collective-permute-done | bytes 294944 | tf_op jit(solution)/shard_map/ppermute | solution.py:590
  58.7 3.4 %late_weight_grad_halves.1 = (bf16[576,1152]{1,0:T(8,128)(2,1)S(1)}, bf16[576,1152]{1,0:T(8,128)(2,1)S(1)}, bf16[512,1728]{1,0:T(8,128)(2,1)S(1)}, bf16[512,576]{1,0:T(8,128)(2,1)S(1)}) custom-call(s32[1]{0:T(128)} %bitcast.own_ref, bf16[4,40,1152]{2,1,0:T(8,128)(2,1)S(1)} %get-tuple-element.40.first, bf16[4,40,1152]{2,1,0:T(8,128)(2,1)S(1)} %get-tuple-element.41.second, ...), custom_call_target="tpu_custom_call" | custom-call | flops 1 | bytes 1 | tf_op jit(solution)/shard_map/late_weight_grad_halves/pallas_call | solution.py:398
  62.2 2.5 %convolution_convert_fusion.refs_2_ = bf16[512,1152]{1,0:T(8,128)(2,1)S(1)} fusion(bf16[512,1728]{1,0:T(8,128)(2,1)S(1)} %get-tuple-element.50, bf16[1152,1728]{0,1:T(8,128)(2,1)S(1)} %copy-done.18), kind=kOutput, calls=%fused_computation | convolution fusion | flops 2039021568 | bytes 6930432 | tf_op jit(solution)/shard_map/dot_general | solution.py:31
  64.8 1.2 %convolution_convert_fusion.1.refs_1_ = bf16[512,1152]{1,0:T(8,128)(2,1)S(1)} fusion(bf16[512,576]{1,0:T(8,128)(2,1)S(1)} %get-tuple-element.49, bf16[1152,576]{0,1:T(8,128)(2,1)S(1)} %copy-done), kind=kOutput, calls=%fused_computation.1 | convolution fusion | flops 680067072 | bytes 3096576 | tf_op jit(solution)/shard_map/dot_general | solution.py:31
  66.0 4.7 %collective-permute-done.10 = bf16[4,40,1152]{2,1,0:T(8,128)(2,1)S(1)} collective-permute-done((bf16[4,40,1152]{2,1,0:T(8,128)(2,1)S(1)}, bf16[4,40,1152]{2,1,0:T(8,128)(2,1)S(1)}, u32[]{:S(2)}, u32[]{:S(2)}) %collective-permute-start.10) | collective-permute-done | bytes 368672 | tf_op jit(solution)/shard_map/ppermute | solution.py:549
  70.7 1.2 %collective-permute-done.9 = bf16[4,40,1152]{2,1,0:T(8,128)(2,1)S(1)} collective-permute-done((bf16[4,40,1152]{2,1,0:T(8,128)(2,1)S(1)}, bf16[4,40,1152]{2,1,0:T(8,128)(2,1)S(1)}, u32[]{:S(2)}, u32[]{:S(2)}) %collective-permute-start.9) | collective-permute-done | bytes 368672 | tf_op jit(solution)/shard_map/ppermute | solution.py:549
  71.9 0.2 add_convert_fusion.1.refs_0_
  72.1 1.4 %core_parts.3 = (bf16[4,40,1152]{2,1,0:T(8,128)(2,1)S(1)}, bf16[4,40,1152]{2,1,0:T(8,128)(2,1)}, bf16[4,40,1152]{2,1,0:T(8,128)(2,1)}, bf16[4,40,1152]{2,1,0:T(8,128)(2,1)}) custom-call(s32[1]{0:T(128)} %bitcast.1.own_ref, bf16[576,1152]{1,0:T(8,128)(2,1)S(1)} %get-tuple-element.52.kept_ref, bf16[576,1152]{1,0:T(8,128)(2,1)S(1)} %collective-permute-done.15.got_ref, ...), custom_call_target="tpu_custom_call" | custom-call | flops 1 | bytes 1 | tf_op jit(solution)/shard_map/core_parts/pallas_call | solution.py:435
  73.6 0.7 copy-done.10
  74.3 1.5 %collective-permute-start.16 = (bf16[4,40,1152]{2,1,0:T(8,128)(2,1)}, bf16[4,40,1152]{2,1,0:T(8,128)(2,1)S(1)}, u32[]{:S(2)}, u32[]{:S(2)}) collective-permute-start(bf16[4,40,1152]{2,1,0:T(8,128)(2,1)} %get-tuple-element.54), channel_id=1, source_target_pairs={{0,8},{8,0},{16,24},{24,16},{1,9},{9,1},{17,25},{25,17},{2,10},{10... | collective-permute-start | bytes 1105928 | tf_op jit(solution)/shard_map/ppermute | solution.py:549
  75.8 1.5 %collective-permute-start.20 = (bf16[4,40,1152]{2,1,0:T(8,128)(2,1)}, bf16[4,40,1152]{2,1,0:T(8,128)(2,1)S(1)}, u32[]{:S(2)}, u32[]{:S(2)}) collective-permute-start(bf16[4,40,1152]{2,1,0:T(8,128)(2,1)} %get-tuple-element.57), channel_id=1, source_target_pairs={{0,16},{8,24},{16,0},{24,8},{1,17},{9,25},{17,1},{25,9},{2,18},{10... | collective-permute-start | bytes 1105928 | tf_op jit(solution)/shard_map/ppermute | solution.py:549
  77.3 0.5 collective-permute-start.21
  77.9 2.4 %collective-permute-start.12 = (bf16[40,1152]{1,0:T(8,128)(2,1)S(1)}, bf16[40,1152]{1,0:T(8,128)(2,1)S(1)}, u32[]{:S(2)}, u32[]{:S(2)}) collective-permute-start(bf16[40,1152]{1,0:T(8,128)(2,1)S(1)} %get-tuple-element.70), channel_id=1, source_target_pairs={{0,2},{2,0},{4,6},{6,4},{1,3},{3,1},{5,7},{7,5},{8,10},{10,8},{12,... | collective-permute-start | bytes 276488 | tf_op jit(solution)/shard_map/ppermute | solution.py:549
  80.3 2.0 %collective-permute-start.13 = (bf16[40,1152]{1,0:T(8,128)(2,1)S(1)}, bf16[40,1152]{1,0:T(8,128)(2,1)S(1)}, u32[]{:S(2)}, u32[]{:S(2)}) collective-permute-start(bf16[40,1152]{1,0:T(8,128)(2,1)S(1)} %get-tuple-element.69), channel_id=1, source_target_pairs={{0,4},{2,6},{4,0},{6,2},{1,5},{3,7},{5,1},{7,3},{8,12},{10,14},{12... | collective-permute-start | bytes 276488 | tf_op jit(solution)/shard_map/ppermute | solution.py:549
  82.3 3.7 %collective-permute-done.16.refs_0_ = bf16[4,40,1152]{2,1,0:T(8,128)(2,1)S(1)} collective-permute-done((bf16[4,40,1152]{2,1,0:T(8,128)(2,1)}, bf16[4,40,1152]{2,1,0:T(8,128)(2,1)S(1)}, u32[]{:S(2)}, u32[]{:S(2)}) %collective-permute-start.16) | collective-permute-done | bytes 368672 | tf_op jit(solution)/shard_map/ppermute | solution.py:549
  86.1 3.8 %collective-permute-start.14 = (bf16[40,1152]{1,0:T(8,128)(2,1)S(1)}, bf16[40,1152]{1,0:T(8,128)(2,1)S(1)}, u32[]{:S(2)}, u32[]{:S(2)}) collective-permute-start(bf16[40,1152]{1,0:T(8,128)(2,1)S(1)} %get-tuple-element.68), channel_id=1, source_target_pairs={{0,6},{2,4},{4,2},{6,0},{1,7},{3,5},{5,3},{7,1},{8,14},{10,12},{12... | collective-permute-start | bytes 276488 | tf_op jit(solution)/shard_map/ppermute | solution.py:549
  89.9 3.2 %collective-permute-done.20 = bf16[4,40,1152]{2,1,0:T(8,128)(2,1)S(1)} collective-permute-done((bf16[4,40,1152]{2,1,0:T(8,128)(2,1)}, bf16[4,40,1152]{2,1,0:T(8,128)(2,1)S(1)}, u32[]{:S(2)}, u32[]{:S(2)}) %collective-permute-start.20) | collective-permute-done | bytes 368672 | tf_op jit(solution)/shard_map/ppermute | solution.py:549
  93.1 1.2 %add_convert_fusion = bf16[4,40,1152]{2,1,0:T(8,128)(2,1)S(1)} fusion(bf16[4,40,1152]{2,1,0:T(8,128)(2,1)S(1)} %collective-permute-done.21, bf16[4,40,1152]{2,1,0:T(8,128)(2,1)S(1)} %collective-permute-done.20, bf16[4,40,1152]{2,1,0:T(8,128)(2,1)S(1)} %collective-permute-done.16.refs_0_, bf16[4,40,1152]{2,1,0:T(8,128)(2,1)} %copy-done.10), kind=kLoop, calls=%fused_computation.11 | loop fusion | flops 1474560 | bytes 1843200 | tf_op jit(solution)/shard_map/convert_element_type | solution.py:559
  94.4 2.1 %collective-permute-start.22 = (bf16[40,1152]{1,0:T(8,128)(2,1)S(1)}, bf16[40,1152]{1,0:T(8,128)(2,1)S(1)}, u32[]{:S(2)}, u32[]{:S(2)}) collective-permute-start(bf16[40,1152]{1,0:T(8,128)(2,1)S(1)} %get-tuple-element.67), channel_id=1, source_target_pairs={{0,2},{2,0},{4,6},{6,4},{1,3},{3,1},{5,7},{7,5},{8,10},{10,8},{12,... | collective-permute-start | bytes 276488 | tf_op jit(solution)/shard_map/ppermute | solution.py:549
  96.5 2.4 %collective-permute-start.23 = (bf16[40,1152]{1,0:T(8,128)(2,1)S(1)}, bf16[40,1152]{1,0:T(8,128)(2,1)S(1)}, u32[]{:S(2)}, u32[]{:S(2)}) collective-permute-start(bf16[40,1152]{1,0:T(8,128)(2,1)S(1)} %get-tuple-element.66), channel_id=1, source_target_pairs={{0,4},{2,6},{4,0},{6,2},{1,5},{3,7},{5,1},{7,3},{8,12},{10,14},{12... | collective-permute-start | bytes 276488 | tf_op jit(solution)/shard_map/ppermute | solution.py:549
  98.9 0.1 collective-permute-start.24
  99.0 1.3 %collective-permute-start.17 = (bf16[40,1152]{1,0:T(8,128)(2,1)S(1)}, bf16[40,1152]{1,0:T(8,128)(2,1)S(1)}, u32[]{:S(2)}, u32[]{:S(2)}) collective-permute-start(bf16[40,1152]{1,0:T(8,128)(2,1)S(1)} %row_sum.1.refs_0_), channel_id=1, source_target_pairs={{0,8},{8,0},{16,24},{24,16},{1,9},{9,1},{17,25},{25,17},{2,10},{10... | collective-permute-start | bytes 276488 | tf_op jit(solution)/shard_map/ppermute | solution.py:549
  100.3 0.8 collective-permute-start.18
  101.2 1.4 %collective-permute-start.19 = (bf16[40,1152]{1,0:T(8,128)(2,1)S(1)}, bf16[40,1152]{1,0:T(8,128)(2,1)S(1)}, u32[]{:S(2)}, u32[]{:S(2)}) collective-permute-start(bf16[40,1152]{1,0:T(8,128)(2,1)S(1)} %row_sum.1.refs_0_), channel_id=1, source_target_pairs={{0,24},{8,16},{16,8},{24,0},{1,25},{9,17},{17,9},{25,1},{2,26},{10... | collective-permute-start | bytes 276488 | tf_op jit(solution)/shard_map/ppermute | solution.py:549
  102.6 1.1 collective-permute-done.23
  103.7 1.6 %collective-permute-done.24 = bf16[40,1152]{1,0:T(8,128)(2,1)S(1)} collective-permute-done((bf16[40,1152]{1,0:T(8,128)(2,1)S(1)}, bf16[40,1152]{1,0:T(8,128)(2,1)S(1)}, u32[]{:S(2)}, u32[]{:S(2)}) %collective-permute-start.24) | collective-permute-done | bytes 92192 | tf_op jit(solution)/shard_map/ppermute | solution.py:549
  105.4 1.3 %collective-permute-start.25 = (bf16[40,1152]{1,0:T(8,128)(2,1)S(1)}, bf16[40,1152]{1,0:T(8,128)(2,1)S(1)}, u32[]{:S(2)}, u32[]{:S(2)}) collective-permute-start(bf16[40,1152]{1,0:T(8,128)(2,1)S(1)} %add_convert_fusion.2.refs_4_), channel_id=1, source_target_pairs={{0,8},{8,0},{16,24},{24,16},{1,9},{9,1},{17,25},{25,17},{2,10},{10... | collective-permute-start | bytes 276488 | tf_op jit(solution)/shard_map/ppermute | solution.py:549
  106.7 0.8 collective-permute-start.26
  107.5 1.4 %collective-permute-start.27 = (bf16[40,1152]{1,0:T(8,128)(2,1)S(1)}, bf16[40,1152]{1,0:T(8,128)(2,1)S(1)}, u32[]{:S(2)}, u32[]{:S(2)}) collective-permute-start(bf16[40,1152]{1,0:T(8,128)(2,1)S(1)} %add_convert_fusion.2.refs_4_), channel_id=1, source_target_pairs={{0,24},{8,16},{16,8},{24,0},{1,25},{9,17},{17,9},{25,1},{2,26},{10... | collective-permute-start | bytes 276488 | tf_op jit(solution)/shard_map/ppermute | solution.py:549
  108.9 1.1 collective-permute-done.25.refs_5_
  110.0 1.2 %collective-permute-done.26.refs_6_ = bf16[40,1152]{1,0:T(8,128)(2,1)S(1)} collective-permute-done((bf16[40,1152]{1,0:T(8,128)(2,1)S(1)}, bf16[40,1152]{1,0:T(8,128)(2,1)S(1)}, u32[]{:S(2)}, u32[]{:S(2)}) %collective-permute-start.26) | collective-permute-done | bytes 92192 | tf_op jit(solution)/shard_map/ppermute | solution.py:549
  111.2 1.7 %collective-permute-done.27.refs_7_ = bf16[40,1152]{1,0:T(8,128)(2,1)S(1)} collective-permute-done((bf16[40,1152]{1,0:T(8,128)(2,1)S(1)}, bf16[40,1152]{1,0:T(8,128)(2,1)S(1)}, u32[]{:S(2)}, u32[]{:S(2)}) %collective-permute-start.27) | collective-permute-done | bytes 92192 | tf_op jit(solution)/shard_map/ppermute | solution.py:549
  112.9 1.4 %weight_grads.1 = (f32[144,1728]{1,0:T(8,128)}, f32[144,576]{1,0:T(8,128)}) custom-call(s32[1]{0:T(128)} %bitcast.1.own_ref, bf16[40,1152]{1,0:T(8,128)(2,1)S(1)} %row_sum.1.refs_0_, bf16[40,1152]{1,0:T(8,128)(2,1)S(1)} %collective-permute-done.17.refs_1_, bf16[40,1152]{1,0:T(8,128)(2,1)S(1)} %collective-permute-done.18.refs_2_, ...), custom_call_target="tpu_custom_call" | custom-call | flops 1 | bytes 1 | tf_op jit(solution)/shard_map/weight_grads/pallas_call | solution.py:488
  (80 shorter events, 1.2 us)
Async XLA Ops:
  0.6 20.5 %copy-start = (bf16[1152,576]{0,1:T(8,128)(2,1)S(1)}, bf16[1152,576]{0,1:T(8,128)(2,1)}, u32[]{:S(2)}) copy-start(bf16[1152,576]{0,1:T(8,128)(2,1)} %param.6) | copy-start | bytes 3981316
  0.6 11.5 %copy-start.1 = (bf16[1,32,16,1152]{3,2,1,0:T(8,128)(2,1)S(1)}, bf16[1,32,16,1152]{3,2,1,0:T(8,128)(2,1)}, u32[]{:S(2)}) copy-start(bf16[1,32,16,1152]{3,2,1,0:T(8,128)(2,1)} %param.4) | copy-start | bytes 3538948
  4.6 15.8 %collective-permute-start.1 = (bf16[128,1152]{1,0:T(8,128)(2,1)}, bf16[128,1152]{1,0:T(8,128)(2,1)S(1)}, u32[]{:S(2)}, u32[]{:S(2)}) collective-permute-start(bf16[128,1152]{1,0:T(8,128)(2,1)} %get-tuple-element.33), channel_id=1, source_target_pairs={{2,0},{3,1},{4,2},{5,3},{6,4},{7,5},{10,8},{11,9},{12,10},{13,11},... | collective-permute-start | bytes 884744 | tf_op jit(solution)/shard_map/ppermute | solution.py:590
  5.9 14.6 %collective-permute-start = (bf16[128,1152]{1,0:T(8,128)(2,1)}, bf16[128,1152]{1,0:T(8,128)(2,1)S(1)}, u32[]{:S(2)}, u32[]{:S(2)}) collective-permute-start(bf16[128,1152]{1,0:T(8,128)(2,1)} %get-tuple-element.36), channel_id=1, source_target_pairs={{0,2},{1,3},{2,4},{3,5},{4,6},{5,7},{8,10},{9,11},{10,12},{11,13},... | collective-permute-start | bytes 884744 | tf_op jit(solution)/shard_map/ppermute | solution.py:590
  17.2 1.0 copy-start.14
  18.3 0.8 copy-start.16
  19.1 3.2 %collective-permute-start.2 = (bf16[256,1152]{1,0:T(8,128)(2,1)}, bf16[256,1152]{1,0:T(8,128)(2,1)}, u32[]{:S(2)}, u32[]{:S(2)}) collective-permute-start(bf16[256,1152]{1,0:T(8,128)(2,1)} %get-tuple-element.37), channel_id=1, source_target_pairs={{0,1},{1,0},{2,3},{3,2},{4,5},{5,4},{6,7},{7,6},{8,9},{9,8},{10,11... | collective-permute-start | bytes 1769480 | tf_op jit(solution)/shard_map/ppermute | solution.py:590
  20.0 1.3 %copy-start.13 = (bf16[1,32,16,1152]{3,2,1,0:T(8,128)(2,1)S(1)}, bf16[1,32,16,1152]{3,2,1,0:T(8,128)(2,1)}, u32[]{:S(2)}) copy-start(bf16[1,32,16,1152]{3,2,1,0:T(8,128)(2,1)} %param.7) | copy-start | bytes 3538948
  20.5 1.8 %copy-start.11 = (bf16[128,1152]{1,0:T(8,128)(2,1)}, bf16[128,1152]{1,0:T(8,128)(2,1)S(1)}, u32[]{:S(2)}) copy-start(bf16[128,1152]{1,0:T(8,128)(2,1)S(1)} %collective-permute-done.above_ref) | copy-start | bytes 884740
  20.5 1.8 %collective-permute-start.3 = (bf16[16,8,1152]{2,1,0:T(8,128)(2,1)S(1)}, bf16[16,8,1152]{2,1,0:T(8,128)(2,1)S(1)}, u32[]{:S(2)}, u32[]{:S(2)}) collective-permute-start(bf16[16,8,1152]{2,1,0:T(8,128)(2,1)S(1)} %pad_maximum_fusion), channel_id=1, source_target_pairs={{0,1},{1,0},{2,3},{3,2},{4,5},{5,4},{6,7},{7,6},{8,9},{9,8},{10,11... | collective-permute-start | bytes 884744 | tf_op jit(solution)/shard_map/ppermute | solution.py:590
  21.3 1.3 %copy-start.15 = (bf16[512,1152]{1,0:T(8,128)(2,1)S(1)}, bf16[512,1152]{1,0:T(8,128)(2,1)}, u32[]{:S(2)}) copy-start(bf16[512,1152]{1,0:T(8,128)(2,1)} %copy-done.14) | copy-start | bytes 3538948
  21.3 1.4 %copy-start.17 = (bf16[576,512]{1,0:T(8,128)(2,1)S(1)}, bf16[576,512]{1,0:T(8,128)(2,1)}, u32[]{:S(2)}) copy-start(bf16[576,512]{1,0:T(8,128)(2,1)} %copy-done.16) | copy-start | bytes 1769476
  22.7 1.0 copy-start.12
  39.6 0.8 copy-start.8
  40.4 2.2 %copy-start.2 = (bf16[576,1152]{1,0:T(8,128)(2,1)}, bf16[576,1152]{1,0:T(8,128)(2,1)S(1)}, u32[]{:S(2)}) copy-start(bf16[576,1152]{1,0:T(8,128)(2,1)S(1)} %get-tuple-element.38.kept_ref) | copy-start | bytes 3981316
  40.4 2.2 %copy-start.6 = (bf16[512,1152]{1,0:T(8,128)(2,1)}, bf16[512,1152]{1,0:T(8,128)(2,1)S(1)}, u32[]{:S(2)}) copy-start(bf16[512,1152]{1,0:T(8,128)(2,1)S(1)} %get-tuple-element.43.inner_ref) | copy-start | bytes 3538948
  40.4 2.0 %collective-permute-start.6 = (bf16[128,1152]{1,0:T(8,128)(2,1)S(1)}, bf16[128,1152]{1,0:T(8,128)(2,1)S(1)}, u32[]{:S(2)}, u32[]{:S(2)}) collective-permute-start(bf16[128,1152]{1,0:T(8,128)(2,1)S(1)} %get-tuple-element.46), channel_id=1, source_target_pairs={{0,1},{1,0},{2,3},{3,2},{4,5},{5,4},{6,7},{7,6},{8,9},{9,8},{10,11... | collective-permute-start | bytes 884744 | tf_op jit(solution)/shard_map/ppermute | solution.py:590
  40.9 7.9 %collective-permute-start.4 = (bf16[576,1152]{1,0:T(8,128)(2,1)}, bf16[576,1152]{1,0:T(8,128)(2,1)}, u32[]{:S(2)}, u32[]{:S(2)}) collective-permute-start(bf16[576,1152]{1,0:T(8,128)(2,1)} %get-tuple-element.39), channel_id=1, source_target_pairs={{0,1},{1,0},{2,3},{3,2},{4,5},{5,4},{6,7},{7,6},{8,9},{9,8},{10,11... | collective-permute-start | bytes 3981320 | tf_op jit(solution)/shard_map/ppermute | solution.py:430
  40.9 17.8 %collective-permute-start.5 = (bf16[256,1152]{1,0:T(8,128)(2,1)}, bf16[256,1152]{1,0:T(8,128)(2,1)}, u32[]{:S(2)}, u32[]{:S(2)}) collective-permute-start(bf16[256,1152]{1,0:T(8,128)(2,1)} %get-tuple-element.44), channel_id=1, source_target_pairs={{0,1},{1,0},{2,3},{3,2},{4,5},{5,4},{6,7},{7,6},{8,9},{9,8},{10,11... | collective-permute-start | bytes 1769480 | tf_op jit(solution)/shard_map/ppermute | solution.py:590
  43.6 11.6 %collective-permute-start.7 = (bf16[128,1152]{1,0:T(8,128)(2,1)}, bf16[128,1152]{1,0:T(8,128)(2,1)S(1)}, u32[]{:S(2)}, u32[]{:S(2)}) collective-permute-start(bf16[128,1152]{1,0:T(8,128)(2,1)} %get-tuple-element.63), channel_id=1, source_target_pairs={{0,2},{1,3},{2,4},{3,5},{4,6},{5,7},{8,10},{9,11},{10,12},{11,13},... | collective-permute-start | bytes 884744 | tf_op jit(solution)/shard_map/ppermute | solution.py:590
  47.5 11.2 %collective-permute-start.8 = (bf16[128,1152]{1,0:T(8,128)(2,1)}, bf16[128,1152]{1,0:T(8,128)(2,1)}, u32[]{:S(2)}, u32[]{:S(2)}) collective-permute-start(bf16[128,1152]{1,0:T(8,128)(2,1)} %get-tuple-element.62), channel_id=1, source_target_pairs={{2,0},{3,1},{4,2},{5,3},{6,4},{7,5},{10,8},{11,9},{12,10},{13,11},... | collective-permute-start | bytes 884744 | tf_op jit(solution)/shard_map/ppermute | solution.py:590
  48.8 1.3 %copy-start.3 = (bf16[576,1152]{1,0:T(8,128)(2,1)S(1)}, bf16[576,1152]{1,0:T(8,128)(2,1)}, u32[]{:S(2)}) copy-start(bf16[576,1152]{1,0:T(8,128)(2,1)} %copy-done.2) | copy-start | bytes 3981316
  50.1 8.6 %copy-start.7 = (bf16[512,1152]{1,0:T(8,128)(2,1)S(1)}, bf16[512,1152]{1,0:T(8,128)(2,1)}, u32[]{:S(2)}) copy-start(bf16[512,1152]{1,0:T(8,128)(2,1)} %copy-done.6) | copy-start | bytes 3538948
  50.1 8.6 %copy-start.9 = (bf16[512,640]{1,0:T(8,128)(2,1)S(1)}, bf16[512,640]{1,0:T(8,128)(2,1)}, u32[]{:S(2)}) copy-start(bf16[512,640]{1,0:T(8,128)(2,1)} %copy-done.8) | copy-start | bytes 1966084
  52.1 18.5 %collective-permute-start.10 = (bf16[4,40,1152]{2,1,0:T(8,128)(2,1)S(1)}, bf16[4,40,1152]{2,1,0:T(8,128)(2,1)S(1)}, u32[]{:S(2)}, u32[]{:S(2)}) collective-permute-start(bf16[4,40,1152]{2,1,0:T(8,128)(2,1)S(1)} %get-tuple-element.41.second), channel_id=1, source_target_pairs={{0,16},{8,24},{16,0},{24,8},{1,17},{9,25},{17,1},{25,9},{2,18},{10... | collective-permute-start | bytes 1105928 | tf_op jit(solution)/shard_map/ppermute | solution.py:549
  53.7 17.0 %collective-permute-start.11 = (bf16[4,40,1152]{2,1,0:T(8,128)(2,1)S(1)}, bf16[4,40,1152]{2,1,0:T(8,128)(2,1)S(1)}, u32[]{:S(2)}, u32[]{:S(2)}) collective-permute-start(bf16[4,40,1152]{2,1,0:T(8,128)(2,1)S(1)} %get-tuple-element.42.third), channel_id=1, source_target_pairs={{0,24},{8,16},{16,8},{24,0},{1,25},{9,17},{17,9},{25,1},{2,26},{10... | collective-permute-start | bytes 1105928 | tf_op jit(solution)/shard_map/ppermute | solution.py:549
  55.2 16.7 %collective-permute-start.9 = (bf16[4,40,1152]{2,1,0:T(8,128)(2,1)S(1)}, bf16[4,40,1152]{2,1,0:T(8,128)(2,1)S(1)}, u32[]{:S(2)}, u32[]{:S(2)}) collective-permute-start(bf16[4,40,1152]{2,1,0:T(8,128)(2,1)S(1)} %get-tuple-element.40.first), channel_id=1, source_target_pairs={{0,8},{8,0},{16,24},{24,16},{1,9},{9,1},{17,25},{25,17},{2,10},{10... | collective-permute-start | bytes 1105928 | tf_op jit(solution)/shard_map/ppermute | solution.py:549
  58.7 3.5 %copy-start.18 = (bf16[1152,1728]{0,1:T(8,128)(2,1)S(1)}, bf16[1152,1728]{0,1:T(8,128)(2,1)}, u32[]{:S(2)}) copy-start(bf16[1152,1728]{0,1:T(8,128)(2,1)} %param.5) | copy-start | bytes 11943940
  62.1 10.0 %collective-permute-start.15 = (bf16[576,1152]{1,0:T(8,128)(2,1)S(1)}, bf16[576,1152]{1,0:T(8,128)(2,1)S(1)}, u32[]{:S(2)}, u32[]{:S(2)}) collective-permute-start(bf16[576,1152]{1,0:T(8,128)(2,1)S(1)} %get-tuple-element.53), channel_id=1, source_target_pairs={{0,1},{1,0},{2,3},{3,2},{4,5},{5,4},{6,7},{7,6},{8,9},{9,8},{10,11... | collective-permute-start | bytes 3981320 | tf_op jit(solution)/shard_map/ppermute | solution.py:430
  64.8 7.4 %copy-start.4 = (bf16[512,1152]{1,0:T(8,128)(2,1)}, bf16[512,1152]{1,0:T(8,128)(2,1)S(1)}, u32[]{:S(2)}) copy-start(bf16[512,1152]{1,0:T(8,128)(2,1)S(1)} %convolution_convert_fusion.refs_2_) | copy-start | bytes 3538948
  66.0 7.6 %copy-start.5 = (bf16[512,1152]{1,0:T(8,128)(2,1)}, bf16[512,1152]{1,0:T(8,128)(2,1)S(1)}, u32[]{:S(2)}) copy-start(bf16[512,1152]{1,0:T(8,128)(2,1)S(1)} %convolution_convert_fusion.1.refs_1_) | copy-start | bytes 3538948
  73.6 0.7 copy-start.10
  74.3 11.7 %collective-permute-start.16 = (bf16[4,40,1152]{2,1,0:T(8,128)(2,1)}, bf16[4,40,1152]{2,1,0:T(8,128)(2,1)S(1)}, u32[]{:S(2)}, u32[]{:S(2)}) collective-permute-start(bf16[4,40,1152]{2,1,0:T(8,128)(2,1)} %get-tuple-element.54), channel_id=1, source_target_pairs={{0,8},{8,0},{16,24},{24,16},{1,9},{9,1},{17,25},{25,17},{2,10},{10... | collective-permute-start | bytes 1105928 | tf_op jit(solution)/shard_map/ppermute | solution.py:549
  75.8 17.3 %collective-permute-start.20 = (bf16[4,40,1152]{2,1,0:T(8,128)(2,1)}, bf16[4,40,1152]{2,1,0:T(8,128)(2,1)S(1)}, u32[]{:S(2)}, u32[]{:S(2)}) collective-permute-start(bf16[4,40,1152]{2,1,0:T(8,128)(2,1)} %get-tuple-element.57), channel_id=1, source_target_pairs={{0,16},{8,24},{16,0},{24,8},{1,17},{9,25},{17,1},{25,9},{2,18},{10... | collective-permute-start | bytes 1105928 | tf_op jit(solution)/shard_map/ppermute | solution.py:549
  77.3 15.8 %collective-permute-start.21 = (bf16[4,40,1152]{2,1,0:T(8,128)(2,1)}, bf16[4,40,1152]{2,1,0:T(8,128)(2,1)S(1)}, u32[]{:S(2)}, u32[]{:S(2)}) collective-permute-start(bf16[4,40,1152]{2,1,0:T(8,128)(2,1)} %get-tuple-element.58), channel_id=1, source_target_pairs={{0,24},{8,16},{16,8},{24,0},{1,25},{9,17},{17,9},{25,1},{2,26},{10... | collective-permute-start | bytes 1105928 | tf_op jit(solution)/shard_map/ppermute | solution.py:549
  77.9 21.0 %collective-permute-start.12 = (bf16[40,1152]{1,0:T(8,128)(2,1)S(1)}, bf16[40,1152]{1,0:T(8,128)(2,1)S(1)}, u32[]{:S(2)}, u32[]{:S(2)}) collective-permute-start(bf16[40,1152]{1,0:T(8,128)(2,1)S(1)} %get-tuple-element.70), channel_id=1, source_target_pairs={{0,2},{2,0},{4,6},{6,4},{1,3},{3,1},{5,7},{7,5},{8,10},{10,8},{12,... | collective-permute-start | bytes 276488 | tf_op jit(solution)/shard_map/ppermute | solution.py:549
  80.3 18.7 %collective-permute-start.13 = (bf16[40,1152]{1,0:T(8,128)(2,1)S(1)}, bf16[40,1152]{1,0:T(8,128)(2,1)S(1)}, u32[]{:S(2)}, u32[]{:S(2)}) collective-permute-start(bf16[40,1152]{1,0:T(8,128)(2,1)S(1)} %get-tuple-element.69), channel_id=1, source_target_pairs={{0,4},{2,6},{4,0},{6,2},{1,5},{3,7},{5,1},{7,3},{8,12},{10,14},{12... | collective-permute-start | bytes 276488 | tf_op jit(solution)/shard_map/ppermute | solution.py:549
  86.1 12.9 %collective-permute-start.14 = (bf16[40,1152]{1,0:T(8,128)(2,1)S(1)}, bf16[40,1152]{1,0:T(8,128)(2,1)S(1)}, u32[]{:S(2)}, u32[]{:S(2)}) collective-permute-start(bf16[40,1152]{1,0:T(8,128)(2,1)S(1)} %get-tuple-element.68), channel_id=1, source_target_pairs={{0,6},{2,4},{4,2},{6,0},{1,7},{3,5},{5,3},{7,1},{8,14},{10,12},{12... | collective-permute-start | bytes 276488 | tf_op jit(solution)/shard_map/ppermute | solution.py:549
  94.4 6.8 %collective-permute-start.22 = (bf16[40,1152]{1,0:T(8,128)(2,1)S(1)}, bf16[40,1152]{1,0:T(8,128)(2,1)S(1)}, u32[]{:S(2)}, u32[]{:S(2)}) collective-permute-start(bf16[40,1152]{1,0:T(8,128)(2,1)S(1)} %get-tuple-element.67), channel_id=1, source_target_pairs={{0,2},{2,0},{4,6},{6,4},{1,3},{3,1},{5,7},{7,5},{8,10},{10,8},{12,... | collective-permute-start | bytes 276488 | tf_op jit(solution)/shard_map/ppermute | solution.py:549
  96.5 7.2 %collective-permute-start.23 = (bf16[40,1152]{1,0:T(8,128)(2,1)S(1)}, bf16[40,1152]{1,0:T(8,128)(2,1)S(1)}, u32[]{:S(2)}, u32[]{:S(2)}) collective-permute-start(bf16[40,1152]{1,0:T(8,128)(2,1)S(1)} %get-tuple-element.66), channel_id=1, source_target_pairs={{0,4},{2,6},{4,0},{6,2},{1,5},{3,7},{5,1},{7,3},{8,12},{10,14},{12... | collective-permute-start | bytes 276488 | tf_op jit(solution)/shard_map/ppermute | solution.py:549
  98.9 6.5 %collective-permute-start.24 = (bf16[40,1152]{1,0:T(8,128)(2,1)S(1)}, bf16[40,1152]{1,0:T(8,128)(2,1)S(1)}, u32[]{:S(2)}, u32[]{:S(2)}) collective-permute-start(bf16[40,1152]{1,0:T(8,128)(2,1)S(1)} %get-tuple-element.65), channel_id=1, source_target_pairs={{0,6},{2,4},{4,2},{6,0},{1,7},{3,5},{5,3},{7,1},{8,14},{10,12},{12... | collective-permute-start | bytes 276488 | tf_op jit(solution)/shard_map/ppermute | solution.py:549
  99.0 8.4 %collective-permute-start.17 = (bf16[40,1152]{1,0:T(8,128)(2,1)S(1)}, bf16[40,1152]{1,0:T(8,128)(2,1)S(1)}, u32[]{:S(2)}, u32[]{:S(2)}) collective-permute-start(bf16[40,1152]{1,0:T(8,128)(2,1)S(1)} %row_sum.1.refs_0_), channel_id=1, source_target_pairs={{0,8},{8,0},{16,24},{24,16},{1,9},{9,1},{17,25},{25,17},{2,10},{10... | collective-permute-start | bytes 276488 | tf_op jit(solution)/shard_map/ppermute | solution.py:549
  100.3 8.6 %collective-permute-start.18 = (bf16[40,1152]{1,0:T(8,128)(2,1)S(1)}, bf16[40,1152]{1,0:T(8,128)(2,1)S(1)}, u32[]{:S(2)}, u32[]{:S(2)}) collective-permute-start(bf16[40,1152]{1,0:T(8,128)(2,1)S(1)} %row_sum.1.refs_0_), channel_id=1, source_target_pairs={{0,16},{8,24},{16,0},{24,8},{1,17},{9,25},{17,1},{25,9},{2,18},{10... | collective-permute-start | bytes 276488 | tf_op jit(solution)/shard_map/ppermute | solution.py:549
  101.2 7.8 %collective-permute-start.19 = (bf16[40,1152]{1,0:T(8,128)(2,1)S(1)}, bf16[40,1152]{1,0:T(8,128)(2,1)S(1)}, u32[]{:S(2)}, u32[]{:S(2)}) collective-permute-start(bf16[40,1152]{1,0:T(8,128)(2,1)S(1)} %row_sum.1.refs_0_), channel_id=1, source_target_pairs={{0,24},{8,16},{16,8},{24,0},{1,25},{9,17},{17,9},{25,1},{2,26},{10... | collective-permute-start | bytes 276488 | tf_op jit(solution)/shard_map/ppermute | solution.py:549
  105.4 4.6 %collective-permute-start.25 = (bf16[40,1152]{1,0:T(8,128)(2,1)S(1)}, bf16[40,1152]{1,0:T(8,128)(2,1)S(1)}, u32[]{:S(2)}, u32[]{:S(2)}) collective-permute-start(bf16[40,1152]{1,0:T(8,128)(2,1)S(1)} %add_convert_fusion.2.refs_4_), channel_id=1, source_target_pairs={{0,8},{8,0},{16,24},{24,16},{1,9},{9,1},{17,25},{25,17},{2,10},{10... | collective-permute-start | bytes 276488 | tf_op jit(solution)/shard_map/ppermute | solution.py:549
  106.7 4.6 %collective-permute-start.26 = (bf16[40,1152]{1,0:T(8,128)(2,1)S(1)}, bf16[40,1152]{1,0:T(8,128)(2,1)S(1)}, u32[]{:S(2)}, u32[]{:S(2)}) collective-permute-start(bf16[40,1152]{1,0:T(8,128)(2,1)S(1)} %add_convert_fusion.2.refs_4_), channel_id=1, source_target_pairs={{0,16},{8,24},{16,0},{24,8},{1,17},{9,25},{17,1},{25,9},{2,18},{10... | collective-permute-start | bytes 276488 | tf_op jit(solution)/shard_map/ppermute | solution.py:549
  107.5 5.5 %collective-permute-start.27 = (bf16[40,1152]{1,0:T(8,128)(2,1)S(1)}, bf16[40,1152]{1,0:T(8,128)(2,1)S(1)}, u32[]{:S(2)}, u32[]{:S(2)}) collective-permute-start(bf16[40,1152]{1,0:T(8,128)(2,1)S(1)} %add_convert_fusion.2.refs_4_), channel_id=1, source_target_pairs={{0,24},{8,16},{16,8},{24,0},{1,25},{9,17},{17,9},{25,1},{2,26},{10... | collective-permute-start | bytes 276488 | tf_op jit(solution)/shard_map/ppermute | solution.py:549

commit v11 on v9

--- a/solution.py
+++ b/solution.py
@@ -1,3 +1,5 @@
+import functools
+
 import jax
 import jax.numpy as jnp
 from jax import lax
@@ -132,8 +134,8 @@
 
 
 def attention_kernel(
-    start_ref,
-    core_ref,
+    counts,
+    tile_ref,
     tokens_ref,
     upstream_ref,
     qt_ref,
@@ -143,7 +145,6 @@
     below_ref,
     cols_ref,
     corner_ref,
-    bias_ref,
     o_ref,
     dq_ref,
     inner_ref,
@@ -159,9 +160,11 @@
     dqt,
     left,
     turned,
+    key_row,
+    col_bias,
     sems,
 ):
-    strips = bias_ref.shape[0]
+    strips, row_tiles, col_tiles = counts
     chunk = kv.shape[1]
     chunk_own = own_ref.shape[0] // strips
     chunk_side = chunk - chunk_own
@@ -210,10 +213,39 @@
     def pick(both):
         return jnp.where(first_head, both[:, :chunk_own], both[:, chunk_own:])
 
+    tile_cols = chunk_own // SIDE
+    log_cols = tile_cols.bit_length() - 1
+    row_id, col_id = tile_ref[0], tile_ref[1]
+    col_first = col_id * tile_cols
+    left_first, right_first = col_first - REACH, col_first + tile_cols
+    if col_tiles == 2:
+        left_first = jnp.where(col_id == 0, right_first, left_first)
+    key = lax.broadcasted_iota(jnp.int32, (band, chunk_own), 0)
+    query = lax.broadcasted_iota(jnp.int32, (band, chunk_own), 1)
+    query_row = query >> log_cols
+    part = jnp.where(key >= 2 * chunk, 2, jnp.where(key >= chunk, 1, 0))
+    within = key - chunk * part
+    is_own = within < chunk_own
+    beside = within - chunk_own
+    is_right = beside >= SIDE * REACH
+    beside = jnp.where(is_right, beside - SIDE * REACH, beside)
+    side_col = jnp.where(is_right, right_first, left_first) + (beside & (REACH - 1))
+    key_col = jnp.where(is_own, col_first + (within & (tile_cols - 1)), side_col)
+    key_row[...] = SIDE * part + jnp.where(is_own, within >> log_cols, beside >> 3)
+    query_col = col_first + (query & (tile_cols - 1))
+    col_off = key_col - jnp.clip(query_col - REACH, 0, tile_cols * col_tiles - WINDOW)
+    col_bias[...] = jnp.where((col_off >= 0) & (col_off < WINDOW), 0.0, MASKED)
+
     def strip(s, carry):
-        top = start_ref[s]
+        here = row_id * strips + s
+        first = jnp.clip(here - 1, 0, strips * row_tiles - 3)
+        top = first - (row_id * strips - 1)
         rows = pl.ds(pl.multiple_of(s * chunk_own, chunk_own), chunk_own)
-        bias = bias_ref[s]
+        row_start = jnp.clip(
+            SIDE * here + query_row - REACH, 0, SIDE * strips * row_tiles - WINDOW
+        )
+        row_off = key_row[...] + SIDE * first - row_start
+        bias = jnp.where((row_off >= 0) & (row_off < WINDOW), col_bias[...], MASKED)
         bias = jnp.concatenate([bias, bias], axis=1)
         heads = [slice(2 * DH * i, 2 * DH * (i + 1)) for i in range(PAIRS)]
         k_lanes = [slice(128 * i, 128 * i + SLAB) for i in range(PAIRS)]
@@ -275,7 +307,7 @@
         copy.wait()
     lax.fori_loop(0, strips, strip, 0)
     share = sent_ref.shape[0] // 4
-    for out_ref, half in ((sent_ref, 1 - core_ref[0]), (kept_ref, core_ref[0])):
+    for out_ref, half in ((sent_ref, 1 - tile_ref[1] % 2), (kept_ref, tile_ref[1] % 2)):
         products = []
         for side, right in enumerate((dq_ref, o_ref)):
             picked = [
@@ -301,9 +333,13 @@
             corner_grad_ref[chunk_side * at : chunk_side * (at + 1), :] = side_grad
 
 
-def attention(start, token_rows, grad_rows, queries, own, grads, above, below, cols, corner, bias):
-    strips, band, chunk_own = bias.shape
-    chunk = band // 3
+def attention(token_rows, grad_rows, queries, own, grads, above, below, cols, corner):
+    chunk_own = above.shape[0]
+    strips = own.shape[0] // chunk_own
+    chunk = chunk_own + cols.shape[0] // strips
+    band = 3 * chunk
+    counts = (strips, lax.axis_size("row"), lax.axis_size("col"))
+    tile = jnp.stack([lax.axis_index("row"), lax.axis_index("col")]).astype(jnp.int32)
     token_count, width = own.shape
     whole = lambda a: pl.BlockSpec(
         a.shape, lambda _: (0,) * a.ndim, pipeline_mode=pl.Buffered(1)
@@ -318,13 +354,11 @@
         jax.ShapeDtypeStruct((token_rows.shape[1] // 2, width), jnp.bfloat16),
         jax.ShapeDtypeStruct((token_rows.shape[1] // 2, width), jnp.bfloat16),
     )
-    core = lax.axis_index("col").astype(jnp.int32).reshape(1) % 2
     return pl.pallas_call(
-        attention_kernel,
+        functools.partial(attention_kernel, counts),
         grid=(1,),
         out_shape=outs,
         in_specs=[
-            pl.BlockSpec(memory_space=pltpu.SMEM),
             pl.BlockSpec(memory_space=pltpu.SMEM),
             pl.BlockSpec(memory_space=pl.ANY),
             pl.BlockSpec(memory_space=pl.ANY),
@@ -335,7 +369,6 @@
             whole(below),
             whole(cols),
             whole(corner),
-            whole(bias),
         ],
         out_specs=tuple(whole(o) for o in outs),
         scratch_shapes=[
@@ -346,6 +379,8 @@
             pltpu.VMEM((640, chunk_own), jnp.float32),
             pltpu.VMEM((2,) + token_rows.shape, jnp.bfloat16),
             pltpu.VMEM((2,) + token_rows.shape[::-1], jnp.bfloat16),
+            pltpu.VMEM((band, chunk_own), jnp.int32),
+            pltpu.VMEM((band, chunk_own), jnp.float32),
             pltpu.SemaphoreType.DMA((2,)),
         ],
         compiler_params=pltpu.CompilerParams(vmem_limit_bytes=34 * 1024 * 1024),
@@ -355,7 +390,7 @@
             transcendentals=token_count * band * H,
         ),
         name="window_attention",
-    )(start, core, token_rows, grad_rows, queries, own, grads, above, below, cols, corner, bias)
+    )(tile, token_rows, grad_rows, queries, own, grads, above, below, cols, corner)
 
 
 def late_kernel(
@@ -499,40 +534,6 @@
     )(own, *parts)
 
 
-def window_starts(places, extent):
-    return jnp.clip(places - REACH, 0, extent - WINDOW)
-
-
-def window_bias(tile_rows, tile_cols, two_columns):
-    row_id = lax.axis_index("row")
-    col_id = lax.axis_index("col")
-    frame_rows = tile_rows * lax.axis_size("row")
-    frame_cols = tile_cols * lax.axis_size("col")
-    strips = tile_rows // SIDE
-    col_first = col_id * tile_cols
-    strip_id = jnp.arange(strips, dtype=jnp.int32)
-    first_chunk = row_id * strips - 1
-    band_chunk = jnp.clip(row_id * strips + strip_id - 1, 0, frame_rows // SIDE - 3)
-    side = jnp.arange(SIDE, dtype=jnp.int32)
-    own_cols = col_first + jnp.arange(tile_cols, dtype=jnp.int32)
-    low, high = col_first - REACH + side, col_first + tile_cols + side
-    spans = [own_cols, jnp.where(col_id == 0, high, low)] if two_columns else [own_cols, low, high]
-    chunk_rows = jnp.concatenate([jnp.repeat(side, span.shape[0]) for span in spans])
-    chunk_cols = jnp.concatenate([jnp.tile(span, SIDE) for span in spans])
-    in_band = jnp.concatenate([SIDE * j + chunk_rows for j in range(3)])
-    key_col = jnp.tile(chunk_cols, 3)
-    key_row = SIDE * band_chunk[:, None] + in_band[None, :]
-    query_row = row_id * tile_rows + SIDE * strip_id[:, None] + jnp.repeat(side, tile_cols)[None, :]
-    row_start = window_starts(query_row, frame_rows)
-    col_start = window_starts(jnp.tile(own_cols, SIDE), frame_cols)
-    row_off = key_row[:, :, None] - row_start[:, None, :]
-    col_off = key_col[:, None] - col_start[None, :]
-    row_ok = (row_off >= 0) & (row_off < WINDOW)
-    col_ok = (col_off >= 0) & (col_off < WINDOW)
-    bias = jnp.where(row_ok & col_ok[None], 0.0, MASKED).astype(jnp.float32)
-    return (band_chunk - first_chunk).astype(jnp.int32), bias
-
-
 def after(value, *earlier):
     return lax.optimization_barrier((value,) + earlier)[0]
 
@@ -614,9 +615,8 @@
     grad_att = lax.dot_general(
         out_weight, grad_rows, (((0,), (1,)), ((), ())), preferred_element_type=jnp.float32
     ).astype(jnp.bfloat16)
-    start, bias = window_bias(tile_rows, tile_cols, two_columns)
     attended, dquery, inner_grad, edge_grad, side_grad, corner_grad, sent, kept = attention(
-        start, token_rows, grad_rows, queries, keyvals, grad_att, above, below, cols, corner, bias
+        token_rows, grad_rows, queries, keyvals, grad_att, above, below, cols, corner
     )
 
     def outer(a, b):

time: 113 us -> 119 us (1.053)
  local copies, waits for them, and re-layouts: 6.49 us -> 12 us
  starting transfers between devices: 41.6 us -> 44.3 us
  matrix products: 4.67 us -> 6.06 us
  waiting for transfers between devices: 22.4 us -> 21.1 us
  Pallas kernels: 33.5 us -> 32.3 us
    unnamed x39 -> x46, local copies, waits for them, and re-layouts: 5.08 us -> 11 us
    ppermute x18, starting transfers between devices: 27.7 us -> 30.3 us  [exchanged(): got.append(lax.ppermute(part, axis, pairs))]
    ppermute x18, waiting for transfers between devices: 19 us -> 17.1 us  [exchanged(): got.append(lax.ppermute(part, axis, pairs))]
    dot_general x1, matrix products: 0.96 us -> 2.38 us  [local(): lax.dot_general(out_weight, grad_rows, (((0,), (1,)), ((), ())), preferre...]
  transfers between devices with their start and end apart: 28 -> 28, of which waited for: 11 -> 12; matrix products, arithmetic and copies ran while one was open for 8% -> 8% of each run, Pallas kernels for 10% -> 10%
where the time goes in v11:
time: 119 us
  starting transfers between devices  44.3 us (37%)
  Pallas kernels  32.3 us (27%)
  waiting for transfers between devices  21.1 us (18%)
  local copies, waits for them, and re-layouts  12 us (10%)
  matrix products  6.06 us (5%)
  other arithmetic  1.9 us (2%)
    ppermute x18, starting transfers between devices, exchanged(): got.append(lax.ppermute(part, axis, pairs))  30.3 us
    ppermute x18, waiting for transfers between devices, exchanged(): got.append(lax.ppermute(part, axis, pairs))  17.1 us
    pallas_call x1, Pallas kernels, attention(): pl.pallas_call(functools.partial(attention_kernel, counts), grid=(1,), ou...  15 us
    ppermute x8, starting transfers between devices, moved(): return lax.ppermute(block, ('row', 'col'), pairs)  13.6 us
    unnamed x46, local copies, waits for them, and re-layouts  11 us
    pallas_call x1, Pallas kernels, project(): pl.pallas_call(project_kernel, grid=(1,), out_shape=[jax.ShapeDtypeStruct...  5.98 us
    ppermute x8, waiting for transfers between devices, moved(): return lax.ppermute(block, ('row', 'col'), pairs)  4 us
    pallas_call x1, Pallas kernels, project(): pl.pallas_call(edges_kernel, grid=(1,), out_shape=[shape(edge)] * 2, in_s...  3.91 us
  transfers between devices with their start and end apart: 28, of which 12 were waited for; matrix products, arithmetic and copies ran while one was open for 8% of the time, Pallas kernels for 10%

profile of v11, /device:TPU:0, one launch (start us, length us, event | category | flops | bytes accessed | tf_op | source)
XLA Modules:
  0.0 118.6 jit_solution(14262197380739898293)
XLA Ops:
  0.6 3.9 %project_edges.1 = (bf16[128,1152]{1,0:T(8,128)(2,1)}, bf16[128,1152]{1,0:T(8,128)(2,1)}) custom-call(bf16[512,1152]{1,0:T(8,128)(2,1)} %bitcast.39, bf16[1728,1152]{1,0:T(8,128)(2,1)} %bitcast.50), custom_call_target="tpu_custom_call" | custom-call | flops 1 | bytes 1 | tf_op jit(solution)/shard_map/project_edges/pallas_call | solution.py:101
  4.6 1.3 %collective-permute-start.1 = (bf16[128,1152]{1,0:T(8,128)(2,1)}, bf16[128,1152]{1,0:T(8,128)(2,1)S(1)}, u32[]{:S(2)}, u32[]{:S(2)}) collective-permute-start(bf16[128,1152]{1,0:T(8,128)(2,1)} %get-tuple-element.33.top_ref), channel_id=1, source_target_pairs={{2,0},{3,1},{4,2},{5,3},{6,4},{7,5},{10,8},{11,9},{12,10},{13,11},... | collective-permute-start | bytes 884744 | tf_op jit(solution)/shard_map/ppermute | solution.py:591
  5.9 5.6 %collective-permute-start = (bf16[128,1152]{1,0:T(8,128)(2,1)}, bf16[128,1152]{1,0:T(8,128)(2,1)S(1)}, u32[]{:S(2)}, u32[]{:S(2)}) collective-permute-start(bf16[128,1152]{1,0:T(8,128)(2,1)} %get-tuple-element.36), channel_id=1, source_target_pairs={{0,2},{1,3},{2,4},{3,5},{4,6},{5,7},{8,10},{9,11},{10,12},{11,13},... | collective-permute-start | bytes 884744 | tf_op jit(solution)/shard_map/ppermute | solution.py:591
  11.4 6.0 %project.1 = (bf16[576,512]{1,0:T(8,128)(2,1)}, bf16[512,1152]{1,0:T(8,128)(2,1)}, bf16[256,1152]{1,0:T(8,128)(2,1)}) custom-call(s32[1]{0:T(128)} %bitcast.own_ref, bf16[128,1152]{1,0:T(8,128)(2,1)} %get-tuple-element.33.top_ref, bf16[512,1152]{1,0:T(8,128)(2,1)} %bitcast.40, bf16[1728,1152]{1,0:T(8,128)(2,1)} %bitcast.51), custom_call_target="tpu_custom_call" | custom-call | flops 1 | bytes 1 | tf_op jit(solution)/shard_map/project/pallas_call | solution.py:117
  17.6 0.4 collective-permute-done.above_ref
  18.0 0.2 collective-permute-start.3
  18.3 0.4 copy-done.13
  18.7 2.4 %convolution_convert_fusion.2.g_ref = bf16[576,512]{1,0:T(8,128)(2,1)S(1)} fusion(bf16[1152,576]{0,1:T(8,128)(2,1)S(1)} %copy-done, bf16[512,1152]{1,0:T(8,128)(2,1)} %bitcast.47), kind=kOutput, calls=%fused_computation.2 | convolution fusion | flops 679772160 | bytes 3096576 | tf_op jit(solution)/shard_map/dot_general | solution.py:615
  21.1 0.8 copy-done.20
  22.0 1.1 copy-done.21
  23.0 15.0 %window_attention.1 = (bf16[512,640]{1,0:T(8,128)(2,1)S(1)}, bf16[512,640]{1,0:T(8,128)(2,1)S(1)}, bf16[512,1152]{1,0:T(8,128)(2,1)S(1)}, bf16[256,1152]{1,0:T(8...) custom-call(s32[2]{0:T(128)S(1)} %pad_add_fusion.tile_ref, ...), custom_call_target="tpu_custom_call" | custom-call | flops 4076863488 | bytes 16777216 | tf_op jit(solution)/shard_map/window_attention/pallas_call | solution.py:357
  38.1 1.1 copy-done.2
  39.1 1.0 copy-done.6
  40.2 0.8 copy-done.8
  41.0 0.8 copy-done.10
  41.8 1.1 copy-done.15
  42.9 0.8 copy-done.18
  43.7 0.1 collective-permute-start.6
  43.9 0.4 collective-permute-start.4
  44.2 0.1 collective-permute-start.5
  44.4 1.1 collective-permute-done.6
  45.5 0.1 pad_select_fusion
  45.6 0.9 copy-done.11
  46.6 0.1 fusion
  46.7 0.9 fusion.1
  47.5 4.7 %collective-permute-start.7 = (bf16[128,1152]{1,0:T(8,128)(2,1)}, bf16[128,1152]{1,0:T(8,128)(2,1)S(1)}, u32[]{:S(2)}, u32[]{:S(2)}) collective-permute-start(bf16[128,1152]{1,0:T(8,128)(2,1)} %get-tuple-element.63), channel_id=1, source_target_pairs={{0,2},{1,3},{2,4},{3,5},{4,6},{5,7},{8,10},{9,11},{10,12},{11,13},... | collective-permute-start | bytes 884744 | tf_op jit(solution)/shard_map/ppermute | solution.py:591
  52.2 1.5 %collective-permute-start.8 = (bf16[128,1152]{1,0:T(8,128)(2,1)}, bf16[128,1152]{1,0:T(8,128)(2,1)}, u32[]{:S(2)}, u32[]{:S(2)}) collective-permute-start(bf16[128,1152]{1,0:T(8,128)(2,1)} %get-tuple-element.62), channel_id=1, source_target_pairs={{2,0},{3,1},{4,2},{5,3},{6,4},{7,5},{10,8},{11,9},{12,10},{13,11},... | collective-permute-start | bytes 884744 | tf_op jit(solution)/shard_map/ppermute | solution.py:591
  53.7 1.3 %copy-done.3 = bf16[576,1152]{1,0:T(8,128)(2,1)S(1)} copy-done((bf16[576,1152]{1,0:T(8,128)(2,1)S(1)}, bf16[576,1152]{1,0:T(8,128)(2,1)}, u32[]{:S(2)}) %copy-start.3) | copy-done | bytes 1327128
  55.0 2.0 %core_parts.2 = (bf16[4,40,1152]{2,1,0:T(8,128)(2,1)S(1)}, bf16[4,40,1152]{2,1,0:T(8,128)(2,1)S(1)}, bf16[4,40,1152]{2,1,0:T(8,128)(2,1)S(1)}, bf16[4,40,1152]{2,1,0:T(8,128)(2,1)S(1)}) custom-call(s32[1]{0:T(128)} %bitcast.1.own_ref, bf16[576,1152]{1,0:T(8,128)(2,1)S(1)} %copy-done.3, bf16[576,1152]{1,0:T(8,128)(2,1)} %collective-permute-done.4.got_ref), custom_call_target="tpu_custom_call" | custom-call | flops 1 | bytes 1 | tf_op jit(solution)/shard_map/core_parts/pallas_call | solution.py:470
  57.0 1.7 %collective-permute-start.10 = (bf16[4,40,1152]{2,1,0:T(8,128)(2,1)S(1)}, bf16[4,40,1152]{2,1,0:T(8,128)(2,1)S(1)}, u32[]{:S(2)}, u32[]{:S(2)}) collective-permute-start(bf16[4,40,1152]{2,1,0:T(8,128)(2,1)S(1)} %get-tuple-element.41.second), channel_id=1, source_target_pairs={{0,16},{8,24},{16,0},{24,8},{1,17},{9,25},{17,1},{25,9},{2,18},{10... | collective-permute-start | bytes 1105928 | tf_op jit(solution)/shard_map/ppermute | solution.py:550
  58.8 1.4 %collective-permute-start.11 = (bf16[4,40,1152]{2,1,0:T(8,128)(2,1)S(1)}, bf16[4,40,1152]{2,1,0:T(8,128)(2,1)S(1)}, u32[]{:S(2)}, u32[]{:S(2)}) collective-permute-start(bf16[4,40,1152]{2,1,0:T(8,128)(2,1)S(1)} %get-tuple-element.42.third), channel_id=1, source_target_pairs={{0,24},{8,16},{16,8},{24,0},{1,25},{9,17},{17,9},{25,1},{2,26},{10... | collective-permute-start | bytes 1105928 | tf_op jit(solution)/shard_map/ppermute | solution.py:550
  60.2 0.5 collective-permute-start.9
  60.7 2.5 %collective-permute-done.8.below_ref = bf16[128,1152]{1,0:T(8,128)(2,1)} collective-permute-done((bf16[128,1152]{1,0:T(8,128)(2,1)}, bf16[128,1152]{1,0:T(8,128)(2,1)}, u32[]{:S(2)}, u32[]{:S(2)}) %collective-permute-start.8) | collective-permute-done | bytes 294944 | tf_op jit(solution)/shard_map/ppermute | solution.py:591
  63.2 3.4 %late_weight_grad_halves.1 = (bf16[576,1152]{1,0:T(8,128)(2,1)S(1)}, bf16[576,1152]{1,0:T(8,128)(2,1)S(1)}, bf16[512,1728]{1,0:T(8,128)(2,1)S(1)}, bf16[512,576]{1,0:T(8,128)(2,1)S(1)}) custom-call(s32[1]{0:T(128)} %bitcast.own_ref, bf16[4,40,1152]{2,1,0:T(8,128)(2,1)S(1)} %get-tuple-element.40.first, bf16[4,40,1152]{2,1,0:T(8,128)(2,1)S(1)} %get-tuple-element.41.second, ...), custom_call_target="tpu_custom_call" | custom-call | flops 1 | bytes 1 | tf_op jit(solution)/shard_map/late_weight_grad_halves/pallas_call | solution.py:433
  66.7 2.5 %convolution_convert_fusion.refs_2_ = bf16[512,1152]{1,0:T(8,128)(2,1)S(1)} fusion(bf16[512,1728]{1,0:T(8,128)(2,1)S(1)} %get-tuple-element.50, bf16[1152,1728]{0,1:T(8,128)(2,1)S(1)} %copy-done.22), kind=kOutput, calls=%fused_computation | convolution fusion | flops 2039021568 | bytes 6930432 | tf_op jit(solution)/shard_map/dot_general | solution.py:33
  69.3 1.2 convolution_convert_fusion.1.refs_1_
  70.4 4.9 %collective-permute-done.10 = bf16[4,40,1152]{2,1,0:T(8,128)(2,1)S(1)} collective-permute-done((bf16[4,40,1152]{2,1,0:T(8,128)(2,1)S(1)}, bf16[4,40,1152]{2,1,0:T(8,128)(2,1)S(1)}, u32[]{:S(2)}, u32[]{:S(2)}) %collective-permute-start.10) | collective-permute-done | bytes 368672 | tf_op jit(solution)/shard_map/ppermute | solution.py:550
  75.4 1.2 %collective-permute-done.9 = bf16[4,40,1152]{2,1,0:T(8,128)(2,1)S(1)} collective-permute-done((bf16[4,40,1152]{2,1,0:T(8,128)(2,1)S(1)}, bf16[4,40,1152]{2,1,0:T(8,128)(2,1)S(1)}, u32[]{:S(2)}, u32[]{:S(2)}) %collective-permute-start.9) | collective-permute-done | bytes 368672 | tf_op jit(solution)/shard_map/ppermute | solution.py:550
  76.6 0.2 add_convert_fusion.1.refs_0_
  76.8 0.5 core_parts.3
  77.4 0.7 copy-done.12
  78.1 1.6 %collective-permute-start.16 = (bf16[4,40,1152]{2,1,0:T(8,128)(2,1)S(1)}, bf16[4,40,1152]{2,1,0:T(8,128)(2,1)S(1)}, u32[]{:S(2)}, u32[]{:S(2)}) collective-permute-start(bf16[4,40,1152]{2,1,0:T(8,128)(2,1)S(1)} %get-tuple-element.54), channel_id=1, source_target_pairs={{0,8},{8,0},{16,24},{24,16},{1,9},{9,1},{17,25},{25,17},{2,10},{10... | collective-permute-start | bytes 1105928 | tf_op jit(solution)/shard_map/ppermute | solution.py:550
  79.8 1.5 %collective-permute-start.20 = (bf16[4,40,1152]{2,1,0:T(8,128)(2,1)S(1)}, bf16[4,40,1152]{2,1,0:T(8,128)(2,1)S(1)}, u32[]{:S(2)}, u32[]{:S(2)}) collective-permute-start(bf16[4,40,1152]{2,1,0:T(8,128)(2,1)S(1)} %get-tuple-element.57), channel_id=1, source_target_pairs={{0,16},{8,24},{16,0},{24,8},{1,17},{9,25},{17,1},{25,9},{2,18},{10... | collective-permute-start | bytes 1105928 | tf_op jit(solution)/shard_map/ppermute | solution.py:550
  81.3 0.3 collective-permute-start.21
  81.7 2.4 %collective-permute-start.12 = (bf16[40,1152]{1,0:T(8,128)(2,1)S(1)}, bf16[40,1152]{1,0:T(8,128)(2,1)S(1)}, u32[]{:S(2)}, u32[]{:S(2)}) collective-permute-start(bf16[40,1152]{1,0:T(8,128)(2,1)S(1)} %get-tuple-element.70), channel_id=1, source_target_pairs={{0,2},{2,0},{4,6},{6,4},{1,3},{3,1},{5,7},{7,5},{8,10},{10,8},{12,... | collective-permute-start | bytes 276488 | tf_op jit(solution)/shard_map/ppermute | solution.py:550
  84.1 3.3 %collective-permute-start.13 = (bf16[40,1152]{1,0:T(8,128)(2,1)S(1)}, bf16[40,1152]{1,0:T(8,128)(2,1)S(1)}, u32[]{:S(2)}, u32[]{:S(2)}) collective-permute-start(bf16[40,1152]{1,0:T(8,128)(2,1)S(1)} %get-tuple-element.69), channel_id=1, source_target_pairs={{0,4},{2,6},{4,0},{6,2},{1,5},{3,7},{5,1},{7,3},{8,12},{10,14},{12... | collective-permute-start | bytes 276488 | tf_op jit(solution)/shard_map/ppermute | solution.py:550
  87.3 2.3 %collective-permute-done.16.refs_0_ = bf16[4,40,1152]{2,1,0:T(8,128)(2,1)S(1)} collective-permute-done((bf16[4,40,1152]{2,1,0:T(8,128)(2,1)S(1)}, bf16[4,40,1152]{2,1,0:T(8,128)(2,1)S(1)}, u32[]{:S(2)}, u32[]{:S(2)}) %collective-permute-start.16) | collective-permute-done | bytes 368672 | tf_op jit(solution)/shard_map/ppermute | solution.py:550
  89.7 5.1 %collective-permute-start.14 = (bf16[40,1152]{1,0:T(8,128)(2,1)S(1)}, bf16[40,1152]{1,0:T(8,128)(2,1)S(1)}, u32[]{:S(2)}, u32[]{:S(2)}) collective-permute-start(bf16[40,1152]{1,0:T(8,128)(2,1)S(1)} %get-tuple-element.68), channel_id=1, source_target_pairs={{0,6},{2,4},{4,2},{6,0},{1,7},{3,5},{5,3},{7,1},{8,14},{10,12},{12... | collective-permute-start | bytes 276488 | tf_op jit(solution)/shard_map/ppermute | solution.py:550
  94.7 1.9 %collective-permute-done.20 = bf16[4,40,1152]{2,1,0:T(8,128)(2,1)S(1)} collective-permute-done((bf16[4,40,1152]{2,1,0:T(8,128)(2,1)S(1)}, bf16[4,40,1152]{2,1,0:T(8,128)(2,1)S(1)}, u32[]{:S(2)}, u32[]{:S(2)}) %collective-permute-start.20) | collective-permute-done | bytes 368672 | tf_op jit(solution)/shard_map/ppermute | solution.py:550
  96.6 1.3 %add_convert_fusion = bf16[4,40,1152]{2,1,0:T(8,128)(2,1)S(1)} fusion(bf16[4,40,1152]{2,1,0:T(8,128)(2,1)} %collective-permute-done.21, bf16[4,40,1152]{2,1,0:T(8,128)(2,1)S(1)} %collective-permute-done.20, bf16[4,40,1152]{2,1,0:T(8,128)(2,1)S(1)} %collective-permute-done.16.refs_0_, bf16[4,40,1152]{2,1,0:T(8,128)(2,1)} %copy-done.12), kind=kLoop, calls=%fused_computation.6 | loop fusion | flops 1474560 | bytes 1843200 | tf_op jit(solution)/shard_map/convert_element_type | solution.py:560
  98.0 2.1 %collective-permute-start.22 = (bf16[40,1152]{1,0:T(8,128)(2,1)S(1)}, bf16[40,1152]{1,0:T(8,128)(2,1)S(1)}, u32[]{:S(2)}, u32[]{:S(2)}) collective-permute-start(bf16[40,1152]{1,0:T(8,128)(2,1)S(1)} %get-tuple-element.67), channel_id=1, source_target_pairs={{0,2},{2,0},{4,6},{6,4},{1,3},{3,1},{5,7},{7,5},{8,10},{10,8},{12,... | collective-permute-start | bytes 276488 | tf_op jit(solution)/shard_map/ppermute | solution.py:550
  100.1 3.1 %collective-permute-start.23 = (bf16[40,1152]{1,0:T(8,128)(2,1)S(1)}, bf16[40,1152]{1,0:T(8,128)(2,1)S(1)}, u32[]{:S(2)}, u32[]{:S(2)}) collective-permute-start(bf16[40,1152]{1,0:T(8,128)(2,1)S(1)} %get-tuple-element.66), channel_id=1, source_target_pairs={{0,4},{2,6},{4,0},{6,2},{1,5},{3,7},{5,1},{7,3},{8,12},{10,14},{12... | collective-permute-start | bytes 276488 | tf_op jit(solution)/shard_map/ppermute | solution.py:550
  103.3 1.4 %collective-permute-start.17 = (bf16[40,1152]{1,0:T(8,128)(2,1)S(1)}, bf16[40,1152]{1,0:T(8,128)(2,1)S(1)}, u32[]{:S(2)}, u32[]{:S(2)}) collective-permute-start(bf16[40,1152]{1,0:T(8,128)(2,1)S(1)} %row_sum.1.refs_0_), channel_id=1, source_target_pairs={{0,8},{8,0},{16,24},{24,16},{1,9},{9,1},{17,25},{25,17},{2,10},{10... | collective-permute-start | bytes 276488 | tf_op jit(solution)/shard_map/ppermute | solution.py:550
  104.7 0.7 collective-permute-start.18
  105.4 1.4 %collective-permute-start.19 = (bf16[40,1152]{1,0:T(8,128)(2,1)S(1)}, bf16[40,1152]{1,0:T(8,128)(2,1)S(1)}, u32[]{:S(2)}, u32[]{:S(2)}) collective-permute-start(bf16[40,1152]{1,0:T(8,128)(2,1)S(1)} %row_sum.1.refs_0_), channel_id=1, source_target_pairs={{0,24},{8,16},{16,8},{24,0},{1,25},{9,17},{17,9},{25,1},{2,26},{10... | collective-permute-start | bytes 276488 | tf_op jit(solution)/shard_map/ppermute | solution.py:550
  106.8 0.7 collective-permute-done.23
  107.5 2.0 %collective-permute-done.24 = bf16[40,1152]{1,0:T(8,128)(2,1)S(1)} collective-permute-done((bf16[40,1152]{1,0:T(8,128)(2,1)S(1)}, bf16[40,1152]{1,0:T(8,128)(2,1)S(1)}, u32[]{:S(2)}, u32[]{:S(2)}) %collective-permute-start.24) | collective-permute-done | bytes 92192 | tf_op jit(solution)/shard_map/ppermute | solution.py:550
  109.6 1.4 %collective-permute-start.25 = (bf16[40,1152]{1,0:T(8,128)(2,1)S(1)}, bf16[40,1152]{1,0:T(8,128)(2,1)S(1)}, u32[]{:S(2)}, u32[]{:S(2)}) collective-permute-start(bf16[40,1152]{1,0:T(8,128)(2,1)S(1)} %add_convert_fusion.2.refs_4_), channel_id=1, source_target_pairs={{0,8},{8,0},{16,24},{24,16},{1,9},{9,1},{17,25},{25,17},{2,10},{10... | collective-permute-start | bytes 276488 | tf_op jit(solution)/shard_map/ppermute | solution.py:550
  111.0 0.7 collective-permute-start.26
  111.7 1.4 %collective-permute-start.27 = (bf16[40,1152]{1,0:T(8,128)(2,1)S(1)}, bf16[40,1152]{1,0:T(8,128)(2,1)S(1)}, u32[]{:S(2)}, u32[]{:S(2)}) collective-permute-start(bf16[40,1152]{1,0:T(8,128)(2,1)S(1)} %add_convert_fusion.2.refs_4_), channel_id=1, source_target_pairs={{0,24},{8,16},{16,8},{24,0},{1,25},{9,17},{17,9},{25,1},{2,26},{10... | collective-permute-start | bytes 276488 | tf_op jit(solution)/shard_map/ppermute | solution.py:550
  113.2 1.1 collective-permute-done.25.refs_5_
  114.2 1.3 %collective-permute-done.26.refs_6_ = bf16[40,1152]{1,0:T(8,128)(2,1)S(1)} collective-permute-done((bf16[40,1152]{1,0:T(8,128)(2,1)S(1)}, bf16[40,1152]{1,0:T(8,128)(2,1)S(1)}, u32[]{:S(2)}, u32[]{:S(2)}) %collective-permute-start.26) | collective-permute-done | bytes 92192 | tf_op jit(solution)/shard_map/ppermute | solution.py:550
  115.6 1.6 %collective-permute-done.27.refs_7_ = bf16[40,1152]{1,0:T(8,128)(2,1)S(1)} collective-permute-done((bf16[40,1152]{1,0:T(8,128)(2,1)S(1)}, bf16[40,1152]{1,0:T(8,128)(2,1)S(1)}, u32[]{:S(2)}, u32[]{:S(2)}) %collective-permute-start.27) | collective-permute-done | bytes 92192 | tf_op jit(solution)/shard_map/ppermute | solution.py:550
  117.2 1.4 %weight_grads.1 = (f32[144,1728]{1,0:T(8,128)}, f32[144,576]{1,0:T(8,128)}) custom-call(s32[1]{0:T(128)} %bitcast.1.own_ref, bf16[40,1152]{1,0:T(8,128)(2,1)S(1)} %row_sum.1.refs_0_, bf16[40,1152]{1,0:T(8,128)(2,1)S(1)} %collective-permute-done.17.refs_1_, bf16[40,1152]{1,0:T(8,128)(2,1)S(1)} %collective-permute-done.18.refs_2_, ...), custom_call_target="tpu_custom_call" | custom-call | flops 1 | bytes 1 | tf_op jit(solution)/shard_map/weight_grads/pallas_call | solution.py:523
  (62 shorter events, 0.6 us)
Async XLA Ops:
  0.6 18.1 %copy-start = (bf16[1152,576]{0,1:T(8,128)(2,1)S(1)}, bf16[1152,576]{0,1:T(8,128)(2,1)}, u32[]{:S(2)}) copy-start(bf16[1152,576]{0,1:T(8,128)(2,1)} %param.6) | copy-start | bytes 3981316
  4.6 13.0 %collective-permute-start.1 = (bf16[128,1152]{1,0:T(8,128)(2,1)}, bf16[128,1152]{1,0:T(8,128)(2,1)S(1)}, u32[]{:S(2)}, u32[]{:S(2)}) collective-permute-start(bf16[128,1152]{1,0:T(8,128)(2,1)} %get-tuple-element.33.top_ref), channel_id=1, source_target_pairs={{2,0},{3,1},{4,2},{5,3},{6,4},{7,5},{10,8},{11,9},{12,10},{13,11},... | collective-permute-start | bytes 884744 | tf_op jit(solution)/shard_map/ppermute | solution.py:591
  5.9 12.1 %collective-permute-start = (bf16[128,1152]{1,0:T(8,128)(2,1)}, bf16[128,1152]{1,0:T(8,128)(2,1)S(1)}, u32[]{:S(2)}, u32[]{:S(2)}) collective-permute-start(bf16[128,1152]{1,0:T(8,128)(2,1)} %get-tuple-element.36), channel_id=1, source_target_pairs={{0,2},{1,3},{2,4},{3,5},{4,6},{5,7},{8,10},{9,11},{10,12},{11,13},... | collective-permute-start | bytes 884744 | tf_op jit(solution)/shard_map/ppermute | solution.py:591
  17.4 3.7 %collective-permute-start.2 = (bf16[256,1152]{1,0:T(8,128)(2,1)}, bf16[256,1152]{1,0:T(8,128)(2,1)S(1)}, u32[]{:S(2)}, u32[]{:S(2)}) collective-permute-start(bf16[256,1152]{1,0:T(8,128)(2,1)} %get-tuple-element.37), channel_id=1, source_target_pairs={{0,1},{1,0},{2,3},{3,2},{4,5},{5,4},{6,7},{7,6},{8,9},{9,8},{10,11... | collective-permute-start | bytes 1769480 | tf_op jit(solution)/shard_map/ppermute | solution.py:591
  18.0 0.7 copy-start.13
  18.0 3.1 %collective-permute-start.3 = (bf16[16,8,1152]{2,1,0:T(8,128)(2,1)S(1)}, bf16[16,8,1152]{2,1,0:T(8,128)(2,1)S(1)}, u32[]{:S(2)}, u32[]{:S(2)}) collective-permute-start(bf16[16,8,1152]{2,1,0:T(8,128)(2,1)S(1)} %pad_maximum_fusion), channel_id=1, source_target_pairs={{0,1},{1,0},{2,3},{3,2},{4,5},{5,4},{6,7},{7,6},{8,9},{9,8},{10,11... | collective-permute-start | bytes 884744 | tf_op jit(solution)/shard_map/ppermute | solution.py:591
  18.7 3.3 %copy-start.1 = (bf16[1,32,16,1152]{3,2,1,0:T(8,128)(2,1)S(1)}, bf16[1,32,16,1152]{3,2,1,0:T(8,128)(2,1)}, u32[]{:S(2)}) copy-start(bf16[1,32,16,1152]{3,2,1,0:T(8,128)(2,1)} %param.4) | copy-start | bytes 3538948
  18.7 3.3 %copy-start.14 = (bf16[128,1152]{1,0:T(8,128)(2,1)S(1)}, bf16[128,1152]{1,0:T(8,128)(2,1)}, u32[]{:S(2)}) copy-start(bf16[128,1152]{1,0:T(8,128)(2,1)} %copy-done.13) | copy-start | bytes 884740
  18.7 3.3 %copy-start.16 = (bf16[1,32,16,1152]{3,2,1,0:T(8,128)(2,1)S(1)}, bf16[1,32,16,1152]{3,2,1,0:T(8,128)(2,1)}, u32[]{:S(2)}) copy-start(bf16[1,32,16,1152]{3,2,1,0:T(8,128)(2,1)} %param.7) | copy-start | bytes 3538948
  18.7 3.3 %copy-start.17 = (bf16[512,1152]{1,0:T(8,128)(2,1)S(1)}, bf16[512,1152]{1,0:T(8,128)(2,1)}, u32[]{:S(2)}) copy-start(bf16[512,1152]{1,0:T(8,128)(2,1)} %get-tuple-element.35.own_ref) | copy-start | bytes 3538948
  18.7 3.2 %copy-start.19 = (bf16[576,512]{1,0:T(8,128)(2,1)S(1)}, bf16[576,512]{1,0:T(8,128)(2,1)}, u32[]{:S(2)}) copy-start(bf16[576,512]{1,0:T(8,128)(2,1)} %get-tuple-element.34.qt_ref) | copy-start | bytes 1769476
  21.1 0.8 copy-start.20
  22.0 1.1 copy-start.21
  38.0 1.1 copy-start.2
  39.1 1.0 copy-start.6
  40.2 0.8 copy-start.8
  41.0 0.8 copy-start.10
  41.8 1.1 copy-start.15
  42.9 0.8 copy-start.18
  43.7 1.8 %collective-permute-start.6 = (bf16[128,1152]{1,0:T(8,128)(2,1)}, bf16[128,1152]{1,0:T(8,128)(2,1)S(1)}, u32[]{:S(2)}, u32[]{:S(2)}) collective-permute-start(bf16[128,1152]{1,0:T(8,128)(2,1)} %get-tuple-element.46), channel_id=1, source_target_pairs={{0,1},{1,0},{2,3},{3,2},{4,5},{5,4},{6,7},{7,6},{8,9},{9,8},{10,11... | collective-permute-start | bytes 884744 | tf_op jit(solution)/shard_map/ppermute | solution.py:591
  43.9 9.8 %collective-permute-start.4 = (bf16[576,1152]{1,0:T(8,128)(2,1)}, bf16[576,1152]{1,0:T(8,128)(2,1)}, u32[]{:S(2)}, u32[]{:S(2)}) collective-permute-start(bf16[576,1152]{1,0:T(8,128)(2,1)} %copy-done.15), channel_id=1, source_target_pairs={{0,1},{1,0},{2,3},{3,2},{4,5},{5,4},{6,7},{7,6},{8,9},{9,8},{10,11... | collective-permute-start | bytes 3981320 | tf_op jit(solution)/shard_map/ppermute | solution.py:465
  44.2 19.0 %collective-permute-start.5 = (bf16[256,1152]{1,0:T(8,128)(2,1)}, bf16[256,1152]{1,0:T(8,128)(2,1)}, u32[]{:S(2)}, u32[]{:S(2)}) collective-permute-start(bf16[256,1152]{1,0:T(8,128)(2,1)} %copy-done.18), channel_id=1, source_target_pairs={{0,1},{1,0},{2,3},{3,2},{4,5},{5,4},{6,7},{7,6},{8,9},{9,8},{10,11... | collective-permute-start | bytes 1769480 | tf_op jit(solution)/shard_map/ppermute | solution.py:591
  45.5 1.1 copy-start.11
  47.5 12.7 %collective-permute-start.7 = (bf16[128,1152]{1,0:T(8,128)(2,1)}, bf16[128,1152]{1,0:T(8,128)(2,1)S(1)}, u32[]{:S(2)}, u32[]{:S(2)}) collective-permute-start(bf16[128,1152]{1,0:T(8,128)(2,1)} %get-tuple-element.63), channel_id=1, source_target_pairs={{0,2},{1,3},{2,4},{3,5},{4,6},{5,7},{8,10},{9,11},{10,12},{11,13},... | collective-permute-start | bytes 884744 | tf_op jit(solution)/shard_map/ppermute | solution.py:591
  52.2 11.0 %collective-permute-start.8 = (bf16[128,1152]{1,0:T(8,128)(2,1)}, bf16[128,1152]{1,0:T(8,128)(2,1)}, u32[]{:S(2)}, u32[]{:S(2)}) collective-permute-start(bf16[128,1152]{1,0:T(8,128)(2,1)} %get-tuple-element.62), channel_id=1, source_target_pairs={{2,0},{3,1},{4,2},{5,3},{6,4},{7,5},{10,8},{11,9},{12,10},{13,11},... | collective-permute-start | bytes 884744 | tf_op jit(solution)/shard_map/ppermute | solution.py:591
  53.7 1.3 %copy-start.3 = (bf16[576,1152]{1,0:T(8,128)(2,1)S(1)}, bf16[576,1152]{1,0:T(8,128)(2,1)}, u32[]{:S(2)}) copy-start(bf16[576,1152]{1,0:T(8,128)(2,1)} %copy-done.2) | copy-start | bytes 3981316
  55.0 8.2 %copy-start.7 = (bf16[512,1152]{1,0:T(8,128)(2,1)S(1)}, bf16[512,1152]{1,0:T(8,128)(2,1)}, u32[]{:S(2)}) copy-start(bf16[512,1152]{1,0:T(8,128)(2,1)} %copy-done.6) | copy-start | bytes 3538948
  55.0 8.2 %copy-start.9 = (bf16[512,640]{1,0:T(8,128)(2,1)S(1)}, bf16[512,640]{1,0:T(8,128)(2,1)}, u32[]{:S(2)}) copy-start(bf16[512,640]{1,0:T(8,128)(2,1)} %copy-done.8) | copy-start | bytes 1966084
  57.0 18.3 %collective-permute-start.10 = (bf16[4,40,1152]{2,1,0:T(8,128)(2,1)S(1)}, bf16[4,40,1152]{2,1,0:T(8,128)(2,1)S(1)}, u32[]{:S(2)}, u32[]{:S(2)}) collective-permute-start(bf16[4,40,1152]{2,1,0:T(8,128)(2,1)S(1)} %get-tuple-element.41.second), channel_id=1, source_target_pairs={{0,16},{8,24},{16,0},{24,8},{1,17},{9,25},{17,1},{25,9},{2,18},{10... | collective-permute-start | bytes 1105928 | tf_op jit(solution)/shard_map/ppermute | solution.py:550
  58.8 16.6 %collective-permute-start.11 = (bf16[4,40,1152]{2,1,0:T(8,128)(2,1)S(1)}, bf16[4,40,1152]{2,1,0:T(8,128)(2,1)S(1)}, u32[]{:S(2)}, u32[]{:S(2)}) collective-permute-start(bf16[4,40,1152]{2,1,0:T(8,128)(2,1)S(1)} %get-tuple-element.42.third), channel_id=1, source_target_pairs={{0,24},{8,16},{16,8},{24,0},{1,25},{9,17},{17,9},{25,1},{2,26},{10... | collective-permute-start | bytes 1105928 | tf_op jit(solution)/shard_map/ppermute | solution.py:550
  60.2 16.4 %collective-permute-start.9 = (bf16[4,40,1152]{2,1,0:T(8,128)(2,1)S(1)}, bf16[4,40,1152]{2,1,0:T(8,128)(2,1)S(1)}, u32[]{:S(2)}, u32[]{:S(2)}) collective-permute-start(bf16[4,40,1152]{2,1,0:T(8,128)(2,1)S(1)} %get-tuple-element.40.first), channel_id=1, source_target_pairs={{0,8},{8,0},{16,24},{24,16},{1,9},{9,1},{17,25},{25,17},{2,10},{10... | collective-permute-start | bytes 1105928 | tf_op jit(solution)/shard_map/ppermute | solution.py:550
  63.2 3.5 %copy-start.22 = (bf16[1152,1728]{0,1:T(8,128)(2,1)S(1)}, bf16[1152,1728]{0,1:T(8,128)(2,1)}, u32[]{:S(2)}) copy-start(bf16[1152,1728]{0,1:T(8,128)(2,1)} %param.5) | copy-start | bytes 11943940
  66.6 10.2 %collective-permute-start.15 = (bf16[576,1152]{1,0:T(8,128)(2,1)S(1)}, bf16[576,1152]{1,0:T(8,128)(2,1)S(1)}, u32[]{:S(2)}, u32[]{:S(2)}) collective-permute-start(bf16[576,1152]{1,0:T(8,128)(2,1)S(1)} %get-tuple-element.53), channel_id=1, source_target_pairs={{0,1},{1,0},{2,3},{3,2},{4,5},{5,4},{6,7},{7,6},{8,9},{9,8},{10,11... | collective-permute-start | bytes 3981320 | tf_op jit(solution)/shard_map/ppermute | solution.py:465
  69.2 7.6 %copy-start.4 = (bf16[512,1152]{1,0:T(8,128)(2,1)}, bf16[512,1152]{1,0:T(8,128)(2,1)S(1)}, u32[]{:S(2)}) copy-start(bf16[512,1152]{1,0:T(8,128)(2,1)S(1)} %convolution_convert_fusion.refs_2_) | copy-start | bytes 3538948
  70.4 7.0 %copy-start.5 = (bf16[512,1152]{1,0:T(8,128)(2,1)}, bf16[512,1152]{1,0:T(8,128)(2,1)S(1)}, u32[]{:S(2)}) copy-start(bf16[512,1152]{1,0:T(8,128)(2,1)S(1)} %convolution_convert_fusion.1.refs_1_) | copy-start | bytes 3538948
  77.4 0.7 copy-start.12
  78.1 11.5 %collective-permute-start.16 = (bf16[4,40,1152]{2,1,0:T(8,128)(2,1)S(1)}, bf16[4,40,1152]{2,1,0:T(8,128)(2,1)S(1)}, u32[]{:S(2)}, u32[]{:S(2)}) collective-permute-start(bf16[4,40,1152]{2,1,0:T(8,128)(2,1)S(1)} %get-tuple-element.54), channel_id=1, source_target_pairs={{0,8},{8,0},{16,24},{24,16},{1,9},{9,1},{17,25},{25,17},{2,10},{10... | collective-permute-start | bytes 1105928 | tf_op jit(solution)/shard_map/ppermute | solution.py:550
  79.8 16.8 %collective-permute-start.20 = (bf16[4,40,1152]{2,1,0:T(8,128)(2,1)S(1)}, bf16[4,40,1152]{2,1,0:T(8,128)(2,1)S(1)}, u32[]{:S(2)}, u32[]{:S(2)}) collective-permute-start(bf16[4,40,1152]{2,1,0:T(8,128)(2,1)S(1)} %get-tuple-element.57), channel_id=1, source_target_pairs={{0,16},{8,24},{16,0},{24,8},{1,17},{9,25},{17,1},{25,9},{2,18},{10... | collective-permute-start | bytes 1105928 | tf_op jit(solution)/shard_map/ppermute | solution.py:550
  81.3 15.3 %collective-permute-start.21 = (bf16[4,40,1152]{2,1,0:T(8,128)(2,1)S(1)}, bf16[4,40,1152]{2,1,0:T(8,128)(2,1)}, u32[]{:S(2)}, u32[]{:S(2)}) collective-permute-start(bf16[4,40,1152]{2,1,0:T(8,128)(2,1)S(1)} %get-tuple-element.58), channel_id=1, source_target_pairs={{0,24},{8,16},{16,8},{24,0},{1,25},{9,17},{17,9},{25,1},{2,26},{10... | collective-permute-start | bytes 1105928 | tf_op jit(solution)/shard_map/ppermute | solution.py:550
  81.7 21.6 %collective-permute-start.12 = (bf16[40,1152]{1,0:T(8,128)(2,1)S(1)}, bf16[40,1152]{1,0:T(8,128)(2,1)S(1)}, u32[]{:S(2)}, u32[]{:S(2)}) collective-permute-start(bf16[40,1152]{1,0:T(8,128)(2,1)S(1)} %get-tuple-element.70), channel_id=1, source_target_pairs={{0,2},{2,0},{4,6},{6,4},{1,3},{3,1},{5,7},{7,5},{8,10},{10,8},{12,... | collective-permute-start | bytes 276488 | tf_op jit(solution)/shard_map/ppermute | solution.py:550
  84.1 19.1 %collective-permute-start.13 = (bf16[40,1152]{1,0:T(8,128)(2,1)S(1)}, bf16[40,1152]{1,0:T(8,128)(2,1)S(1)}, u32[]{:S(2)}, u32[]{:S(2)}) collective-permute-start(bf16[40,1152]{1,0:T(8,128)(2,1)S(1)} %get-tuple-element.69), channel_id=1, source_target_pairs={{0,4},{2,6},{4,0},{6,2},{1,5},{3,7},{5,1},{7,3},{8,12},{10,14},{12... | collective-permute-start | bytes 276488 | tf_op jit(solution)/shard_map/ppermute | solution.py:550
  89.7 13.6 %collective-permute-start.14 = (bf16[40,1152]{1,0:T(8,128)(2,1)S(1)}, bf16[40,1152]{1,0:T(8,128)(2,1)S(1)}, u32[]{:S(2)}, u32[]{:S(2)}) collective-permute-start(bf16[40,1152]{1,0:T(8,128)(2,1)S(1)} %get-tuple-element.68), channel_id=1, source_target_pairs={{0,6},{2,4},{4,2},{6,0},{1,7},{3,5},{5,3},{7,1},{8,14},{10,12},{12... | collective-permute-start | bytes 276488 | tf_op jit(solution)/shard_map/ppermute | solution.py:550
  98.0 7.5 %collective-permute-start.22 = (bf16[40,1152]{1,0:T(8,128)(2,1)S(1)}, bf16[40,1152]{1,0:T(8,128)(2,1)S(1)}, u32[]{:S(2)}, u32[]{:S(2)}) collective-permute-start(bf16[40,1152]{1,0:T(8,128)(2,1)S(1)} %get-tuple-element.67), channel_id=1, source_target_pairs={{0,2},{2,0},{4,6},{6,4},{1,3},{3,1},{5,7},{7,5},{8,10},{10,8},{12,... | collective-permute-start | bytes 276488 | tf_op jit(solution)/shard_map/ppermute | solution.py:550
  100.1 7.5 %collective-permute-start.23 = (bf16[40,1152]{1,0:T(8,128)(2,1)S(1)}, bf16[40,1152]{1,0:T(8,128)(2,1)S(1)}, u32[]{:S(2)}, u32[]{:S(2)}) collective-permute-start(bf16[40,1152]{1,0:T(8,128)(2,1)S(1)} %get-tuple-element.66), channel_id=1, source_target_pairs={{0,4},{2,6},{4,0},{6,2},{1,5},{3,7},{5,1},{7,3},{8,12},{10,14},{12... | collective-permute-start | bytes 276488 | tf_op jit(solution)/shard_map/ppermute | solution.py:550
  103.2 6.3 %collective-permute-start.24 = (bf16[40,1152]{1,0:T(8,128)(2,1)S(1)}, bf16[40,1152]{1,0:T(8,128)(2,1)S(1)}, u32[]{:S(2)}, u32[]{:S(2)}) collective-permute-start(bf16[40,1152]{1,0:T(8,128)(2,1)S(1)} %get-tuple-element.65), channel_id=1, source_target_pairs={{0,6},{2,4},{4,2},{6,0},{1,7},{3,5},{5,3},{7,1},{8,14},{10,12},{12... | collective-permute-start | bytes 276488 | tf_op jit(solution)/shard_map/ppermute | solution.py:550
  103.3 8.4 %collective-permute-start.17 = (bf16[40,1152]{1,0:T(8,128)(2,1)S(1)}, bf16[40,1152]{1,0:T(8,128)(2,1)S(1)}, u32[]{:S(2)}, u32[]{:S(2)}) collective-permute-start(bf16[40,1152]{1,0:T(8,128)(2,1)S(1)} %row_sum.1.refs_0_), channel_id=1, source_target_pairs={{0,8},{8,0},{16,24},{24,16},{1,9},{9,1},{17,25},{25,17},{2,10},{10... | collective-permute-start | bytes 276488 | tf_op jit(solution)/shard_map/ppermute | solution.py:550
  104.7 8.5 %collective-permute-start.18 = (bf16[40,1152]{1,0:T(8,128)(2,1)S(1)}, bf16[40,1152]{1,0:T(8,128)(2,1)S(1)}, u32[]{:S(2)}, u32[]{:S(2)}) collective-permute-start(bf16[40,1152]{1,0:T(8,128)(2,1)S(1)} %row_sum.1.refs_0_), channel_id=1, source_target_pairs={{0,16},{8,24},{16,0},{24,8},{1,17},{9,25},{17,1},{25,9},{2,18},{10... | collective-permute-start | bytes 276488 | tf_op jit(solution)/shard_map/ppermute | solution.py:550
  105.4 7.8 %collective-permute-start.19 = (bf16[40,1152]{1,0:T(8,128)(2,1)S(1)}, bf16[40,1152]{1,0:T(8,128)(2,1)S(1)}, u32[]{:S(2)}, u32[]{:S(2)}) collective-permute-start(bf16[40,1152]{1,0:T(8,128)(2,1)S(1)} %row_sum.1.refs_0_), channel_id=1, source_target_pairs={{0,24},{8,16},{16,8},{24,0},{1,25},{9,17},{17,9},{25,1},{2,26},{10... | collective-permute-start | bytes 276488 | tf_op jit(solution)/shard_map/ppermute | solution.py:550
  109.6 4.6 %collective-permute-start.25 = (bf16[40,1152]{1,0:T(8,128)(2,1)S(1)}, bf16[40,1152]{1,0:T(8,128)(2,1)S(1)}, u32[]{:S(2)}, u32[]{:S(2)}) collective-permute-start(bf16[40,1152]{1,0:T(8,128)(2,1)S(1)} %add_convert_fusion.2.refs_4_), channel_id=1, source_target_pairs={{0,8},{8,0},{16,24},{24,16},{1,9},{9,1},{17,25},{25,17},{2,10},{10... | collective-permute-start | bytes 276488 | tf_op jit(solution)/shard_map/ppermute | solution.py:550
  111.0 4.6 %collective-permute-start.26 = (bf16[40,1152]{1,0:T(8,128)(2,1)S(1)}, bf16[40,1152]{1,0:T(8,128)(2,1)S(1)}, u32[]{:S(2)}, u32[]{:S(2)}) collective-permute-start(bf16[40,1152]{1,0:T(8,128)(2,1)S(1)} %add_convert_fusion.2.refs_4_), channel_id=1, source_target_pairs={{0,16},{8,24},{16,0},{24,8},{1,17},{9,25},{17,1},{25,9},{2,18},{10... | collective-permute-start | bytes 276488 | tf_op jit(solution)/shard_map/ppermute | solution.py:550
  111.7 5.5 %collective-permute-start.27 = (bf16[40,1152]{1,0:T(8,128)(2,1)S(1)}, bf16[40,1152]{1,0:T(8,128)(2,1)S(1)}, u32[]{:S(2)}, u32[]{:S(2)}) collective-permute-start(bf16[40,1152]{1,0:T(8,128)(2,1)S(1)} %add_convert_fusion.2.refs_4_), channel_id=1, source_target_pairs={{0,24},{8,16},{16,8},{24,0},{1,25},{9,17},{17,9},{25,1},{2,26},{10... | collective-permute-start | bytes 276488 | tf_op jit(solution)/shard_map/ppermute | solution.py:550

commit v12 on v11

--- a/solution.py
+++ b/solution.py
@@ -383,7 +383,7 @@
             pltpu.VMEM((band, chunk_own), jnp.float32),
             pltpu.SemaphoreType.DMA((2,)),
         ],
-        compiler_params=pltpu.CompilerParams(vmem_limit_bytes=34 * 1024 * 1024),
+        compiler_params=pltpu.CompilerParams(vmem_limit_bytes=30 * 1024 * 1024),
         cost_estimate=pl.CostEstimate(
             flops=12 * token_count * band * 2 * INNER,
             bytes_accessed=16 * 1024 * 1024,

time: 119 us -> 119 us (level)
  no operation moved by 1% of the time
where the time goes in v12:
time: 119 us
  starting transfers between devices  44.3 us (37%)
  Pallas kernels  32.3 us (27%)
  waiting for transfers between devices  21.1 us (18%)
  local copies, waits for them, and re-layouts  12 us (10%)
  matrix products  6.06 us (5%)
  other arithmetic  1.9 us (2%)
    ppermute x18, starting transfers between devices, exchanged(): got.append(lax.ppermute(part, axis, pairs))  30.3 us
    ppermute x18, waiting for transfers between devices, exchanged(): got.append(lax.ppermute(part, axis, pairs))  17.1 us
    pallas_call x1, Pallas kernels, attention(): pl.pallas_call(functools.partial(attention_kernel, counts), grid=(1,), ou...  15 us
    ppermute x8, starting transfers between devices, moved(): return lax.ppermute(block, ('row', 'col'), pairs)  13.6 us
    unnamed x46, local copies, waits for them, and re-layouts  11 us
    pallas_call x1, Pallas kernels, project(): pl.pallas_call(project_kernel, grid=(1,), out_shape=[jax.ShapeDtypeStruct...  5.98 us
    ppermute x8, waiting for transfers between devices, moved(): return lax.ppermute(block, ('row', 'col'), pairs)  4 us
    pallas_call x1, Pallas kernels, project(): pl.pallas_call(edges_kernel, grid=(1,), out_shape=[shape(edge)] * 2, in_s...  3.91 us
  transfers between devices with their start and end apart: 28, of which 12 were waited for; matrix products, arithmetic and copies ran while one was open for 8% of the time, Pallas kernels for 10%

profile of v12, /device:TPU:0, one launch (start us, length us, event | category | flops | bytes accessed | tf_op | source)
XLA Modules:
  0.0 118.6 jit_solution(15719493136353741106)
XLA Ops:
  0.6 3.9 %project_edges.1 = (bf16[128,1152]{1,0:T(8,128)(2,1)}, bf16[128,1152]{1,0:T(8,128)(2,1)}) custom-call(bf16[512,1152]{1,0:T(8,128)(2,1)} %bitcast.39, bf16[1728,1152]{1,0:T(8,128)(2,1)} %bitcast.50), custom_call_target="tpu_custom_call" | custom-call | flops 1 | bytes 1 | tf_op jit(solution)/shard_map/project_edges/pallas_call | solution.py:101
  4.6 1.3 %collective-permute-start.1 = (bf16[128,1152]{1,0:T(8,128)(2,1)}, bf16[128,1152]{1,0:T(8,128)(2,1)S(1)}, u32[]{:S(2)}, u32[]{:S(2)}) collective-permute-start(bf16[128,1152]{1,0:T(8,128)(2,1)} %get-tuple-element.33.top_ref), channel_id=1, source_target_pairs={{2,0},{3,1},{4,2},{5,3},{6,4},{7,5},{10,8},{11,9},{12,10},{13,11},... | collective-permute-start | bytes 884744 | tf_op jit(solution)/shard_map/ppermute | solution.py:591
  5.9 5.6 %collective-permute-start = (bf16[128,1152]{1,0:T(8,128)(2,1)}, bf16[128,1152]{1,0:T(8,128)(2,1)S(1)}, u32[]{:S(2)}, u32[]{:S(2)}) collective-permute-start(bf16[128,1152]{1,0:T(8,128)(2,1)} %get-tuple-element.36), channel_id=1, source_target_pairs={{0,2},{1,3},{2,4},{3,5},{4,6},{5,7},{8,10},{9,11},{10,12},{11,13},... | collective-permute-start | bytes 884744 | tf_op jit(solution)/shard_map/ppermute | solution.py:591
  11.4 6.0 %project.1 = (bf16[576,512]{1,0:T(8,128)(2,1)}, bf16[512,1152]{1,0:T(8,128)(2,1)}, bf16[256,1152]{1,0:T(8,128)(2,1)}) custom-call(s32[1]{0:T(128)} %bitcast.own_ref, bf16[128,1152]{1,0:T(8,128)(2,1)} %get-tuple-element.33.top_ref, bf16[512,1152]{1,0:T(8,128)(2,1)} %bitcast.40, bf16[1728,1152]{1,0:T(8,128)(2,1)} %bitcast.51), custom_call_target="tpu_custom_call" | custom-call | flops 1 | bytes 1 | tf_op jit(solution)/shard_map/project/pallas_call | solution.py:117
  17.6 0.4 collective-permute-done.above_ref
  18.0 0.2 collective-permute-start.3
  18.3 0.4 copy-done.13
  18.7 2.4 %convolution_convert_fusion.2.g_ref = bf16[576,512]{1,0:T(8,128)(2,1)S(1)} fusion(bf16[1152,576]{0,1:T(8,128)(2,1)S(1)} %copy-done, bf16[512,1152]{1,0:T(8,128)(2,1)} %bitcast.47), kind=kOutput, calls=%fused_computation.2 | convolution fusion | flops 679772160 | bytes 3096576 | tf_op jit(solution)/shard_map/dot_general | solution.py:615
  21.1 0.8 copy-done.20
  22.0 1.1 copy-done.21
  23.0 15.0 %window_attention.1 = (bf16[512,640]{1,0:T(8,128)(2,1)S(1)}, bf16[512,640]{1,0:T(8,128)(2,1)S(1)}, bf16[512,1152]{1,0:T(8,128)(2,1)S(1)}, bf16[256,1152]{1,0:T(8...) custom-call(s32[2]{0:T(128)S(1)} %pad_add_fusion.tile_ref, ...), custom_call_target="tpu_custom_call" | custom-call | flops 4076863488 | bytes 16777216 | tf_op jit(solution)/shard_map/window_attention/pallas_call | solution.py:357
  38.1 1.1 copy-done.2
  39.1 1.0 copy-done.6
  40.2 0.8 copy-done.8
  41.0 0.8 copy-done.10
  41.8 1.1 copy-done.15
  42.9 0.8 copy-done.18
  43.7 0.1 collective-permute-start.6
  43.9 0.4 collective-permute-start.4
  44.2 0.1 collective-permute-start.5
  44.4 1.1 collective-permute-done.6
  45.5 0.1 pad_select_fusion
  45.6 0.9 copy-done.11
  46.6 0.1 fusion
  46.7 0.9 fusion.1
  47.5 4.7 %collective-permute-start.7 = (bf16[128,1152]{1,0:T(8,128)(2,1)}, bf16[128,1152]{1,0:T(8,128)(2,1)S(1)}, u32[]{:S(2)}, u32[]{:S(2)}) collective-permute-start(bf16[128,1152]{1,0:T(8,128)(2,1)} %get-tuple-element.63), channel_id=1, source_target_pairs={{0,2},{1,3},{2,4},{3,5},{4,6},{5,7},{8,10},{9,11},{10,12},{11,13},... | collective-permute-start | bytes 884744 | tf_op jit(solution)/shard_map/ppermute | solution.py:591
  52.2 1.5 %collective-permute-start.8 = (bf16[128,1152]{1,0:T(8,128)(2,1)}, bf16[128,1152]{1,0:T(8,128)(2,1)}, u32[]{:S(2)}, u32[]{:S(2)}) collective-permute-start(bf16[128,1152]{1,0:T(8,128)(2,1)} %get-tuple-element.62), channel_id=1, source_target_pairs={{2,0},{3,1},{4,2},{5,3},{6,4},{7,5},{10,8},{11,9},{12,10},{13,11},... | collective-permute-start | bytes 884744 | tf_op jit(solution)/shard_map/ppermute | solution.py:591
  53.7 1.3 %copy-done.3 = bf16[576,1152]{1,0:T(8,128)(2,1)S(1)} copy-done((bf16[576,1152]{1,0:T(8,128)(2,1)S(1)}, bf16[576,1152]{1,0:T(8,128)(2,1)}, u32[]{:S(2)}) %copy-start.3) | copy-done | bytes 1327128
  55.0 2.0 %core_parts.2 = (bf16[4,40,1152]{2,1,0:T(8,128)(2,1)S(1)}, bf16[4,40,1152]{2,1,0:T(8,128)(2,1)S(1)}, bf16[4,40,1152]{2,1,0:T(8,128)(2,1)S(1)}, bf16[4,40,1152]{2,1,0:T(8,128)(2,1)S(1)}) custom-call(s32[1]{0:T(128)} %bitcast.1.own_ref, bf16[576,1152]{1,0:T(8,128)(2,1)S(1)} %copy-done.3, bf16[576,1152]{1,0:T(8,128)(2,1)} %collective-permute-done.4.got_ref), custom_call_target="tpu_custom_call" | custom-call | flops 1 | bytes 1 | tf_op jit(solution)/shard_map/core_parts/pallas_call | solution.py:470
  57.0 1.7 %collective-permute-start.10 = (bf16[4,40,1152]{2,1,0:T(8,128)(2,1)S(1)}, bf16[4,40,1152]{2,1,0:T(8,128)(2,1)S(1)}, u32[]{:S(2)}, u32[]{:S(2)}) collective-permute-start(bf16[4,40,1152]{2,1,0:T(8,128)(2,1)S(1)} %get-tuple-element.41.second), channel_id=1, source_target_pairs={{0,16},{8,24},{16,0},{24,8},{1,17},{9,25},{17,1},{25,9},{2,18},{10... | collective-permute-start | bytes 1105928 | tf_op jit(solution)/shard_map/ppermute | solution.py:550
  58.8 1.4 %collective-permute-start.11 = (bf16[4,40,1152]{2,1,0:T(8,128)(2,1)S(1)}, bf16[4,40,1152]{2,1,0:T(8,128)(2,1)S(1)}, u32[]{:S(2)}, u32[]{:S(2)}) collective-permute-start(bf16[4,40,1152]{2,1,0:T(8,128)(2,1)S(1)} %get-tuple-element.42.third), channel_id=1, source_target_pairs={{0,24},{8,16},{16,8},{24,0},{1,25},{9,17},{17,9},{25,1},{2,26},{10... | collective-permute-start | bytes 1105928 | tf_op jit(solution)/shard_map/ppermute | solution.py:550
  60.2 0.5 collective-permute-start.9
  60.7 2.5 %collective-permute-done.8.below_ref = bf16[128,1152]{1,0:T(8,128)(2,1)} collective-permute-done((bf16[128,1152]{1,0:T(8,128)(2,1)}, bf16[128,1152]{1,0:T(8,128)(2,1)}, u32[]{:S(2)}, u32[]{:S(2)}) %collective-permute-start.8) | collective-permute-done | bytes 294944 | tf_op jit(solution)/shard_map/ppermute | solution.py:591
  63.2 3.4 %late_weight_grad_halves.1 = (bf16[576,1152]{1,0:T(8,128)(2,1)S(1)}, bf16[576,1152]{1,0:T(8,128)(2,1)S(1)}, bf16[512,1728]{1,0:T(8,128)(2,1)S(1)}, bf16[512,576]{1,0:T(8,128)(2,1)S(1)}) custom-call(s32[1]{0:T(128)} %bitcast.own_ref, bf16[4,40,1152]{2,1,0:T(8,128)(2,1)S(1)} %get-tuple-element.40.first, bf16[4,40,1152]{2,1,0:T(8,128)(2,1)S(1)} %get-tuple-element.41.second, ...), custom_call_target="tpu_custom_call" | custom-call | flops 1 | bytes 1 | tf_op jit(solution)/shard_map/late_weight_grad_halves/pallas_call | solution.py:433
  66.7 2.5 %convolution_convert_fusion.refs_2_ = bf16[512,1152]{1,0:T(8,128)(2,1)S(1)} fusion(bf16[512,1728]{1,0:T(8,128)(2,1)S(1)} %get-tuple-element.50, bf16[1152,1728]{0,1:T(8,128)(2,1)S(1)} %copy-done.22), kind=kOutput, calls=%fused_computation | convolution fusion | flops 2039021568 | bytes 6930432 | tf_op jit(solution)/shard_map/dot_general | solution.py:33
  69.3 1.2 convolution_convert_fusion.1.refs_1_
  70.4 4.9 %collective-permute-done.10 = bf16[4,40,1152]{2,1,0:T(8,128)(2,1)S(1)} collective-permute-done((bf16[4,40,1152]{2,1,0:T(8,128)(2,1)S(1)}, bf16[4,40,1152]{2,1,0:T(8,128)(2,1)S(1)}, u32[]{:S(2)}, u32[]{:S(2)}) %collective-permute-start.10) | collective-permute-done | bytes 368672 | tf_op jit(solution)/shard_map/ppermute | solution.py:550
  75.4 1.2 %collective-permute-done.9 = bf16[4,40,1152]{2,1,0:T(8,128)(2,1)S(1)} collective-permute-done((bf16[4,40,1152]{2,1,0:T(8,128)(2,1)S(1)}, bf16[4,40,1152]{2,1,0:T(8,128)(2,1)S(1)}, u32[]{:S(2)}, u32[]{:S(2)}) %collective-permute-start.9) | collective-permute-done | bytes 368672 | tf_op jit(solution)/shard_map/ppermute | solution.py:550
  76.6 0.2 add_convert_fusion.1.refs_0_
  76.8 0.5 core_parts.3
  77.4 0.7 copy-done.12
  78.1 1.6 %collective-permute-start.16 = (bf16[4,40,1152]{2,1,0:T(8,128)(2,1)S(1)}, bf16[4,40,1152]{2,1,0:T(8,128)(2,1)S(1)}, u32[]{:S(2)}, u32[]{:S(2)}) collective-permute-start(bf16[4,40,1152]{2,1,0:T(8,128)(2,1)S(1)} %get-tuple-element.54), channel_id=1, source_target_pairs={{0,8},{8,0},{16,24},{24,16},{1,9},{9,1},{17,25},{25,17},{2,10},{10... | collective-permute-start | bytes 1105928 | tf_op jit(solution)/shard_map/ppermute | solution.py:550
  79.8 1.5 %collective-permute-start.20 = (bf16[4,40,1152]{2,1,0:T(8,128)(2,1)S(1)}, bf16[4,40,1152]{2,1,0:T(8,128)(2,1)S(1)}, u32[]{:S(2)}, u32[]{:S(2)}) collective-permute-start(bf16[4,40,1152]{2,1,0:T(8,128)(2,1)S(1)} %get-tuple-element.57), channel_id=1, source_target_pairs={{0,16},{8,24},{16,0},{24,8},{1,17},{9,25},{17,1},{25,9},{2,18},{10... | collective-permute-start | bytes 1105928 | tf_op jit(solution)/shard_map/ppermute | solution.py:550
  81.3 0.3 collective-permute-start.21
  81.7 2.4 %collective-permute-start.12 = (bf16[40,1152]{1,0:T(8,128)(2,1)S(1)}, bf16[40,1152]{1,0:T(8,128)(2,1)S(1)}, u32[]{:S(2)}, u32[]{:S(2)}) collective-permute-start(bf16[40,1152]{1,0:T(8,128)(2,1)S(1)} %get-tuple-element.70), channel_id=1, source_target_pairs={{0,2},{2,0},{4,6},{6,4},{1,3},{3,1},{5,7},{7,5},{8,10},{10,8},{12,... | collective-permute-start | bytes 276488 | tf_op jit(solution)/shard_map/ppermute | solution.py:550
  84.1 3.3 %collective-permute-start.13 = (bf16[40,1152]{1,0:T(8,128)(2,1)S(1)}, bf16[40,1152]{1,0:T(8,128)(2,1)S(1)}, u32[]{:S(2)}, u32[]{:S(2)}) collective-permute-start(bf16[40,1152]{1,0:T(8,128)(2,1)S(1)} %get-tuple-element.69), channel_id=1, source_target_pairs={{0,4},{2,6},{4,0},{6,2},{1,5},{3,7},{5,1},{7,3},{8,12},{10,14},{12... | collective-permute-start | bytes 276488 | tf_op jit(solution)/shard_map/ppermute | solution.py:550
  87.3 2.3 %collective-permute-done.16.refs_0_ = bf16[4,40,1152]{2,1,0:T(8,128)(2,1)S(1)} collective-permute-done((bf16[4,40,1152]{2,1,0:T(8,128)(2,1)S(1)}, bf16[4,40,1152]{2,1,0:T(8,128)(2,1)S(1)}, u32[]{:S(2)}, u32[]{:S(2)}) %collective-permute-start.16) | collective-permute-done | bytes 368672 | tf_op jit(solution)/shard_map/ppermute | solution.py:550
  89.7 5.1 %collective-permute-start.14 = (bf16[40,1152]{1,0:T(8,128)(2,1)S(1)}, bf16[40,1152]{1,0:T(8,128)(2,1)S(1)}, u32[]{:S(2)}, u32[]{:S(2)}) collective-permute-start(bf16[40,1152]{1,0:T(8,128)(2,1)S(1)} %get-tuple-element.68), channel_id=1, source_target_pairs={{0,6},{2,4},{4,2},{6,0},{1,7},{3,5},{5,3},{7,1},{8,14},{10,12},{12... | collective-permute-start | bytes 276488 | tf_op jit(solution)/shard_map/ppermute | solution.py:550
  94.7 1.9 %collective-permute-done.20 = bf16[4,40,1152]{2,1,0:T(8,128)(2,1)S(1)} collective-permute-done((bf16[4,40,1152]{2,1,0:T(8,128)(2,1)S(1)}, bf16[4,40,1152]{2,1,0:T(8,128)(2,1)S(1)}, u32[]{:S(2)}, u32[]{:S(2)}) %collective-permute-start.20) | collective-permute-done | bytes 368672 | tf_op jit(solution)/shard_map/ppermute | solution.py:550
  96.6 1.3 %add_convert_fusion = bf16[4,40,1152]{2,1,0:T(8,128)(2,1)S(1)} fusion(bf16[4,40,1152]{2,1,0:T(8,128)(2,1)} %collective-permute-done.21, bf16[4,40,1152]{2,1,0:T(8,128)(2,1)S(1)} %collective-permute-done.20, bf16[4,40,1152]{2,1,0:T(8,128)(2,1)S(1)} %collective-permute-done.16.refs_0_, bf16[4,40,1152]{2,1,0:T(8,128)(2,1)} %copy-done.12), kind=kLoop, calls=%fused_computation.6 | loop fusion | flops 1474560 | bytes 1843200 | tf_op jit(solution)/shard_map/convert_element_type | solution.py:560
  98.0 2.1 %collective-permute-start.22 = (bf16[40,1152]{1,0:T(8,128)(2,1)S(1)}, bf16[40,1152]{1,0:T(8,128)(2,1)S(1)}, u32[]{:S(2)}, u32[]{:S(2)}) collective-permute-start(bf16[40,1152]{1,0:T(8,128)(2,1)S(1)} %get-tuple-element.67), channel_id=1, source_target_pairs={{0,2},{2,0},{4,6},{6,4},{1,3},{3,1},{5,7},{7,5},{8,10},{10,8},{12,... | collective-permute-start | bytes 276488 | tf_op jit(solution)/shard_map/ppermute | solution.py:550
  100.1 3.1 %collective-permute-start.23 = (bf16[40,1152]{1,0:T(8,128)(2,1)S(1)}, bf16[40,1152]{1,0:T(8,128)(2,1)S(1)}, u32[]{:S(2)}, u32[]{:S(2)}) collective-permute-start(bf16[40,1152]{1,0:T(8,128)(2,1)S(1)} %get-tuple-element.66), channel_id=1, source_target_pairs={{0,4},{2,6},{4,0},{6,2},{1,5},{3,7},{5,1},{7,3},{8,12},{10,14},{12... | collective-permute-start | bytes 276488 | tf_op jit(solution)/shard_map/ppermute | solution.py:550
  103.3 1.4 %collective-permute-start.17 = (bf16[40,1152]{1,0:T(8,128)(2,1)S(1)}, bf16[40,1152]{1,0:T(8,128)(2,1)S(1)}, u32[]{:S(2)}, u32[]{:S(2)}) collective-permute-start(bf16[40,1152]{1,0:T(8,128)(2,1)S(1)} %row_sum.1.refs_0_), channel_id=1, source_target_pairs={{0,8},{8,0},{16,24},{24,16},{1,9},{9,1},{17,25},{25,17},{2,10},{10... | collective-permute-start | bytes 276488 | tf_op jit(solution)/shard_map/ppermute | solution.py:550
  104.7 0.7 collective-permute-start.18
  105.4 1.4 %collective-permute-start.19 = (bf16[40,1152]{1,0:T(8,128)(2,1)S(1)}, bf16[40,1152]{1,0:T(8,128)(2,1)S(1)}, u32[]{:S(2)}, u32[]{:S(2)}) collective-permute-start(bf16[40,1152]{1,0:T(8,128)(2,1)S(1)} %row_sum.1.refs_0_), channel_id=1, source_target_pairs={{0,24},{8,16},{16,8},{24,0},{1,25},{9,17},{17,9},{25,1},{2,26},{10... | collective-permute-start | bytes 276488 | tf_op jit(solution)/shard_map/ppermute | solution.py:550
  106.8 0.7 collective-permute-done.23
  107.5 2.0 %collective-permute-done.24 = bf16[40,1152]{1,0:T(8,128)(2,1)S(1)} collective-permute-done((bf16[40,1152]{1,0:T(8,128)(2,1)S(1)}, bf16[40,1152]{1,0:T(8,128)(2,1)S(1)}, u32[]{:S(2)}, u32[]{:S(2)}) %collective-permute-start.24) | collective-permute-done | bytes 92192 | tf_op jit(solution)/shard_map/ppermute | solution.py:550
  109.6 1.4 %collective-permute-start.25 = (bf16[40,1152]{1,0:T(8,128)(2,1)S(1)}, bf16[40,1152]{1,0:T(8,128)(2,1)S(1)}, u32[]{:S(2)}, u32[]{:S(2)}) collective-permute-start(bf16[40,1152]{1,0:T(8,128)(2,1)S(1)} %add_convert_fusion.2.refs_4_), channel_id=1, source_target_pairs={{0,8},{8,0},{16,24},{24,16},{1,9},{9,1},{17,25},{25,17},{2,10},{10... | collective-permute-start | bytes 276488 | tf_op jit(solution)/shard_map/ppermute | solution.py:550
  111.0 0.7 collective-permute-start.26
  111.7 1.4 %collective-permute-start.27 = (bf16[40,1152]{1,0:T(8,128)(2,1)S(1)}, bf16[40,1152]{1,0:T(8,128)(2,1)S(1)}, u32[]{:S(2)}, u32[]{:S(2)}) collective-permute-start(bf16[40,1152]{1,0:T(8,128)(2,1)S(1)} %add_convert_fusion.2.refs_4_), channel_id=1, source_target_pairs={{0,24},{8,16},{16,8},{24,0},{1,25},{9,17},{17,9},{25,1},{2,26},{10... | collective-permute-start | bytes 276488 | tf_op jit(solution)/shard_map/ppermute | solution.py:550
  113.2 1.1 collective-permute-done.25.refs_5_
  114.2 1.3 %collective-permute-done.26.refs_6_ = bf16[40,1152]{1,0:T(8,128)(2,1)S(1)} collective-permute-done((bf16[40,1152]{1,0:T(8,128)(2,1)S(1)}, bf16[40,1152]{1,0:T(8,128)(2,1)S(1)}, u32[]{:S(2)}, u32[]{:S(2)}) %collective-permute-start.26) | collective-permute-done | bytes 92192 | tf_op jit(solution)/shard_map/ppermute | solution.py:550
  115.6 1.6 %collective-permute-done.27.refs_7_ = bf16[40,1152]{1,0:T(8,128)(2,1)S(1)} collective-permute-done((bf16[40,1152]{1,0:T(8,128)(2,1)S(1)}, bf16[40,1152]{1,0:T(8,128)(2,1)S(1)}, u32[]{:S(2)}, u32[]{:S(2)}) %collective-permute-start.27) | collective-permute-done | bytes 92192 | tf_op jit(solution)/shard_map/ppermute | solution.py:550
  117.2 1.4 %weight_grads.1 = (f32[144,1728]{1,0:T(8,128)}, f32[144,576]{1,0:T(8,128)}) custom-call(s32[1]{0:T(128)} %bitcast.1.own_ref, bf16[40,1152]{1,0:T(8,128)(2,1)S(1)} %row_sum.1.refs_0_, bf16[40,1152]{1,0:T(8,128)(2,1)S(1)} %collective-permute-done.17.refs_1_, bf16[40,1152]{1,0:T(8,128)(2,1)S(1)} %collective-permute-done.18.refs_2_, ...), custom_call_target="tpu_custom_call" | custom-call | flops 1 | bytes 1 | tf_op jit(solution)/shard_map/weight_grads/pallas_call | solution.py:523
  (62 shorter events, 0.6 us)
Async XLA Ops:
  0.6 18.1 %copy-start = (bf16[1152,576]{0,1:T(8,128)(2,1)S(1)}, bf16[1152,576]{0,1:T(8,128)(2,1)}, u32[]{:S(2)}) copy-start(bf16[1152,576]{0,1:T(8,128)(2,1)} %param.6) | copy-start | bytes 3981316
  4.6 13.0 %collective-permute-start.1 = (bf16[128,1152]{1,0:T(8,128)(2,1)}, bf16[128,1152]{1,0:T(8,128)(2,1)S(1)}, u32[]{:S(2)}, u32[]{:S(2)}) collective-permute-start(bf16[128,1152]{1,0:T(8,128)(2,1)} %get-tuple-element.33.top_ref), channel_id=1, source_target_pairs={{2,0},{3,1},{4,2},{5,3},{6,4},{7,5},{10,8},{11,9},{12,10},{13,11},... | collective-permute-start | bytes 884744 | tf_op jit(solution)/shard_map/ppermute | solution.py:591
  5.9 12.1 %collective-permute-start = (bf16[128,1152]{1,0:T(8,128)(2,1)}, bf16[128,1152]{1,0:T(8,128)(2,1)S(1)}, u32[]{:S(2)}, u32[]{:S(2)}) collective-permute-start(bf16[128,1152]{1,0:T(8,128)(2,1)} %get-tuple-element.36), channel_id=1, source_target_pairs={{0,2},{1,3},{2,4},{3,5},{4,6},{5,7},{8,10},{9,11},{10,12},{11,13},... | collective-permute-start | bytes 884744 | tf_op jit(solution)/shard_map/ppermute | solution.py:591
  17.4 3.7 %collective-permute-start.2 = (bf16[256,1152]{1,0:T(8,128)(2,1)}, bf16[256,1152]{1,0:T(8,128)(2,1)S(1)}, u32[]{:S(2)}, u32[]{:S(2)}) collective-permute-start(bf16[256,1152]{1,0:T(8,128)(2,1)} %get-tuple-element.37), channel_id=1, source_target_pairs={{0,1},{1,0},{2,3},{3,2},{4,5},{5,4},{6,7},{7,6},{8,9},{9,8},{10,11... | collective-permute-start | bytes 1769480 | tf_op jit(solution)/shard_map/ppermute | solution.py:591
  18.0 0.7 copy-start.13
  18.0 3.1 %collective-permute-start.3 = (bf16[16,8,1152]{2,1,0:T(8,128)(2,1)S(1)}, bf16[16,8,1152]{2,1,0:T(8,128)(2,1)S(1)}, u32[]{:S(2)}, u32[]{:S(2)}) collective-permute-start(bf16[16,8,1152]{2,1,0:T(8,128)(2,1)S(1)} %pad_maximum_fusion), channel_id=1, source_target_pairs={{0,1},{1,0},{2,3},{3,2},{4,5},{5,4},{6,7},{7,6},{8,9},{9,8},{10,11... | collective-permute-start | bytes 884744 | tf_op jit(solution)/shard_map/ppermute | solution.py:591
  18.7 3.3 %copy-start.1 = (bf16[1,32,16,1152]{3,2,1,0:T(8,128)(2,1)S(1)}, bf16[1,32,16,1152]{3,2,1,0:T(8,128)(2,1)}, u32[]{:S(2)}) copy-start(bf16[1,32,16,1152]{3,2,1,0:T(8,128)(2,1)} %param.4) | copy-start | bytes 3538948
  18.7 3.3 %copy-start.14 = (bf16[128,1152]{1,0:T(8,128)(2,1)S(1)}, bf16[128,1152]{1,0:T(8,128)(2,1)}, u32[]{:S(2)}) copy-start(bf16[128,1152]{1,0:T(8,128)(2,1)} %copy-done.13) | copy-start | bytes 884740
  18.7 3.3 %copy-start.16 = (bf16[1,32,16,1152]{3,2,1,0:T(8,128)(2,1)S(1)}, bf16[1,32,16,1152]{3,2,1,0:T(8,128)(2,1)}, u32[]{:S(2)}) copy-start(bf16[1,32,16,1152]{3,2,1,0:T(8,128)(2,1)} %param.7) | copy-start | bytes 3538948
  18.7 3.3 %copy-start.17 = (bf16[512,1152]{1,0:T(8,128)(2,1)S(1)}, bf16[512,1152]{1,0:T(8,128)(2,1)}, u32[]{:S(2)}) copy-start(bf16[512,1152]{1,0:T(8,128)(2,1)} %get-tuple-element.35.own_ref) | copy-start | bytes 3538948
  18.7 3.2 %copy-start.19 = (bf16[576,512]{1,0:T(8,128)(2,1)S(1)}, bf16[576,512]{1,0:T(8,128)(2,1)}, u32[]{:S(2)}) copy-start(bf16[576,512]{1,0:T(8,128)(2,1)} %get-tuple-element.34.qt_ref) | copy-start | bytes 1769476
  21.1 0.8 copy-start.20
  22.0 1.1 copy-start.21
  38.0 1.1 copy-start.2
  39.1 1.0 copy-start.6
  40.2 0.8 copy-start.8
  41.0 0.8 copy-start.10
  41.8 1.1 copy-start.15
  42.9 0.8 copy-start.18
  43.7 1.8 %collective-permute-start.6 = (bf16[128,1152]{1,0:T(8,128)(2,1)}, bf16[128,1152]{1,0:T(8,128)(2,1)S(1)}, u32[]{:S(2)}, u32[]{:S(2)}) collective-permute-start(bf16[128,1152]{1,0:T(8,128)(2,1)} %get-tuple-element.46), channel_id=1, source_target_pairs={{0,1},{1,0},{2,3},{3,2},{4,5},{5,4},{6,7},{7,6},{8,9},{9,8},{10,11... | collective-permute-start | bytes 884744 | tf_op jit(solution)/shard_map/ppermute | solution.py:591
  43.9 9.8 %collective-permute-start.4 = (bf16[576,1152]{1,0:T(8,128)(2,1)}, bf16[576,1152]{1,0:T(8,128)(2,1)}, u32[]{:S(2)}, u32[]{:S(2)}) collective-permute-start(bf16[576,1152]{1,0:T(8,128)(2,1)} %copy-done.15), channel_id=1, source_target_pairs={{0,1},{1,0},{2,3},{3,2},{4,5},{5,4},{6,7},{7,6},{8,9},{9,8},{10,11... | collective-permute-start | bytes 3981320 | tf_op jit(solution)/shard_map/ppermute | solution.py:465
  44.2 19.0 %collective-permute-start.5 = (bf16[256,1152]{1,0:T(8,128)(2,1)}, bf16[256,1152]{1,0:T(8,128)(2,1)}, u32[]{:S(2)}, u32[]{:S(2)}) collective-permute-start(bf16[256,1152]{1,0:T(8,128)(2,1)} %copy-done.18), channel_id=1, source_target_pairs={{0,1},{1,0},{2,3},{3,2},{4,5},{5,4},{6,7},{7,6},{8,9},{9,8},{10,11... | collective-permute-start | bytes 1769480 | tf_op jit(solution)/shard_map/ppermute | solution.py:591
  45.5 1.1 copy-start.11
  47.5 12.7 %collective-permute-start.7 = (bf16[128,1152]{1,0:T(8,128)(2,1)}, bf16[128,1152]{1,0:T(8,128)(2,1)S(1)}, u32[]{:S(2)}, u32[]{:S(2)}) collective-permute-start(bf16[128,1152]{1,0:T(8,128)(2,1)} %get-tuple-element.63), channel_id=1, source_target_pairs={{0,2},{1,3},{2,4},{3,5},{4,6},{5,7},{8,10},{9,11},{10,12},{11,13},... | collective-permute-start | bytes 884744 | tf_op jit(solution)/shard_map/ppermute | solution.py:591
  52.2 11.0 %collective-permute-start.8 = (bf16[128,1152]{1,0:T(8,128)(2,1)}, bf16[128,1152]{1,0:T(8,128)(2,1)}, u32[]{:S(2)}, u32[]{:S(2)}) collective-permute-start(bf16[128,1152]{1,0:T(8,128)(2,1)} %get-tuple-element.62), channel_id=1, source_target_pairs={{2,0},{3,1},{4,2},{5,3},{6,4},{7,5},{10,8},{11,9},{12,10},{13,11},... | collective-permute-start | bytes 884744 | tf_op jit(solution)/shard_map/ppermute | solution.py:591
  53.7 1.3 %copy-start.3 = (bf16[576,1152]{1,0:T(8,128)(2,1)S(1)}, bf16[576,1152]{1,0:T(8,128)(2,1)}, u32[]{:S(2)}) copy-start(bf16[576,1152]{1,0:T(8,128)(2,1)} %copy-done.2) | copy-start | bytes 3981316
  55.0 8.2 %copy-start.7 = (bf16[512,1152]{1,0:T(8,128)(2,1)S(1)}, bf16[512,1152]{1,0:T(8,128)(2,1)}, u32[]{:S(2)}) copy-start(bf16[512,1152]{1,0:T(8,128)(2,1)} %copy-done.6) | copy-start | bytes 3538948
  55.0 8.2 %copy-start.9 = (bf16[512,640]{1,0:T(8,128)(2,1)S(1)}, bf16[512,640]{1,0:T(8,128)(2,1)}, u32[]{:S(2)}) copy-start(bf16[512,640]{1,0:T(8,128)(2,1)} %copy-done.8) | copy-start | bytes 1966084
  57.0 18.3 %collective-permute-start.10 = (bf16[4,40,1152]{2,1,0:T(8,128)(2,1)S(1)}, bf16[4,40,1152]{2,1,0:T(8,128)(2,1)S(1)}, u32[]{:S(2)}, u32[]{:S(2)}) collective-permute-start(bf16[4,40,1152]{2,1,0:T(8,128)(2,1)S(1)} %get-tuple-element.41.second), channel_id=1, source_target_pairs={{0,16},{8,24},{16,0},{24,8},{1,17},{9,25},{17,1},{25,9},{2,18},{10... | collective-permute-start | bytes 1105928 | tf_op jit(solution)/shard_map/ppermute | solution.py:550
  58.8 16.6 %collective-permute-start.11 = (bf16[4,40,1152]{2,1,0:T(8,128)(2,1)S(1)}, bf16[4,40,1152]{2,1,0:T(8,128)(2,1)S(1)}, u32[]{:S(2)}, u32[]{:S(2)}) collective-permute-start(bf16[4,40,1152]{2,1,0:T(8,128)(2,1)S(1)} %get-tuple-element.42.third), channel_id=1, source_target_pairs={{0,24},{8,16},{16,8},{24,0},{1,25},{9,17},{17,9},{25,1},{2,26},{10... | collective-permute-start | bytes 1105928 | tf_op jit(solution)/shard_map/ppermute | solution.py:550
  60.2 16.4 %collective-permute-start.9 = (bf16[4,40,1152]{2,1,0:T(8,128)(2,1)S(1)}, bf16[4,40,1152]{2,1,0:T(8,128)(2,1)S(1)}, u32[]{:S(2)}, u32[]{:S(2)}) collective-permute-start(bf16[4,40,1152]{2,1,0:T(8,128)(2,1)S(1)} %get-tuple-element.40.first), channel_id=1, source_target_pairs={{0,8},{8,0},{16,24},{24,16},{1,9},{9,1},{17,25},{25,17},{2,10},{10... | collective-permute-start | bytes 1105928 | tf_op jit(solution)/shard_map/ppermute | solution.py:550
  63.2 3.5 %copy-start.22 = (bf16[1152,1728]{0,1:T(8,128)(2,1)S(1)}, bf16[1152,1728]{0,1:T(8,128)(2,1)}, u32[]{:S(2)}) copy-start(bf16[1152,1728]{0,1:T(8,128)(2,1)} %param.5) | copy-start | bytes 11943940
  66.6 10.2 %collective-permute-start.15 = (bf16[576,1152]{1,0:T(8,128)(2,1)S(1)}, bf16[576,1152]{1,0:T(8,128)(2,1)S(1)}, u32[]{:S(2)}, u32[]{:S(2)}) collective-permute-start(bf16[576,1152]{1,0:T(8,128)(2,1)S(1)} %get-tuple-element.53), channel_id=1, source_target_pairs={{0,1},{1,0},{2,3},{3,2},{4,5},{5,4},{6,7},{7,6},{8,9},{9,8},{10,11... | collective-permute-start | bytes 3981320 | tf_op jit(solution)/shard_map/ppermute | solution.py:465
  69.2 7.6 %copy-start.4 = (bf16[512,1152]{1,0:T(8,128)(2,1)}, bf16[512,1152]{1,0:T(8,128)(2,1)S(1)}, u32[]{:S(2)}) copy-start(bf16[512,1152]{1,0:T(8,128)(2,1)S(1)} %convolution_convert_fusion.refs_2_) | copy-start | bytes 3538948
  70.4 7.0 %copy-start.5 = (bf16[512,1152]{1,0:T(8,128)(2,1)}, bf16[512,1152]{1,0:T(8,128)(2,1)S(1)}, u32[]{:S(2)}) copy-start(bf16[512,1152]{1,0:T(8,128)(2,1)S(1)} %convolution_convert_fusion.1.refs_1_) | copy-start | bytes 3538948
  77.4 0.7 copy-start.12
  78.1 11.5 %collective-permute-start.16 = (bf16[4,40,1152]{2,1,0:T(8,128)(2,1)S(1)}, bf16[4,40,1152]{2,1,0:T(8,128)(2,1)S(1)}, u32[]{:S(2)}, u32[]{:S(2)}) collective-permute-start(bf16[4,40,1152]{2,1,0:T(8,128)(2,1)S(1)} %get-tuple-element.54), channel_id=1, source_target_pairs={{0,8},{8,0},{16,24},{24,16},{1,9},{9,1},{17,25},{25,17},{2,10},{10... | collective-permute-start | bytes 1105928 | tf_op jit(solution)/shard_map/ppermute | solution.py:550
  79.8 16.8 %collective-permute-start.20 = (bf16[4,40,1152]{2,1,0:T(8,128)(2,1)S(1)}, bf16[4,40,1152]{2,1,0:T(8,128)(2,1)S(1)}, u32[]{:S(2)}, u32[]{:S(2)}) collective-permute-start(bf16[4,40,1152]{2,1,0:T(8,128)(2,1)S(1)} %get-tuple-element.57), channel_id=1, source_target_pairs={{0,16},{8,24},{16,0},{24,8},{1,17},{9,25},{17,1},{25,9},{2,18},{10... | collective-permute-start | bytes 1105928 | tf_op jit(solution)/shard_map/ppermute | solution.py:550
  81.3 15.3 %collective-permute-start.21 = (bf16[4,40,1152]{2,1,0:T(8,128)(2,1)S(1)}, bf16[4,40,1152]{2,1,0:T(8,128)(2,1)}, u32[]{:S(2)}, u32[]{:S(2)}) collective-permute-start(bf16[4,40,1152]{2,1,0:T(8,128)(2,1)S(1)} %get-tuple-element.58), channel_id=1, source_target_pairs={{0,24},{8,16},{16,8},{24,0},{1,25},{9,17},{17,9},{25,1},{2,26},{10... | collective-permute-start | bytes 1105928 | tf_op jit(solution)/shard_map/ppermute | solution.py:550
  81.7 21.6 %collective-permute-start.12 = (bf16[40,1152]{1,0:T(8,128)(2,1)S(1)}, bf16[40,1152]{1,0:T(8,128)(2,1)S(1)}, u32[]{:S(2)}, u32[]{:S(2)}) collective-permute-start(bf16[40,1152]{1,0:T(8,128)(2,1)S(1)} %get-tuple-element.70), channel_id=1, source_target_pairs={{0,2},{2,0},{4,6},{6,4},{1,3},{3,1},{5,7},{7,5},{8,10},{10,8},{12,... | collective-permute-start | bytes 276488 | tf_op jit(solution)/shard_map/ppermute | solution.py:550
  84.1 19.1 %collective-permute-start.13 = (bf16[40,1152]{1,0:T(8,128)(2,1)S(1)}, bf16[40,1152]{1,0:T(8,128)(2,1)S(1)}, u32[]{:S(2)}, u32[]{:S(2)}) collective-permute-start(bf16[40,1152]{1,0:T(8,128)(2,1)S(1)} %get-tuple-element.69), channel_id=1, source_target_pairs={{0,4},{2,6},{4,0},{6,2},{1,5},{3,7},{5,1},{7,3},{8,12},{10,14},{12... | collective-permute-start | bytes 276488 | tf_op jit(solution)/shard_map/ppermute | solution.py:550
  89.7 13.6 %collective-permute-start.14 = (bf16[40,1152]{1,0:T(8,128)(2,1)S(1)}, bf16[40,1152]{1,0:T(8,128)(2,1)S(1)}, u32[]{:S(2)}, u32[]{:S(2)}) collective-permute-start(bf16[40,1152]{1,0:T(8,128)(2,1)S(1)} %get-tuple-element.68), channel_id=1, source_target_pairs={{0,6},{2,4},{4,2},{6,0},{1,7},{3,5},{5,3},{7,1},{8,14},{10,12},{12... | collective-permute-start | bytes 276488 | tf_op jit(solution)/shard_map/ppermute | solution.py:550
  98.0 7.5 %collective-permute-start.22 = (bf16[40,1152]{1,0:T(8,128)(2,1)S(1)}, bf16[40,1152]{1,0:T(8,128)(2,1)S(1)}, u32[]{:S(2)}, u32[]{:S(2)}) collective-permute-start(bf16[40,1152]{1,0:T(8,128)(2,1)S(1)} %get-tuple-element.67), channel_id=1, source_target_pairs={{0,2},{2,0},{4,6},{6,4},{1,3},{3,1},{5,7},{7,5},{8,10},{10,8},{12,... | collective-permute-start | bytes 276488 | tf_op jit(solution)/shard_map/ppermute | solution.py:550
  100.1 7.5 %collective-permute-start.23 = (bf16[40,1152]{1,0:T(8,128)(2,1)S(1)}, bf16[40,1152]{1,0:T(8,128)(2,1)S(1)}, u32[]{:S(2)}, u32[]{:S(2)}) collective-permute-start(bf16[40,1152]{1,0:T(8,128)(2,1)S(1)} %get-tuple-element.66), channel_id=1, source_target_pairs={{0,4},{2,6},{4,0},{6,2},{1,5},{3,7},{5,1},{7,3},{8,12},{10,14},{12... | collective-permute-start | bytes 276488 | tf_op jit(solution)/shard_map/ppermute | solution.py:550
  103.2 6.3 %collective-permute-start.24 = (bf16[40,1152]{1,0:T(8,128)(2,1)S(1)}, bf16[40,1152]{1,0:T(8,128)(2,1)S(1)}, u32[]{:S(2)}, u32[]{:S(2)}) collective-permute-start(bf16[40,1152]{1,0:T(8,128)(2,1)S(1)} %get-tuple-element.65), channel_id=1, source_target_pairs={{0,6},{2,4},{4,2},{6,0},{1,7},{3,5},{5,3},{7,1},{8,14},{10,12},{12... | collective-permute-start | bytes 276488 | tf_op jit(solution)/shard_map/ppermute | solution.py:550
  103.3 8.4 %collective-permute-start.17 = (bf16[40,1152]{1,0:T(8,128)(2,1)S(1)}, bf16[40,1152]{1,0:T(8,128)(2,1)S(1)}, u32[]{:S(2)}, u32[]{:S(2)}) collective-permute-start(bf16[40,1152]{1,0:T(8,128)(2,1)S(1)} %row_sum.1.refs_0_), channel_id=1, source_target_pairs={{0,8},{8,0},{16,24},{24,16},{1,9},{9,1},{17,25},{25,17},{2,10},{10... | collective-permute-start | bytes 276488 | tf_op jit(solution)/shard_map/ppermute | solution.py:550
  104.7 8.5 %collective-permute-start.18 = (bf16[40,1152]{1,0:T(8,128)(2,1)S(1)}, bf16[40,1152]{1,0:T(8,128)(2,1)S(1)}, u32[]{:S(2)}, u32[]{:S(2)}) collective-permute-start(bf16[40,1152]{1,0:T(8,128)(2,1)S(1)} %row_sum.1.refs_0_), channel_id=1, source_target_pairs={{0,16},{8,24},{16,0},{24,8},{1,17},{9,25},{17,1},{25,9},{2,18},{10... | collective-permute-start | bytes 276488 | tf_op jit(solution)/shard_map/ppermute | solution.py:550
  105.4 7.8 %collective-permute-start.19 = (bf16[40,1152]{1,0:T(8,128)(2,1)S(1)}, bf16[40,1152]{1,0:T(8,128)(2,1)S(1)}, u32[]{:S(2)}, u32[]{:S(2)}) collective-permute-start(bf16[40,1152]{1,0:T(8,128)(2,1)S(1)} %row_sum.1.refs_0_), channel_id=1, source_target_pairs={{0,24},{8,16},{16,8},{24,0},{1,25},{9,17},{17,9},{25,1},{2,26},{10... | collective-permute-start | bytes 276488 | tf_op jit(solution)/shard_map/ppermute | solution.py:550
  109.6 4.6 %collective-permute-start.25 = (bf16[40,1152]{1,0:T(8,128)(2,1)S(1)}, bf16[40,1152]{1,0:T(8,128)(2,1)S(1)}, u32[]{:S(2)}, u32[]{:S(2)}) collective-permute-start(bf16[40,1152]{1,0:T(8,128)(2,1)S(1)} %add_convert_fusion.2.refs_4_), channel_id=1, source_target_pairs={{0,8},{8,0},{16,24},{24,16},{1,9},{9,1},{17,25},{25,17},{2,10},{10... | collective-permute-start | bytes 276488 | tf_op jit(solution)/shard_map/ppermute | solution.py:550
  111.0 4.6 %collective-permute-start.26 = (bf16[40,1152]{1,0:T(8,128)(2,1)S(1)}, bf16[40,1152]{1,0:T(8,128)(2,1)S(1)}, u32[]{:S(2)}, u32[]{:S(2)}) collective-permute-start(bf16[40,1152]{1,0:T(8,128)(2,1)S(1)} %add_convert_fusion.2.refs_4_), channel_id=1, source_target_pairs={{0,16},{8,24},{16,0},{24,8},{1,17},{9,25},{17,1},{25,9},{2,18},{10... | collective-permute-start | bytes 276488 | tf_op jit(solution)/shard_map/ppermute | solution.py:550
  111.7 5.5 %collective-permute-start.27 = (bf16[40,1152]{1,0:T(8,128)(2,1)S(1)}, bf16[40,1152]{1,0:T(8,128)(2,1)S(1)}, u32[]{:S(2)}, u32[]{:S(2)}) collective-permute-start(bf16[40,1152]{1,0:T(8,128)(2,1)S(1)} %add_convert_fusion.2.refs_4_), channel_id=1, source_target_pairs={{0,24},{8,16},{16,8},{24,0},{1,25},{9,17},{17,9},{25,1},{2,26},{10... | collective-permute-start | bytes 276488 | tf_op jit(solution)/shard_map/ppermute | solution.py:550

commit v13 on v9

--- a/solution.py
+++ b/solution.py
@@ -348,7 +348,7 @@
             pltpu.VMEM((2,) + token_rows.shape[::-1], jnp.bfloat16),
             pltpu.SemaphoreType.DMA((2,)),
         ],
-        compiler_params=pltpu.CompilerParams(vmem_limit_bytes=34 * 1024 * 1024),
+        compiler_params=pltpu.CompilerParams(vmem_limit_bytes=40 * 1024 * 1024),
         cost_estimate=pl.CostEstimate(
             flops=12 * token_count * band * 2 * INNER,
             bytes_accessed=16 * 1024 * 1024,

time: 113 us -> 113 us (level)
  no operation moved by 1% of the time
where the time goes in v13:
time: 113 us; the launch traced here: 112 us
  starting transfers between devices  41.6 us (37%)
  Pallas kernels  33.5 us (30%)
  waiting for transfers between devices  22.4 us (20%)
  local copies, waits for them, and re-layouts  6.49 us (6%)
  matrix products  4.67 us (4%)
  other arithmetic  2.55 us (2%)
    ppermute x18, starting transfers between devices, exchanged(): got.append(lax.ppermute(part, axis, pairs))  27.7 us
    ppermute x18, waiting for transfers between devices, exchanged(): got.append(lax.ppermute(part, axis, pairs))  19 us
    pallas_call x1, Pallas kernels, attention(): pl.pallas_call(attention_kernel, grid=(1,), out_shape=outs, in_specs=[pl....  15.4 us
    ppermute x8, starting transfers between devices, moved(): return lax.ppermute(block, ('row', 'col'), pairs)  13.8 us
    pallas_call x1, Pallas kernels, project(): pl.pallas_call(project_kernel, grid=(1,), out_shape=[jax.ShapeDtypeStruct...  5.99 us
    unnamed x39, local copies, waits for them, and re-layouts  5.08 us
    pallas_call x1, Pallas kernels, project(): pl.pallas_call(edges_kernel, grid=(1,), out_shape=[shape(edge)] * 2, in_s...  3.88 us
    dot_general x2, matrix products, nt_dot(): lax.dot_general(a, b, (((1,), (1,)), ((), ())), preferred_element_type=jn...  3.71 us
  transfers between devices with their start and end apart: 28, of which 11 were waited for; matrix products, arithmetic and copies ran while one was open for 8% of the time, Pallas kernels for 10%

profile of v13, /device:TPU:0, one launch (start us, length us, event | category | flops | bytes accessed | tf_op | source)
XLA Modules:
  0.0 112.3 jit_solution(6526139167213077432)
XLA Ops:
  0.6 3.9 %project_edges.1 = (bf16[128,1152]{1,0:T(8,128)(2,1)}, bf16[128,1152]{1,0:T(8,128)(2,1)}) custom-call(bf16[512,1152]{1,0:T(8,128)(2,1)} %bitcast.38, bf16[1728,1152]{1,0:T(8,128)(2,1)} %bitcast.49), custom_call_target="tpu_custom_call" | custom-call | flops 1 | bytes 1 | tf_op jit(solution)/shard_map/project_edges/pallas_call | solution.py:99
  4.5 1.3 %collective-permute-start.1 = (bf16[128,1152]{1,0:T(8,128)(2,1)}, bf16[128,1152]{1,0:T(8,128)(2,1)S(1)}, u32[]{:S(2)}, u32[]{:S(2)}) collective-permute-start(bf16[128,1152]{1,0:T(8,128)(2,1)} %get-tuple-element.33.top_ref), channel_id=1, source_target_pairs={{2,0},{3,1},{4,2},{5,3},{6,4},{7,5},{10,8},{11,9},{12,10},{13,11},... | collective-permute-start | bytes 884744 | tf_op jit(solution)/shard_map/ppermute | solution.py:590
  5.8 5.6 %collective-permute-start = (bf16[128,1152]{1,0:T(8,128)(2,1)}, bf16[128,1152]{1,0:T(8,128)(2,1)S(1)}, u32[]{:S(2)}, u32[]{:S(2)}) collective-permute-start(bf16[128,1152]{1,0:T(8,128)(2,1)} %get-tuple-element.36), channel_id=1, source_target_pairs={{0,2},{1,3},{2,4},{3,5},{4,6},{5,7},{8,10},{9,11},{10,12},{11,13},... | collective-permute-start | bytes 884744 | tf_op jit(solution)/shard_map/ppermute | solution.py:590
  11.4 6.0 %project.1 = (bf16[576,512]{1,0:T(8,128)(2,1)}, bf16[512,1152]{1,0:T(8,128)(2,1)}, bf16[256,1152]{1,0:T(8,128)(2,1)}) custom-call(s32[1]{0:T(128)} %bitcast.own_ref, bf16[128,1152]{1,0:T(8,128)(2,1)} %get-tuple-element.33.top_ref, bf16[512,1152]{1,0:T(8,128)(2,1)} %bitcast.39, bf16[1728,1152]{1,0:T(8,128)(2,1)} %bitcast.50), custom_call_target="tpu_custom_call" | custom-call | flops 1 | bytes 1 | tf_op jit(solution)/shard_map/project/pallas_call | solution.py:115
  17.6 0.1 tile.13
  17.6 0.1 tile.11
  17.8 0.1 reshape.181
  17.9 0.1 reshape.182
  18.1 0.1 fusion.4
  18.5 0.4 fusion.3.bias_ref
  19.0 0.5 collective-permute-start.3
  19.5 0.1 copy-done.11
  19.6 0.1 copy-done.13
  19.7 1.0 convolution_convert_fusion.2.g_ref
  20.7 0.8 copy-done.16
  21.6 1.1 copy-done.17
  22.7 15.4 %window_attention.1 = (bf16[512,640]{1,0:T(8,128)(2,1)S(1)}, bf16[512,640]{1,0:T(8,128)(2,1)S(1)}, bf16[512,1152]{1,0:T(8,128)(2,1)S(1)}, bf16[256,1152]{1,0:T(8...) custom-call(s32[4]{0:T(128)S(1)} %broadcast_subtract_fusion.start_re, ...), custom_call_target="tpu_custom_call" | custom-call | flops 4076863488 | bytes 16777216 | tf_op jit(solution)/shard_map/window_attention/pallas_call | solution.py:322
  38.0 0.8 copy-done.8
  38.9 0.5 collective-permute-start.6
  39.4 0.5 collective-permute-start.5
  39.8 0.7 collective-permute-done.6
  40.6 0.1 pad_select_fusion
  40.7 0.1 fusion
  40.8 0.9 fusion.5
  41.7 3.9 %collective-permute-start.7 = (bf16[128,1152]{1,0:T(8,128)(2,1)}, bf16[128,1152]{1,0:T(8,128)(2,1)S(1)}, u32[]{:S(2)}, u32[]{:S(2)}) collective-permute-start(bf16[128,1152]{1,0:T(8,128)(2,1)} %get-tuple-element.63), channel_id=1, source_target_pairs={{0,2},{1,3},{2,4},{3,5},{4,6},{5,7},{8,10},{9,11},{10,12},{11,13},... | collective-permute-start | bytes 884744 | tf_op jit(solution)/shard_map/ppermute | solution.py:590
  45.6 1.5 %collective-permute-start.8 = (bf16[128,1152]{1,0:T(8,128)(2,1)}, bf16[128,1152]{1,0:T(8,128)(2,1)}, u32[]{:S(2)}, u32[]{:S(2)}) collective-permute-start(bf16[128,1152]{1,0:T(8,128)(2,1)} %get-tuple-element.62), channel_id=1, source_target_pairs={{2,0},{3,1},{4,2},{5,3},{6,4},{7,5},{10,8},{11,9},{12,10},{13,11},... | collective-permute-start | bytes 884744 | tf_op jit(solution)/shard_map/ppermute | solution.py:590
  47.1 1.3 %copy-done.3 = bf16[576,1152]{1,0:T(8,128)(2,1)S(1)} copy-done((bf16[576,1152]{1,0:T(8,128)(2,1)S(1)}, bf16[576,1152]{1,0:T(8,128)(2,1)}, u32[]{:S(2)}) %copy-start.3) | copy-done | bytes 1327128
  48.4 2.0 %core_parts.2 = (bf16[4,40,1152]{2,1,0:T(8,128)(2,1)S(1)}, bf16[4,40,1152]{2,1,0:T(8,128)(2,1)S(1)}, bf16[4,40,1152]{2,1,0:T(8,128)(2,1)S(1)}, bf16[4,40,1152]{2,1,0:T(8,128)(2,1)S(1)}) custom-call(s32[1]{0:T(128)} %bitcast.1.own_ref, bf16[576,1152]{1,0:T(8,128)(2,1)S(1)} %copy-done.3, bf16[576,1152]{1,0:T(8,128)(2,1)} %collective-permute-done.4.got_ref), custom_call_target="tpu_custom_call" | custom-call | flops 1 | bytes 1 | tf_op jit(solution)/shard_map/core_parts/pallas_call | solution.py:435
  50.4 1.6 %collective-permute-start.10 = (bf16[4,40,1152]{2,1,0:T(8,128)(2,1)S(1)}, bf16[4,40,1152]{2,1,0:T(8,128)(2,1)S(1)}, u32[]{:S(2)}, u32[]{:S(2)}) collective-permute-start(bf16[4,40,1152]{2,1,0:T(8,128)(2,1)S(1)} %get-tuple-element.41.second), channel_id=1, source_target_pairs={{0,16},{8,24},{16,0},{24,8},{1,17},{9,25},{17,1},{25,9},{2,18},{10... | collective-permute-start | bytes 1105928 | tf_op jit(solution)/shard_map/ppermute | solution.py:549
  52.0 1.4 %collective-permute-start.11 = (bf16[4,40,1152]{2,1,0:T(8,128)(2,1)S(1)}, bf16[4,40,1152]{2,1,0:T(8,128)(2,1)S(1)}, u32[]{:S(2)}, u32[]{:S(2)}) collective-permute-start(bf16[4,40,1152]{2,1,0:T(8,128)(2,1)S(1)} %get-tuple-element.42.third), channel_id=1, source_target_pairs={{0,24},{8,16},{16,8},{24,0},{1,25},{9,17},{17,9},{25,1},{2,26},{10... | collective-permute-start | bytes 1105928 | tf_op jit(solution)/shard_map/ppermute | solution.py:549
  53.5 0.7 collective-permute-start.9
  54.2 2.6 %collective-permute-done.8.below_ref = bf16[128,1152]{1,0:T(8,128)(2,1)} collective-permute-done((bf16[128,1152]{1,0:T(8,128)(2,1)}, bf16[128,1152]{1,0:T(8,128)(2,1)}, u32[]{:S(2)}, u32[]{:S(2)}) %collective-permute-start.8) | collective-permute-done | bytes 294944 | tf_op jit(solution)/shard_map/ppermute | solution.py:590
  56.8 3.4 %late_weight_grad_halves.1 = (bf16[576,1152]{1,0:T(8,128)(2,1)S(1)}, bf16[576,1152]{1,0:T(8,128)(2,1)S(1)}, bf16[512,1728]{1,0:T(8,128)(2,1)S(1)}, bf16[512,576]{1,0:T(8,128)(2,1)S(1)}) custom-call(s32[1]{0:T(128)} %bitcast.own_ref, bf16[4,40,1152]{2,1,0:T(8,128)(2,1)S(1)} %get-tuple-element.40.first, bf16[4,40,1152]{2,1,0:T(8,128)(2,1)S(1)} %get-tuple-element.41.second, ...), custom_call_target="tpu_custom_call" | custom-call | flops 1 | bytes 1 | tf_op jit(solution)/shard_map/late_weight_grad_halves/pallas_call | solution.py:398
  60.3 2.5 %convolution_convert_fusion.refs_2_ = bf16[512,1152]{1,0:T(8,128)(2,1)S(1)} fusion(bf16[512,1728]{1,0:T(8,128)(2,1)S(1)} %get-tuple-element.50, bf16[1152,1728]{0,1:T(8,128)(2,1)S(1)} %copy-done.18), kind=kOutput, calls=%fused_computation | convolution fusion | flops 2039021568 | bytes 6930432 | tf_op jit(solution)/shard_map/dot_general | solution.py:31
  62.9 1.2 %convolution_convert_fusion.1.refs_1_ = bf16[512,1152]{1,0:T(8,128)(2,1)S(1)} fusion(bf16[512,576]{1,0:T(8,128)(2,1)S(1)} %get-tuple-element.49, bf16[1152,576]{0,1:T(8,128)(2,1)S(1)} %copy-done), kind=kOutput, calls=%fused_computation.1 | convolution fusion | flops 680067072 | bytes 3096576 | tf_op jit(solution)/shard_map/dot_general | solution.py:31
  64.1 4.9 %collective-permute-done.10 = bf16[4,40,1152]{2,1,0:T(8,128)(2,1)S(1)} collective-permute-done((bf16[4,40,1152]{2,1,0:T(8,128)(2,1)S(1)}, bf16[4,40,1152]{2,1,0:T(8,128)(2,1)S(1)}, u32[]{:S(2)}, u32[]{:S(2)}) %collective-permute-start.10) | collective-permute-done | bytes 368672 | tf_op jit(solution)/shard_map/ppermute | solution.py:549
  69.0 1.2 %collective-permute-done.9 = bf16[4,40,1152]{2,1,0:T(8,128)(2,1)S(1)} collective-permute-done((bf16[4,40,1152]{2,1,0:T(8,128)(2,1)S(1)}, bf16[4,40,1152]{2,1,0:T(8,128)(2,1)S(1)}, u32[]{:S(2)}, u32[]{:S(2)}) %collective-permute-start.9) | collective-permute-done | bytes 368672 | tf_op jit(solution)/shard_map/ppermute | solution.py:549
  70.2 0.2 add_convert_fusion.1.refs_0_
  70.4 1.4 %core_parts.3 = (bf16[4,40,1152]{2,1,0:T(8,128)(2,1)S(1)}, bf16[4,40,1152]{2,1,0:T(8,128)(2,1)}, bf16[4,40,1152]{2,1,0:T(8,128)(2,1)}, bf16[4,40,1152]{2,1,0:T(8,128)(2,1)}) custom-call(s32[1]{0:T(128)} %bitcast.1.own_ref, bf16[576,1152]{1,0:T(8,128)(2,1)S(1)} %get-tuple-element.52.kept_ref, bf16[576,1152]{1,0:T(8,128)(2,1)S(1)} %collective-permute-done.15.got_ref, ...), custom_call_target="tpu_custom_call" | custom-call | flops 1 | bytes 1 | tf_op jit(solution)/shard_map/core_parts/pallas_call | solution.py:435
  71.9 0.7 copy-done.10
  72.6 1.5 %collective-permute-start.16 = (bf16[4,40,1152]{2,1,0:T(8,128)(2,1)}, bf16[4,40,1152]{2,1,0:T(8,128)(2,1)S(1)}, u32[]{:S(2)}, u32[]{:S(2)}) collective-permute-start(bf16[4,40,1152]{2,1,0:T(8,128)(2,1)} %get-tuple-element.54), channel_id=1, source_target_pairs={{0,8},{8,0},{16,24},{24,16},{1,9},{9,1},{17,25},{25,17},{2,10},{10... | collective-permute-start | bytes 1105928 | tf_op jit(solution)/shard_map/ppermute | solution.py:549
  74.1 1.5 %collective-permute-start.20 = (bf16[4,40,1152]{2,1,0:T(8,128)(2,1)}, bf16[4,40,1152]{2,1,0:T(8,128)(2,1)S(1)}, u32[]{:S(2)}, u32[]{:S(2)}) collective-permute-start(bf16[4,40,1152]{2,1,0:T(8,128)(2,1)} %get-tuple-element.57), channel_id=1, source_target_pairs={{0,16},{8,24},{16,0},{24,8},{1,17},{9,25},{17,1},{25,9},{2,18},{10... | collective-permute-start | bytes 1105928 | tf_op jit(solution)/shard_map/ppermute | solution.py:549
  75.6 0.5 collective-permute-start.21
  76.2 2.4 %collective-permute-start.12 = (bf16[40,1152]{1,0:T(8,128)(2,1)S(1)}, bf16[40,1152]{1,0:T(8,128)(2,1)S(1)}, u32[]{:S(2)}, u32[]{:S(2)}) collective-permute-start(bf16[40,1152]{1,0:T(8,128)(2,1)S(1)} %get-tuple-element.70), channel_id=1, source_target_pairs={{0,2},{2,0},{4,6},{6,4},{1,3},{3,1},{5,7},{7,5},{8,10},{10,8},{12,... | collective-permute-start | bytes 276488 | tf_op jit(solution)/shard_map/ppermute | solution.py:549
  78.6 2.3 %collective-permute-start.13 = (bf16[40,1152]{1,0:T(8,128)(2,1)S(1)}, bf16[40,1152]{1,0:T(8,128)(2,1)S(1)}, u32[]{:S(2)}, u32[]{:S(2)}) collective-permute-start(bf16[40,1152]{1,0:T(8,128)(2,1)S(1)} %get-tuple-element.69), channel_id=1, source_target_pairs={{0,4},{2,6},{4,0},{6,2},{1,5},{3,7},{5,1},{7,3},{8,12},{10,14},{12... | collective-permute-start | bytes 276488 | tf_op jit(solution)/shard_map/ppermute | solution.py:549
  80.9 3.5 %collective-permute-done.16.refs_0_ = bf16[4,40,1152]{2,1,0:T(8,128)(2,1)S(1)} collective-permute-done((bf16[4,40,1152]{2,1,0:T(8,128)(2,1)}, bf16[4,40,1152]{2,1,0:T(8,128)(2,1)S(1)}, u32[]{:S(2)}, u32[]{:S(2)}) %collective-permute-start.16) | collective-permute-done | bytes 368672 | tf_op jit(solution)/shard_map/ppermute | solution.py:549
  84.4 4.1 %collective-permute-start.14 = (bf16[40,1152]{1,0:T(8,128)(2,1)S(1)}, bf16[40,1152]{1,0:T(8,128)(2,1)S(1)}, u32[]{:S(2)}, u32[]{:S(2)}) collective-permute-start(bf16[40,1152]{1,0:T(8,128)(2,1)S(1)} %get-tuple-element.68), channel_id=1, source_target_pairs={{0,6},{2,4},{4,2},{6,0},{1,7},{3,5},{5,3},{7,1},{8,14},{10,12},{12... | collective-permute-start | bytes 276488 | tf_op jit(solution)/shard_map/ppermute | solution.py:549
  88.5 3.0 %collective-permute-done.20 = bf16[4,40,1152]{2,1,0:T(8,128)(2,1)S(1)} collective-permute-done((bf16[4,40,1152]{2,1,0:T(8,128)(2,1)}, bf16[4,40,1152]{2,1,0:T(8,128)(2,1)S(1)}, u32[]{:S(2)}, u32[]{:S(2)}) %collective-permute-start.20) | collective-permute-done | bytes 368672 | tf_op jit(solution)/shard_map/ppermute | solution.py:549
  91.4 1.2 %add_convert_fusion = bf16[4,40,1152]{2,1,0:T(8,128)(2,1)S(1)} fusion(bf16[4,40,1152]{2,1,0:T(8,128)(2,1)S(1)} %collective-permute-done.21, bf16[4,40,1152]{2,1,0:T(8,128)(2,1)S(1)} %collective-permute-done.20, bf16[4,40,1152]{2,1,0:T(8,128)(2,1)S(1)} %collective-permute-done.16.refs_0_, bf16[4,40,1152]{2,1,0:T(8,128)(2,1)} %copy-done.10), kind=kLoop, calls=%fused_computation.11 | loop fusion | flops 1474560 | bytes 1843200 | tf_op jit(solution)/shard_map/convert_element_type | solution.py:559
  92.7 2.1 %collective-permute-start.22 = (bf16[40,1152]{1,0:T(8,128)(2,1)S(1)}, bf16[40,1152]{1,0:T(8,128)(2,1)S(1)}, u32[]{:S(2)}, u32[]{:S(2)}) collective-permute-start(bf16[40,1152]{1,0:T(8,128)(2,1)S(1)} %get-tuple-element.67), channel_id=1, source_target_pairs={{0,2},{2,0},{4,6},{6,4},{1,3},{3,1},{5,7},{7,5},{8,10},{10,8},{12,... | collective-permute-start | bytes 276488 | tf_op jit(solution)/shard_map/ppermute | solution.py:549
  94.8 2.1 %collective-permute-start.23 = (bf16[40,1152]{1,0:T(8,128)(2,1)S(1)}, bf16[40,1152]{1,0:T(8,128)(2,1)S(1)}, u32[]{:S(2)}, u32[]{:S(2)}) collective-permute-start(bf16[40,1152]{1,0:T(8,128)(2,1)S(1)} %get-tuple-element.66), channel_id=1, source_target_pairs={{0,4},{2,6},{4,0},{6,2},{1,5},{3,7},{5,1},{7,3},{8,12},{10,14},{12... | collective-permute-start | bytes 276488 | tf_op jit(solution)/shard_map/ppermute | solution.py:549
  96.8 0.4 collective-permute-start.24
  97.3 1.3 %collective-permute-start.17 = (bf16[40,1152]{1,0:T(8,128)(2,1)S(1)}, bf16[40,1152]{1,0:T(8,128)(2,1)S(1)}, u32[]{:S(2)}, u32[]{:S(2)}) collective-permute-start(bf16[40,1152]{1,0:T(8,128)(2,1)S(1)} %row_sum.1.refs_0_), channel_id=1, source_target_pairs={{0,8},{8,0},{16,24},{24,16},{1,9},{9,1},{17,25},{25,17},{2,10},{10... | collective-permute-start | bytes 276488 | tf_op jit(solution)/shard_map/ppermute | solution.py:549
  98.6 0.8 collective-permute-start.18
  99.4 1.4 %collective-permute-start.19 = (bf16[40,1152]{1,0:T(8,128)(2,1)S(1)}, bf16[40,1152]{1,0:T(8,128)(2,1)S(1)}, u32[]{:S(2)}, u32[]{:S(2)}) collective-permute-start(bf16[40,1152]{1,0:T(8,128)(2,1)S(1)} %row_sum.1.refs_0_), channel_id=1, source_target_pairs={{0,24},{8,16},{16,8},{24,0},{1,25},{9,17},{17,9},{25,1},{2,26},{10... | collective-permute-start | bytes 276488 | tf_op jit(solution)/shard_map/ppermute | solution.py:549
  100.9 0.6 collective-permute-done.23
  101.4 1.9 %collective-permute-done.24 = bf16[40,1152]{1,0:T(8,128)(2,1)S(1)} collective-permute-done((bf16[40,1152]{1,0:T(8,128)(2,1)S(1)}, bf16[40,1152]{1,0:T(8,128)(2,1)S(1)}, u32[]{:S(2)}, u32[]{:S(2)}) %collective-permute-start.24) | collective-permute-done | bytes 92192 | tf_op jit(solution)/shard_map/ppermute | solution.py:549
  103.4 1.3 %collective-permute-start.25 = (bf16[40,1152]{1,0:T(8,128)(2,1)S(1)}, bf16[40,1152]{1,0:T(8,128)(2,1)S(1)}, u32[]{:S(2)}, u32[]{:S(2)}) collective-permute-start(bf16[40,1152]{1,0:T(8,128)(2,1)S(1)} %add_convert_fusion.2.refs_4_), channel_id=1, source_target_pairs={{0,8},{8,0},{16,24},{24,16},{1,9},{9,1},{17,25},{25,17},{2,10},{10... | collective-permute-start | bytes 276488 | tf_op jit(solution)/shard_map/ppermute | solution.py:549
  104.7 0.8 collective-permute-start.26
  105.5 1.4 %collective-permute-start.27 = (bf16[40,1152]{1,0:T(8,128)(2,1)S(1)}, bf16[40,1152]{1,0:T(8,128)(2,1)S(1)}, u32[]{:S(2)}, u32[]{:S(2)}) collective-permute-start(bf16[40,1152]{1,0:T(8,128)(2,1)S(1)} %add_convert_fusion.2.refs_4_), channel_id=1, source_target_pairs={{0,24},{8,16},{16,8},{24,0},{1,25},{9,17},{17,9},{25,1},{2,26},{10... | collective-permute-start | bytes 276488 | tf_op jit(solution)/shard_map/ppermute | solution.py:549
  106.9 1.1 collective-permute-done.25.refs_5_
  108.0 1.2 %collective-permute-done.26.refs_6_ = bf16[40,1152]{1,0:T(8,128)(2,1)S(1)} collective-permute-done((bf16[40,1152]{1,0:T(8,128)(2,1)S(1)}, bf16[40,1152]{1,0:T(8,128)(2,1)S(1)}, u32[]{:S(2)}, u32[]{:S(2)}) %collective-permute-start.26) | collective-permute-done | bytes 92192 | tf_op jit(solution)/shard_map/ppermute | solution.py:549
  109.2 1.7 %collective-permute-done.27.refs_7_ = bf16[40,1152]{1,0:T(8,128)(2,1)S(1)} collective-permute-done((bf16[40,1152]{1,0:T(8,128)(2,1)S(1)}, bf16[40,1152]{1,0:T(8,128)(2,1)S(1)}, u32[]{:S(2)}, u32[]{:S(2)}) %collective-permute-start.27) | collective-permute-done | bytes 92192 | tf_op jit(solution)/shard_map/ppermute | solution.py:549
  110.9 1.4 %weight_grads.1 = (f32[144,1728]{1,0:T(8,128)}, f32[144,576]{1,0:T(8,128)}) custom-call(s32[1]{0:T(128)} %bitcast.1.own_ref, bf16[40,1152]{1,0:T(8,128)(2,1)S(1)} %row_sum.1.refs_0_, bf16[40,1152]{1,0:T(8,128)(2,1)S(1)} %collective-permute-done.17.refs_1_, bf16[40,1152]{1,0:T(8,128)(2,1)S(1)} %collective-permute-done.18.refs_2_, ...), custom_call_target="tpu_custom_call" | custom-call | flops 1 | bytes 1 | tf_op jit(solution)/shard_map/weight_grads/pallas_call | solution.py:488
  (79 shorter events, 1.1 us)
Async XLA Ops:
  0.6 19.0 %copy-start = (bf16[1152,576]{0,1:T(8,128)(2,1)S(1)}, bf16[1152,576]{0,1:T(8,128)(2,1)}, u32[]{:S(2)}) copy-start(bf16[1152,576]{0,1:T(8,128)(2,1)} %param.6) | copy-start | bytes 3981316
  4.5 14.3 %collective-permute-start.1 = (bf16[128,1152]{1,0:T(8,128)(2,1)}, bf16[128,1152]{1,0:T(8,128)(2,1)S(1)}, u32[]{:S(2)}, u32[]{:S(2)}) collective-permute-start(bf16[128,1152]{1,0:T(8,128)(2,1)} %get-tuple-element.33.top_ref), channel_id=1, source_target_pairs={{2,0},{3,1},{4,2},{5,3},{6,4},{7,5},{10,8},{11,9},{12,10},{13,11},... | collective-permute-start | bytes 884744 | tf_op jit(solution)/shard_map/ppermute | solution.py:590
  5.8 13.1 %collective-permute-start = (bf16[128,1152]{1,0:T(8,128)(2,1)}, bf16[128,1152]{1,0:T(8,128)(2,1)S(1)}, u32[]{:S(2)}, u32[]{:S(2)}) collective-permute-start(bf16[128,1152]{1,0:T(8,128)(2,1)} %get-tuple-element.36), channel_id=1, source_target_pairs={{0,2},{1,3},{2,4},{3,5},{4,6},{5,7},{8,10},{9,11},{10,12},{11,13},... | collective-permute-start | bytes 884744 | tf_op jit(solution)/shard_map/ppermute | solution.py:590
  17.4 3.3 %collective-permute-start.2 = (bf16[256,1152]{1,0:T(8,128)(2,1)}, bf16[256,1152]{1,0:T(8,128)(2,1)S(1)}, u32[]{:S(2)}, u32[]{:S(2)}) collective-permute-start(bf16[256,1152]{1,0:T(8,128)(2,1)} %get-tuple-element.37), channel_id=1, source_target_pairs={{0,1},{1,0},{2,3},{3,2},{4,5},{5,4},{6,7},{7,6},{8,9},{9,8},{10,11... | collective-permute-start | bytes 1769480 | tf_op jit(solution)/shard_map/ppermute | solution.py:590
  18.5 1.3 %copy-start.13 = (bf16[1,32,16,1152]{3,2,1,0:T(8,128)(2,1)S(1)}, bf16[1,32,16,1152]{3,2,1,0:T(8,128)(2,1)}, u32[]{:S(2)}) copy-start(bf16[1,32,16,1152]{3,2,1,0:T(8,128)(2,1)} %param.7) | copy-start | bytes 3538948
  18.9 0.7 copy-start.11
  19.0 1.7 %collective-permute-start.3 = (bf16[16,8,1152]{2,1,0:T(8,128)(2,1)S(1)}, bf16[16,8,1152]{2,1,0:T(8,128)(2,1)S(1)}, u32[]{:S(2)}, u32[]{:S(2)}) collective-permute-start(bf16[16,8,1152]{2,1,0:T(8,128)(2,1)S(1)} %pad_maximum_fusion), channel_id=1, source_target_pairs={{0,1},{1,0},{2,3},{3,2},{4,5},{5,4},{6,7},{7,6},{8,9},{9,8},{10,11... | collective-permute-start | bytes 884744 | tf_op jit(solution)/shard_map/ppermute | solution.py:590
  19.7 1.8 %copy-start.1 = (bf16[1,32,16,1152]{3,2,1,0:T(8,128)(2,1)S(1)}, bf16[1,32,16,1152]{3,2,1,0:T(8,128)(2,1)}, u32[]{:S(2)}) copy-start(bf16[1,32,16,1152]{3,2,1,0:T(8,128)(2,1)} %param.4) | copy-start | bytes 3538948
  19.7 1.8 %copy-start.12 = (bf16[128,1152]{1,0:T(8,128)(2,1)S(1)}, bf16[128,1152]{1,0:T(8,128)(2,1)}, u32[]{:S(2)}) copy-start(bf16[128,1152]{1,0:T(8,128)(2,1)} %copy-done.11) | copy-start | bytes 884740
  19.7 1.8 %copy-start.14 = (bf16[512,1152]{1,0:T(8,128)(2,1)S(1)}, bf16[512,1152]{1,0:T(8,128)(2,1)}, u32[]{:S(2)}) copy-start(bf16[512,1152]{1,0:T(8,128)(2,1)} %get-tuple-element.35.own_ref) | copy-start | bytes 3538948
  19.7 1.9 %copy-start.15 = (bf16[576,512]{1,0:T(8,128)(2,1)S(1)}, bf16[576,512]{1,0:T(8,128)(2,1)}, u32[]{:S(2)}) copy-start(bf16[576,512]{1,0:T(8,128)(2,1)} %get-tuple-element.34.qt_ref) | copy-start | bytes 1769476
  20.7 0.8 copy-start.16
  21.6 1.1 copy-start.17
  38.0 0.8 copy-start.8
  38.9 1.8 %copy-start.2 = (bf16[576,1152]{1,0:T(8,128)(2,1)}, bf16[576,1152]{1,0:T(8,128)(2,1)S(1)}, u32[]{:S(2)}) copy-start(bf16[576,1152]{1,0:T(8,128)(2,1)S(1)} %get-tuple-element.38.kept_ref) | copy-start | bytes 3981316
  38.9 1.8 %copy-start.6 = (bf16[512,1152]{1,0:T(8,128)(2,1)}, bf16[512,1152]{1,0:T(8,128)(2,1)S(1)}, u32[]{:S(2)}) copy-start(bf16[512,1152]{1,0:T(8,128)(2,1)S(1)} %get-tuple-element.43.inner_ref) | copy-start | bytes 3538948
  38.9 1.7 %collective-permute-start.6 = (bf16[128,1152]{1,0:T(8,128)(2,1)S(1)}, bf16[128,1152]{1,0:T(8,128)(2,1)S(1)}, u32[]{:S(2)}, u32[]{:S(2)}) collective-permute-start(bf16[128,1152]{1,0:T(8,128)(2,1)S(1)} %get-tuple-element.46), channel_id=1, source_target_pairs={{0,1},{1,0},{2,3},{3,2},{4,5},{5,4},{6,7},{7,6},{8,9},{9,8},{10,11... | collective-permute-start | bytes 884744 | tf_op jit(solution)/shard_map/ppermute | solution.py:590
  39.3 7.8 %collective-permute-start.4 = (bf16[576,1152]{1,0:T(8,128)(2,1)}, bf16[576,1152]{1,0:T(8,128)(2,1)}, u32[]{:S(2)}, u32[]{:S(2)}) collective-permute-start(bf16[576,1152]{1,0:T(8,128)(2,1)} %get-tuple-element.39), channel_id=1, source_target_pairs={{0,1},{1,0},{2,3},{3,2},{4,5},{5,4},{6,7},{7,6},{8,9},{9,8},{10,11... | collective-permute-start | bytes 3981320 | tf_op jit(solution)/shard_map/ppermute | solution.py:430
  39.4 17.4 %collective-permute-start.5 = (bf16[256,1152]{1,0:T(8,128)(2,1)}, bf16[256,1152]{1,0:T(8,128)(2,1)}, u32[]{:S(2)}, u32[]{:S(2)}) collective-permute-start(bf16[256,1152]{1,0:T(8,128)(2,1)} %get-tuple-element.44), channel_id=1, source_target_pairs={{0,1},{1,0},{2,3},{3,2},{4,5},{5,4},{6,7},{7,6},{8,9},{9,8},{10,11... | collective-permute-start | bytes 1769480 | tf_op jit(solution)/shard_map/ppermute | solution.py:590
  41.7 11.8 %collective-permute-start.7 = (bf16[128,1152]{1,0:T(8,128)(2,1)}, bf16[128,1152]{1,0:T(8,128)(2,1)S(1)}, u32[]{:S(2)}, u32[]{:S(2)}) collective-permute-start(bf16[128,1152]{1,0:T(8,128)(2,1)} %get-tuple-element.63), channel_id=1, source_target_pairs={{0,2},{1,3},{2,4},{3,5},{4,6},{5,7},{8,10},{9,11},{10,12},{11,13},... | collective-permute-start | bytes 884744 | tf_op jit(solution)/shard_map/ppermute | solution.py:590
  45.6 11.2 %collective-permute-start.8 = (bf16[128,1152]{1,0:T(8,128)(2,1)}, bf16[128,1152]{1,0:T(8,128)(2,1)}, u32[]{:S(2)}, u32[]{:S(2)}) collective-permute-start(bf16[128,1152]{1,0:T(8,128)(2,1)} %get-tuple-element.62), channel_id=1, source_target_pairs={{2,0},{3,1},{4,2},{5,3},{6,4},{7,5},{10,8},{11,9},{12,10},{13,11},... | collective-permute-start | bytes 884744 | tf_op jit(solution)/shard_map/ppermute | solution.py:590
  47.1 1.3 %copy-start.3 = (bf16[576,1152]{1,0:T(8,128)(2,1)S(1)}, bf16[576,1152]{1,0:T(8,128)(2,1)}, u32[]{:S(2)}) copy-start(bf16[576,1152]{1,0:T(8,128)(2,1)} %copy-done.2) | copy-start | bytes 3981316
  48.4 8.4 %copy-start.7 = (bf16[512,1152]{1,0:T(8,128)(2,1)S(1)}, bf16[512,1152]{1,0:T(8,128)(2,1)}, u32[]{:S(2)}) copy-start(bf16[512,1152]{1,0:T(8,128)(2,1)} %copy-done.6) | copy-start | bytes 3538948
  48.4 8.4 %copy-start.9 = (bf16[512,640]{1,0:T(8,128)(2,1)S(1)}, bf16[512,640]{1,0:T(8,128)(2,1)}, u32[]{:S(2)}) copy-start(bf16[512,640]{1,0:T(8,128)(2,1)} %copy-done.8) | copy-start | bytes 1966084
  50.4 18.5 %collective-permute-start.10 = (bf16[4,40,1152]{2,1,0:T(8,128)(2,1)S(1)}, bf16[4,40,1152]{2,1,0:T(8,128)(2,1)S(1)}, u32[]{:S(2)}, u32[]{:S(2)}) collective-permute-start(bf16[4,40,1152]{2,1,0:T(8,128)(2,1)S(1)} %get-tuple-element.41.second), channel_id=1, source_target_pairs={{0,16},{8,24},{16,0},{24,8},{1,17},{9,25},{17,1},{25,9},{2,18},{10... | collective-permute-start | bytes 1105928 | tf_op jit(solution)/shard_map/ppermute | solution.py:549
  52.0 17.0 %collective-permute-start.11 = (bf16[4,40,1152]{2,1,0:T(8,128)(2,1)S(1)}, bf16[4,40,1152]{2,1,0:T(8,128)(2,1)S(1)}, u32[]{:S(2)}, u32[]{:S(2)}) collective-permute-start(bf16[4,40,1152]{2,1,0:T(8,128)(2,1)S(1)} %get-tuple-element.42.third), channel_id=1, source_target_pairs={{0,24},{8,16},{16,8},{24,0},{1,25},{9,17},{17,9},{25,1},{2,26},{10... | collective-permute-start | bytes 1105928 | tf_op jit(solution)/shard_map/ppermute | solution.py:549
  53.5 16.7 %collective-permute-start.9 = (bf16[4,40,1152]{2,1,0:T(8,128)(2,1)S(1)}, bf16[4,40,1152]{2,1,0:T(8,128)(2,1)S(1)}, u32[]{:S(2)}, u32[]{:S(2)}) collective-permute-start(bf16[4,40,1152]{2,1,0:T(8,128)(2,1)S(1)} %get-tuple-element.40.first), channel_id=1, source_target_pairs={{0,8},{8,0},{16,24},{24,16},{1,9},{9,1},{17,25},{25,17},{2,10},{10... | collective-permute-start | bytes 1105928 | tf_op jit(solution)/shard_map/ppermute | solution.py:549
  56.8 3.5 %copy-start.18 = (bf16[1152,1728]{0,1:T(8,128)(2,1)S(1)}, bf16[1152,1728]{0,1:T(8,128)(2,1)}, u32[]{:S(2)}) copy-start(bf16[1152,1728]{0,1:T(8,128)(2,1)} %param.5) | copy-start | bytes 11943940
  60.2 10.2 %collective-permute-start.15 = (bf16[576,1152]{1,0:T(8,128)(2,1)S(1)}, bf16[576,1152]{1,0:T(8,128)(2,1)S(1)}, u32[]{:S(2)}, u32[]{:S(2)}) collective-permute-start(bf16[576,1152]{1,0:T(8,128)(2,1)S(1)} %get-tuple-element.53), channel_id=1, source_target_pairs={{0,1},{1,0},{2,3},{3,2},{4,5},{5,4},{6,7},{7,6},{8,9},{9,8},{10,11... | collective-permute-start | bytes 3981320 | tf_op jit(solution)/shard_map/ppermute | solution.py:430
  62.9 7.6 %copy-start.4 = (bf16[512,1152]{1,0:T(8,128)(2,1)}, bf16[512,1152]{1,0:T(8,128)(2,1)S(1)}, u32[]{:S(2)}) copy-start(bf16[512,1152]{1,0:T(8,128)(2,1)S(1)} %convolution_convert_fusion.refs_2_) | copy-start | bytes 3538948
  64.1 7.8 %copy-start.5 = (bf16[512,1152]{1,0:T(8,128)(2,1)}, bf16[512,1152]{1,0:T(8,128)(2,1)S(1)}, u32[]{:S(2)}) copy-start(bf16[512,1152]{1,0:T(8,128)(2,1)S(1)} %convolution_convert_fusion.1.refs_1_) | copy-start | bytes 3538948
  71.9 0.7 copy-start.10
  72.6 11.7 %collective-permute-start.16 = (bf16[4,40,1152]{2,1,0:T(8,128)(2,1)}, bf16[4,40,1152]{2,1,0:T(8,128)(2,1)S(1)}, u32[]{:S(2)}, u32[]{:S(2)}) collective-permute-start(bf16[4,40,1152]{2,1,0:T(8,128)(2,1)} %get-tuple-element.54), channel_id=1, source_target_pairs={{0,8},{8,0},{16,24},{24,16},{1,9},{9,1},{17,25},{25,17},{2,10},{10... | collective-permute-start | bytes 1105928 | tf_op jit(solution)/shard_map/ppermute | solution.py:549
  74.1 17.3 %collective-permute-start.20 = (bf16[4,40,1152]{2,1,0:T(8,128)(2,1)}, bf16[4,40,1152]{2,1,0:T(8,128)(2,1)S(1)}, u32[]{:S(2)}, u32[]{:S(2)}) collective-permute-start(bf16[4,40,1152]{2,1,0:T(8,128)(2,1)} %get-tuple-element.57), channel_id=1, source_target_pairs={{0,16},{8,24},{16,0},{24,8},{1,17},{9,25},{17,1},{25,9},{2,18},{10... | collective-permute-start | bytes 1105928 | tf_op jit(solution)/shard_map/ppermute | solution.py:549
  75.6 15.8 %collective-permute-start.21 = (bf16[4,40,1152]{2,1,0:T(8,128)(2,1)}, bf16[4,40,1152]{2,1,0:T(8,128)(2,1)S(1)}, u32[]{:S(2)}, u32[]{:S(2)}) collective-permute-start(bf16[4,40,1152]{2,1,0:T(8,128)(2,1)} %get-tuple-element.58), channel_id=1, source_target_pairs={{0,24},{8,16},{16,8},{24,0},{1,25},{9,17},{17,9},{25,1},{2,26},{10... | collective-permute-start | bytes 1105928 | tf_op jit(solution)/shard_map/ppermute | solution.py:549
  76.2 20.7 %collective-permute-start.12 = (bf16[40,1152]{1,0:T(8,128)(2,1)S(1)}, bf16[40,1152]{1,0:T(8,128)(2,1)S(1)}, u32[]{:S(2)}, u32[]{:S(2)}) collective-permute-start(bf16[40,1152]{1,0:T(8,128)(2,1)S(1)} %get-tuple-element.70), channel_id=1, source_target_pairs={{0,2},{2,0},{4,6},{6,4},{1,3},{3,1},{5,7},{7,5},{8,10},{10,8},{12,... | collective-permute-start | bytes 276488 | tf_op jit(solution)/shard_map/ppermute | solution.py:549
  78.6 18.7 %collective-permute-start.13 = (bf16[40,1152]{1,0:T(8,128)(2,1)S(1)}, bf16[40,1152]{1,0:T(8,128)(2,1)S(1)}, u32[]{:S(2)}, u32[]{:S(2)}) collective-permute-start(bf16[40,1152]{1,0:T(8,128)(2,1)S(1)} %get-tuple-element.69), channel_id=1, source_target_pairs={{0,4},{2,6},{4,0},{6,2},{1,5},{3,7},{5,1},{7,3},{8,12},{10,14},{12... | collective-permute-start | bytes 276488 | tf_op jit(solution)/shard_map/ppermute | solution.py:549
  84.4 12.9 %collective-permute-start.14 = (bf16[40,1152]{1,0:T(8,128)(2,1)S(1)}, bf16[40,1152]{1,0:T(8,128)(2,1)S(1)}, u32[]{:S(2)}, u32[]{:S(2)}) collective-permute-start(bf16[40,1152]{1,0:T(8,128)(2,1)S(1)} %get-tuple-element.68), channel_id=1, source_target_pairs={{0,6},{2,4},{4,2},{6,0},{1,7},{3,5},{5,3},{7,1},{8,14},{10,12},{12... | collective-permute-start | bytes 276488 | tf_op jit(solution)/shard_map/ppermute | solution.py:549
  92.7 6.8 %collective-permute-start.22 = (bf16[40,1152]{1,0:T(8,128)(2,1)S(1)}, bf16[40,1152]{1,0:T(8,128)(2,1)S(1)}, u32[]{:S(2)}, u32[]{:S(2)}) collective-permute-start(bf16[40,1152]{1,0:T(8,128)(2,1)S(1)} %get-tuple-element.67), channel_id=1, source_target_pairs={{0,2},{2,0},{4,6},{6,4},{1,3},{3,1},{5,7},{7,5},{8,10},{10,8},{12,... | collective-permute-start | bytes 276488 | tf_op jit(solution)/shard_map/ppermute | solution.py:549
  94.8 6.6 %collective-permute-start.23 = (bf16[40,1152]{1,0:T(8,128)(2,1)S(1)}, bf16[40,1152]{1,0:T(8,128)(2,1)S(1)}, u32[]{:S(2)}, u32[]{:S(2)}) collective-permute-start(bf16[40,1152]{1,0:T(8,128)(2,1)S(1)} %get-tuple-element.66), channel_id=1, source_target_pairs={{0,4},{2,6},{4,0},{6,2},{1,5},{3,7},{5,1},{7,3},{8,12},{10,14},{12... | collective-permute-start | bytes 276488 | tf_op jit(solution)/shard_map/ppermute | solution.py:549
  96.8 6.5 %collective-permute-start.24 = (bf16[40,1152]{1,0:T(8,128)(2,1)S(1)}, bf16[40,1152]{1,0:T(8,128)(2,1)S(1)}, u32[]{:S(2)}, u32[]{:S(2)}) collective-permute-start(bf16[40,1152]{1,0:T(8,128)(2,1)S(1)} %get-tuple-element.65), channel_id=1, source_target_pairs={{0,6},{2,4},{4,2},{6,0},{1,7},{3,5},{5,3},{7,1},{8,14},{10,12},{12... | collective-permute-start | bytes 276488 | tf_op jit(solution)/shard_map/ppermute | solution.py:549
  97.3 8.2 %collective-permute-start.17 = (bf16[40,1152]{1,0:T(8,128)(2,1)S(1)}, bf16[40,1152]{1,0:T(8,128)(2,1)S(1)}, u32[]{:S(2)}, u32[]{:S(2)}) collective-permute-start(bf16[40,1152]{1,0:T(8,128)(2,1)S(1)} %row_sum.1.refs_0_), channel_id=1, source_target_pairs={{0,8},{8,0},{16,24},{24,16},{1,9},{9,1},{17,25},{25,17},{2,10},{10... | collective-permute-start | bytes 276488 | tf_op jit(solution)/shard_map/ppermute | solution.py:549
  98.6 8.3 %collective-permute-start.18 = (bf16[40,1152]{1,0:T(8,128)(2,1)S(1)}, bf16[40,1152]{1,0:T(8,128)(2,1)S(1)}, u32[]{:S(2)}, u32[]{:S(2)}) collective-permute-start(bf16[40,1152]{1,0:T(8,128)(2,1)S(1)} %row_sum.1.refs_0_), channel_id=1, source_target_pairs={{0,16},{8,24},{16,0},{24,8},{1,17},{9,25},{17,1},{25,9},{2,18},{10... | collective-permute-start | bytes 276488 | tf_op jit(solution)/shard_map/ppermute | solution.py:549
  99.4 7.5 %collective-permute-start.19 = (bf16[40,1152]{1,0:T(8,128)(2,1)S(1)}, bf16[40,1152]{1,0:T(8,128)(2,1)S(1)}, u32[]{:S(2)}, u32[]{:S(2)}) collective-permute-start(bf16[40,1152]{1,0:T(8,128)(2,1)S(1)} %row_sum.1.refs_0_), channel_id=1, source_target_pairs={{0,24},{8,16},{16,8},{24,0},{1,25},{9,17},{17,9},{25,1},{2,26},{10... | collective-permute-start | bytes 276488 | tf_op jit(solution)/shard_map/ppermute | solution.py:549
  103.4 4.6 %collective-permute-start.25 = (bf16[40,1152]{1,0:T(8,128)(2,1)S(1)}, bf16[40,1152]{1,0:T(8,128)(2,1)S(1)}, u32[]{:S(2)}, u32[]{:S(2)}) collective-permute-start(bf16[40,1152]{1,0:T(8,128)(2,1)S(1)} %add_convert_fusion.2.refs_4_), channel_id=1, source_target_pairs={{0,8},{8,0},{16,24},{24,16},{1,9},{9,1},{17,25},{25,17},{2,10},{10... | collective-permute-start | bytes 276488 | tf_op jit(solution)/shard_map/ppermute | solution.py:549
  104.7 4.6 %collective-permute-start.26 = (bf16[40,1152]{1,0:T(8,128)(2,1)S(1)}, bf16[40,1152]{1,0:T(8,128)(2,1)S(1)}, u32[]{:S(2)}, u32[]{:S(2)}) collective-permute-start(bf16[40,1152]{1,0:T(8,128)(2,1)S(1)} %add_convert_fusion.2.refs_4_), channel_id=1, source_target_pairs={{0,16},{8,24},{16,0},{24,8},{1,17},{9,25},{17,1},{25,9},{2,18},{10... | collective-permute-start | bytes 276488 | tf_op jit(solution)/shard_map/ppermute | solution.py:549
  105.5 5.5 %collective-permute-start.27 = (bf16[40,1152]{1,0:T(8,128)(2,1)S(1)}, bf16[40,1152]{1,0:T(8,128)(2,1)S(1)}, u32[]{:S(2)}, u32[]{:S(2)}) collective-permute-start(bf16[40,1152]{1,0:T(8,128)(2,1)S(1)} %add_convert_fusion.2.refs_4_), channel_id=1, source_target_pairs={{0,24},{8,16},{16,8},{24,0},{1,25},{9,17},{17,9},{25,1},{2,26},{10... | collective-permute-start | bytes 276488 | tf_op jit(solution)/shard_map/ppermute | solution.py:549
